TPU v7x, 512 devices: a whole 4x4x16 slice. The times are simulated.
512 devices in a mesh: dp: 32 (over x, z_lo, core), owner: 16 (over z_hi, y).
Axes of the slice: x: 4, y: 4, z: 16 (z_hi: 4, z_lo: 4; z = z_hi * 4 + z_lo), core: 2. Of those that a mesh axis runs over, the one named last changes fastest.
Arguments:
- feats: bfloat16 [4, 32, 32, 80, 128], P(None, 'dp', 'owner'), may hold values from -16 to 16
- top_grad: bfloat16 [32, 32, 80, 128], P('dp', 'owner'), may hold values from -6 to 6
- weights: bfloat16 [4, 1152, 128], replicated, may hold values from -0.1875 to 0.1875
- table: int32 [4], replicated, may hold values from 0 to 15, as said below
- a_inv: bfloat16 [16, 1152, 1152], P('owner', 'dp'), may hold values from -3 to 3
- g_inv: float32 [16, 128, 128], P('owner'), may hold values from -3 to 3
Outputs:
- step: bfloat16 [4, 1152, 128], P(None, 'dp')
- a_stat: float32 [16, 1152, 1152], P('owner', 'dp')
- g_stat: float32 [16, 128, 128], P('owner')
- in_grad: bfloat16 [32, 32, 80, 128], P('dp', 'owner')
Inputs may be any that keep to these rules, and one draw needn't show every extreme that they name: `table`: 4 distinct owner indices; 0 and 15 are always among them.
All inputs are finite; a program needn't handle non-finite values.
Results may differ from a plain program's by a relative error of at most 0.023.
Values may be sent and summed in bfloat16 or wider, within the bound.
No kernel may reach another device: no remote copies, remote signals or barrier semaphores. Data moves between devices by JAX's collectives and lax.ppermute only.
A program may use at most 64 MiB of HBM per device.

v0:
```python
import jax
import jax.numpy as jnp
from jax import lax
from jax.sharding import PartitionSpec as P


def extended(cells, sides, width):
    for axis, dim in sides:
        count = lax.axis_size(axis)
        ends = count - 1
        head = lax.slice_in_dim(cells, 0, width, axis=dim)
        tail = lax.slice_in_dim(cells, cells.shape[dim] - width, cells.shape[dim], axis=dim)
        cells = jnp.concatenate(
            [
                lax.ppermute(tail, axis, [(i, (i + 1) % count) for i in range(ends)]),
                cells,
                lax.ppermute(head, axis, [((i + 1) % count, i) for i in range(ends)]),
            ],
            axis=dim,
        )
    return cells


def broadcast(x, axis, root):
    mine = lax.axis_index(axis) == root
    return lax.psum(jnp.where(mine, x, jnp.zeros_like(x)), axis)


def to_columns(padded, rows, width):
    taps = [padded[ky : ky + rows, kx : kx + width] for ky in range(3) for kx in range(3)]
    joined = jnp.concatenate(taps, axis=-1)
    return joined.reshape(rows * width, joined.shape[-1])


def back_columns(padded, rows, width):
    taps = [
        padded[2 - ky : 2 - ky + rows, 2 - kx : 2 - kx + width]
        for ky in range(3)
        for kx in range(3)
    ]
    joined = jnp.concatenate(taps, axis=-1)
    return joined.reshape(rows * width, joined.shape[-1])


def silu_slope(value):
    sig = jax.nn.sigmoid(value)
    return sig * (1.0 + value * (1.0 - sig))


def inner_rows(left, right):
    return lax.dot_general(
        left, right, (((0,), (0,)), ((), ())), preferred_element_type=jnp.float32
    )


def shards(feats, top_grad, weights, table, a_inv, g_inv):
    num_layers, _, rows_dev, width, chans = feats.shape
    owners = lax.axis_size("owner")
    owner_id = lax.axis_index("owner")
    height = rows_dev * owners
    npos = lax.axis_size("dp") * height * width
    patch = 9 * chans
    images = lax.all_gather(feats, "owner", axis=2, tiled=True)[:, 0]
    padded = jnp.pad(images, ((0, 0), (1, 1), (1, 1), (0, 0)))
    owned = table == owner_id
    have = jnp.any(owned).astype(jnp.float32)
    layer_ids = jnp.arange(num_layers, dtype=jnp.int32)
    lay = jnp.sum(jnp.where(owned, layer_ids, 0))
    mine = lax.dynamic_index_in_dim(padded, lay, 0, keepdims=False)
    full_cols = to_columns(mine, height, width)
    a_rows = lax.psum_scatter(
        inner_rows(full_cols, full_cols).astype(jnp.bfloat16), "dp", scatter_dimension=0, tiled=True
    ).astype(jnp.float32)
    a_out = (a_rows * (have / npos))[None]
    strips = lax.dynamic_slice_in_dim(padded, owner_id * rows_dev, rows_dev + 2, 1)
    flipped = jnp.transpose(weights.reshape(num_layers, 9, chans, chans), (0, 1, 3, 2)).reshape(
        num_layers, patch, chans
    )
    grad_in = top_grad[0].reshape(rows_dev * width, chans)
    dpres = [None] * num_layers
    grad_parts = [None] * num_layers
    fac_parts = [None] * num_layers
    for step_idx in range(num_layers):
        layer = num_layers - 1 - step_idx
        cols = to_columns(strips[layer], rows_dev, width)
        pre = jnp.dot(cols, weights[layer], preferred_element_type=jnp.float32)
        dpre = (grad_in.astype(jnp.float32) * silu_slope(pre)).astype(jnp.bfloat16)
        dpres[layer] = dpre
        grad_parts[layer] = inner_rows(cols, dpre)
        fac_parts[layer] = inner_rows(dpre, dpre)
        rimmed = extended(dpre.reshape(rows_dev, width, chans), (("owner", 0),), 1)
        rimmed = jnp.pad(rimmed, ((0, 0), (1, 1), (0, 0)))
        grad_in = jnp.dot(
            back_columns(rimmed, rows_dev, width),
            flipped[layer],
            preferred_element_type=jnp.float32,
        ).astype(jnp.bfloat16)
    in_grad = grad_in.reshape(1, rows_dev, width, chans)
    summed_grads, summed_facs = lax.psum(
        (jnp.stack(grad_parts), jnp.stack(fac_parts)), ("dp", "owner")
    )
    grad_mine = lax.dynamic_index_in_dim(summed_grads, lay, 0, keepdims=False)
    fac_mine = lax.dynamic_index_in_dim(summed_facs, lay, 0, keepdims=False)
    grad_scaled = grad_mine / jnp.sqrt(jnp.float32(npos))
    g_out = (fac_mine * (have / npos))[None]
    mixed = jnp.dot(grad_scaled, g_inv[0], precision=lax.Precision.HIGHEST)
    panel = jnp.dot(a_inv[0].astype(jnp.float32), mixed, precision=lax.Precision.HIGHEST)
    panel_low = panel.astype(jnp.bfloat16)
    step_out = jnp.stack(
        [broadcast(panel_low, "owner", table[layer]) for layer in range(num_layers)]
    )
    return (step_out, a_out, g_out, in_grad)


def solution(mesh):
    placed = (
        P(None, "dp", "owner", None, None),
        P("dp", "owner", None, None),
        P(),
        P(),
        P("owner", "dp", None),
        P("owner", None, None),
    )
    return jax.shard_map(
        shards,
        mesh=mesh,
        in_specs=placed,
        out_specs=(
            P(None, "dp", None),
            P("owner", "dp", None),
            P("owner", None, None),
            P("dp", "owner", None, None),
        ),
        check_vma=False,
    )
```

profile of v0, /device:TPU:6, one launch (start us, length us, event | category | flops | bytes accessed | tf_op | source)
XLA Modules:
  0.0 866.7 jit_solution(15440491272292147856)
XLA Ops:
  21.0 101.2 %all-gather.2.cloned.1.call-done = bf16[4,1,32,80,128]{4,3,2,1,0:T(8,128)(2,1)} async-done(((bf16[4,1,2,80,128]{4,3,2,1,0:T(8,128)(2,1)}), bf16[4,1,32,80,128]{4,3,2,1,0:T(8,128)(2,1)}) %all-gather.2.cloned.1.call-update) | async-done | bytes 2621456 | tf_op jit(solution)/shard_map/all_gather | solution.py:63
  127.6 9.4 %fusion.1 = bf16[1152,1152]{1,0:T(8,128)(2,1)} fusion(bf16[32,80,1152]{2,1,0:T(8,128)(2,1)S(1)} %slice_dynamic-update-slice_fusion), kind=kOutput, calls=%fused_computation.1 | convolution fusion | flops 6796099584 | bytes 8552448 | tf_op jit(solution)/shard_map/dot_general | solution.py:51
  137.0 73.2 %fusion = bf16[48,1152]{1,0:T(8,128)(2,1)S(1)} fusion(bf16[1152,1152]{1,0:T(8,128)(2,1)} %fusion.1), kind=kCustom, calls=%all-reduce-scatter | all-reduce-scatter fusion | flops 1769473 | bytes 2766848
  210.2 9.0 %collective-permute-start.14 = (bf16[48,1152]{1,0:T(8,128)(2,1)S(1)}, bf16[48,1152]{1,0:T(8,128)(2,1)}, u32[]{:S(2)}, u32[]{:S(2)}) collective-permute-start(bf16[48,1152]{1,0:T(8,128)(2,1)S(1)} %fusion), channel_id=1, source_target_pairs={{0,112},{16,128},{32,144},{48,160},{64,176},{80,192},{96,208},{112... | collective-permute-start | bytes 331784
  219.2 1.9 collective-permute-start.13
  221.1 1.9 collective-permute-start.12
  223.3 3.3 collective-permute-start
  229.1 3.4 collective-permute-done.1
  233.4 3.4 collective-permute-start.2
  238.3 4.2 collective-permute-done.3
  243.4 8.6 collective-permute-start.4
  253.5 4.2 collective-permute-done.5
  258.8 7.9 collective-permute-start.6
  270.5 1.9 collective-permute-start.11
  274.0 6.4 collective-permute-done.15
  280.5 1.9 collective-permute-start.10
  282.4 2.0 collective-permute-start.9
  284.4 2.9 collective-permute-start.8
  288.2 2.0 collective-permute-done.10
  290.2 2.7 collective-permute-done.9
  294.1 4.4 concatenate.184
  299.5 459.4 %all-reduce.11.cloned.1.call-done = (f32[4,1152,128]{2,1,0:T(8,128)}, f32[4,128,128]{2,1,0:T(8,128)}) async-done(((f32[4,1152,128]{2,1,0:T(8,128)}, f32[4,128,128]{2,1,0:T(8,128)}), (f32[4,1152,128]{2,1,0:T(8,128)}, f32[4,128,128]{2,1,0:T(8,128)})) %all-reduce.11.cloned.1.call-update) | async-done | bytes 2621456 | tf_op jit(solution)/shard_map/psum | solution.py:99
  760.4 1.7 fusion.12
  762.4 96.8 %all-reduce.8 = (bf16[1,36,128]{2,1,0:T(8,128)(2,1)S(1)}, bf16[1,36,128]{2,1,0:T(8,128)(2,1)S(1)}, bf16[1,36,128]{2,1,0:T(8,128)(2,1)S(1)}, bf16[1,36,128]{2,1,0:T(8,128)(2,1)S(1)}) all-reduce(bf16[1,36,128]{2,1,0:T(8,128)(2,1)S(1)} %get-tuple-element.75, ...), channel_id=1, replica_groups=mesh['dp'=32,'owner'=16] {'owner'}, use_global_device_ids=true, to_apply=%region_5.6 | all-reduce | flops 18432 | bytes 73728 | tf_op jit(solution)/shard_map/psum | solution.py:26
  (164 shorter events, 32.3 us)
Async XLA Ops:
  7.2 754.9 %copy-start = (bf16[1,36,1152]{2,1,0:T(8,128)(2,1)S(1)}, bf16[1,36,1152]{2,1,0:T(8,128)(2,1)}, u32[]{:S(2)}) copy-start(bf16[1,36,1152]{2,1,0:T(8,128)(2,1)} %param.10) | copy-start | bytes 248836
  7.2 12.6 %copy-start.5 = (s32[4]{0:T(128)S(1)}, s32[4]{0:T(128)}, u32[]{:S(2)}) copy-start(s32[4]{0:T(128)} %param.9) | copy-start | bytes 52
  7.2 115.0 %all-gather.2.cloned.1.call-start = ((), (), s32[]{:S(2)}) async-start(), calls=%async_computation | async-start | bytes 2785280 | tf_op jit(solution)/shard_map/all_gather | solution.py:63
  7.9 751.0 %all-reduce.11.cloned.1.call-start = ((), (), s32[]{:S(2)}) async-start(), calls=%async_computation.1 | async-start | bytes 5242880 | tf_op jit(solution)/shard_map/psum | solution.py:99
  15.7 108.2 %copy-start.2 = (bf16[4,1152,128]{2,1,0:T(8,128)(2,1)S(1)}, bf16[4,1152,128]{2,1,0:T(8,128)(2,1)}, u32[]{:S(2)}) copy-start(bf16[4,1152,128]{2,1,0:T(8,128)(2,1)} %param.8) | copy-start | bytes 3538948
  15.7 108.2 %copy-start.6 = (bf16[1,2,80,128]{3,2,1,0:T(8,128)(2,1)S(1)}, bf16[1,2,80,128]{3,2,1,0:T(8,128)(2,1)}, u32[]{:S(2)}) copy-start(bf16[1,2,80,128]{3,2,1,0:T(8,128)(2,1)} %param.7) | copy-start | bytes 122884
  210.2 22.6 %copy-start.3 = (bf16[1,9,128,128]{3,2,1,0:T(8,128)(2,1)S(1)}, bf16[1,9,128,128]{3,2,1,0:T(8,128)(2,1)}, u32[]{:S(2)}) copy-start(bf16[1,9,128,128]{3,2,1,0:T(8,128)(2,1)} %copy.20) | copy-start | bytes 884740
  210.2 72.2 %collective-permute-start.14 = (bf16[48,1152]{1,0:T(8,128)(2,1)S(1)}, bf16[48,1152]{1,0:T(8,128)(2,1)}, u32[]{:S(2)}, u32[]{:S(2)}) collective-permute-start(bf16[48,1152]{1,0:T(8,128)(2,1)S(1)} %fusion), channel_id=1, source_target_pairs={{0,112},{16,128},{32,144},{48,160},{64,176},{80,192},{96,208},{112... | collective-permute-start | bytes 331784
  219.2 65.2 %collective-permute-start.13 = (bf16[48,1152]{1,0:T(8,128)(2,1)S(1)}, bf16[48,1152]{1,0:T(8,128)(2,1)}, u32[]{:S(2)}, u32[]{:S(2)}) collective-permute-start(bf16[48,1152]{1,0:T(8,128)(2,1)S(1)} %fusion), channel_id=1, source_target_pairs={{0,96},{16,112},{32,128},{48,144},{64,160},{80,176},{96,192},{112,... | collective-permute-start | bytes 331784
  221.1 67.1 %collective-permute-start.12 = (bf16[48,1152]{1,0:T(8,128)(2,1)S(1)}, bf16[48,1152]{1,0:T(8,128)(2,1)}, u32[]{:S(2)}, u32[]{:S(2)}) collective-permute-start(bf16[48,1152]{1,0:T(8,128)(2,1)S(1)} %fusion), channel_id=1, source_target_pairs={{0,80},{16,96},{32,112},{48,128},{64,144},{80,160},{96,176},{112,1... | collective-permute-start | bytes 331784
  223.3 5.8 collective-permute-start
  226.6 5.9 collective-permute-start.1
  233.4 4.9 collective-permute-start.2
  236.8 5.7 collective-permute-start.3
  243.4 10.1 %collective-permute-start.4 = (bf16[1,80,128]{2,1,0:T(8,128)(2,1)S(1)}, bf16[1,80,128]{2,1,0:T(8,128)(2,1)S(1)}, u32[]{:S(2)}, u32[]{:S(2)}) collective-permute-start(bf16[1,80,128]{2,1,0:T(8,128)(2,1)S(1)} %get-tuple-element.64), channel_id=1, source_target_pairs={{0,1},{1,2},{2,3},{3,4},{4,5},{5,6},{6,7},{7,8},{8,9},{9,10},{10,1... | collective-permute-start | bytes 61448 | tf_op jit(solution)/shard_map/ppermute | solution.py:15
  252.0 5.7 collective-permute-start.5
  258.8 11.7 %collective-permute-start.6 = (bf16[1,80,128]{2,1,0:T(8,128)(2,1)S(1)}, bf16[1,80,128]{2,1,0:T(8,128)(2,1)S(1)}, u32[]{:S(2)}, u32[]{:S(2)}) collective-permute-start(bf16[1,80,128]{2,1,0:T(8,128)(2,1)S(1)} %get-tuple-element.60), channel_id=1, source_target_pairs={{0,1},{1,2},{2,3},{3,4},{4,5},{5,6},{6,7},{7,8},{8,9},{9,10},{10,1... | collective-permute-start | bytes 61448 | tf_op jit(solution)/shard_map/ppermute | solution.py:15
  266.8 5.7 collective-permute-start.7
  270.5 489.9 %copy-start.4 = (f32[1,128,128]{2,1,0:T(8,128)S(1)}, f32[1,128,128]{2,1,0:T(8,128)}, u32[]{:S(2)}) copy-start(f32[1,128,128]{2,1,0:T(8,128)} %param.11) | copy-start | bytes 196612
  270.5 17.7 %collective-permute-start.11 = (bf16[48,1152]{1,0:T(8,128)(2,1)S(1)}, bf16[48,1152]{1,0:T(8,128)(2,1)S(1)}, u32[]{:S(2)}, u32[]{:S(2)}) collective-permute-start(bf16[48,1152]{1,0:T(8,128)(2,1)S(1)} %fusion), channel_id=1, source_target_pairs={{0,64},{16,80},{32,96},{48,112},{64,128},{80,144},{96,160},{112,17... | collective-permute-start | bytes 331784
  272.5 8.0 collective-permute-start.15
  280.5 9.8 %collective-permute-start.10 = (bf16[48,1152]{1,0:T(8,128)(2,1)S(1)}, bf16[48,1152]{1,0:T(8,128)(2,1)S(1)}, u32[]{:S(2)}, u32[]{:S(2)}) collective-permute-start(bf16[48,1152]{1,0:T(8,128)(2,1)S(1)} %fusion), channel_id=1, source_target_pairs={{0,48},{16,64},{32,80},{48,96},{64,112},{80,128},{96,144},{112,160... | collective-permute-start | bytes 331784
  282.4 10.6 %collective-permute-start.9 = (bf16[48,1152]{1,0:T(8,128)(2,1)S(1)}, bf16[48,1152]{1,0:T(8,128)(2,1)S(1)}, u32[]{:S(2)}, u32[]{:S(2)}) collective-permute-start(bf16[48,1152]{1,0:T(8,128)(2,1)S(1)} %fusion), channel_id=1, source_target_pairs={{0,32},{16,48},{32,64},{48,80},{64,96},{80,112},{96,128},{112,144}... | collective-permute-start | bytes 331784
  284.4 9.7 %collective-permute-start.8 = (bf16[48,1152]{1,0:T(8,128)(2,1)S(1)}, bf16[48,1152]{1,0:T(8,128)(2,1)S(1)}, u32[]{:S(2)}, u32[]{:S(2)}) collective-permute-start(bf16[48,1152]{1,0:T(8,128)(2,1)S(1)} %fusion), channel_id=1, source_target_pairs={{0,16},{16,32},{32,48},{48,64},{64,80},{80,96},{96,112},{112,128},... | collective-permute-start | bytes 331784
  (1 other events, 2.9 us)
Sparse Core Ops, SparseCore 0:
  11.0 111.1 all-gather.1
  270.6 488.2 all-reduce.10
where the time goes:
time: 868 us; the launch traced here: 867 us
  waiting for transfers between devices  585 us (67%)
  blocking collectives  170 us (20%)
  starting transfers between devices  51.3 us (6%)
  between operations  20.6 us (2%)
  local copies, waits for them, and re-layouts  17.1 us (2%)
  matrix products  16.3 us (2%)
    psum x1, waiting for transfers between devices, shards(): lax.psum((jnp.stack(grad_parts), jnp.stack(fac_parts)), ('dp', 'owner'))  459 us
    all_gather x1, waiting for transfers between devices, shards(): images = lax.all_gather(feats, 'owner', axis=2, tiled=True)[:, 0]  101 us
    psum x1, blocking collectives, broadcast(): return lax.psum(jnp.where(mine, x, jnp.zeros_like(x)), axis)  96.8 us
    unnamed x1, blocking collectives  73.2 us
    ppermute x4, starting transfers between devices, extended(): lax.ppermute(tail, axis, [(i, (i + 1) % count) for i in range(ends)])  23.2 us
    unnamed x8, starting transfers between devices  22.8 us
  transfers between devices with their start and end apart: 18, of which 9 were waited for; matrix products, arithmetic and copies ran while one was open for 2% of the time, Pallas kernels for 0%

commit v1 on v0

v1 whole, which is shorter than its diff:
```python
import jax
import jax.numpy as jnp
from jax import lax
from jax.sharding import PartitionSpec as P

Y = 4
Z_HI = 4


def halo(cells, width, dim):
    count = lax.axis_size("owner")
    head = lax.slice_in_dim(cells, 0, width, axis=dim)
    tail = lax.slice_in_dim(cells, cells.shape[dim] - width, cells.shape[dim], axis=dim)
    above = lax.ppermute(tail, "owner", [(i, i + 1) for i in range(count - 1)])
    below = lax.ppermute(head, "owner", [(i + 1, i) for i in range(count - 1)])
    return jnp.concatenate([above, cells, below], axis=dim)


def along_y(x, shift):
    pairs = [(z * Y + y, z * Y + (y + shift) % Y) for z in range(Z_HI) for y in range(Y)]
    return lax.ppermute(x, "owner", pairs)


def along_z(x, shift):
    pairs = [(z * Y + y, (z + shift) % Z_HI * Y + y) for z in range(Z_HI) for y in range(Y)]
    return lax.ppermute(x, "owner", pairs)


def to_columns(padded, rows, width):
    taps = [padded[ky : ky + rows, kx : kx + width] for ky in range(3) for kx in range(3)]
    joined = jnp.concatenate(taps, axis=-1)
    return joined.reshape(rows * width, joined.shape[-1])


def back_columns(padded, rows, width):
    taps = [
        padded[2 - ky : 2 - ky + rows, 2 - kx : 2 - kx + width]
        for ky in range(3)
        for kx in range(3)
    ]
    joined = jnp.concatenate(taps, axis=-1)
    return joined.reshape(rows * width, joined.shape[-1])


def silu_slope(value):
    sig = jax.nn.sigmoid(value)
    return sig * (1.0 + value * (1.0 - sig))


def inner_rows(left, right):
    return lax.dot_general(
        left, right, (((0,), (0,)), ((), ())), preferred_element_type=jnp.float32
    )


def block_classes():
    found = {}
    pairs = []
    where = {}
    for a in range(9):
        for b in range(9):
            first, second, flip = a, b, False
            dy, dx = b // 3 - a // 3, b % 3 - a % 3
            if dy < 0 or (dy == 0 and dx < 0):
                first, second, flip = b, a, True
                dy, dx = -dy, -dx
            key = (dy, dx, first // 3 if dy == 0 else -1, first % 3 if dx == 0 else -1)
            if key not in found:
                found[key] = len(pairs)
                pairs.append((first, second))
            where[a, b] = (found[key], flip)
    return pairs, where


PAIRS, WHERE = block_classes()
NG = len(PAIRS)
NBLOCKS = 40


def shards(feats, top_grad, weights, table, a_inv, g_inv):
    num_layers, _, rows_dev, width, chans = feats.shape
    owners = lax.axis_size("owner")
    samples = lax.axis_size("dp")
    owner_id = lax.axis_index("owner")
    dp_id = lax.axis_index("dp")
    y_id = owner_id % Y
    z_id = owner_id // Y
    npos = samples * rows_dev * owners * width
    patch = 9 * chans
    strips = halo(feats[:, 0], 1, 1)
    strips = jnp.pad(strips, ((0, 0), (0, 0), (1, 1), (0, 0)))
    layer_strips = [lax.dynamic_index_in_dim(strips, y_id, 0, keepdims=False)]
    for s in range(1, Y):
        out = lax.dynamic_index_in_dim(strips, (y_id + s) % Y, 0, keepdims=False)
        layer_strips.append(along_y(out, s))

    flipped = jnp.transpose(weights.reshape(num_layers, 9, chans, chans), (0, 1, 3, 2)).reshape(
        num_layers, patch, chans
    )
    grad_in = top_grad[0].reshape(rows_dev * width, chans)
    dpres = [None] * num_layers
    for step_idx in range(num_layers):
        layer = num_layers - 1 - step_idx
        cols = to_columns(strips[layer], rows_dev, width)
        pre = jnp.dot(cols, weights[layer], preferred_element_type=jnp.float32)
        dpre = (grad_in.astype(jnp.float32) * silu_slope(pre)).astype(jnp.bfloat16)
        dpres[layer] = dpre
        rimmed = halo(dpre.reshape(rows_dev, width, chans), 1, 0)
        rimmed = jnp.pad(rimmed, ((0, 0), (1, 1), (0, 0)))
        grad_in = jnp.dot(
            back_columns(rimmed, rows_dev, width),
            flipped[layer],
            preferred_element_type=jnp.float32,
        ).astype(jnp.bfloat16)
    in_grad = grad_in.reshape(1, rows_dev, width, chans)

    all_dpre = jnp.stack(dpres)
    layer_dpre = [lax.dynamic_index_in_dim(all_dpre, y_id, 0, keepdims=False)]
    for s in range(1, Y):
        out = lax.dynamic_index_in_dim(all_dpre, (y_id + s) % Y, 0, keepdims=False)
        layer_dpre.append(along_y(out, s))

    big_cols = jnp.concatenate([to_columns(s, rows_dev, width) for s in layer_strips], axis=0)
    big_dpre = jnp.concatenate(layer_dpre, axis=0)
    gram = inner_rows(big_cols, big_cols).astype(jnp.bfloat16)
    grad = inner_rows(big_cols, big_dpre).astype(jnp.bfloat16)
    gfac = inner_rows(big_dpre, big_dpre).astype(jnp.bfloat16)
    blocks = [
        gram[a * chans : (a + 1) * chans, b * chans : (b + 1) * chans] for a, b in PAIRS
    ]
    pad = jnp.zeros(((NBLOCKS - NG - 10) * chans, chans), jnp.bfloat16)
    parts = jnp.concatenate(blocks + [grad, gfac, pad], axis=0)

    piece = lax.psum_scatter(parts, "dp", scatter_dimension=0, tiled=True)

    held = jnp.stack([piece] + [along_y(piece, s) for s in range(1, Y)])
    layer_ids = jnp.arange(num_layers, dtype=jnp.int32)

    def pick(z):
        owned = table == (z % Z_HI) * Y + y_id
        lay = jnp.sum(jnp.where(owned, layer_ids, 0))
        return lax.dynamic_index_in_dim(held, (y_id - lay) % Y, 0, keepdims=False)

    total = pick(z_id).astype(jnp.float32)
    for t in range(1, Z_HI):
        total = total + along_z(pick(z_id + t), t).astype(jnp.float32)
    summed = lax.all_gather(total.astype(jnp.bfloat16), "dp", axis=0, tiled=True)

    summed = summed.reshape(NBLOCKS, chans, chans)
    have = jnp.any(table == owner_id).astype(jnp.float32)
    turned = jnp.swapaxes(summed[:NG], 1, 2)
    factor = jnp.concatenate(
        [
            jnp.concatenate(
                [turned[WHERE[a, b][0]] if WHERE[a, b][1] else summed[WHERE[a, b][0]] for b in range(9)],
                axis=1,
            )
            for a in range(9)
        ],
        axis=0,
    )
    rows_out = patch // samples
    a_rows = lax.dynamic_slice_in_dim(factor, dp_id * rows_out, rows_out, 0).astype(jnp.float32)
    a_out = (a_rows * (have / npos))[None]
    g_out = (summed[NG + 9].astype(jnp.float32) * (have / npos))[None]
    grad_sum = summed[NG : NG + 9].reshape(patch, chans).astype(jnp.float32)
    grad_scaled = grad_sum / jnp.sqrt(jnp.float32(npos))
    mixed = jnp.dot(grad_scaled, g_inv[0], precision=lax.Precision.HIGHEST)
    panel = jnp.dot(a_inv[0].astype(jnp.float32), mixed, precision=lax.Precision.HIGHEST)
    panels = lax.all_gather(panel.astype(jnp.bfloat16), "owner", axis=0)
    step_out = panels[table]
    return (step_out, a_out, g_out, in_grad)


def solution(mesh):
    placed = (
        P(None, "dp", "owner", None, None),
        P("dp", "owner", None, None),
        P(),
        P(),
        P("owner", "dp", None),
        P("owner", None, None),
    )
    return jax.shard_map(
        shards,
        mesh=mesh,
        in_specs=placed,
        out_specs=(
            P(None, "dp", None),
            P("owner", "dp", None),
            P("owner", None, None),
            P("dp", "owner", None, None),
        ),
        check_vma=False,
    )
```

time: 868 us -> 418 us (0.48)
  waiting for transfers between devices: 585 us -> 217 us
  blocking collectives: 170 us -> 52.9 us
  starting transfers between devices: 51.3 us -> 103 us
  matrix products: 16.3 us -> 6.97 us
    psum x1 -> x0, waiting for transfers between devices: 459 us -> none  [shards(): lax.psum((jnp.stack(grad_parts), jnp.stack(fac_parts)), ('dp', 'owner'))]
    reduce_scatter x0 -> x1, waiting for transfers between devices: none -> 129 us  [shards(): piece = lax.psum_scatter(parts, 'dp', scatter_dimension=0, tiled=True)]
    psum x1 -> x0, blocking collectives: 96.8 us -> none  [broadcast(): return lax.psum(jnp.where(mine, x, jnp.zeros_like(x)), axis)]
    ppermute x8 -> x22, starting transfers between devices: 28.4 us -> 103 us  [the longest x9 43.5 us: along_y(): return lax.ppermute(x, 'owner', pairs)]
    unnamed x1 -> x0, blocking collectives: 73.2 us -> none
    all_gather x0 -> x1, blocking collectives: none -> 52.9 us  [shards(): panels = lax.all_gather(panel.astype(jnp.bfloat16), 'owner', axis=0)]
    all_gather x1, waiting for transfers between devices: 101 us -> 68.7 us  [shards(): lax.all_gather(total.astype(jnp.bfloat16), 'dp', axis=0, tiled=True)]
    unnamed x8 -> x0, starting transfers between devices: 22.8 us -> none
  transfers between devices with their start and end apart: 18 -> 24, of which waited for: 9 -> 8; matrix products, arithmetic and copies ran while one was open for 2% -> 2% of each run, Pallas kernels for 0% -> 0%
where the time goes in v1:
time: 418 us; the launch traced here: 416 us
  waiting for transfers between devices  217 us (52%)
  starting transfers between devices  103 us (25%)
  blocking collectives  52.9 us (13%)
  between operations  19.2 us (5%)
  local copies, waits for them, and re-layouts  13.1 us (3%)
  matrix products  6.97 us (2%)
    reduce_scatter x1, waiting for transfers between devices, shards(): piece = lax.psum_scatter(parts, 'dp', scatter_dimension=0, tiled=True)  129 us
    all_gather x1, waiting for transfers between devices, shards(): lax.all_gather(total.astype(jnp.bfloat16), 'dp', axis=0, tiled=True)  68.7 us
    all_gather x1, blocking collectives, shards(): panels = lax.all_gather(panel.astype(jnp.bfloat16), 'owner', axis=0)  52.9 us
    ppermute x9, starting transfers between devices, along_y(): return lax.ppermute(x, 'owner', pairs)  43.5 us
    ppermute x5, starting transfers between devices, halo(): above = lax.ppermute(tail, 'owner', [(i, i + 1) for i in range(count - 1)])  32.7 us
    ppermute x3, starting transfers between devices, along_z(): return lax.ppermute(x, 'owner', pairs)  20.3 us
    ppermute x5, waiting for transfers between devices, halo(): below = lax.ppermute(head, 'owner', [(i + 1, i) for i in range(count - 1)])  17 us
  transfers between devices with their start and end apart: 24, of which 8 were waited for; matrix products, arithmetic and copies ran while one was open for 2% of the time, Pallas kernels for 0%

profile of v1, /device:TPU:6, one launch (start us, length us, event | category | flops | bytes accessed | tf_op | source)
XLA Modules:
  0.0 416.3 jit_solution(10331873268557318306)
XLA Ops:
  8.2 3.5 collective-permute-start
  15.1 2.9 collective-permute-done.1
  19.0 3.5 collective-permute-start.5
  25.0 7.3 %collective-permute-done.6 = bf16[1,80,128]{2,1,0:T(8,128)(2,1)S(1)} collective-permute-done((bf16[1,80,128]{2,1,0:T(8,128)(2,1)S(1)}, bf16[1,80,128]{2,1,0:T(8,128)(2,1)S(1)}, u32[]{:S(2)}, u32[]{:S(2)}) %collective-permute-start.6) | collective-permute-done | bytes 20512 | tf_op jit(solution)/shard_map/ppermute | solution.py:15
  32.8 14.7 %collective-permute-start.7 = (bf16[1,80,128]{2,1,0:T(8,128)(2,1)S(1)}, bf16[1,80,128]{2,1,0:T(8,128)(2,1)S(1)}, u32[]{:S(2)}, u32[]{:S(2)}) collective-permute-start(bf16[1,80,128]{2,1,0:T(8,128)(2,1)S(1)} %get-tuple-element.79), channel_id=1, source_target_pairs={{0,1},{1,2},{2,3},{3,4},{4,5},{5,6},{6,7},{7,8},{8,9},{9,10},{10,1... | collective-permute-start | bytes 61448 | tf_op jit(solution)/shard_map/ppermute | solution.py:14
  49.1 4.1 collective-permute-done.8
  55.1 8.6 %collective-permute-start.9 = (bf16[1,80,128]{2,1,0:T(8,128)(2,1)S(1)}, bf16[1,80,128]{2,1,0:T(8,128)(2,1)S(1)}, u32[]{:S(2)}, u32[]{:S(2)}) collective-permute-start(bf16[1,80,128]{2,1,0:T(8,128)(2,1)S(1)} %get-tuple-element.75), channel_id=1, source_target_pairs={{0,1},{1,2},{2,3},{3,4},{4,5},{5,6},{6,7},{7,8},{8,9},{9,10},{10,1... | collective-permute-start | bytes 61448 | tf_op jit(solution)/shard_map/ppermute | solution.py:14
  63.7 3.9 collective-permute-start.2
  67.7 16.0 %collective-permute-start.3 = (bf16[4,82,128]{2,1,0:T(8,128)(2,1)S(1)}, bf16[4,82,128]{2,1,0:T(8,128)(2,1)S(1)}, u32[]{:S(2)}, u32[]{:S(2)}) collective-permute-start(bf16[4,82,128]{2,1,0:T(8,128)(2,1)S(1)} %get-tuple-element.33), channel_id=1, source_target_pairs={{0,2},{1,3},{2,0},{3,1},{4,6},{5,7},{6,4},{7,5},{8,10},{9,11},{10,... | collective-permute-start | bytes 251912 | tf_op jit(solution)/shard_map/ppermute | solution.py:21
  86.2 3.9 collective-permute-start.11
  92.1 4.6 %collective-permute-start.13 = (bf16[160,128]{1,0:T(8,128)(2,1)S(1)}, bf16[160,128]{1,0:T(8,128)(2,1)S(1)}, u32[]{:S(2)}, u32[]{:S(2)}) collective-permute-start(bf16[160,128]{1,0:T(8,128)(2,1)S(1)} %get-tuple-element.40), channel_id=1, source_target_pairs={{0,3},{1,0},{2,1},{3,2},{4,7},{5,4},{6,5},{7,6},{8,11},{9,8},{10,9... | collective-permute-start | bytes 122888 | tf_op jit(solution)/shard_map/ppermute | solution.py:21
  97.4 2.4 convolution_convert_fusion
  102.5 129.2 %reduce-scatter.2.cloned.1.call-done = bf16[160,128]{1,0:T(8,128)(2,1)} async-done(((bf16[5120,128]{1,0:T(8,128)(2,1)}), bf16[160,128]{1,0:T(8,128)(2,1)}) %reduce-scatter.2.cloned.1.call-update) | async-done | bytes 40976 | tf_op jit(solution)/shard_map/reduce_scatter | solution.py:134
  231.7 3.0 collective-permute-start.14
  234.7 4.6 %collective-permute-start.15 = (bf16[160,128]{1,0:T(8,128)(2,1)}, bf16[160,128]{1,0:T(8,128)(2,1)S(1)}, u32[]{:S(2)}, u32[]{:S(2)}) collective-permute-start(bf16[160,128]{1,0:T(8,128)(2,1)} %reduce-scatter.2.cloned.1.call-done), channel_id=1, source_target_pairs={{0,2},{1,3},{2,0},{3,1},{4,6},{5,7},{6,4},{7,5},{8,10},{9,11},{10,... | collective-permute-start | bytes 122888 | tf_op jit(solution)/shard_map/ppermute | solution.py:21
  239.3 3.6 collective-permute-start.16
  246.5 7.6 %collective-permute-start.17 = (bf16[160,128]{1,0:T(8,128)(2,1)S(1)}, bf16[160,128]{1,0:T(8,128)(2,1)S(1)}, u32[]{:S(2)}, u32[]{:S(2)}) collective-permute-start(bf16[160,128]{1,0:T(8,128)(2,1)S(1)} %get-tuple-element.36), channel_id=1, source_target_pairs={{0,4},{1,5},{2,6},{3,7},{4,8},{5,9},{6,10},{7,11},{8,12},{9,13},{1... | collective-permute-start | bytes 122888 | tf_op jit(solution)/shard_map/ppermute | solution.py:26
  254.1 5.8 %collective-permute-start.18 = (bf16[160,128]{1,0:T(8,128)(2,1)S(1)}, bf16[160,128]{1,0:T(8,128)(2,1)S(1)}, u32[]{:S(2)}, u32[]{:S(2)}) collective-permute-start(bf16[160,128]{1,0:T(8,128)(2,1)S(1)} %get-tuple-element.38), channel_id=1, source_target_pairs={{0,8},{1,9},{2,10},{3,11},{4,12},{5,13},{6,14},{7,15},{8,0},{9,1},... | collective-permute-start | bytes 122888 | tf_op jit(solution)/shard_map/ppermute | solution.py:26
  259.9 6.9 %collective-permute-start.19 = (bf16[160,128]{1,0:T(8,128)(2,1)S(1)}, bf16[160,128]{1,0:T(8,128)(2,1)S(1)}, u32[]{:S(2)}, u32[]{:S(2)}) collective-permute-start(bf16[160,128]{1,0:T(8,128)(2,1)S(1)} %get-tuple-element.37), channel_id=1, source_target_pairs={{0,12},{1,13},{2,14},{3,15},{4,0},{5,1},{6,2},{7,3},{8,4},{9,5},{1... | collective-permute-start | bytes 122888 | tf_op jit(solution)/shard_map/ppermute | solution.py:26
  267.4 2.0 collective-permute-done.18
  270.4 2.5 collective-permute-start.20
  275.9 2.7 collective-permute-done.21
  279.7 68.7 %all-gather.4.cloned.1.call-done = bf16[5120,128]{1,0:T(8,128)(2,1)} async-done(((bf16[160,128]{1,0:T(8,128)(2,1)}), bf16[5120,128]{1,0:T(8,128)(2,1)}) %all-gather.4.cloned.1.call-update) | async-done | bytes 1310736 | tf_op jit(solution)/shard_map/all_gather | solution.py:147
  354.7 52.9 %all-gather.1 = bf16[16,36,128]{2,1,0:T(8,128)(2,1)S(1)} all-gather(bf16[1,36,128]{2,1,0:T(8,128)(2,1)S(1)} %fusion.11), channel_id=2, replica_groups=mesh['dp'=32,'owner'=16] {'owner'}, dimensions={0}, use_global_device_ids=true | all-gather | bytes 156672 | tf_op jit(solution)/shard_map/all_gather | solution.py:170
  (312 shorter events, 32.3 us)
Async XLA Ops:
  7.2 224.5 %reduce-scatter.2.cloned.1.call-start = ((), (), s32[]{:S(2)}) async-start(), calls=%async_computation.1 | async-start | bytes 1351680 | tf_op jit(solution)/shard_map/reduce_scatter | solution.py:134
  8.2 6.9 %collective-permute-start = (bf16[4,1,80,128]{3,2,1,0:T(8,128)(2,1)S(1)}, bf16[4,1,80,128]{3,2,1,0:T(8,128)(2,1)S(1)}, u32[]{:S(2)}, u32[]{:S(2)}) collective-permute-start(bf16[4,1,80,128]{3,2,1,0:T(8,128)(2,1)S(1)} %get-tuple-element.43), channel_id=1, source_target_pairs={{0,1},{1,2},{2,3},{3,4},{4,5},{5,6},{6,7},{7,8},{8,9},{9,10},{10,1... | collective-permute-start | bytes 245768 | tf_op jit(solution)/shard_map/ppermute | solution.py:14
  11.7 6.3 %collective-permute-start.1 = (bf16[4,1,80,128]{3,2,1,0:T(8,128)(2,1)S(1)}, bf16[4,1,80,128]{3,2,1,0:T(8,128)(2,1)S(1)}, u32[]{:S(2)}, u32[]{:S(2)}) collective-permute-start(bf16[4,1,80,128]{3,2,1,0:T(8,128)(2,1)S(1)} %get-tuple-element.44), channel_id=1, source_target_pairs={{1,0},{2,1},{3,2},{4,3},{5,4},{6,5},{7,6},{8,7},{9,8},{10,9},{11,1... | collective-permute-start | bytes 245768 | tf_op jit(solution)/shard_map/ppermute | solution.py:15
  19.0 6.0 %collective-permute-start.5 = (bf16[1,80,128]{2,1,0:T(8,128)(2,1)S(1)}, bf16[1,80,128]{2,1,0:T(8,128)(2,1)S(1)}, u32[]{:S(2)}, u32[]{:S(2)}) collective-permute-start(bf16[1,80,128]{2,1,0:T(8,128)(2,1)S(1)} %get-tuple-element.83), channel_id=1, source_target_pairs={{0,1},{1,2},{2,3},{3,4},{4,5},{5,6},{6,7},{7,8},{8,9},{9,10},{10,1... | collective-permute-start | bytes 61448 | tf_op jit(solution)/shard_map/ppermute | solution.py:14
  22.5 9.8 %collective-permute-start.6 = (bf16[1,80,128]{2,1,0:T(8,128)(2,1)S(1)}, bf16[1,80,128]{2,1,0:T(8,128)(2,1)S(1)}, u32[]{:S(2)}, u32[]{:S(2)}) collective-permute-start(bf16[1,80,128]{2,1,0:T(8,128)(2,1)S(1)} %get-tuple-element.84), channel_id=1, source_target_pairs={{1,0},{2,1},{3,2},{4,3},{5,4},{6,5},{7,6},{8,7},{9,8},{10,9},{11,1... | collective-permute-start | bytes 61448 | tf_op jit(solution)/shard_map/ppermute | solution.py:15
  32.8 16.2 %collective-permute-start.7 = (bf16[1,80,128]{2,1,0:T(8,128)(2,1)S(1)}, bf16[1,80,128]{2,1,0:T(8,128)(2,1)S(1)}, u32[]{:S(2)}, u32[]{:S(2)}) collective-permute-start(bf16[1,80,128]{2,1,0:T(8,128)(2,1)S(1)} %get-tuple-element.79), channel_id=1, source_target_pairs={{0,1},{1,2},{2,3},{3,4},{4,5},{5,6},{6,7},{7,8},{8,9},{9,10},{10,1... | collective-permute-start | bytes 61448 | tf_op jit(solution)/shard_map/ppermute | solution.py:14
  47.5 5.7 %collective-permute-start.8 = (bf16[1,80,128]{2,1,0:T(8,128)(2,1)S(1)}, bf16[1,80,128]{2,1,0:T(8,128)(2,1)S(1)}, u32[]{:S(2)}, u32[]{:S(2)}) collective-permute-start(bf16[1,80,128]{2,1,0:T(8,128)(2,1)S(1)} %get-tuple-element.80), channel_id=1, source_target_pairs={{1,0},{2,1},{3,2},{4,3},{5,4},{6,5},{7,6},{8,7},{9,8},{10,9},{11,1... | collective-permute-start | bytes 61448 | tf_op jit(solution)/shard_map/ppermute | solution.py:15
  53.8 31.9 %collective-permute-start.10 = (bf16[1,80,128]{2,1,0:T(8,128)(2,1)S(1)}, bf16[1,80,128]{2,1,0:T(8,128)(2,1)S(1)}, u32[]{:S(2)}, u32[]{:S(2)}) collective-permute-start(bf16[1,80,128]{2,1,0:T(8,128)(2,1)S(1)} %get-tuple-element.76), channel_id=1, source_target_pairs={{1,0},{2,1},{3,2},{4,3},{5,4},{6,5},{7,6},{8,7},{9,8},{10,9},{11,1... | collective-permute-start | bytes 61448 | tf_op jit(solution)/shard_map/ppermute | solution.py:15
  55.1 30.6 %collective-permute-start.9 = (bf16[1,80,128]{2,1,0:T(8,128)(2,1)S(1)}, bf16[1,80,128]{2,1,0:T(8,128)(2,1)S(1)}, u32[]{:S(2)}, u32[]{:S(2)}) collective-permute-start(bf16[1,80,128]{2,1,0:T(8,128)(2,1)S(1)} %get-tuple-element.75), channel_id=1, source_target_pairs={{0,1},{1,2},{2,3},{3,4},{4,5},{5,6},{6,7},{7,8},{8,9},{9,10},{10,1... | collective-permute-start | bytes 61448 | tf_op jit(solution)/shard_map/ppermute | solution.py:14
  63.7 28.4 %collective-permute-start.2 = (bf16[4,82,128]{2,1,0:T(8,128)(2,1)S(1)}, bf16[4,82,128]{2,1,0:T(8,128)(2,1)S(1)}, u32[]{:S(2)}, u32[]{:S(2)}) collective-permute-start(bf16[4,82,128]{2,1,0:T(8,128)(2,1)S(1)} %get-tuple-element.34), channel_id=1, source_target_pairs={{0,1},{1,2},{2,3},{3,0},{4,5},{5,6},{6,7},{7,4},{8,9},{9,10},{10,1... | collective-permute-start | bytes 251912 | tf_op jit(solution)/shard_map/ppermute | solution.py:21
  67.7 29.3 %collective-permute-start.3 = (bf16[4,82,128]{2,1,0:T(8,128)(2,1)S(1)}, bf16[4,82,128]{2,1,0:T(8,128)(2,1)S(1)}, u32[]{:S(2)}, u32[]{:S(2)}) collective-permute-start(bf16[4,82,128]{2,1,0:T(8,128)(2,1)S(1)} %get-tuple-element.33), channel_id=1, source_target_pairs={{0,2},{1,3},{2,0},{3,1},{4,6},{5,7},{6,4},{7,5},{8,10},{9,11},{10,... | collective-permute-start | bytes 251912 | tf_op jit(solution)/shard_map/ppermute | solution.py:21
  83.7 13.5 %collective-permute-start.4 = (bf16[4,82,128]{2,1,0:T(8,128)(2,1)S(1)}, bf16[4,82,128]{2,1,0:T(8,128)(2,1)S(1)}, u32[]{:S(2)}, u32[]{:S(2)}) collective-permute-start(bf16[4,82,128]{2,1,0:T(8,128)(2,1)S(1)} %get-tuple-element.32), channel_id=1, source_target_pairs={{0,3},{1,0},{2,1},{3,2},{4,7},{5,4},{6,5},{7,6},{8,11},{9,8},{10,9... | collective-permute-start | bytes 251912 | tf_op jit(solution)/shard_map/ppermute | solution.py:21
  86.2 14.1 %collective-permute-start.11 = (bf16[160,128]{1,0:T(8,128)(2,1)S(1)}, bf16[160,128]{1,0:T(8,128)(2,1)S(1)}, u32[]{:S(2)}, u32[]{:S(2)}) collective-permute-start(bf16[160,128]{1,0:T(8,128)(2,1)S(1)} %get-tuple-element.42), channel_id=1, source_target_pairs={{0,1},{1,2},{2,3},{3,0},{4,5},{5,6},{6,7},{7,4},{8,9},{9,10},{10,1... | collective-permute-start | bytes 122888 | tf_op jit(solution)/shard_map/ppermute | solution.py:21
  90.2 10.1 %collective-permute-start.12 = (bf16[160,128]{1,0:T(8,128)(2,1)S(1)}, bf16[160,128]{1,0:T(8,128)(2,1)S(1)}, u32[]{:S(2)}, u32[]{:S(2)}) collective-permute-start(bf16[160,128]{1,0:T(8,128)(2,1)S(1)} %get-tuple-element.41), channel_id=1, source_target_pairs={{0,2},{1,3},{2,0},{3,1},{4,6},{5,7},{6,4},{7,5},{8,10},{9,11},{10,... | collective-permute-start | bytes 122888 | tf_op jit(solution)/shard_map/ppermute | solution.py:21
  92.1 8.2 %collective-permute-start.13 = (bf16[160,128]{1,0:T(8,128)(2,1)S(1)}, bf16[160,128]{1,0:T(8,128)(2,1)S(1)}, u32[]{:S(2)}, u32[]{:S(2)}) collective-permute-start(bf16[160,128]{1,0:T(8,128)(2,1)S(1)} %get-tuple-element.40), channel_id=1, source_target_pairs={{0,3},{1,0},{2,1},{3,2},{4,7},{5,4},{6,5},{7,6},{8,11},{9,8},{10,9... | collective-permute-start | bytes 122888 | tf_op jit(solution)/shard_map/ppermute | solution.py:21
  102.4 246.0 %all-gather.4.cloned.1.call-start = ((), (), s32[]{:S(2)}) async-start(), calls=%async_computation.2 | async-start | bytes 1351680 | tf_op jit(solution)/shard_map/all_gather | solution.py:147
  231.7 13.9 %collective-permute-start.14 = (bf16[160,128]{1,0:T(8,128)(2,1)}, bf16[160,128]{1,0:T(8,128)(2,1)S(1)}, u32[]{:S(2)}, u32[]{:S(2)}) collective-permute-start(bf16[160,128]{1,0:T(8,128)(2,1)} %reduce-scatter.2.cloned.1.call-done), channel_id=1, source_target_pairs={{0,1},{1,2},{2,3},{3,0},{4,5},{5,6},{6,7},{7,4},{8,9},{9,10},{10,1... | collective-permute-start | bytes 122888 | tf_op jit(solution)/shard_map/ppermute | solution.py:21
  234.7 10.9 %collective-permute-start.15 = (bf16[160,128]{1,0:T(8,128)(2,1)}, bf16[160,128]{1,0:T(8,128)(2,1)S(1)}, u32[]{:S(2)}, u32[]{:S(2)}) collective-permute-start(bf16[160,128]{1,0:T(8,128)(2,1)} %reduce-scatter.2.cloned.1.call-done), channel_id=1, source_target_pairs={{0,2},{1,3},{2,0},{3,1},{4,6},{5,7},{6,4},{7,5},{8,10},{9,11},{10,... | collective-permute-start | bytes 122888 | tf_op jit(solution)/shard_map/ppermute | solution.py:21
  239.3 6.4 %collective-permute-start.16 = (bf16[160,128]{1,0:T(8,128)(2,1)}, bf16[160,128]{1,0:T(8,128)(2,1)S(1)}, u32[]{:S(2)}, u32[]{:S(2)}) collective-permute-start(bf16[160,128]{1,0:T(8,128)(2,1)} %reduce-scatter.2.cloned.1.call-done), channel_id=1, source_target_pairs={{0,3},{1,0},{2,1},{3,2},{4,7},{5,4},{6,5},{7,6},{8,11},{9,8},{10,9... | collective-permute-start | bytes 122888 | tf_op jit(solution)/shard_map/ppermute | solution.py:21
  246.5 21.0 %collective-permute-start.17 = (bf16[160,128]{1,0:T(8,128)(2,1)S(1)}, bf16[160,128]{1,0:T(8,128)(2,1)S(1)}, u32[]{:S(2)}, u32[]{:S(2)}) collective-permute-start(bf16[160,128]{1,0:T(8,128)(2,1)S(1)} %get-tuple-element.36), channel_id=1, source_target_pairs={{0,4},{1,5},{2,6},{3,7},{4,8},{5,9},{6,10},{7,11},{8,12},{9,13},{1... | collective-permute-start | bytes 122888 | tf_op jit(solution)/shard_map/ppermute | solution.py:26
  254.1 15.4 %collective-permute-start.18 = (bf16[160,128]{1,0:T(8,128)(2,1)S(1)}, bf16[160,128]{1,0:T(8,128)(2,1)S(1)}, u32[]{:S(2)}, u32[]{:S(2)}) collective-permute-start(bf16[160,128]{1,0:T(8,128)(2,1)S(1)} %get-tuple-element.38), channel_id=1, source_target_pairs={{0,8},{1,9},{2,10},{3,11},{4,12},{5,13},{6,14},{7,15},{8,0},{9,1},... | collective-permute-start | bytes 122888 | tf_op jit(solution)/shard_map/ppermute | solution.py:26
  259.9 9.8 %collective-permute-start.19 = (bf16[160,128]{1,0:T(8,128)(2,1)S(1)}, bf16[160,128]{1,0:T(8,128)(2,1)S(1)}, u32[]{:S(2)}, u32[]{:S(2)}) collective-permute-start(bf16[160,128]{1,0:T(8,128)(2,1)S(1)} %get-tuple-element.37), channel_id=1, source_target_pairs={{0,12},{1,13},{2,14},{3,15},{4,0},{5,1},{6,2},{7,3},{8,4},{9,5},{1... | collective-permute-start | bytes 122888 | tf_op jit(solution)/shard_map/ppermute | solution.py:26
  270.4 5.5 %collective-permute-start.20 = (bf16[1,80,128]{2,1,0:T(8,128)(2,1)S(1)}, bf16[1,80,128]{2,1,0:T(8,128)(2,1)S(1)}, u32[]{:S(2)}, u32[]{:S(2)}) collective-permute-start(bf16[1,80,128]{2,1,0:T(8,128)(2,1)S(1)} %get-tuple-element.71), channel_id=1, source_target_pairs={{0,1},{1,2},{2,3},{3,4},{4,5},{5,6},{6,7},{7,8},{8,9},{9,10},{10,1... | collective-permute-start | bytes 61448 | tf_op jit(solution)/shard_map/ppermute | solution.py:14
  272.9 5.7 %collective-permute-start.21 = (bf16[1,80,128]{2,1,0:T(8,128)(2,1)S(1)}, bf16[1,80,128]{2,1,0:T(8,128)(2,1)S(1)}, u32[]{:S(2)}, u32[]{:S(2)}) collective-permute-start(bf16[1,80,128]{2,1,0:T(8,128)(2,1)S(1)} %get-tuple-element.72), channel_id=1, source_target_pairs={{1,0},{2,1},{3,2},{4,3},{5,4},{6,5},{7,6},{8,7},{9,8},{10,9},{11,1... | collective-permute-start | bytes 61448 | tf_op jit(solution)/shard_map/ppermute | solution.py:15
  (8 other events, 515.5 us)
Sparse Core Ops, SparseCore 0:
  102.5 129.1 reduce-scatter.1
  270.5 77.8 all-gather.3

commit v2 on v1

v2 whole, which is shorter than its diff:
```python
import jax
import jax.numpy as jnp
from jax import lax
from jax.sharding import Mesh, PartitionSpec as P

X, ZL, CORE, ZH, Y = 4, 4, 2, 4, 4
OWNER = ("zh", "y")
DP = ("x", "zl", "core")


def shifted(x, shift, cyclic):
    count = ZH * Y
    pairs = [(i, (i + shift) % count) for i in range(count)]
    if not cyclic:
        pairs = [(a, b) for a, b in pairs if b - a == shift]
    return lax.ppermute(x, OWNER, pairs)


def exchange(x, axis):
    return lax.all_to_all(x, axis, split_axis=0, concat_axis=0, tiled=True)


def spread(x, axis):
    count = lax.axis_size(axis)
    return exchange(jnp.broadcast_to(x[None], (count,) + x.shape), axis)


def scatter_sum(x, axis):
    count = lax.axis_size(axis)
    got = exchange(x.reshape((count, x.shape[0] // count) + x.shape[1:]), axis)
    return jnp.sum(got.astype(jnp.float32), axis=0).astype(jnp.bfloat16)


def windows(rows):
    rows = jnp.pad(rows, ((0, 0), (1, 1), (0, 0)))
    return jnp.stack([rows[i : i + 3] for i in range(rows.shape[0] - 2)])


def cut_windows(rows, whole):
    first, second = rows[:3], rows[1:]
    first = jnp.where(whole, first, first * jnp.array([1, 1, 0], rows.dtype)[:, None, None])
    second = jnp.where(whole, second, second * jnp.array([0, 1, 1], rows.dtype)[:, None, None])
    return jnp.pad(jnp.stack([first, second]), ((0, 0), (0, 0), (1, 1), (0, 0)))


def to_columns(win):
    width = win.shape[2] - 2
    taps = [win[:, ky, kx : kx + width] for ky in range(3) for kx in range(3)]
    return jnp.concatenate(taps, axis=-1).reshape(-1, 9 * win.shape[-1])


def back_columns(win):
    width = win.shape[2] - 2
    taps = [win[:, 2 - ky, 2 - kx : 2 - kx + width] for ky in range(3) for kx in range(3)]
    return jnp.concatenate(taps, axis=-1).reshape(-1, 9 * win.shape[-1])


def silu_slope(value):
    sig = jax.nn.sigmoid(value)
    return sig * (1.0 + value * (1.0 - sig))


def inner_rows(left, right):
    return lax.dot_general(
        left, right, (((0,), (0,)), ((), ())), preferred_element_type=jnp.float32
    )


def block_classes():
    found = {}
    pairs = []
    where = {}
    for a in range(9):
        for b in range(9):
            first, second, flip = a, b, False
            dy, dx = b // 3 - a // 3, b % 3 - a % 3
            if dy < 0 or (dy == 0 and dx < 0):
                first, second, flip = b, a, True
                dy, dx = -dy, -dx
            key = (dy, dx, first // 3 if dy == 0 else -1, first % 3 if dx == 0 else -1)
            if key not in found:
                found[key] = len(pairs)
                pairs.append((first, second))
            where[a, b] = (found[key], flip)
    return pairs, where


PAIRS, WHERE = block_classes()
NG = len(PAIRS)
NBLOCKS = 40


def shards(feats, top_grad, weights, table, a_inv, g_inv):
    num_layers, _, rows_dev, width, chans = feats.shape
    owners = lax.axis_size(OWNER)
    samples = lax.axis_size(DP)
    owner_id = lax.axis_index(OWNER)
    dp_id = lax.axis_index(DP)
    y_id = lax.axis_index("y")
    z_id = lax.axis_index("zh")
    npos = samples * rows_dev * owners * width
    patch = 9 * chans
    inner = owner_id < owners - 1
    f = feats[:, 0]
    top = top_grad[0]

    above = shifted(jnp.concatenate([f[3], f[2, 1:], f[0, 1:], top[1:]]), 1, False)
    below = shifted(jnp.concatenate([f[3], f[2, :1], f[0, :1], top[:1], f[1]]), -1, True)
    below1 = below[5:]
    below = jnp.where(inner, below[:5], jnp.zeros_like(below[:5]))
    wide3 = jnp.concatenate([above[:2], f[3], below[:2]])
    strips = [
        jnp.concatenate([above[3:4], f[0], below[3:4]]),
        jnp.concatenate([f[1], below1]),
        jnp.concatenate([above[2:3], f[2], below[2:3]]),
        wide3[1:5],
    ]
    layer_strips = exchange(jnp.stack(strips), "y")

    flipped = jnp.transpose(weights.reshape(num_layers, 9, chans, chans), (0, 1, 3, 2)).reshape(
        num_layers, patch, chans
    )

    def slope(layer, win):
        pre = jnp.dot(to_columns(win), weights[layer], preferred_element_type=jnp.float32)
        return silu_slope(pre)

    def times(grad_in, slopes):
        return (grad_in.reshape(slopes.shape).astype(jnp.float32) * slopes).astype(jnp.bfloat16)

    def back(layer, win):
        return jnp.dot(
            back_columns(win), flipped[layer], preferred_element_type=jnp.float32
        ).astype(jnp.bfloat16)

    image = (rows_dev, width, chans)
    top_wide = jnp.concatenate([above[4:5], top, below[4:5]])
    dpre3 = times(top_wide, slope(3, windows(wide3))).reshape((rows_dev + 2, width, chans))
    dpre2 = times(back(3, windows(dpre3)), slope(2, windows(strips[2]))).reshape(image)
    after = shifted(dpre2, -1, True)
    dy1 = back(2, cut_windows(jnp.concatenate([dpre2, after]), inner))
    dpre1 = times(dy1, slope(1, cut_windows(strips[1], inner))).reshape(image)
    before = shifted(dpre1, 1, True)
    edge_top = jnp.where(owner_id > 0, before[:1], jnp.zeros_like(before[:1]))
    edge_end = jnp.where(inner, dpre1[1:], jnp.zeros_like(dpre1[1:]))
    dy0 = back(1, windows(jnp.concatenate([edge_top, before[1:], dpre1[:1], edge_end])))
    dpre0 = times(dy0, slope(0, windows(strips[0]))).reshape(image)

    layer_dpre = exchange(jnp.stack([dpre0, dpre1, dpre2, dpre3[1:3]]), "y")
    big_dpre = layer_dpre.reshape(-1, chans)
    last_one = (y_id == 1) & (z_id == ZH - 1)
    big_cols = jnp.concatenate(
        [
            to_columns(
                windows(layer_strips[j])
                if j < Y - 1
                else cut_windows(layer_strips[j], jnp.logical_not(last_one))
            )
            for j in range(Y)
        ]
    )
    gram = inner_rows(big_cols, big_cols).astype(jnp.bfloat16)
    grad = inner_rows(big_cols, big_dpre).astype(jnp.bfloat16)
    gfac = inner_rows(big_dpre, big_dpre).astype(jnp.bfloat16)
    blocks = [
        gram[a * chans : (a + 1) * chans, b * chans : (b + 1) * chans] for a, b in PAIRS
    ]
    pad = jnp.zeros(((NBLOCKS - NG - 10) * chans, chans), jnp.bfloat16)
    parts = jnp.concatenate(blocks + [grad, gfac, pad], axis=0)

    piece = scatter_sum(scatter_sum(scatter_sum(parts, "core"), "x"), "zl")
    held = spread(piece, "y")
    layer_ids = jnp.arange(num_layers, dtype=jnp.int32)

    def pick(z):
        lay = jnp.sum(jnp.where(table == z * Y + y_id, layer_ids, 0))
        return lax.dynamic_index_in_dim(held, lay, 0, keepdims=False)

    total = exchange(jnp.stack([pick(z) for z in range(ZH)]), "zh")
    total = jnp.sum(total.astype(jnp.float32), axis=0).astype(jnp.bfloat16)
    summed = spread(spread(spread(total, "zl"), "x"), "core")

    in_grad_win = jnp.concatenate([shifted(dpre0[1:], 1, False), dpre0, shifted(dpre0[:1], -1, False)])
    in_grad = back(0, windows(in_grad_win)).reshape((1,) + image)

    summed = summed.reshape(NBLOCKS, chans, chans)
    have = jnp.any(table == owner_id).astype(jnp.float32)
    turned = jnp.swapaxes(summed[:NG], 1, 2)
    factor = jnp.concatenate(
        [
            jnp.concatenate(
                [turned[WHERE[a, b][0]] if WHERE[a, b][1] else summed[WHERE[a, b][0]] for b in range(9)],
                axis=1,
            )
            for a in range(9)
        ],
        axis=0,
    )
    rows_out = patch // samples
    a_rows = lax.dynamic_slice_in_dim(factor, dp_id * rows_out, rows_out, 0).astype(jnp.float32)
    a_out = (a_rows * (have / npos))[None]
    g_out = (summed[NG + 9].astype(jnp.float32) * (have / npos))[None]
    grad_sum = summed[NG : NG + 9].reshape(patch, chans).astype(jnp.float32)
    grad_scaled = grad_sum / jnp.sqrt(jnp.float32(npos))
    mixed = jnp.dot(grad_scaled, g_inv[0], precision=lax.Precision.HIGHEST)
    panel = jnp.dot(a_inv[0].astype(jnp.float32), mixed, precision=lax.Precision.HIGHEST)
    panels = spread(panel.astype(jnp.bfloat16), OWNER)
    step_out = panels[table]
    return (step_out, a_out, g_out, in_grad)


def solution(mesh):
    fine = Mesh(mesh.devices.reshape(X, ZL, CORE, ZH, Y), DP + OWNER)
    placed = (
        P(None, DP, OWNER, None, None),
        P(DP, OWNER, None, None),
        P(),
        P(),
        P(OWNER, DP, None),
        P(OWNER, None, None),
    )
    return jax.shard_map(
        shards,
        mesh=fine,
        in_specs=placed,
        out_specs=(
            P(None, DP, None),
            P(OWNER, DP, None),
            P(OWNER, None, None),
            P(DP, OWNER, None, None),
        ),
        check_vma=False,
    )
```

time: 418 us -> 256 us (0.61)
  waiting for transfers between devices: 217 us -> 59.5 us
  local copies, waits for them, and re-layouts: 13.1 us -> 69.3 us
  starting transfers between devices: 103 us -> 73.1 us
  blocking collectives: 52.9 us -> 23.3 us
  between operations: 19.2 us -> 10.4 us
  other arithmetic: 3.75 us -> 8.44 us
    reduce_scatter x1 -> x0, waiting for transfers between devices: 129 us -> none  [shards(): piece = lax.psum_scatter(parts, 'dp', scatter_dimension=0, tiled=True)]
    all_gather x1 -> x0, waiting for transfers between devices: 68.7 us -> none  [shards(): lax.all_gather(total.astype(jnp.bfloat16), 'dp', axis=0, tiled=True)]
    ppermute x22 -> x6, starting transfers between devices: 103 us -> 35.9 us  [shifted(): return lax.ppermute(x, OWNER, pairs)]
    all_gather x1 -> x0, blocking collectives: 52.9 us -> none  [shards(): panels = lax.all_gather(panel.astype(jnp.bfloat16), 'owner', axis=0)]
    unnamed x223 -> x237, local copies, waits for them, and re-layouts: 5.79 us -> 57.1 us
    all_to_all x0 -> x8, waiting for transfers between devices: none -> 45.6 us  [exchange(): return lax.all_to_all(x, axis, split_axis=0, concat_axis=0, tiled=True)]
    all_to_all x0 -> x8, starting transfers between devices: none -> 37.2 us  [exchange(): return lax.all_to_all(x, axis, split_axis=0, concat_axis=0, tiled=True)]
    all_to_all x0 -> x3, blocking collectives: none -> 23.3 us  [exchange(): return lax.all_to_all(x, axis, split_axis=0, concat_axis=0, tiled=True)]
  transfers between devices with their start and end apart: 24 -> 14, of which waited for: 8 -> 8; matrix products, arithmetic and copies ran while one was open for 2% -> 8% of each run, Pallas kernels for 0% -> 0%
where the time goes in v2:
time: 256 us; the launch traced here: 253 us
  starting transfers between devices  73.1 us (29%)
  local copies, waits for them, and re-layouts  69.3 us (27%)
  waiting for transfers between devices  59.5 us (23%)
  blocking collectives  23.3 us (9%)
  between operations  10.4 us (4%)
  matrix products  8.9 us (3%)
  other arithmetic  8.44 us (3%)
    unnamed x237, local copies, waits for them, and re-layouts  57.1 us
    all_to_all x8, waiting for transfers between devices, exchange(): return lax.all_to_all(x, axis, split_axis=0, concat_axis=0, tiled=True)  45.6 us
    all_to_all x8, starting transfers between devices, exchange(): return lax.all_to_all(x, axis, split_axis=0, concat_axis=0, tiled=True)  37.2 us
    ppermute x6, starting transfers between devices, shifted(): return lax.ppermute(x, OWNER, pairs)  35.9 us
    all_to_all x3, blocking collectives, exchange(): return lax.all_to_all(x, axis, split_axis=0, concat_axis=0, tiled=True)  23.3 us
    ppermute x6, waiting for transfers between devices, shifted(): return lax.ppermute(x, OWNER, pairs)  13.9 us
  transfers between devices with their start and end apart: 14, of which 8 were waited for; matrix products, arithmetic and copies ran while one was open for 8% of the time, Pallas kernels for 0%

profile of v2, /device:TPU:6, one launch (start us, length us, event | category | flops | bytes accessed | tf_op | source)
XLA Modules:
  0.0 252.8 jit_solution(16256076768533107868)
XLA Ops:
  4.5 15.2 %collective-permute-start.1 = (bf16[7,80,128]{2,1,0:T(8,128)(2,1)S(1)}, bf16[7,80,128]{2,1,0:T(8,128)(2,1)S(1)}, u32[]{:S(2)}, u32[]{:S(2)}) collective-permute-start(bf16[7,80,128]{2,1,0:T(8,128)(2,1)S(1)} %constant_dynamic-update-slice_fusion), channel_id=1, source_target_pairs={{0,15},{1,0},{2,1},{3,2},{4,3},{5,4},{6,5},{7,6},{8,7},{9,8},{10,9... | collective-permute-start | bytes 430088 | tf_op jit(solution)/shard_map/ppermute | solution.py:16
  26.1 5.9 %collective-permute-done.1 = bf16[7,80,128]{2,1,0:T(8,128)(2,1)S(1)} collective-permute-done((bf16[7,80,128]{2,1,0:T(8,128)(2,1)S(1)}, bf16[7,80,128]{2,1,0:T(8,128)(2,1)S(1)}, u32[]{:S(2)}, u32[]{:S(2)}) %collective-permute-start.1) | collective-permute-done | bytes 143392 | tf_op jit(solution)/shard_map/ppermute | solution.py:16
  34.2 10.4 %collective-permute-start.2 = (bf16[2,80,128]{2,1,0:T(8,128)(2,1)S(1)}, bf16[2,80,128]{2,1,0:T(8,128)(2,1)S(1)}, u32[]{:S(2)}, u32[]{:S(2)}) collective-permute-start(bf16[2,80,128]{2,1,0:T(8,128)(2,1)S(1)} %bitcast.649), channel_id=1, source_target_pairs={{0,15},{1,0},{2,1},{3,2},{4,3},{5,4},{6,5},{7,6},{8,7},{9,8},{10,9... | collective-permute-start | bytes 122888 | tf_op jit(solution)/shard_map/ppermute | solution.py:16
  46.5 3.5 %all-to-all-start = ((bf16[4,4,80,128]{3,2,1,0:T(8,128)(2,1)}), bf16[4,4,80,128]{3,2,1,0:T(8,128)(2,1)S(1)}, u32[]{:S(2)}, u32[]{:S(2)}) async-start(bf16[4,4,80,128]{3,2,1,0:T(8,128)(2,1)} %pad_maximum_fusion.1), calls=%async_computation | async-start | bytes 655360 | tf_op jit(solution)/shard_map/all_to_all | solution.py:20
  51.2 3.9 %collective-permute-start.3 = (bf16[2,80,128]{2,1,0:T(8,128)(2,1)S(1)}, bf16[2,80,128]{2,1,0:T(8,128)(2,1)S(1)}, u32[]{:S(2)}, u32[]{:S(2)}) collective-permute-start(bf16[2,80,128]{2,1,0:T(8,128)(2,1)S(1)} %bitcast.652), channel_id=1, source_target_pairs={{0,1},{1,2},{2,3},{3,4},{4,5},{5,6},{6,7},{7,8},{8,9},{9,10},{10,1... | collective-permute-start | bytes 122888 | tf_op jit(solution)/shard_map/ppermute | solution.py:16
  55.1 8.0 %collective-permute-done.3 = bf16[2,80,128]{2,1,0:T(8,128)(2,1)S(1)} collective-permute-done((bf16[2,80,128]{2,1,0:T(8,128)(2,1)S(1)}, bf16[2,80,128]{2,1,0:T(8,128)(2,1)S(1)}, u32[]{:S(2)}, u32[]{:S(2)}) %collective-permute-start.3) | collective-permute-done | bytes 40992 | tf_op jit(solution)/shard_map/ppermute | solution.py:16
  64.4 3.3 %all-to-all-start.1 = ((bf16[4,2,80,128]{3,2,1,0:T(8,128)(2,1)}), bf16[4,2,80,128]{3,2,1,0:T(8,128)(2,1)S(1)}, u32[]{:S(2)}, u32[]{:S(2)}) async-start(bf16[4,2,80,128]{3,2,1,0:T(8,128)(2,1)} %pad_maximum_fusion.8), calls=%async_computation.1 | async-start | bytes 327680 | tf_op jit(solution)/shard_map/all_to_all | solution.py:20
  69.7 2.4 convolution_convert_fusion
  73.9 1.9 fusion
  76.0 4.8 %all_to_all.55 = bf16[2,2560,128]{2,1,0:T(8,128)(2,1)S(1)} all-to-all(bf16[2,2560,128]{2,1,0:T(8,128)(2,1)S(1)} %bitcast.629), channel_id=1, replica_groups=mesh['x'=4,'zl'=4,'core'=2,'zh'=4,'y'=4] {'core'}, dimensions={0} | all-to-all | bytes 2621440 | tf_op jit(solution)/shard_map/all_to_all | solution.py:20
  81.5 13.7 %all_to_all.56 = bf16[4,640,128]{2,1,0:T(8,128)(2,1)S(1)} all-to-all(bf16[4,640,128]{2,1,0:T(8,128)(2,1)S(1)} %bitcast.626), channel_id=1, replica_groups=mesh['x'=4,'zl'=4,'core'=2,'zh'=4,'y'=4] {'x'}, dimensions={0} | all-to-all | bytes 1310720 | tf_op jit(solution)/shard_map/all_to_all | solution.py:20
  96.0 3.3 %all-to-all-start.4 = ((bf16[4,160,128]{2,1,0:T(8,128)(2,1)}), bf16[4,160,128]{2,1,0:T(8,128)(2,1)S(1)}, u32[]{:S(2)}, u32[]{:S(2)}) async-start(bf16[4,160,128]{2,1,0:T(8,128)(2,1)} %bitcast.165), calls=%async_computation.4 | async-start | bytes 327680 | tf_op jit(solution)/shard_map/all_to_all | solution.py:20
  109.7 3.4 %all-to-all-start.5 = ((bf16[4,160,128]{2,1,0:T(8,128)(2,1)}), bf16[4,160,128]{2,1,0:T(8,128)(2,1)S(1)}, u32[]{:S(2)}, u32[]{:S(2)}) async-start(bf16[4,160,128]{2,1,0:T(8,128)(2,1)} %broadcast_in_dim.27), calls=%async_computation.5 | async-start | bytes 327680 | tf_op jit(solution)/shard_map/all_to_all | solution.py:20
  113.2 3.9 %collective-permute-start.4 = (bf16[1,80,128]{2,1,0:T(8,128)(2,1)S(1)}, bf16[1,80,128]{2,1,0:T(8,128)(2,1)S(1)}, u32[]{:S(2)}, u32[]{:S(2)}) collective-permute-start(bf16[1,80,128]{2,1,0:T(8,128)(2,1)S(1)} %get-tuple-element.181), channel_id=1, source_target_pairs={{0,1},{1,2},{2,3},{3,4},{4,5},{5,6},{6,7},{7,8},{8,9},{9,10},{10,1... | collective-permute-start | bytes 61448 | tf_op jit(solution)/shard_map/ppermute | solution.py:16
  120.3 11.0 %all-to-all-start.6 = ((bf16[4,160,128]{2,1,0:T(8,128)(2,1)}), bf16[4,160,128]{2,1,0:T(8,128)(2,1)S(1)}, u32[]{:S(2)}, u32[]{:S(2)}) async-start(bf16[4,160,128]{2,1,0:T(8,128)(2,1)} %pad_maximum_fusion.9), calls=%async_computation.6 | async-start | bytes 327680 | tf_op jit(solution)/shard_map/all_to_all | solution.py:20
  131.5 16.1 %all-to-all-done.6 = bf16[4,160,128]{2,1,0:T(8,128)(2,1)S(1)} async-done(((bf16[4,160,128]{2,1,0:T(8,128)(2,1)}), bf16[4,160,128]{2,1,0:T(8,128)(2,1)S(1)}, u32[]{:S(2)}, u32[]{:S(2)}) %all-to-all-start.6) | async-done | bytes 163872 | tf_op jit(solution)/shard_map/all_to_all | solution.py:20
  148.2 3.5 %all-to-all-start.7 = ((bf16[4,160,128]{2,1,0:T(8,128)(2,1)}), bf16[4,160,128]{2,1,0:T(8,128)(2,1)S(1)}, u32[]{:S(2)}, u32[]{:S(2)}) async-start(bf16[4,160,128]{2,1,0:T(8,128)(2,1)} %broadcast_in_dim.29), calls=%async_computation.7 | async-start | bytes 327680 | tf_op jit(solution)/shard_map/all_to_all | solution.py:20
  151.9 5.7 %all-to-all-done.7 = bf16[4,160,128]{2,1,0:T(8,128)(2,1)S(1)} async-done(((bf16[4,160,128]{2,1,0:T(8,128)(2,1)}), bf16[4,160,128]{2,1,0:T(8,128)(2,1)S(1)}, u32[]{:S(2)}, u32[]{:S(2)}) %all-to-all-start.7) | async-done | bytes 163872 | tf_op jit(solution)/shard_map/all_to_all | solution.py:20
  158.5 5.5 %all-to-all-start.8 = ((bf16[4,4,160,128]{3,2,1,0:T(8,128)(2,1)}), bf16[4,4,160,128]{3,2,1,0:T(8,128)(2,1)S(1)}, u32[]{:S(2)}, u32[]{:S(2)}) async-start(bf16[4,4,160,128]{3,2,1,0:T(8,128)(2,1)} %broadcast_in_dim.30), calls=%async_computation.8 | async-start | bytes 1310720 | tf_op jit(solution)/shard_map/all_to_all | solution.py:20
  164.9 5.8 %all-to-all-done.8 = bf16[4,4,160,128]{3,2,1,0:T(8,128)(2,1)S(1)} async-done(((bf16[4,4,160,128]{3,2,1,0:T(8,128)(2,1)}), bf16[4,4,160,128]{3,2,1,0:T(8,128)(2,1)S(1)}, u32[]{:S(2)}, u32[]{:S(2)}) %all-to-all-start.8) | async-done | bytes 655392 | tf_op jit(solution)/shard_map/all_to_all | solution.py:20
  171.0 4.8 %all_to_all.57 = bf16[2,4,4,160,128]{4,3,2,1,0:T(8,128)(2,1)S(1)} all-to-all(bf16[2,4,4,160,128]{4,3,2,1,0:T(8,128)(2,1)S(1)} %broadcast_in_dim.31), channel_id=1, replica_groups=mesh['x'=4,'zl'=4,'core'=2,'zh'=4,'y'=4] {'core'}, dimensions={0} | all-to-all | bytes 2621440 | tf_op jit(solution)/shard_map/all_to_all | solution.py:20
  182.3 1.6 copy.32
  229.6 3.5 %all-to-all-start.10 = ((bf16[16,36,128]{2,1,0:T(8,128)(2,1)}), bf16[16,36,128]{2,1,0:T(8,128)(2,1)S(1)}, u32[]{:S(2)}, u32[]{:S(2)}) async-start(bf16[16,36,128]{2,1,0:T(8,128)(2,1)} %broadcast_in_dim.32), calls=%async_computation.10 | async-start | bytes 327680 | tf_op jit(solution)/shard_map/all_to_all | solution.py:20
  236.1 15.5 %all-to-all-done.10 = bf16[16,36,128]{2,1,0:T(8,128)(2,1)S(1)} async-done(((bf16[16,36,128]{2,1,0:T(8,128)(2,1)}), bf16[16,36,128]{2,1,0:T(8,128)(2,1)S(1)}, u32[]{:S(2)}, u32[]{:S(2)}) %all-to-all-start.10) | async-done | bytes 147488 | tf_op jit(solution)/shard_map/all_to_all | solution.py:20
  (351 shorter events, 85.8 us)
Async XLA Ops:
  0.6 227.9 %copy-start = (bf16[1,36,1152]{2,1,0:T(8,128)(2,1)S(1)}, bf16[1,36,1152]{2,1,0:T(8,128)(2,1)}, u32[]{:S(2)}) copy-start(bf16[1,36,1152]{2,1,0:T(8,128)(2,1)} %param.16) | copy-start | bytes 248836
  4.5 27.5 %collective-permute-start.1 = (bf16[7,80,128]{2,1,0:T(8,128)(2,1)S(1)}, bf16[7,80,128]{2,1,0:T(8,128)(2,1)S(1)}, u32[]{:S(2)}, u32[]{:S(2)}) collective-permute-start(bf16[7,80,128]{2,1,0:T(8,128)(2,1)S(1)} %constant_dynamic-update-slice_fusion), channel_id=1, source_target_pairs={{0,15},{1,0},{2,1},{3,2},{4,3},{5,4},{6,5},{7,6},{8,7},{9,8},{10,9... | collective-permute-start | bytes 430088 | tf_op jit(solution)/shard_map/ppermute | solution.py:16
  22.0 4.0 %collective-permute-start = (bf16[5,80,128]{2,1,0:T(8,128)(2,1)S(1)}, bf16[5,80,128]{2,1,0:T(8,128)(2,1)S(1)}, u32[]{:S(2)}, u32[]{:S(2)}) collective-permute-start(bf16[5,80,128]{2,1,0:T(8,128)(2,1)S(1)} %pad_maximum_fusion.12), channel_id=1, source_target_pairs={{0,1},{1,2},{2,3},{3,4},{4,5},{5,6},{6,7},{7,8},{8,9},{9,10},{10,1... | collective-permute-start | bytes 307208 | tf_op jit(solution)/shard_map/ppermute | solution.py:16
  25.8 6.8 %copy-start.4 = (bf16[1,2,80,128]{3,2,1,0:T(8,128)(2,1)S(1)}, bf16[1,2,80,128]{3,2,1,0:T(8,128)(2,1)}, u32[]{:S(2)}) copy-start(bf16[1,2,80,128]{3,2,1,0:T(8,128)(2,1)} %param.13) | copy-start | bytes 122884
  26.0 6.5 %copy-start.1 = (bf16[4,1152,128]{2,1,0:T(8,128)(2,1)S(1)}, bf16[4,1152,128]{2,1,0:T(8,128)(2,1)}, u32[]{:S(2)}) copy-start(bf16[4,1152,128]{2,1,0:T(8,128)(2,1)} %param.14) | copy-start | bytes 3538948
  33.8 16.2 %copy-start.10 = (bf16[3]{0:T(256)(128)(2,1)S(1)}, bf16[3]{0:T(256)(128)(2,1)}, u32[]{:S(2)}) copy-start(bf16[3]{0:T(256)(128)(2,1)} %constant.81.clone) | copy-start | bytes 22
  33.8 16.2 %copy-start.11 = (bf16[3]{0:T(256)(128)(2,1)S(1)}, bf16[3]{0:T(256)(128)(2,1)}, u32[]{:S(2)}) copy-start(bf16[3]{0:T(256)(128)(2,1)} %constant.82.clone) | copy-start | bytes 22
  34.2 15.8 %collective-permute-start.2 = (bf16[2,80,128]{2,1,0:T(8,128)(2,1)S(1)}, bf16[2,80,128]{2,1,0:T(8,128)(2,1)S(1)}, u32[]{:S(2)}, u32[]{:S(2)}) collective-permute-start(bf16[2,80,128]{2,1,0:T(8,128)(2,1)S(1)} %bitcast.649), channel_id=1, source_target_pairs={{0,15},{1,0},{2,1},{3,2},{4,3},{5,4},{6,5},{7,6},{8,7},{9,8},{10,9... | collective-permute-start | bytes 122888 | tf_op jit(solution)/shard_map/ppermute | solution.py:16
  46.5 17.9 %all-to-all-start = ((bf16[4,4,80,128]{3,2,1,0:T(8,128)(2,1)}), bf16[4,4,80,128]{3,2,1,0:T(8,128)(2,1)S(1)}, u32[]{:S(2)}, u32[]{:S(2)}) async-start(bf16[4,4,80,128]{3,2,1,0:T(8,128)(2,1)} %pad_maximum_fusion.1), calls=%async_computation | async-start | bytes 655360 | tf_op jit(solution)/shard_map/all_to_all | solution.py:20
  50.3 13.2 %copy-start.5 = (f32[160,128]{1,0:T(8,128)S(1)}, f32[160,128]{1,0:T(8,128)}, u32[]{:S(2)}) copy-start(f32[160,128]{1,0:T(8,128)} %fusion.13) | copy-start | bytes 245764
  51.2 11.9 %collective-permute-start.3 = (bf16[2,80,128]{2,1,0:T(8,128)(2,1)S(1)}, bf16[2,80,128]{2,1,0:T(8,128)(2,1)S(1)}, u32[]{:S(2)}, u32[]{:S(2)}) collective-permute-start(bf16[2,80,128]{2,1,0:T(8,128)(2,1)S(1)} %bitcast.652), channel_id=1, source_target_pairs={{0,1},{1,2},{2,3},{3,4},{4,5},{5,6},{6,7},{7,8},{8,9},{9,10},{10,1... | collective-permute-start | bytes 122888 | tf_op jit(solution)/shard_map/ppermute | solution.py:16
  64.4 9.5 %all-to-all-start.1 = ((bf16[4,2,80,128]{3,2,1,0:T(8,128)(2,1)}), bf16[4,2,80,128]{3,2,1,0:T(8,128)(2,1)S(1)}, u32[]{:S(2)}, u32[]{:S(2)}) async-start(bf16[4,2,80,128]{3,2,1,0:T(8,128)(2,1)} %pad_maximum_fusion.8), calls=%async_computation.1 | async-start | bytes 327680 | tf_op jit(solution)/shard_map/all_to_all | solution.py:20
  68.6 3.8 %copy-start.9 = (bf16[160,1152]{1,0:T(8,128)(2,1)}, bf16[160,1152]{1,0:T(8,128)(2,1)S(1)}, u32[]{:S(2)}) copy-start(bf16[160,1152]{1,0:T(8,128)(2,1)S(1)} %constant_dynamic-update-slice_fusion.5) | copy-start | bytes 1105924
  80.8 18.5 %copy-start.12 = (s32[4]{0:T(128)S(1)}, s32[4]{0:T(128)}, u32[]{:S(2)}) copy-start(s32[4]{0:T(128)} %param.15) | copy-start | bytes 52
  96.0 13.0 %all-to-all-start.4 = ((bf16[4,160,128]{2,1,0:T(8,128)(2,1)}), bf16[4,160,128]{2,1,0:T(8,128)(2,1)S(1)}, u32[]{:S(2)}, u32[]{:S(2)}) async-start(bf16[4,160,128]{2,1,0:T(8,128)(2,1)} %bitcast.165), calls=%async_computation.4 | async-start | bytes 327680 | tf_op jit(solution)/shard_map/all_to_all | solution.py:20
  109.7 9.8 %all-to-all-start.5 = ((bf16[4,160,128]{2,1,0:T(8,128)(2,1)}), bf16[4,160,128]{2,1,0:T(8,128)(2,1)S(1)}, u32[]{:S(2)}, u32[]{:S(2)}) async-start(bf16[4,160,128]{2,1,0:T(8,128)(2,1)} %broadcast_in_dim.27), calls=%async_computation.5 | async-start | bytes 327680 | tf_op jit(solution)/shard_map/all_to_all | solution.py:20
  113.2 18.1 %collective-permute-start.4 = (bf16[1,80,128]{2,1,0:T(8,128)(2,1)S(1)}, bf16[1,80,128]{2,1,0:T(8,128)(2,1)S(1)}, u32[]{:S(2)}, u32[]{:S(2)}) collective-permute-start(bf16[1,80,128]{2,1,0:T(8,128)(2,1)S(1)} %get-tuple-element.181), channel_id=1, source_target_pairs={{0,1},{1,2},{2,3},{3,4},{4,5},{5,6},{6,7},{7,8},{8,9},{9,10},{10,1... | collective-permute-start | bytes 61448 | tf_op jit(solution)/shard_map/ppermute | solution.py:16
  117.1 14.2 %collective-permute-start.5 = (bf16[1,80,128]{2,1,0:T(8,128)(2,1)S(1)}, bf16[1,80,128]{2,1,0:T(8,128)(2,1)S(1)}, u32[]{:S(2)}, u32[]{:S(2)}) collective-permute-start(bf16[1,80,128]{2,1,0:T(8,128)(2,1)S(1)} %get-tuple-element.182), channel_id=1, source_target_pairs={{1,0},{2,1},{3,2},{4,3},{5,4},{6,5},{7,6},{8,7},{9,8},{10,9},{11,1... | collective-permute-start | bytes 61448 | tf_op jit(solution)/shard_map/ppermute | solution.py:16
  120.3 27.3 %all-to-all-start.6 = ((bf16[4,160,128]{2,1,0:T(8,128)(2,1)}), bf16[4,160,128]{2,1,0:T(8,128)(2,1)S(1)}, u32[]{:S(2)}, u32[]{:S(2)}) async-start(bf16[4,160,128]{2,1,0:T(8,128)(2,1)} %pad_maximum_fusion.9), calls=%async_computation.6 | async-start | bytes 327680 | tf_op jit(solution)/shard_map/all_to_all | solution.py:20
  148.2 9.3 %all-to-all-start.7 = ((bf16[4,160,128]{2,1,0:T(8,128)(2,1)}), bf16[4,160,128]{2,1,0:T(8,128)(2,1)S(1)}, u32[]{:S(2)}, u32[]{:S(2)}) async-start(bf16[4,160,128]{2,1,0:T(8,128)(2,1)} %broadcast_in_dim.29), calls=%async_computation.7 | async-start | bytes 327680 | tf_op jit(solution)/shard_map/all_to_all | solution.py:20
  158.5 12.2 %all-to-all-start.8 = ((bf16[4,4,160,128]{3,2,1,0:T(8,128)(2,1)}), bf16[4,4,160,128]{3,2,1,0:T(8,128)(2,1)S(1)}, u32[]{:S(2)}, u32[]{:S(2)}) async-start(bf16[4,4,160,128]{3,2,1,0:T(8,128)(2,1)} %broadcast_in_dim.30), calls=%async_computation.8 | async-start | bytes 1310720 | tf_op jit(solution)/shard_map/all_to_all | solution.py:20
  183.9 44.0 %copy-start.2 = (f32[9,128,128]{2,1,0:T(8,128)S(1)}, f32[9,128,128]{2,1,0:T(8,128)}, u32[]{:S(2)}) copy-start(f32[9,128,128]{2,1,0:T(8,128)} %convert_multiply_fusion) | copy-start | bytes 1769476
  183.9 44.0 %copy-start.6 = (f32[1,128,128]{2,1,0:T(8,128)S(1)}, f32[1,128,128]{2,1,0:T(8,128)}, u32[]{:S(2)}) copy-start(f32[1,128,128]{2,1,0:T(8,128)} %param.17) | copy-start | bytes 196612
  229.6 22.0 %all-to-all-start.10 = ((bf16[16,36,128]{2,1,0:T(8,128)(2,1)}), bf16[16,36,128]{2,1,0:T(8,128)(2,1)S(1)}, u32[]{:S(2)}, u32[]{:S(2)}) async-start(bf16[16,36,128]{2,1,0:T(8,128)(2,1)} %broadcast_in_dim.32), calls=%async_computation.10 | async-start | bytes 327680 | tf_op jit(solution)/shard_map/all_to_all | solution.py:20
  (3 other events, 2.8 us)

commit v3 on v2

--- a/solution.py
+++ b/solution.py
@@ -1,6 +1,8 @@
 import jax
 import jax.numpy as jnp
 from jax import lax
+from jax.experimental import pallas as pl
+from jax.experimental.pallas import tpu as pltpu
 from jax.sharding import Mesh, PartitionSpec as P
 
 X, ZL, CORE, ZH, Y = 4, 4, 2, 4, 4
@@ -14,6 +16,21 @@
     if not cyclic:
         pairs = [(a, b) for a, b in pairs if b - a == shift]
     return lax.ppermute(x, OWNER, pairs)
+
+
+def swapped(x, first):
+    count = ZH * Y
+    pairs = []
+    for i in range(0 if first else 1, count, 2):
+        pairs += [(i, (i + 1) % count), ((i + 1) % count, i)]
+    return lax.ppermute(x, OWNER, pairs)
+
+
+def both_sides(to_above, to_below):
+    even = lax.axis_index(OWNER) % 2 == 0
+    one = swapped(jnp.where(even, to_below, to_above), True)
+    two = swapped(jnp.where(even, to_above, to_below), False)
+    return jnp.where(even, two, one), jnp.where(even, one, two)
 
 
 def exchange(x, axis):
@@ -87,7 +104,41 @@
 
 PAIRS, WHERE = block_classes()
 NG = len(PAIRS)
-NBLOCKS = 40
+
+
+def factor_rows(blocks, first_row, scale, rows):
+    chans = blocks.shape[-1]
+    index = jnp.array([WHERE[a, b][0] for a in range(9) for b in range(9)], jnp.int32)
+    flips = jnp.array([int(WHERE[a, b][1]) for a in range(9) for b in range(9)], jnp.int32)
+
+    def kernel(index_ref, flip_ref, row_ref, scale_ref, blocks_ref, out_ref, band):
+        start = row_ref[0]
+        tap = lax.div(start, chans)
+        for t in range(2):
+            a = jnp.minimum(tap + t, 8)
+            for b in range(9):
+                block = blocks_ref[index_ref[a * 9 + b]].astype(jnp.float32)
+                flip = flip_ref[a * 9 + b] != 0
+                band[t * chans : (t + 1) * chans, b * chans : (b + 1) * chans] = jnp.where(
+                    flip, block.T, block
+                )
+        inside = start - tap * chans
+        base = pl.multiple_of(lax.div(inside, 8) * 8, 8)
+        got = band[pl.ds(base, rows + 4), :]
+        odd = inside != base
+        out_ref[...] = jnp.where(odd, got[4:], got[:rows]) * scale_ref[0]
+
+    smem = pl.BlockSpec(memory_space=pltpu.SMEM)
+    vmem = pl.BlockSpec(memory_space=pltpu.VMEM)
+    return pl.pallas_call(
+        kernel,
+        out_shape=jax.ShapeDtypeStruct((rows, 9 * chans), jnp.float32),
+        in_specs=[smem, smem, smem, smem, vmem],
+        out_specs=vmem,
+        scratch_shapes=[pltpu.VMEM((2 * chans, 9 * chans), jnp.float32)],
+        compiler_params=pltpu.CompilerParams(vmem_limit_bytes=16 * 2**20),
+        cost_estimate=pl.CostEstimate(flops=10**6, bytes_accessed=2 * 10**6, transcendentals=0),
+    )(index, flips, first_row.reshape(1), scale.reshape(1), blocks)
 
 
 def shards(feats, top_grad, weights, table, a_inv, g_inv):
@@ -104,9 +155,20 @@
     f = feats[:, 0]
     top = top_grad[0]
 
-    above = shifted(jnp.concatenate([f[3], f[2, 1:], f[0, 1:], top[1:]]), 1, False)
-    below = shifted(jnp.concatenate([f[3], f[2, :1], f[0, :1], top[:1], f[1]]), -1, True)
+    def picked(x):
+        source = table[y_id]
+        near = lax.dynamic_index_in_dim(lax.all_gather(x, "y"), source % Y, 0, keepdims=False)
+        return lax.dynamic_index_in_dim(lax.all_gather(near, "zh"), source // Y, 0, keepdims=False)
+
+    a_mine = picked(a_inv[0])
+    g_mine = picked(g_inv[0])
+
+    above, below = both_sides(
+        jnp.concatenate([f[3], f[2, :1], f[0, :1], top[:1], f[1]]),
+        jnp.concatenate([f[3], f[2, 1:], f[0, 1:], top[1:], f[1]]),
+    )
     below1 = below[5:]
+    above = jnp.where(owner_id > 0, above[:5], jnp.zeros_like(above[:5]))
     below = jnp.where(inner, below[:5], jnp.zeros_like(below[:5]))
     wide3 = jnp.concatenate([above[:2], f[3], below[:2]])
     strips = [
@@ -165,47 +227,47 @@
     blocks = [
         gram[a * chans : (a + 1) * chans, b * chans : (b + 1) * chans] for a, b in PAIRS
     ]
-    pad = jnp.zeros(((NBLOCKS - NG - 10) * chans, chans), jnp.bfloat16)
-    parts = jnp.concatenate(blocks + [grad, gfac, pad], axis=0)
+    pad = jnp.zeros((chans, chans), jnp.bfloat16)
+    parts = jnp.concatenate(
+        [
+            jnp.concatenate(blocks + [gfac]).reshape(samples, -1, chans),
+            jnp.concatenate([grad, pad]).reshape(samples, -1, chans),
+        ],
+        axis=1,
+    ).reshape(-1, chans)
+    cut = (NG + 1) * chans // samples
 
     piece = scatter_sum(scatter_sum(scatter_sum(parts, "core"), "x"), "zl")
-    held = spread(piece, "y")
+    held = spread(piece[:cut], "y")
     layer_ids = jnp.arange(num_layers, dtype=jnp.int32)
 
     def pick(z):
         lay = jnp.sum(jnp.where(table == z * Y + y_id, layer_ids, 0))
         return lax.dynamic_index_in_dim(held, lay, 0, keepdims=False)
 
-    total = exchange(jnp.stack([pick(z) for z in range(ZH)]), "zh")
+    sent = jnp.stack([jnp.concatenate([pick(z), piece[cut:]]) for z in range(ZH)])
+    sent, dpre0, a_mine, g_mine = lax.optimization_barrier((sent, dpre0, a_mine, g_mine))
+    total = exchange(sent, "zh")
     total = jnp.sum(total.astype(jnp.float32), axis=0).astype(jnp.bfloat16)
-    summed = spread(spread(spread(total, "zl"), "x"), "core")
-
-    in_grad_win = jnp.concatenate([shifted(dpre0[1:], 1, False), dpre0, shifted(dpre0[:1], -1, False)])
-    in_grad = back(0, windows(in_grad_win)).reshape((1,) + image)
-
-    summed = summed.reshape(NBLOCKS, chans, chans)
+
+    up, down = both_sides(dpre0[:1], dpre0[1:])
+    up = jnp.where(owner_id > 0, up, jnp.zeros_like(up))
+    down = jnp.where(inner, down, jnp.zeros_like(down))
+    in_grad = back(0, windows(jnp.concatenate([up, dpre0, down]))).reshape((1,) + image)
+
+    summed = spread(spread(spread(total, "zl"), "x"), "core").reshape(samples, -1, chans)
+    grad_sum = summed[:, cut:].reshape(-1, chans)[:patch].astype(jnp.float32)
+    grad_scaled = grad_sum / jnp.sqrt(jnp.float32(npos))
+    mixed = jnp.dot(grad_scaled, g_mine, precision=lax.Precision.HIGHEST)
+    panel = jnp.dot(a_mine.astype(jnp.float32), mixed, precision=lax.Precision.HIGHEST)
+    step_out = spread(panel.astype(jnp.bfloat16), "y")
+
+    stats = summed[:, :cut].reshape(NG + 1, chans, chans)
     have = jnp.any(table == owner_id).astype(jnp.float32)
-    turned = jnp.swapaxes(summed[:NG], 1, 2)
-    factor = jnp.concatenate(
-        [
-            jnp.concatenate(
-                [turned[WHERE[a, b][0]] if WHERE[a, b][1] else summed[WHERE[a, b][0]] for b in range(9)],
-                axis=1,
-            )
-            for a in range(9)
-        ],
-        axis=0,
-    )
+    scale = have / npos
     rows_out = patch // samples
-    a_rows = lax.dynamic_slice_in_dim(factor, dp_id * rows_out, rows_out, 0).astype(jnp.float32)
-    a_out = (a_rows * (have / npos))[None]
-    g_out = (summed[NG + 9].astype(jnp.float32) * (have / npos))[None]
-    grad_sum = summed[NG : NG + 9].reshape(patch, chans).astype(jnp.float32)
-    grad_scaled = grad_sum / jnp.sqrt(jnp.float32(npos))
-    mixed = jnp.dot(grad_scaled, g_inv[0], precision=lax.Precision.HIGHEST)
-    panel = jnp.dot(a_inv[0].astype(jnp.float32), mixed, precision=lax.Precision.HIGHEST)
-    panels = spread(panel.astype(jnp.bfloat16), OWNER)
-    step_out = panels[table]
+    a_out = factor_rows(stats, dp_id * rows_out, scale, rows_out)[None]
+    g_out = (stats[NG].astype(jnp.float32) * scale)[None]
     return (step_out, a_out, g_out, in_grad)
 
 

time: 256 us -> 279 us (1.090)
  blocking collectives: 23.3 us -> 73.7 us
  local copies, waits for them, and re-layouts: 69.3 us -> 37.4 us
  starting transfers between devices: 73.1 us -> 80.8 us
  waiting for transfers between devices: 59.5 us -> 53 us
    all_gather x0 -> x4, blocking collectives: none -> 63.9 us  [the longest x2 39.2 us: picked(): lax.all_gather(near, 'zh')]
    unnamed x237 -> x153, local copies, waits for them, and re-layouts: 57.1 us -> 29.6 us
    ppermute x0 -> x4, starting transfers between devices: none -> 25.5 us  [swapped(): return lax.ppermute(x, OWNER, pairs)]
    ppermute x6 -> x2, starting transfers between devices: 35.9 us -> 14.3 us  [shifted(): return lax.ppermute(x, OWNER, pairs)]
    all_to_all x3 -> x2, blocking collectives: 23.3 us -> 9.7 us  [exchange(): return lax.all_to_all(x, axis, split_axis=0, concat_axis=0, tiled=True)]
    all_to_all x8 -> x9, waiting for transfers between devices: 45.6 us -> 35.1 us  [exchange(): return lax.all_to_all(x, axis, split_axis=0, concat_axis=0, tiled=True)]
    ppermute x0 -> x4, waiting for transfers between devices: none -> 9.91 us  [swapped(): return lax.ppermute(x, OWNER, pairs)]
    ppermute x6 -> x2, waiting for transfers between devices: 13.9 us -> 8.02 us  [shifted(): return lax.ppermute(x, OWNER, pairs)]
  transfers between devices with their start and end apart: 14 -> 15, of which waited for: 8 -> 8; matrix products, arithmetic and copies ran while one was open for 8% -> 6% of each run, Pallas kernels for 0% -> 0%
where the time goes in v3:
time: 279 us; the launch traced here: 274 us
  starting transfers between devices  80.8 us (29%)
  blocking collectives  73.7 us (26%)
  waiting for transfers between devices  53 us (19%)
  local copies, waits for them, and re-layouts  37.4 us (13%)
  between operations  12.7 us (5%)
  matrix products  8.51 us (3%)
  other arithmetic  7.5 us (3%)
    all_to_all x9, starting transfers between devices, exchange(): return lax.all_to_all(x, axis, split_axis=0, concat_axis=0, tiled=True)  41 us
    all_gather x2, blocking collectives, picked(): lax.all_gather(near, 'zh')  39.2 us
    all_to_all x9, waiting for transfers between devices, exchange(): return lax.all_to_all(x, axis, split_axis=0, concat_axis=0, tiled=True)  35.1 us
    unnamed x153, local copies, waits for them, and re-layouts  29.6 us
    ppermute x4, starting transfers between devices, swapped(): return lax.ppermute(x, OWNER, pairs)  25.5 us
    all_gather x2, blocking collectives, picked(): lax.all_gather(x, 'y')  24.7 us
    ppermute x2, starting transfers between devices, shifted(): return lax.ppermute(x, OWNER, pairs)  14.3 us
    ppermute x4, waiting for transfers between devices, swapped(): return lax.ppermute(x, OWNER, pairs)  9.91 us
  transfers between devices with their start and end apart: 15, of which 8 were waited for; matrix products, arithmetic and copies ran while one was open for 6% of the time, Pallas kernels for 0%

profile of v3, /device:TPU:6, one launch (start us, length us, event | category | flops | bytes accessed | tf_op | source)
XLA Modules:
  0.0 274.5 jit_solution(13096064364238949229)
XLA Ops:
  5.3 3.5 %collective-permute-start.1 = (bf16[7,80,128]{2,1,0:T(8,128)(2,1)S(1)}, bf16[7,80,128]{2,1,0:T(8,128)(2,1)S(1)}, u32[]{:S(2)}, u32[]{:S(2)}) collective-permute-start(bf16[7,80,128]{2,1,0:T(8,128)(2,1)S(1)} %get-tuple-element.46), channel_id=1, source_target_pairs={{0,1},{1,0},{2,3},{3,2},{4,5},{5,4},{6,7},{7,6},{8,9},{9,8},{10,11... | collective-permute-start | bytes 430088 | tf_op jit(solution)/shard_map/ppermute | solution.py:26
  8.8 14.4 %collective-permute-start = (bf16[7,80,128]{2,1,0:T(8,128)(2,1)S(1)}, bf16[7,80,128]{2,1,0:T(8,128)(2,1)S(1)}, u32[]{:S(2)}, u32[]{:S(2)}) collective-permute-start(bf16[7,80,128]{2,1,0:T(8,128)(2,1)S(1)} %get-tuple-element.45), channel_id=1, source_target_pairs={{1,2},{2,1},{3,4},{4,3},{5,6},{6,5},{7,8},{8,7},{9,10},{10,9},{11,... | collective-permute-start | bytes 430088 | tf_op jit(solution)/shard_map/ppermute | solution.py:26
  25.3 9.9 %collective-permute-done = bf16[7,80,128]{2,1,0:T(8,128)(2,1)S(1)} collective-permute-done((bf16[7,80,128]{2,1,0:T(8,128)(2,1)S(1)}, bf16[7,80,128]{2,1,0:T(8,128)(2,1)S(1)}, u32[]{:S(2)}, u32[]{:S(2)}) %collective-permute-start) | collective-permute-done | bytes 143392 | tf_op jit(solution)/shard_map/ppermute | solution.py:26
  38.1 10.4 %collective-permute-start.2 = (bf16[2,80,128]{2,1,0:T(8,128)(2,1)S(1)}, bf16[2,80,128]{2,1,0:T(8,128)(2,1)S(1)}, u32[]{:S(2)}, u32[]{:S(2)}) collective-permute-start(bf16[2,80,128]{2,1,0:T(8,128)(2,1)S(1)} %bitcast.334), channel_id=1, source_target_pairs={{0,15},{1,0},{2,1},{3,2},{4,3},{5,4},{6,5},{7,6},{8,7},{9,8},{10,9... | collective-permute-start | bytes 122888 | tf_op jit(solution)/shard_map/ppermute | solution.py:18
  54.5 3.9 %collective-permute-start.3 = (bf16[2,80,128]{2,1,0:T(8,128)(2,1)S(1)}, bf16[2,80,128]{2,1,0:T(8,128)(2,1)S(1)}, u32[]{:S(2)}, u32[]{:S(2)}) collective-permute-start(bf16[2,80,128]{2,1,0:T(8,128)(2,1)S(1)} %bitcast.337), channel_id=1, source_target_pairs={{0,1},{1,2},{2,3},{3,4},{4,5},{5,6},{6,7},{7,8},{8,9},{9,10},{10,1... | collective-permute-start | bytes 122888 | tf_op jit(solution)/shard_map/ppermute | solution.py:18
  58.4 8.0 %collective-permute-done.3 = bf16[2,80,128]{2,1,0:T(8,128)(2,1)S(1)} collective-permute-done((bf16[2,80,128]{2,1,0:T(8,128)(2,1)S(1)}, bf16[2,80,128]{2,1,0:T(8,128)(2,1)S(1)}, u32[]{:S(2)}, u32[]{:S(2)}) %collective-permute-start.3) | collective-permute-done | bytes 40992 | tf_op jit(solution)/shard_map/ppermute | solution.py:18
  72.4 3.9 %convolution_convert_fusion = bf16[1152,1152]{1,0:T(8,128)(2,1)} fusion(bf16[160,1152]{1,0:T(8,128)(2,1)S(1)} %constant_dynamic-update-slice_fusion.37, bf16[160,1152]{1,0:T(8,128)(2,1)S(1)} %constant_dynamic-update-slice_fusion.28, bf16[160,1152]{1,0:T(8,128)(2,1)S(1)} %constant_dynamic-update-slice_fusion.19, ...), kind=kOutput, calls=%fused_computation | convolution fusion | flops 1705918464 | bytes 4128768 | tf_op jit(solution)/shard_map/dot_general | solution.py:81
  100.4 4.9 %all_to_all.55 = bf16[2,2560,128]{2,1,0:T(8,128)(2,1)S(1)} all-to-all(bf16[2,2560,128]{2,1,0:T(8,128)(2,1)S(1)} %bitcast.306), channel_id=1, replica_groups=mesh['x'=4,'zl'=4,'core'=2,'zh'=4,'y'=4] {'core'}, dimensions={0} | all-to-all | bytes 2621440 | tf_op jit(solution)/shard_map/all_to_all | solution.py:37
  106.6 4.8 %all-to-all-start.3 = ((bf16[4,640,128]{2,1,0:T(8,128)(2,1)}), bf16[4,640,128]{2,1,0:T(8,128)(2,1)S(1)}, u32[]{:S(2)}, u32[]{:S(2)}) async-start(bf16[4,640,128]{2,1,0:T(8,128)(2,1)} %bitcast.166), calls=%async_computation.3 | async-start | bytes 1310720 | tf_op jit(solution)/shard_map/all_to_all | solution.py:37
  111.4 12.2 %all_gather.16 = f32[4,128,128]{2,1,0:T(8,128)S(1)} all-gather(f32[1,128,128]{2,1,0:T(8,128)S(1)} %copy-done.6), channel_id=1, replica_groups=mesh['x'=4,'zl'=4,'core'=2,'zh'=4,'y'=4] {'y'}, dimensions={0}, use_global_device_ids=true | all-gather | bytes 327680 | tf_op jit(solution)/shard_map/all_gather | solution.py:160
  126.2 12.5 %all_gather.14 = bf16[4,36,1152]{2,1,0:T(8,128)(2,1)S(1)} all-gather(bf16[1,36,1152]{2,1,0:T(8,128)(2,1)S(1)} %copy-done.5), channel_id=1, replica_groups=mesh['x'=4,'zl'=4,'core'=2,'zh'=4,'y'=4] {'y'}, dimensions={0}, use_global_device_ids=true | all-gather | bytes 414720 | tf_op jit(solution)/shard_map/all_gather | solution.py:160
  151.7 19.1 %all_gather.17 = f32[4,128,128]{2,1,0:T(8,128)S(1)} all-gather(f32[1,128,128]{2,1,0:T(8,128)S(1)} %constant_dynamic-slice_fusion), channel_id=1, replica_groups=mesh['x'=4,'zl'=4,'core'=2,'zh'=4,'y'=4] {'zh'}, dimensions={0}, use_global_device_ids=true | all-gather | bytes 327680 | tf_op jit(solution)/shard_map/all_gather | solution.py:161
  170.8 20.1 %all_gather.15 = bf16[4,36,1152]{2,1,0:T(8,128)(2,1)S(1)} all-gather(bf16[1,36,1152]{2,1,0:T(8,128)(2,1)S(1)} %constant_dynamic-slice_fusion.1), channel_id=1, replica_groups=mesh['x'=4,'zl'=4,'core'=2,'zh'=4,'y'=4] {'zh'}, dimensions={0}, use_global_device_ids=true | all-gather | bytes 414720 | tf_op jit(solution)/shard_map/all_gather | solution.py:161
  191.6 3.6 %all-to-all-start.5 = ((bf16[4,120,128]{2,1,0:T(8,128)(2,1)}), bf16[4,120,128]{2,1,0:T(8,128)(2,1)S(1)}, u32[]{:S(2)}, u32[]{:S(2)}) async-start(bf16[4,120,128]{2,1,0:T(8,128)(2,1)} %broadcast_in_dim.19), calls=%async_computation.5 | async-start | bytes 245760 | tf_op jit(solution)/shard_map/all_to_all | solution.py:37
  195.3 6.1 %all-to-all-done.5 = bf16[4,120,128]{2,1,0:T(8,128)(2,1)S(1)} async-done(((bf16[4,120,128]{2,1,0:T(8,128)(2,1)}), bf16[4,120,128]{2,1,0:T(8,128)(2,1)S(1)}, u32[]{:S(2)}, u32[]{:S(2)}) %all-to-all-start.5) | async-done | bytes 122912 | tf_op jit(solution)/shard_map/all_to_all | solution.py:37
  202.1 5.6 %collective-permute-start.4 = (bf16[1,80,128]{2,1,0:T(8,128)(2,1)S(1)}, bf16[1,80,128]{2,1,0:T(8,128)(2,1)S(1)}, u32[]{:S(2)}, u32[]{:S(2)}) collective-permute-start(bf16[1,80,128]{2,1,0:T(8,128)(2,1)S(1)} %get-tuple-element.203), channel_id=1, source_target_pairs={{1,2},{2,1},{3,4},{4,3},{5,6},{6,5},{7,8},{8,7},{9,10},{10,9},{11,... | collective-permute-start | bytes 61448 | tf_op jit(solution)/shard_map/ppermute | solution.py:26
  211.3 6.7 %all-to-all-start.6 = ((bf16[4,160,128]{2,1,0:T(8,128)(2,1)}), bf16[4,160,128]{2,1,0:T(8,128)(2,1)S(1)}, u32[]{:S(2)}, u32[]{:S(2)}) async-start(bf16[4,160,128]{2,1,0:T(8,128)(2,1)} %pad_maximum_fusion.10), calls=%async_computation.6 | async-start | bytes 327680 | tf_op jit(solution)/shard_map/all_to_all | solution.py:37
  218.2 13.2 %all-to-all-done.6 = bf16[4,160,128]{2,1,0:T(8,128)(2,1)S(1)} async-done(((bf16[4,160,128]{2,1,0:T(8,128)(2,1)}), bf16[4,160,128]{2,1,0:T(8,128)(2,1)S(1)}, u32[]{:S(2)}, u32[]{:S(2)}) %all-to-all-start.6) | async-done | bytes 163872 | tf_op jit(solution)/shard_map/all_to_all | solution.py:37
  232.1 7.0 %all-to-all-start.7 = ((bf16[4,160,128]{2,1,0:T(8,128)(2,1)}), bf16[4,160,128]{2,1,0:T(8,128)(2,1)S(1)}, u32[]{:S(2)}, u32[]{:S(2)}) async-start(bf16[4,160,128]{2,1,0:T(8,128)(2,1)} %broadcast_in_dim.21), calls=%async_computation.7 | async-start | bytes 327680 | tf_op jit(solution)/shard_map/all_to_all | solution.py:37
  239.2 5.9 %all-to-all-done.7 = bf16[4,160,128]{2,1,0:T(8,128)(2,1)S(1)} async-done(((bf16[4,160,128]{2,1,0:T(8,128)(2,1)}), bf16[4,160,128]{2,1,0:T(8,128)(2,1)S(1)}, u32[]{:S(2)}, u32[]{:S(2)}) %all-to-all-start.7) | async-done | bytes 163872 | tf_op jit(solution)/shard_map/all_to_all | solution.py:37
  246.0 4.5 %all-to-all-start.8 = ((bf16[4,4,160,128]{3,2,1,0:T(8,128)(2,1)}), bf16[4,4,160,128]{3,2,1,0:T(8,128)(2,1)S(1)}, u32[]{:S(2)}, u32[]{:S(2)}) async-start(bf16[4,4,160,128]{3,2,1,0:T(8,128)(2,1)} %broadcast_in_dim.22), calls=%async_computation.8 | async-start | bytes 1310720 | tf_op jit(solution)/shard_map/all_to_all | solution.py:37
  251.5 5.8 %all-to-all-done.8 = bf16[4,4,160,128]{3,2,1,0:T(8,128)(2,1)S(1)} async-done(((bf16[4,4,160,128]{3,2,1,0:T(8,128)(2,1)}), bf16[4,4,160,128]{3,2,1,0:T(8,128)(2,1)S(1)}, u32[]{:S(2)}, u32[]{:S(2)}) %all-to-all-start.8) | async-done | bytes 655392 | tf_op jit(solution)/shard_map/all_to_all | solution.py:37
  257.5 4.8 %all_to_all.56 = bf16[2,4,4,160,128]{4,3,2,1,0:T(8,128)(2,1)S(1)} all-to-all(bf16[2,4,4,160,128]{4,3,2,1,0:T(8,128)(2,1)S(1)} %broadcast_in_dim.23), channel_id=1, replica_groups=mesh['x'=4,'zl'=4,'core'=2,'zh'=4,'y'=4] {'core'}, dimensions={0} | all-to-all | bytes 2621440 | tf_op jit(solution)/shard_map/all_to_all | solution.py:37
  264.0 4.4 %all-to-all-start.10 = ((bf16[4,36,128]{2,1,0:T(8,128)(2,1)}), bf16[4,36,128]{2,1,0:T(8,128)(2,1)S(1)}, u32[]{:S(2)}, u32[]{:S(2)}) async-start(bf16[4,36,128]{2,1,0:T(8,128)(2,1)} %broadcast_in_dim.24), calls=%async_computation.10 | async-start | bytes 81920 | tf_op jit(solution)/shard_map/all_to_all | solution.py:37
  (277 shorter events, 66.6 us)
Async XLA Ops:
  1.4 23.8 %copy-start.3 = (bf16[4,1,2,80,128]{4,3,2,1,0:T(8,128)(2,1)S(1)}, bf16[4,1,2,80,128]{4,3,2,1,0:T(8,128)(2,1)}, u32[]{:S(2)}) copy-start(bf16[4,1,2,80,128]{4,3,2,1,0:T(8,128)(2,1)} %param.14) | copy-start | bytes 491524
  5.3 19.9 %collective-permute-start.1 = (bf16[7,80,128]{2,1,0:T(8,128)(2,1)S(1)}, bf16[7,80,128]{2,1,0:T(8,128)(2,1)S(1)}, u32[]{:S(2)}, u32[]{:S(2)}) collective-permute-start(bf16[7,80,128]{2,1,0:T(8,128)(2,1)S(1)} %get-tuple-element.46), channel_id=1, source_target_pairs={{0,1},{1,0},{2,3},{3,2},{4,5},{5,4},{6,7},{7,6},{8,9},{9,8},{10,11... | collective-permute-start | bytes 430088 | tf_op jit(solution)/shard_map/ppermute | solution.py:26
  8.8 26.4 %collective-permute-start = (bf16[7,80,128]{2,1,0:T(8,128)(2,1)S(1)}, bf16[7,80,128]{2,1,0:T(8,128)(2,1)S(1)}, u32[]{:S(2)}, u32[]{:S(2)}) collective-permute-start(bf16[7,80,128]{2,1,0:T(8,128)(2,1)S(1)} %get-tuple-element.45), channel_id=1, source_target_pairs={{1,2},{2,1},{3,4},{4,3},{5,6},{6,5},{7,8},{8,7},{9,10},{10,9},{11,... | collective-permute-start | bytes 430088 | tf_op jit(solution)/shard_map/ppermute | solution.py:26
  35.2 1.3 copy-start.2
  37.8 15.5 %copy-start.7 = (bf16[3]{0:T(256)(128)(2,1)S(1)}, bf16[3]{0:T(256)(128)(2,1)}, u32[]{:S(2)}) copy-start(bf16[3]{0:T(256)(128)(2,1)} %constant.125.clone) | copy-start | bytes 22
  37.8 15.5 %copy-start.8 = (bf16[3]{0:T(256)(128)(2,1)S(1)}, bf16[3]{0:T(256)(128)(2,1)}, u32[]{:S(2)}) copy-start(bf16[3]{0:T(256)(128)(2,1)} %constant.126.clone) | copy-start | bytes 22
  38.1 15.2 %collective-permute-start.2 = (bf16[2,80,128]{2,1,0:T(8,128)(2,1)S(1)}, bf16[2,80,128]{2,1,0:T(8,128)(2,1)S(1)}, u32[]{:S(2)}, u32[]{:S(2)}) collective-permute-start(bf16[2,80,128]{2,1,0:T(8,128)(2,1)S(1)} %bitcast.334), channel_id=1, source_target_pairs={{0,15},{1,0},{2,1},{3,2},{4,3},{5,4},{6,5},{7,6},{8,7},{9,8},{10,9... | collective-permute-start | bytes 122888 | tf_op jit(solution)/shard_map/ppermute | solution.py:18
  49.8 17.9 %all-to-all-start = ((bf16[4,4,80,128]{3,2,1,0:T(8,128)(2,1)}), bf16[4,4,80,128]{3,2,1,0:T(8,128)(2,1)S(1)}, u32[]{:S(2)}, u32[]{:S(2)}) async-start(bf16[4,4,80,128]{3,2,1,0:T(8,128)(2,1)} %pad_maximum_fusion.2), calls=%async_computation | async-start | bytes 655360 | tf_op jit(solution)/shard_map/all_to_all | solution.py:37
  54.5 11.9 %collective-permute-start.3 = (bf16[2,80,128]{2,1,0:T(8,128)(2,1)S(1)}, bf16[2,80,128]{2,1,0:T(8,128)(2,1)S(1)}, u32[]{:S(2)}, u32[]{:S(2)}) collective-permute-start(bf16[2,80,128]{2,1,0:T(8,128)(2,1)S(1)} %bitcast.337), channel_id=1, source_target_pairs={{0,1},{1,2},{2,3},{3,4},{4,5},{5,6},{6,7},{7,8},{8,9},{9,10},{10,1... | collective-permute-start | bytes 122888 | tf_op jit(solution)/shard_map/ppermute | solution.py:18
  67.7 9.5 %all-to-all-start.1 = ((bf16[4,2,80,128]{3,2,1,0:T(8,128)(2,1)}), bf16[4,2,80,128]{3,2,1,0:T(8,128)(2,1)S(1)}, u32[]{:S(2)}, u32[]{:S(2)}) async-start(bf16[4,2,80,128]{3,2,1,0:T(8,128)(2,1)} %pad_maximum_fusion.9), calls=%async_computation.1 | async-start | bytes 327680 | tf_op jit(solution)/shard_map/all_to_all | solution.py:37
  100.4 11.0 %copy-start.6 = (f32[1,128,128]{2,1,0:T(8,128)S(1)}, f32[1,128,128]{2,1,0:T(8,128)}, u32[]{:S(2)}) copy-start(f32[1,128,128]{2,1,0:T(8,128)} %param.19) | copy-start | bytes 196612
  100.4 23.2 %copy-start.9 = (s32[4]{0:T(128)S(1)}, s32[4]{0:T(128)}, u32[]{:S(2)}) copy-start(s32[4]{0:T(128)} %param.17) | copy-start | bytes 52
  100.4 25.8 %copy-start.5 = (bf16[1,36,1152]{2,1,0:T(8,128)(2,1)S(1)}, bf16[1,36,1152]{2,1,0:T(8,128)(2,1)}, u32[]{:S(2)}) copy-start(bf16[1,36,1152]{2,1,0:T(8,128)(2,1)} %param.18) | copy-start | bytes 248836
  106.6 32.1 %all-to-all-start.3 = ((bf16[4,640,128]{2,1,0:T(8,128)(2,1)}), bf16[4,640,128]{2,1,0:T(8,128)(2,1)S(1)}, u32[]{:S(2)}, u32[]{:S(2)}) async-start(bf16[4,640,128]{2,1,0:T(8,128)(2,1)} %bitcast.166), calls=%async_computation.3 | async-start | bytes 1310720 | tf_op jit(solution)/shard_map/all_to_all | solution.py:37
  139.5 51.4 %all-to-all-start.4 = ((bf16[4,160,128]{2,1,0:T(8,128)(2,1)}), bf16[4,160,128]{2,1,0:T(8,128)(2,1)S(1)}, u32[]{:S(2)}, u32[]{:S(2)}) async-start(bf16[4,160,128]{2,1,0:T(8,128)(2,1)} %bitcast.167), calls=%async_computation.4 | async-start | bytes 327680 | tf_op jit(solution)/shard_map/all_to_all | solution.py:37
  191.6 9.7 %all-to-all-start.5 = ((bf16[4,120,128]{2,1,0:T(8,128)(2,1)}), bf16[4,120,128]{2,1,0:T(8,128)(2,1)S(1)}, u32[]{:S(2)}, u32[]{:S(2)}) async-start(bf16[4,120,128]{2,1,0:T(8,128)(2,1)} %broadcast_in_dim.19), calls=%async_computation.5 | async-start | bytes 245760 | tf_op jit(solution)/shard_map/all_to_all | solution.py:37
  202.1 15.9 %collective-permute-start.4 = (bf16[1,80,128]{2,1,0:T(8,128)(2,1)S(1)}, bf16[1,80,128]{2,1,0:T(8,128)(2,1)S(1)}, u32[]{:S(2)}, u32[]{:S(2)}) collective-permute-start(bf16[1,80,128]{2,1,0:T(8,128)(2,1)S(1)} %get-tuple-element.203), channel_id=1, source_target_pairs={{1,2},{2,1},{3,4},{4,3},{5,6},{6,5},{7,8},{8,7},{9,10},{10,9},{11,... | collective-permute-start | bytes 61448 | tf_op jit(solution)/shard_map/ppermute | solution.py:26
  207.7 10.3 %collective-permute-start.5 = (bf16[1,80,128]{2,1,0:T(8,128)(2,1)S(1)}, bf16[1,80,128]{2,1,0:T(8,128)(2,1)S(1)}, u32[]{:S(2)}, u32[]{:S(2)}) collective-permute-start(bf16[1,80,128]{2,1,0:T(8,128)(2,1)S(1)} %get-tuple-element.204), channel_id=1, source_target_pairs={{0,1},{1,0},{2,3},{3,2},{4,5},{5,4},{6,7},{7,6},{8,9},{9,8},{10,11... | collective-permute-start | bytes 61448 | tf_op jit(solution)/shard_map/ppermute | solution.py:26
  211.3 20.0 %all-to-all-start.6 = ((bf16[4,160,128]{2,1,0:T(8,128)(2,1)}), bf16[4,160,128]{2,1,0:T(8,128)(2,1)S(1)}, u32[]{:S(2)}, u32[]{:S(2)}) async-start(bf16[4,160,128]{2,1,0:T(8,128)(2,1)} %pad_maximum_fusion.10), calls=%async_computation.6 | async-start | bytes 327680 | tf_op jit(solution)/shard_map/all_to_all | solution.py:37
  232.1 13.0 %all-to-all-start.7 = ((bf16[4,160,128]{2,1,0:T(8,128)(2,1)}), bf16[4,160,128]{2,1,0:T(8,128)(2,1)S(1)}, u32[]{:S(2)}, u32[]{:S(2)}) async-start(bf16[4,160,128]{2,1,0:T(8,128)(2,1)} %broadcast_in_dim.21), calls=%async_computation.7 | async-start | bytes 327680 | tf_op jit(solution)/shard_map/all_to_all | solution.py:37
  246.0 11.2 %all-to-all-start.8 = ((bf16[4,4,160,128]{3,2,1,0:T(8,128)(2,1)}), bf16[4,4,160,128]{3,2,1,0:T(8,128)(2,1)S(1)}, u32[]{:S(2)}, u32[]{:S(2)}) async-start(bf16[4,4,160,128]{3,2,1,0:T(8,128)(2,1)} %broadcast_in_dim.22), calls=%async_computation.8 | async-start | bytes 1310720 | tf_op jit(solution)/shard_map/all_to_all | solution.py:37
  262.3 6.7 %copy-start = (s32[81]{0:T(128)S(1)}, s32[81]{0:T(128)}, u32[]{:S(2)}) copy-start(s32[81]{0:T(128)} %constant.127.clone.index_ref) | copy-start | bytes 976
  262.3 6.7 %copy-start.1 = (s32[81]{0:T(128)S(1)}, s32[81]{0:T(128)}, u32[]{:S(2)}) copy-start(s32[81]{0:T(128)} %constant.128.clone.flip_ref) | copy-start | bytes 976
  264.0 9.9 %all-to-all-start.10 = ((bf16[4,36,128]{2,1,0:T(8,128)(2,1)}), bf16[4,36,128]{2,1,0:T(8,128)(2,1)S(1)}, u32[]{:S(2)}, u32[]{:S(2)}) async-start(bf16[4,36,128]{2,1,0:T(8,128)(2,1)} %broadcast_in_dim.24), calls=%async_computation.10 | async-start | bytes 81920 | tf_op jit(solution)/shard_map/all_to_all | solution.py:37
  (1 other events, 0.8 us)

commit v4 on v2

--- a/solution.py
+++ b/solution.py
@@ -1,6 +1,8 @@
 import jax
 import jax.numpy as jnp
 from jax import lax
+from jax.experimental import pallas as pl
+from jax.experimental.pallas import tpu as pltpu
 from jax.sharding import Mesh, PartitionSpec as P
 
 X, ZL, CORE, ZH, Y = 4, 4, 2, 4, 4
@@ -90,6 +92,41 @@
 NBLOCKS = 40
 
 
+def factor_rows(blocks, first_row, scale, rows):
+    chans = blocks.shape[-1]
+    index = jnp.array([WHERE[a, b][0] for a in range(9) for b in range(9)], jnp.int32)
+    flips = jnp.array([int(WHERE[a, b][1]) for a in range(9) for b in range(9)], jnp.int32)
+
+    def kernel(index_ref, flip_ref, row_ref, scale_ref, blocks_ref, out_ref, band):
+        start = row_ref[0]
+        tap = lax.div(start, chans)
+        for t in range(2):
+            a = jnp.minimum(tap + t, 8)
+            for b in range(9):
+                block = blocks_ref[index_ref[a * 9 + b]].astype(jnp.float32)
+                flip = flip_ref[a * 9 + b] != 0
+                band[t * chans : (t + 1) * chans, b * chans : (b + 1) * chans] = jnp.where(
+                    flip, block.T, block
+                )
+        inside = start - tap * chans
+        base = pl.multiple_of(lax.div(inside, 8) * 8, 8)
+        got = band[pl.ds(base, rows + 4), :]
+        odd = inside != base
+        out_ref[...] = jnp.where(odd, got[4:], got[:rows]) * scale_ref[0]
+
+    smem = pl.BlockSpec(memory_space=pltpu.SMEM)
+    vmem = pl.BlockSpec(memory_space=pltpu.VMEM)
+    return pl.pallas_call(
+        kernel,
+        out_shape=jax.ShapeDtypeStruct((rows, 9 * chans), jnp.float32),
+        in_specs=[smem, smem, smem, smem, vmem],
+        out_specs=vmem,
+        scratch_shapes=[pltpu.VMEM((2 * chans, 9 * chans), jnp.float32)],
+        compiler_params=pltpu.CompilerParams(vmem_limit_bytes=16 * 2**20),
+        cost_estimate=pl.CostEstimate(flops=10**6, bytes_accessed=2 * 10**6, transcendentals=0),
+    )(index, flips, first_row.reshape(1), scale.reshape(1), blocks)
+
+
 def shards(feats, top_grad, weights, table, a_inv, g_inv):
     num_layers, _, rows_dev, width, chans = feats.shape
     owners = lax.axis_size(OWNER)
@@ -168,7 +205,7 @@
     pad = jnp.zeros(((NBLOCKS - NG - 10) * chans, chans), jnp.bfloat16)
     parts = jnp.concatenate(blocks + [grad, gfac, pad], axis=0)
 
-    piece = scatter_sum(scatter_sum(scatter_sum(parts, "core"), "x"), "zl")
+    piece = scatter_sum(scatter_sum(parts, "core"), ("x", "zl"))
     held = spread(piece, "y")
     layer_ids = jnp.arange(num_layers, dtype=jnp.int32)
 
@@ -185,21 +222,10 @@
 
     summed = summed.reshape(NBLOCKS, chans, chans)
     have = jnp.any(table == owner_id).astype(jnp.float32)
-    turned = jnp.swapaxes(summed[:NG], 1, 2)
-    factor = jnp.concatenate(
-        [
-            jnp.concatenate(
-                [turned[WHERE[a, b][0]] if WHERE[a, b][1] else summed[WHERE[a, b][0]] for b in range(9)],
-                axis=1,
-            )
-            for a in range(9)
-        ],
-        axis=0,
-    )
+    scale = have / npos
     rows_out = patch // samples
-    a_rows = lax.dynamic_slice_in_dim(factor, dp_id * rows_out, rows_out, 0).astype(jnp.float32)
-    a_out = (a_rows * (have / npos))[None]
-    g_out = (summed[NG + 9].astype(jnp.float32) * (have / npos))[None]
+    a_out = factor_rows(summed, dp_id * rows_out, scale, rows_out)[None]
+    g_out = (summed[NG + 9].astype(jnp.float32) * scale)[None]
     grad_sum = summed[NG : NG + 9].reshape(patch, chans).astype(jnp.float32)
     grad_scaled = grad_sum / jnp.sqrt(jnp.float32(npos))
     mixed = jnp.dot(grad_scaled, g_inv[0], precision=lax.Precision.HIGHEST)

time: 256 us -> 207 us (0.81)
  local copies, waits for them, and re-layouts: 69.3 us -> 18.7 us
  blocking collectives: 23.3 us -> 9.7 us
  waiting for transfers between devices: 59.5 us -> 68.2 us
  starting transfers between devices: 73.1 us -> 81.4 us
    unnamed x237 -> x165, local copies, waits for them, and re-layouts: 57.1 us -> 8.02 us
    all_to_all x3 -> x2, blocking collectives: 23.3 us -> 9.7 us  [exchange(): return lax.all_to_all(x, axis, split_axis=0, concat_axis=0, tiled=True)]
    all_to_all x8, starting transfers between devices: 37.2 us -> 45.5 us  [exchange(): return lax.all_to_all(x, axis, split_axis=0, concat_axis=0, tiled=True)]
    all_to_all x8, waiting for transfers between devices: 45.6 us -> 51.4 us  [exchange(): return lax.all_to_all(x, axis, split_axis=0, concat_axis=0, tiled=True)]
    ppermute x6, waiting for transfers between devices: 13.9 us -> 16.8 us  [shifted(): return lax.ppermute(x, OWNER, pairs)]
  transfers between devices with their start and end apart: 14 -> 14, of which waited for: 8 -> 9; matrix products, arithmetic and copies ran while one was open for 8% -> 8% of each run, Pallas kernels for 0% -> 0%
where the time goes in v4:
time: 207 us; the launch traced here: 203 us
  starting transfers between devices  81.4 us (39%)
  waiting for transfers between devices  68.2 us (33%)
  local copies, waits for them, and re-layouts  18.7 us (9%)
  between operations  10.3 us (5%)
  blocking collectives  9.7 us (5%)
  matrix products  7.69 us (4%)
  other arithmetic  6.57 us (3%)
    all_to_all x8, waiting for transfers between devices, exchange(): return lax.all_to_all(x, axis, split_axis=0, concat_axis=0, tiled=True)  51.4 us
    all_to_all x8, starting transfers between devices, exchange(): return lax.all_to_all(x, axis, split_axis=0, concat_axis=0, tiled=True)  45.5 us
    ppermute x6, starting transfers between devices, shifted(): return lax.ppermute(x, OWNER, pairs)  35.9 us
    ppermute x6, waiting for transfers between devices, shifted(): return lax.ppermute(x, OWNER, pairs)  16.8 us
    all_to_all x2, blocking collectives, exchange(): return lax.all_to_all(x, axis, split_axis=0, concat_axis=0, tiled=True)  9.7 us
    unnamed x165, local copies, waits for them, and re-layouts  8.02 us
  transfers between devices with their start and end apart: 14, of which 9 were waited for; matrix products, arithmetic and copies ran while one was open for 8% of the time, Pallas kernels for 0%

profile of v4, /device:TPU:6, one launch (start us, length us, event | category | flops | bytes accessed | tf_op | source)
XLA Modules:
  0.0 203.5 jit_solution(8741097294832294546)
XLA Ops:
  4.5 15.2 %collective-permute-start.1 = (bf16[7,80,128]{2,1,0:T(8,128)(2,1)S(1)}, bf16[7,80,128]{2,1,0:T(8,128)(2,1)S(1)}, u32[]{:S(2)}, u32[]{:S(2)}) collective-permute-start(bf16[7,80,128]{2,1,0:T(8,128)(2,1)S(1)} %constant_dynamic-update-slice_fusion), channel_id=1, source_target_pairs={{0,15},{1,0},{2,1},{3,2},{4,3},{5,4},{6,5},{7,6},{8,7},{9,8},{10,9... | collective-permute-start | bytes 430088 | tf_op jit(solution)/shard_map/ppermute | solution.py:18
  23.3 1.3 fusion.137
  26.0 5.9 %collective-permute-done.1 = bf16[7,80,128]{2,1,0:T(8,128)(2,1)S(1)} collective-permute-done((bf16[7,80,128]{2,1,0:T(8,128)(2,1)S(1)}, bf16[7,80,128]{2,1,0:T(8,128)(2,1)S(1)}, u32[]{:S(2)}, u32[]{:S(2)}) %collective-permute-start.1) | collective-permute-done | bytes 143392 | tf_op jit(solution)/shard_map/ppermute | solution.py:18
  35.3 10.4 %collective-permute-start.2 = (bf16[2,80,128]{2,1,0:T(8,128)(2,1)S(1)}, bf16[2,80,128]{2,1,0:T(8,128)(2,1)S(1)}, u32[]{:S(2)}, u32[]{:S(2)}) collective-permute-start(bf16[2,80,128]{2,1,0:T(8,128)(2,1)S(1)} %bitcast.309), channel_id=1, source_target_pairs={{0,15},{1,0},{2,1},{3,2},{4,3},{5,4},{6,5},{7,6},{8,7},{9,8},{10,9... | collective-permute-start | bytes 122888 | tf_op jit(solution)/shard_map/ppermute | solution.py:18
  47.6 3.5 %all-to-all-start = ((bf16[4,4,80,128]{3,2,1,0:T(8,128)(2,1)}), bf16[4,4,80,128]{3,2,1,0:T(8,128)(2,1)S(1)}, u32[]{:S(2)}, u32[]{:S(2)}) async-start(bf16[4,4,80,128]{3,2,1,0:T(8,128)(2,1)} %pad_maximum_fusion.1), calls=%async_computation | async-start | bytes 655360 | tf_op jit(solution)/shard_map/all_to_all | solution.py:22
  52.3 3.9 %collective-permute-start.3 = (bf16[2,80,128]{2,1,0:T(8,128)(2,1)S(1)}, bf16[2,80,128]{2,1,0:T(8,128)(2,1)S(1)}, u32[]{:S(2)}, u32[]{:S(2)}) collective-permute-start(bf16[2,80,128]{2,1,0:T(8,128)(2,1)S(1)} %bitcast.312), channel_id=1, source_target_pairs={{0,1},{1,2},{2,3},{3,4},{4,5},{5,6},{6,7},{7,8},{8,9},{9,10},{10,1... | collective-permute-start | bytes 122888 | tf_op jit(solution)/shard_map/ppermute | solution.py:18
  56.2 8.0 %collective-permute-done.3 = bf16[2,80,128]{2,1,0:T(8,128)(2,1)S(1)} collective-permute-done((bf16[2,80,128]{2,1,0:T(8,128)(2,1)S(1)}, bf16[2,80,128]{2,1,0:T(8,128)(2,1)S(1)}, u32[]{:S(2)}, u32[]{:S(2)}) %collective-permute-start.3) | collective-permute-done | bytes 40992 | tf_op jit(solution)/shard_map/ppermute | solution.py:18
  65.5 3.3 %all-to-all-start.1 = ((bf16[4,2,80,128]{3,2,1,0:T(8,128)(2,1)}), bf16[4,2,80,128]{3,2,1,0:T(8,128)(2,1)S(1)}, u32[]{:S(2)}, u32[]{:S(2)}) async-start(bf16[4,2,80,128]{3,2,1,0:T(8,128)(2,1)} %pad_maximum_fusion.8), calls=%async_computation.1 | async-start | bytes 327680 | tf_op jit(solution)/shard_map/all_to_all | solution.py:22
  70.8 2.4 %convolution_convert_fusion = bf16[1152,1152]{1,0:T(8,128)(2,1)S(1)} fusion(bf16[160,1152]{1,0:T(8,128)(2,1)S(1)} %constant_dynamic-update-slice_fusion.32, bf16[160,1152]{1,0:T(8,128)(2,1)S(1)} %constant_dynamic-update-slice_fusion.23, bf16[160,1152]{1,0:T(8,128)(2,1)S(1)} %constant_dynamic-update-slice_fusion.14, ...), kind=kOutput, calls=%fused_computation.1 | convolution fusion | flops 1705918464 | bytes 4128768 | tf_op jit(solution)/shard_map/dot_general | solution.py:66
  76.0 4.8 %all_to_all.50 = bf16[2,2560,128]{2,1,0:T(8,128)(2,1)S(1)} all-to-all(bf16[2,2560,128]{2,1,0:T(8,128)(2,1)S(1)} %bitcast.289), channel_id=1, replica_groups=mesh['x'=4,'zl'=4,'core'=2,'zh'=4,'y'=4] {'core'}, dimensions={0} | all-to-all | bytes 2621440 | tf_op jit(solution)/shard_map/all_to_all | solution.py:22
  82.0 4.9 %all-to-all-start.3 = ((bf16[16,160,128]{2,1,0:T(8,128)(2,1)}), bf16[16,160,128]{2,1,0:T(8,128)(2,1)S(1)}, u32[]{:S(2)}, u32[]{:S(2)}) async-start(bf16[16,160,128]{2,1,0:T(8,128)(2,1)} %bitcast.164), calls=%async_computation.3 | async-start | bytes 1310720 | tf_op jit(solution)/shard_map/all_to_all | solution.py:22
  86.9 17.3 %all-to-all-done.3 = bf16[16,160,128]{2,1,0:T(8,128)(2,1)S(1)} async-done(((bf16[16,160,128]{2,1,0:T(8,128)(2,1)}), bf16[16,160,128]{2,1,0:T(8,128)(2,1)S(1)}, u32[]{:S(2)}, u32[]{:S(2)}) %all-to-all-start.3) | async-done | bytes 655392 | tf_op jit(solution)/shard_map/all_to_all | solution.py:22
  105.1 4.2 %all-to-all-start.4 = ((bf16[4,160,128]{2,1,0:T(8,128)(2,1)}), bf16[4,160,128]{2,1,0:T(8,128)(2,1)S(1)}, u32[]{:S(2)}, u32[]{:S(2)}) async-start(bf16[4,160,128]{2,1,0:T(8,128)(2,1)} %broadcast_in_dim.27), calls=%async_computation.4 | async-start | bytes 327680 | tf_op jit(solution)/shard_map/all_to_all | solution.py:22
  118.1 7.0 %all-to-all-start.5 = ((bf16[4,160,128]{2,1,0:T(8,128)(2,1)}), bf16[4,160,128]{2,1,0:T(8,128)(2,1)S(1)}, u32[]{:S(2)}, u32[]{:S(2)}) async-start(bf16[4,160,128]{2,1,0:T(8,128)(2,1)} %pad_maximum_fusion.9), calls=%async_computation.5 | async-start | bytes 327680 | tf_op jit(solution)/shard_map/all_to_all | solution.py:22
  125.2 3.9 %collective-permute-start.4 = (bf16[1,80,128]{2,1,0:T(8,128)(2,1)S(1)}, bf16[1,80,128]{2,1,0:T(8,128)(2,1)S(1)}, u32[]{:S(2)}, u32[]{:S(2)}) collective-permute-start(bf16[1,80,128]{2,1,0:T(8,128)(2,1)S(1)} %get-tuple-element.185), channel_id=1, source_target_pairs={{0,1},{1,2},{2,3},{3,4},{4,5},{5,6},{6,7},{7,8},{8,9},{9,10},{10,1... | collective-permute-start | bytes 61448 | tf_op jit(solution)/shard_map/ppermute | solution.py:18
  132.0 2.8 %collective-permute-done.5 = bf16[1,80,128]{2,1,0:T(8,128)(2,1)S(1)} collective-permute-done((bf16[1,80,128]{2,1,0:T(8,128)(2,1)S(1)}, bf16[1,80,128]{2,1,0:T(8,128)(2,1)S(1)}, u32[]{:S(2)}, u32[]{:S(2)}) %collective-permute-start.5) | collective-permute-done | bytes 20512 | tf_op jit(solution)/shard_map/ppermute | solution.py:18
  134.9 5.6 %all-to-all-done.5 = bf16[4,160,128]{2,1,0:T(8,128)(2,1)S(1)} async-done(((bf16[4,160,128]{2,1,0:T(8,128)(2,1)}), bf16[4,160,128]{2,1,0:T(8,128)(2,1)S(1)}, u32[]{:S(2)}, u32[]{:S(2)}) %all-to-all-start.5) | async-done | bytes 163872 | tf_op jit(solution)/shard_map/all_to_all | solution.py:22
  141.1 3.3 %all-to-all-start.6 = ((bf16[4,160,128]{2,1,0:T(8,128)(2,1)}), bf16[4,160,128]{2,1,0:T(8,128)(2,1)S(1)}, u32[]{:S(2)}, u32[]{:S(2)}) async-start(bf16[4,160,128]{2,1,0:T(8,128)(2,1)} %broadcast_in_dim.29), calls=%async_computation.6 | async-start | bytes 327680 | tf_op jit(solution)/shard_map/all_to_all | solution.py:22
  144.6 5.8 %all-to-all-done.6 = bf16[4,160,128]{2,1,0:T(8,128)(2,1)S(1)} async-done(((bf16[4,160,128]{2,1,0:T(8,128)(2,1)}), bf16[4,160,128]{2,1,0:T(8,128)(2,1)S(1)}, u32[]{:S(2)}, u32[]{:S(2)}) %all-to-all-start.6) | async-done | bytes 163872 | tf_op jit(solution)/shard_map/all_to_all | solution.py:22
  151.4 5.0 %all-to-all-start.7 = ((bf16[4,4,160,128]{3,2,1,0:T(8,128)(2,1)}), bf16[4,4,160,128]{3,2,1,0:T(8,128)(2,1)S(1)}, u32[]{:S(2)}, u32[]{:S(2)}) async-start(bf16[4,4,160,128]{3,2,1,0:T(8,128)(2,1)} %broadcast_in_dim.30), calls=%async_computation.7 | async-start | bytes 1310720 | tf_op jit(solution)/shard_map/all_to_all | solution.py:22
  156.5 6.6 %all-to-all-done.7 = bf16[4,4,160,128]{3,2,1,0:T(8,128)(2,1)S(1)} async-done(((bf16[4,4,160,128]{3,2,1,0:T(8,128)(2,1)}), bf16[4,4,160,128]{3,2,1,0:T(8,128)(2,1)S(1)}, u32[]{:S(2)}, u32[]{:S(2)}) %all-to-all-start.7) | async-done | bytes 655392 | tf_op jit(solution)/shard_map/all_to_all | solution.py:22
  163.3 4.9 %all_to_all.51 = bf16[2,4,4,160,128]{4,3,2,1,0:T(8,128)(2,1)S(1)} all-to-all(bf16[2,4,4,160,128]{4,3,2,1,0:T(8,128)(2,1)S(1)} %broadcast_in_dim.31), channel_id=1, replica_groups=mesh['x'=4,'zl'=4,'core'=2,'zh'=4,'y'=4] {'core'}, dimensions={0} | all-to-all | bytes 2621440 | tf_op jit(solution)/shard_map/all_to_all | solution.py:22
  170.0 14.2 %all-to-all-start.9 = ((bf16[16,36,128]{2,1,0:T(8,128)(2,1)}), bf16[16,36,128]{2,1,0:T(8,128)(2,1)S(1)}, u32[]{:S(2)}, u32[]{:S(2)}) async-start(bf16[16,36,128]{2,1,0:T(8,128)(2,1)} %broadcast_in_dim.32), calls=%async_computation.9 | async-start | bytes 327680 | tf_op jit(solution)/shard_map/all_to_all | solution.py:22
  187.4 14.8 %all-to-all-done.9 = bf16[16,36,128]{2,1,0:T(8,128)(2,1)S(1)} async-done(((bf16[16,36,128]{2,1,0:T(8,128)(2,1)}), bf16[16,36,128]{2,1,0:T(8,128)(2,1)S(1)}, u32[]{:S(2)}, u32[]{:S(2)}) %all-to-all-start.9) | async-done | bytes 147488 | tf_op jit(solution)/shard_map/all_to_all | solution.py:22
  (274 shorter events, 33.9 us)
Async XLA Ops:
  0.6 168.3 %copy-start = (bf16[1,36,1152]{2,1,0:T(8,128)(2,1)S(1)}, bf16[1,36,1152]{2,1,0:T(8,128)(2,1)}, u32[]{:S(2)}) copy-start(bf16[1,36,1152]{2,1,0:T(8,128)(2,1)} %param.18) | copy-start | bytes 248836
  4.5 27.5 %collective-permute-start.1 = (bf16[7,80,128]{2,1,0:T(8,128)(2,1)S(1)}, bf16[7,80,128]{2,1,0:T(8,128)(2,1)S(1)}, u32[]{:S(2)}, u32[]{:S(2)}) collective-permute-start(bf16[7,80,128]{2,1,0:T(8,128)(2,1)S(1)} %constant_dynamic-update-slice_fusion), channel_id=1, source_target_pairs={{0,15},{1,0},{2,1},{3,2},{4,3},{5,4},{6,5},{7,6},{8,7},{9,8},{10,9... | collective-permute-start | bytes 430088 | tf_op jit(solution)/shard_map/ppermute | solution.py:18
  22.0 4.0 %collective-permute-start = (bf16[5,80,128]{2,1,0:T(8,128)(2,1)S(1)}, bf16[5,80,128]{2,1,0:T(8,128)(2,1)S(1)}, u32[]{:S(2)}, u32[]{:S(2)}) collective-permute-start(bf16[5,80,128]{2,1,0:T(8,128)(2,1)S(1)} %pad_maximum_fusion.12), channel_id=1, source_target_pairs={{0,1},{1,2},{2,3},{3,4},{4,5},{5,6},{6,7},{7,8},{8,9},{9,10},{10,1... | collective-permute-start | bytes 307208 | tf_op jit(solution)/shard_map/ppermute | solution.py:18
  35.3 15.8 %collective-permute-start.2 = (bf16[2,80,128]{2,1,0:T(8,128)(2,1)S(1)}, bf16[2,80,128]{2,1,0:T(8,128)(2,1)S(1)}, u32[]{:S(2)}, u32[]{:S(2)}) collective-permute-start(bf16[2,80,128]{2,1,0:T(8,128)(2,1)S(1)} %bitcast.309), channel_id=1, source_target_pairs={{0,15},{1,0},{2,1},{3,2},{4,3},{5,4},{6,5},{7,6},{8,7},{9,8},{10,9... | collective-permute-start | bytes 122888 | tf_op jit(solution)/shard_map/ppermute | solution.py:18
  45.9 5.2 %copy-start.14 = (bf16[3]{0:T(256)(128)(2,1)S(1)}, bf16[3]{0:T(256)(128)(2,1)}, u32[]{:S(2)}) copy-start(bf16[3]{0:T(256)(128)(2,1)} %constant.82.clone) | copy-start | bytes 22
  45.9 5.2 %copy-start.15 = (bf16[3]{0:T(256)(128)(2,1)S(1)}, bf16[3]{0:T(256)(128)(2,1)}, u32[]{:S(2)}) copy-start(bf16[3]{0:T(256)(128)(2,1)} %constant.83.clone) | copy-start | bytes 22
  47.6 17.9 %all-to-all-start = ((bf16[4,4,80,128]{3,2,1,0:T(8,128)(2,1)}), bf16[4,4,80,128]{3,2,1,0:T(8,128)(2,1)S(1)}, u32[]{:S(2)}, u32[]{:S(2)}) async-start(bf16[4,4,80,128]{3,2,1,0:T(8,128)(2,1)} %pad_maximum_fusion.1), calls=%async_computation | async-start | bytes 655360 | tf_op jit(solution)/shard_map/all_to_all | solution.py:22
  52.1 12.5 %copy-start.6 = (f32[160,128]{1,0:T(8,128)S(1)}, f32[160,128]{1,0:T(8,128)}, u32[]{:S(2)}) copy-start(f32[160,128]{1,0:T(8,128)} %fusion.13) | copy-start | bytes 245764
  52.3 11.9 %collective-permute-start.3 = (bf16[2,80,128]{2,1,0:T(8,128)(2,1)S(1)}, bf16[2,80,128]{2,1,0:T(8,128)(2,1)S(1)}, u32[]{:S(2)}, u32[]{:S(2)}) collective-permute-start(bf16[2,80,128]{2,1,0:T(8,128)(2,1)S(1)} %bitcast.312), channel_id=1, source_target_pairs={{0,1},{1,2},{2,3},{3,4},{4,5},{5,6},{6,7},{7,8},{8,9},{9,10},{10,1... | collective-permute-start | bytes 122888 | tf_op jit(solution)/shard_map/ppermute | solution.py:18
  65.5 9.5 %all-to-all-start.1 = ((bf16[4,2,80,128]{3,2,1,0:T(8,128)(2,1)}), bf16[4,2,80,128]{3,2,1,0:T(8,128)(2,1)S(1)}, u32[]{:S(2)}, u32[]{:S(2)}) async-start(bf16[4,2,80,128]{3,2,1,0:T(8,128)(2,1)} %pad_maximum_fusion.8), calls=%async_computation.1 | async-start | bytes 327680 | tf_op jit(solution)/shard_map/all_to_all | solution.py:22
  69.7 3.5 %copy-start.12 = (bf16[160,1152]{1,0:T(8,128)(2,1)}, bf16[160,1152]{1,0:T(8,128)(2,1)S(1)}, u32[]{:S(2)}) copy-start(bf16[160,1152]{1,0:T(8,128)(2,1)S(1)} %constant_dynamic-update-slice_fusion.5) | copy-start | bytes 1105924
  73.2 1.8 copy-start.9
  82.0 27.2 %copy-start.16 = (s32[4]{0:T(128)S(1)}, s32[4]{0:T(128)}, u32[]{:S(2)}) copy-start(s32[4]{0:T(128)} %param.17) | copy-start | bytes 52
  82.0 22.3 %all-to-all-start.3 = ((bf16[16,160,128]{2,1,0:T(8,128)(2,1)}), bf16[16,160,128]{2,1,0:T(8,128)(2,1)S(1)}, u32[]{:S(2)}, u32[]{:S(2)}) async-start(bf16[16,160,128]{2,1,0:T(8,128)(2,1)} %bitcast.164), calls=%async_computation.3 | async-start | bytes 1310720 | tf_op jit(solution)/shard_map/all_to_all | solution.py:22
  105.1 12.4 %all-to-all-start.4 = ((bf16[4,160,128]{2,1,0:T(8,128)(2,1)}), bf16[4,160,128]{2,1,0:T(8,128)(2,1)S(1)}, u32[]{:S(2)}, u32[]{:S(2)}) async-start(bf16[4,160,128]{2,1,0:T(8,128)(2,1)} %broadcast_in_dim.27), calls=%async_computation.4 | async-start | bytes 327680 | tf_op jit(solution)/shard_map/all_to_all | solution.py:22
  118.1 22.3 %all-to-all-start.5 = ((bf16[4,160,128]{2,1,0:T(8,128)(2,1)}), bf16[4,160,128]{2,1,0:T(8,128)(2,1)S(1)}, u32[]{:S(2)}, u32[]{:S(2)}) async-start(bf16[4,160,128]{2,1,0:T(8,128)(2,1)} %pad_maximum_fusion.9), calls=%async_computation.5 | async-start | bytes 327680 | tf_op jit(solution)/shard_map/all_to_all | solution.py:22
  125.2 6.8 %collective-permute-start.4 = (bf16[1,80,128]{2,1,0:T(8,128)(2,1)S(1)}, bf16[1,80,128]{2,1,0:T(8,128)(2,1)S(1)}, u32[]{:S(2)}, u32[]{:S(2)}) collective-permute-start(bf16[1,80,128]{2,1,0:T(8,128)(2,1)S(1)} %get-tuple-element.185), channel_id=1, source_target_pairs={{0,1},{1,2},{2,3},{3,4},{4,5},{5,6},{6,7},{7,8},{8,9},{9,10},{10,1... | collective-permute-start | bytes 61448 | tf_op jit(solution)/shard_map/ppermute | solution.py:18
  129.1 5.7 %collective-permute-start.5 = (bf16[1,80,128]{2,1,0:T(8,128)(2,1)S(1)}, bf16[1,80,128]{2,1,0:T(8,128)(2,1)S(1)}, u32[]{:S(2)}, u32[]{:S(2)}) collective-permute-start(bf16[1,80,128]{2,1,0:T(8,128)(2,1)S(1)} %get-tuple-element.186), channel_id=1, source_target_pairs={{1,0},{2,1},{3,2},{4,3},{5,4},{6,5},{7,6},{8,7},{9,8},{10,9},{11,1... | collective-permute-start | bytes 61448 | tf_op jit(solution)/shard_map/ppermute | solution.py:18
  141.1 9.3 %all-to-all-start.6 = ((bf16[4,160,128]{2,1,0:T(8,128)(2,1)}), bf16[4,160,128]{2,1,0:T(8,128)(2,1)S(1)}, u32[]{:S(2)}, u32[]{:S(2)}) async-start(bf16[4,160,128]{2,1,0:T(8,128)(2,1)} %broadcast_in_dim.29), calls=%async_computation.6 | async-start | bytes 327680 | tf_op jit(solution)/shard_map/all_to_all | solution.py:22
  151.4 11.7 %all-to-all-start.7 = ((bf16[4,4,160,128]{3,2,1,0:T(8,128)(2,1)}), bf16[4,4,160,128]{3,2,1,0:T(8,128)(2,1)S(1)}, u32[]{:S(2)}, u32[]{:S(2)}) async-start(bf16[4,4,160,128]{3,2,1,0:T(8,128)(2,1)} %broadcast_in_dim.30), calls=%async_computation.7 | async-start | bytes 1310720 | tf_op jit(solution)/shard_map/all_to_all | solution.py:22
  163.3 5.0 %copy-start.7 = (f32[1,128,128]{2,1,0:T(8,128)S(1)}, f32[1,128,128]{2,1,0:T(8,128)}, u32[]{:S(2)}) copy-start(f32[1,128,128]{2,1,0:T(8,128)} %param.19) | copy-start | bytes 196612
  168.3 16.8 %copy-start.1 = (s32[81]{0:T(128)S(1)}, s32[81]{0:T(128)}, u32[]{:S(2)}) copy-start(s32[81]{0:T(128)} %constant.84.clone.index_ref) | copy-start | bytes 976
  168.3 16.8 %copy-start.2 = (s32[81]{0:T(128)S(1)}, s32[81]{0:T(128)}, u32[]{:S(2)}) copy-start(s32[81]{0:T(128)} %constant.85.clone.flip_ref) | copy-start | bytes 976
  170.0 32.2 %all-to-all-start.9 = ((bf16[16,36,128]{2,1,0:T(8,128)(2,1)}), bf16[16,36,128]{2,1,0:T(8,128)(2,1)S(1)}, u32[]{:S(2)}, u32[]{:S(2)}) async-start(bf16[16,36,128]{2,1,0:T(8,128)(2,1)} %broadcast_in_dim.32), calls=%async_computation.9 | async-start | bytes 327680 | tf_op jit(solution)/shard_map/all_to_all | solution.py:22
  (7 other events, 8.0 us)

commit v5 on v4

--- a/solution.py
+++ b/solution.py
@@ -89,7 +89,6 @@
 
 PAIRS, WHERE = block_classes()
 NG = len(PAIRS)
-NBLOCKS = 40
 
 
 def factor_rows(blocks, first_row, scale, rows):
@@ -152,7 +151,14 @@
         jnp.concatenate([above[2:3], f[2], below[2:3]]),
         wide3[1:5],
     ]
-    layer_strips = exchange(jnp.stack(strips), "y")
+    local = jnp.concatenate(
+        [
+            a_inv.reshape(-1, chans),
+            g_inv[0].astype(jnp.bfloat16),
+            jnp.zeros((12, chans), jnp.bfloat16),
+        ]
+    )
+    inverses = lax.all_gather(local, OWNER, axis=0, tiled=True).reshape((owners,) + local.shape)
 
     flipped = jnp.transpose(weights.reshape(num_layers, 9, chans, chans), (0, 1, 3, 2)).reshape(
         num_layers, patch, chans
@@ -177,7 +183,9 @@
     after = shifted(dpre2, -1, True)
     dy1 = back(2, cut_windows(jnp.concatenate([dpre2, after]), inner))
     dpre1 = times(dy1, slope(1, cut_windows(strips[1], inner))).reshape(image)
+    stacked, dpre1 = lax.optimization_barrier((jnp.stack(strips), dpre1))
     before = shifted(dpre1, 1, True)
+    layer_strips = exchange(stacked, "y")
     edge_top = jnp.where(owner_id > 0, before[:1], jnp.zeros_like(before[:1]))
     edge_end = jnp.where(inner, dpre1[1:], jnp.zeros_like(dpre1[1:]))
     dy0 = back(1, windows(jnp.concatenate([edge_top, before[1:], dpre1[:1], edge_end])))
@@ -202,36 +210,53 @@
     blocks = [
         gram[a * chans : (a + 1) * chans, b * chans : (b + 1) * chans] for a, b in PAIRS
     ]
-    pad = jnp.zeros(((NBLOCKS - NG - 10) * chans, chans), jnp.bfloat16)
-    parts = jnp.concatenate(blocks + [grad, gfac, pad], axis=0)
-
-    piece = scatter_sum(scatter_sum(parts, "core"), ("x", "zl"))
-    held = spread(piece, "y")
+    half = (NG + 1) // 2
+    dense = jnp.concatenate([grad, jnp.zeros((chans, chans), jnp.bfloat16)])
+    cut = dense.shape[0] // 2
+    parts = jnp.concatenate(blocks[:half] + [dense[:cut]] + blocks[half:] + [gfac, dense[cut:]])
+
+    mine = scatter_sum(parts, "core")
+    rest = ("x", "zl")
+    count = lax.axis_size(rest)
+    fac_rows = half * chans // count
+    mine = jnp.concatenate(
+        [
+            mine[: half * chans].reshape(count, -1, chans),
+            mine[half * chans :].reshape(count, -1, chans),
+        ],
+        axis=1,
+    )
+    piece = scatter_sum(mine.reshape(-1, chans), rest)
+    held = spread(piece[:fac_rows], "y")
     layer_ids = jnp.arange(num_layers, dtype=jnp.int32)
 
     def pick(z):
         lay = jnp.sum(jnp.where(table == z * Y + y_id, layer_ids, 0))
         return lax.dynamic_index_in_dim(held, lay, 0, keepdims=False)
 
-    total = exchange(jnp.stack([pick(z) for z in range(ZH)]), "zh")
+    sent = jnp.stack([jnp.concatenate([pick(z), piece[fac_rows:]]) for z in range(ZH)])
+    total = exchange(sent, "zh")
     total = jnp.sum(total.astype(jnp.float32), axis=0).astype(jnp.bfloat16)
-    summed = spread(spread(spread(total, "zl"), "x"), "core")
+    summed = spread(spread(spread(total, "zl"), "x"), "core").reshape(samples, -1, chans)
 
     in_grad_win = jnp.concatenate([shifted(dpre0[1:], 1, False), dpre0, shifted(dpre0[:1], -1, False)])
     in_grad = back(0, windows(in_grad_win)).reshape((1,) + image)
 
-    summed = summed.reshape(NBLOCKS, chans, chans)
+    mine_inv = lax.dynamic_index_in_dim(inverses, table[y_id], 0, keepdims=False)
+    rows_out = patch // samples
+    a_mine = mine_inv[: rows_out * 9].reshape(rows_out, patch)
+    g_mine = mine_inv[rows_out * 9 : rows_out * 9 + chans]
+    grad_sum = summed[:, fac_rows:].reshape(-1, chans)[:patch]
+    mixed = jnp.dot(grad_sum, g_mine, preferred_element_type=jnp.float32)
+    mixed = mixed / jnp.sqrt(jnp.float32(npos))
+    panel = jnp.dot(a_mine.astype(jnp.float32), mixed, precision=lax.Precision.HIGHEST)
+    step_out = spread(panel.astype(jnp.bfloat16), "y")
+
+    stats = summed[:, :fac_rows].reshape(NG + 1, chans, chans)
     have = jnp.any(table == owner_id).astype(jnp.float32)
     scale = have / npos
-    rows_out = patch // samples
-    a_out = factor_rows(summed, dp_id * rows_out, scale, rows_out)[None]
-    g_out = (summed[NG + 9].astype(jnp.float32) * scale)[None]
-    grad_sum = summed[NG : NG + 9].reshape(patch, chans).astype(jnp.float32)
-    grad_scaled = grad_sum / jnp.sqrt(jnp.float32(npos))
-    mixed = jnp.dot(grad_scaled, g_inv[0], precision=lax.Precision.HIGHEST)
-    panel = jnp.dot(a_inv[0].astype(jnp.float32), mixed, precision=lax.Precision.HIGHEST)
-    panels = spread(panel.astype(jnp.bfloat16), OWNER)
-    step_out = panels[table]
+    a_out = factor_rows(stats, dp_id * rows_out, scale, rows_out)[None]
+    g_out = (stats[NG].astype(jnp.float32) * scale)[None]
     return (step_out, a_out, g_out, in_grad)
 
 

time: 207 us -> 245 us (1.18)
  the two profiles are of different devices: /device:TPU:6 before, /device:TPU:34 now
where the time goes in v5:
time: 245 us; the launch traced here: 241 us
  starting transfers between devices  82.9 us (34%)
  waiting for transfers between devices  63.7 us (26%)
  local copies, waits for them, and re-layouts  40.9 us (17%)
  between operations  25.6 us (10%)
  matrix products  9.9 us (4%)
  blocking collectives  9.57 us (4%)
  other arithmetic  7.64 us (3%)
    all_to_all x8, starting transfers between devices, exchange(): return lax.all_to_all(x, axis, split_axis=0, concat_axis=0, tiled=True)  50.5 us
    all_to_all x8, waiting for transfers between devices, exchange(): return lax.all_to_all(x, axis, split_axis=0, concat_axis=0, tiled=True)  39 us
    ppermute x6, starting transfers between devices, shifted(): return lax.ppermute(x, OWNER, pairs)  32.5 us
    unnamed x152, local copies, waits for them, and re-layouts  29.7 us
    ppermute x6, waiting for transfers between devices, shifted(): return lax.ppermute(x, OWNER, pairs)  12.7 us
    all_gather x1, waiting for transfers between devices, shards(): lax.all_gather(local, OWNER, axis=0, tiled=True)  11.8 us
    all_to_all x2, blocking collectives, exchange(): return lax.all_to_all(x, axis, split_axis=0, concat_axis=0, tiled=True)  9.57 us
    dot_general x3, matrix products, inner_rows(): lax.dot_general(left, right, (((0,), (0,)), ((), ())), preferred_element_...  5.77 us
  transfers between devices with their start and end apart: 15, of which 10 were waited for; matrix products, arithmetic and copies ran while one was open for 9% of the time, Pallas kernels for 0%

profile of v5, /device:TPU:34, one launch (start us, length us, event | category | flops | bytes accessed | tf_op | source)
XLA Modules:
  0.0 241.1 jit_solution(5307119826493095740)
XLA Ops:
  10.9 14.3 %collective-permute-start.1 = (bf16[7,80,128]{2,1,0:T(8,128)(2,1)S(1)}, bf16[7,80,128]{2,1,0:T(8,128)(2,1)S(1)}, u32[]{:S(2)}, u32[]{:S(2)}) collective-permute-start(bf16[7,80,128]{2,1,0:T(8,128)(2,1)S(1)} %constant_dynamic-update-slice_fusion), channel_id=1, source_target_pairs={{0,15},{1,0},{2,1},{3,2},{4,3},{5,4},{6,5},{7,6},{8,7},{9,8},{10,9... | collective-permute-start | bytes 430088 | tf_op jit(solution)/shard_map/ppermute | solution.py:18
  28.9 1.3 fusion.137
  31.1 5.0 %collective-permute-done.1 = bf16[7,80,128]{2,1,0:T(8,128)(2,1)S(1)} collective-permute-done((bf16[7,80,128]{2,1,0:T(8,128)(2,1)S(1)}, bf16[7,80,128]{2,1,0:T(8,128)(2,1)S(1)}, u32[]{:S(2)}, u32[]{:S(2)}) %collective-permute-start.1) | collective-permute-done | bytes 143392 | tf_op jit(solution)/shard_map/ppermute | solution.py:18
  39.5 10.4 %collective-permute-start.2 = (bf16[2,80,128]{2,1,0:T(8,128)(2,1)S(1)}, bf16[2,80,128]{2,1,0:T(8,128)(2,1)S(1)}, u32[]{:S(2)}, u32[]{:S(2)}) collective-permute-start(bf16[2,80,128]{2,1,0:T(8,128)(2,1)S(1)} %bitcast.325), channel_id=1, source_target_pairs={{0,15},{1,0},{2,1},{3,2},{4,3},{5,4},{6,5},{7,6},{8,7},{9,8},{10,9... | collective-permute-start | bytes 122888 | tf_op jit(solution)/shard_map/ppermute | solution.py:18
  52.8 1.9 collective-permute-start.3
  54.8 3.5 %all-to-all-start = ((bf16[4,4,80,128]{3,2,1,0:T(8,128)(2,1)}), bf16[4,4,80,128]{3,2,1,0:T(8,128)(2,1)S(1)}, u32[]{:S(2)}, u32[]{:S(2)}) async-start(bf16[4,4,80,128]{3,2,1,0:T(8,128)(2,1)} %pad_maximum_fusion.2), calls=%async_computation | async-start | bytes 655360 | tf_op jit(solution)/shard_map/all_to_all | solution.py:22
  58.2 7.3 %collective-permute-done.3 = bf16[2,80,128]{2,1,0:T(8,128)(2,1)S(1)} collective-permute-done((bf16[2,80,128]{2,1,0:T(8,128)(2,1)S(1)}, bf16[2,80,128]{2,1,0:T(8,128)(2,1)S(1)}, u32[]{:S(2)}, u32[]{:S(2)}) %collective-permute-start.3) | collective-permute-done | bytes 40992 | tf_op jit(solution)/shard_map/ppermute | solution.py:18
  66.8 3.3 %all-to-all-start.1 = ((bf16[4,2,80,128]{3,2,1,0:T(8,128)(2,1)}), bf16[4,2,80,128]{3,2,1,0:T(8,128)(2,1)S(1)}, u32[]{:S(2)}, u32[]{:S(2)}) async-start(bf16[4,2,80,128]{3,2,1,0:T(8,128)(2,1)} %pad_maximum_fusion.9), calls=%async_computation.1 | async-start | bytes 327680 | tf_op jit(solution)/shard_map/all_to_all | solution.py:22
  71.7 3.9 %convolution_convert_fusion = bf16[1152,1152]{1,0:T(8,128)(2,1)} fusion(bf16[160,1152]{1,0:T(8,128)(2,1)S(1)} %constant_dynamic-update-slice_fusion.77, bf16[160,1152]{1,0:T(8,128)(2,1)S(1)} %constant_dynamic-update-slice_fusion.68, bf16[160,1152]{1,0:T(8,128)(2,1)S(1)} %constant_dynamic-update-slice_fusion.59, ...), kind=kOutput, calls=%fused_computation | convolution fusion | flops 1705918464 | bytes 4128768 | tf_op jit(solution)/shard_map/dot_general | solution.py:66
  76.3 1.6 convolution_convert_fusion.1
  100.4 4.8 %all_to_all.50 = bf16[2,2560,128]{2,1,0:T(8,128)(2,1)S(1)} all-to-all(bf16[2,2560,128]{2,1,0:T(8,128)(2,1)S(1)} %bitcast.303), channel_id=1, replica_groups=mesh['x'=4,'zl'=4,'core'=2,'zh'=4,'y'=4] {'core'}, dimensions={0} | all-to-all | bytes 2621440 | tf_op jit(solution)/shard_map/all_to_all | solution.py:22
  106.8 6.7 %all-to-all-start.3 = ((bf16[16,160,128]{2,1,0:T(8,128)(2,1)}), bf16[16,160,128]{2,1,0:T(8,128)(2,1)S(1)}, u32[]{:S(2)}, u32[]{:S(2)}) async-start(bf16[16,160,128]{2,1,0:T(8,128)(2,1)} %pad_maximum_fusion.1), calls=%async_computation.3 | async-start | bytes 1310720 | tf_op jit(solution)/shard_map/all_to_all | solution.py:22
  115.3 3.3 %collective-permute-start.4 = (bf16[1,80,128]{2,1,0:T(8,128)(2,1)S(1)}, bf16[1,80,128]{2,1,0:T(8,128)(2,1)S(1)}, u32[]{:S(2)}, u32[]{:S(2)}) collective-permute-start(bf16[1,80,128]{2,1,0:T(8,128)(2,1)S(1)} %get-tuple-element.193), channel_id=1, source_target_pairs={{0,1},{1,2},{2,3},{3,4},{4,5},{5,6},{6,7},{7,8},{8,9},{9,10},{10,1... | collective-permute-start | bytes 61448 | tf_op jit(solution)/shard_map/ppermute | solution.py:18
  132.3 9.2 %all-to-all-start.4 = ((bf16[4,120,128]{2,1,0:T(8,128)(2,1)}), bf16[4,120,128]{2,1,0:T(8,128)(2,1)S(1)}, u32[]{:S(2)}, u32[]{:S(2)}) async-start(bf16[4,120,128]{2,1,0:T(8,128)(2,1)} %broadcast_in_dim.25), calls=%async_computation.4 | async-start | bytes 245760 | tf_op jit(solution)/shard_map/all_to_all | solution.py:22
  141.5 5.9 %all-to-all-done.4 = bf16[4,120,128]{2,1,0:T(8,128)(2,1)S(1)} async-done(((bf16[4,120,128]{2,1,0:T(8,128)(2,1)}), bf16[4,120,128]{2,1,0:T(8,128)(2,1)S(1)}, u32[]{:S(2)}, u32[]{:S(2)}) %all-to-all-start.4) | async-done | bytes 122912 | tf_op jit(solution)/shard_map/all_to_all | solution.py:22
  148.1 14.4 %all-to-all-start.5 = ((bf16[4,160,128]{2,1,0:T(8,128)(2,1)}), bf16[4,160,128]{2,1,0:T(8,128)(2,1)S(1)}, u32[]{:S(2)}, u32[]{:S(2)}) async-start(bf16[4,160,128]{2,1,0:T(8,128)(2,1)} %pad_maximum_fusion.10), calls=%async_computation.5 | async-start | bytes 327680 | tf_op jit(solution)/shard_map/all_to_all | solution.py:22
  162.7 14.4 %all-to-all-done.5 = bf16[4,160,128]{2,1,0:T(8,128)(2,1)S(1)} async-done(((bf16[4,160,128]{2,1,0:T(8,128)(2,1)}), bf16[4,160,128]{2,1,0:T(8,128)(2,1)S(1)}, u32[]{:S(2)}, u32[]{:S(2)}) %all-to-all-start.5) | async-done | bytes 163872 | tf_op jit(solution)/shard_map/all_to_all | solution.py:22
  177.8 5.4 %all-to-all-start.6 = ((bf16[4,160,128]{2,1,0:T(8,128)(2,1)}), bf16[4,160,128]{2,1,0:T(8,128)(2,1)S(1)}, u32[]{:S(2)}, u32[]{:S(2)}) async-start(bf16[4,160,128]{2,1,0:T(8,128)(2,1)} %broadcast_in_dim.27), calls=%async_computation.6 | async-start | bytes 327680 | tf_op jit(solution)/shard_map/all_to_all | solution.py:22
  183.3 15.0 %all-to-all-done.6 = bf16[4,160,128]{2,1,0:T(8,128)(2,1)S(1)} async-done(((bf16[4,160,128]{2,1,0:T(8,128)(2,1)}), bf16[4,160,128]{2,1,0:T(8,128)(2,1)S(1)}, u32[]{:S(2)}, u32[]{:S(2)}) %all-to-all-start.6) | async-done | bytes 163872 | tf_op jit(solution)/shard_map/all_to_all | solution.py:22
  199.3 4.7 %all-to-all-start.7 = ((bf16[4,4,160,128]{3,2,1,0:T(8,128)(2,1)}), bf16[4,4,160,128]{3,2,1,0:T(8,128)(2,1)S(1)}, u32[]{:S(2)}, u32[]{:S(2)}) async-start(bf16[4,4,160,128]{3,2,1,0:T(8,128)(2,1)} %broadcast_in_dim.28), calls=%async_computation.7 | async-start | bytes 1310720 | tf_op jit(solution)/shard_map/all_to_all | solution.py:22
  204.9 11.8 %all-gather.2.cloned.1.call-done = bf16[7424,128]{1,0:T(8,128)(2,1)} async-done(((bf16[464,128]{1,0:T(8,128)(2,1)}), bf16[7424,128]{1,0:T(8,128)(2,1)}) %all-gather.2.cloned.1.call-update) | async-done | bytes 1900560 | tf_op jit(solution)/shard_map/all_gather | solution.py:161
  218.0 4.8 %all_to_all.51 = bf16[2,4,4,160,128]{4,3,2,1,0:T(8,128)(2,1)S(1)} all-to-all(bf16[2,4,4,160,128]{4,3,2,1,0:T(8,128)(2,1)S(1)} %broadcast_in_dim.29), channel_id=1, replica_groups=mesh['x'=4,'zl'=4,'core'=2,'zh'=4,'y'=4] {'core'}, dimensions={0} | all-to-all | bytes 2621440 | tf_op jit(solution)/shard_map/all_to_all | solution.py:22
  224.9 3.3 %all-to-all-start.9 = ((bf16[4,36,128]{2,1,0:T(8,128)(2,1)}), bf16[4,36,128]{2,1,0:T(8,128)(2,1)S(1)}, u32[]{:S(2)}, u32[]{:S(2)}) async-start(bf16[4,36,128]{2,1,0:T(8,128)(2,1)} %broadcast_in_dim.30), calls=%async_computation.9 | async-start | bytes 81920 | tf_op jit(solution)/shard_map/all_to_all | solution.py:22
  230.5 3.1 %all-to-all-done.9 = bf16[4,36,128]{2,1,0:T(8,128)(2,1)S(1)} async-done(((bf16[4,36,128]{2,1,0:T(8,128)(2,1)}), bf16[4,36,128]{2,1,0:T(8,128)(2,1)S(1)}, u32[]{:S(2)}, u32[]{:S(2)}) %all-to-all-start.9) | async-done | bytes 36896 | tf_op jit(solution)/shard_map/all_to_all | solution.py:22
  (277 shorter events, 56.2 us)
Async XLA Ops:
  10.9 25.2 %collective-permute-start.1 = (bf16[7,80,128]{2,1,0:T(8,128)(2,1)S(1)}, bf16[7,80,128]{2,1,0:T(8,128)(2,1)S(1)}, u32[]{:S(2)}, u32[]{:S(2)}) collective-permute-start(bf16[7,80,128]{2,1,0:T(8,128)(2,1)S(1)} %constant_dynamic-update-slice_fusion), channel_id=1, source_target_pairs={{0,15},{1,0},{2,1},{3,2},{4,3},{5,4},{6,5},{7,6},{8,7},{9,8},{10,9... | collective-permute-start | bytes 430088 | tf_op jit(solution)/shard_map/ppermute | solution.py:18
  27.6 3.5 %collective-permute-start = (bf16[5,80,128]{2,1,0:T(8,128)(2,1)S(1)}, bf16[5,80,128]{2,1,0:T(8,128)(2,1)S(1)}, u32[]{:S(2)}, u32[]{:S(2)}) collective-permute-start(bf16[5,80,128]{2,1,0:T(8,128)(2,1)S(1)} %pad_maximum_fusion.13), channel_id=1, source_target_pairs={{0,1},{1,2},{2,3},{3,4},{4,5},{5,6},{6,7},{7,8},{8,9},{9,10},{10,1... | collective-permute-start | bytes 307208 | tf_op jit(solution)/shard_map/ppermute | solution.py:18
  36.2 1.3 copy-start.2
  37.8 0.8 copy-start.3
  39.5 12.1 %collective-permute-start.2 = (bf16[2,80,128]{2,1,0:T(8,128)(2,1)S(1)}, bf16[2,80,128]{2,1,0:T(8,128)(2,1)S(1)}, u32[]{:S(2)}, u32[]{:S(2)}) collective-permute-start(bf16[2,80,128]{2,1,0:T(8,128)(2,1)S(1)} %bitcast.325), channel_id=1, source_target_pairs={{0,15},{1,0},{2,1},{3,2},{4,3},{5,4},{6,5},{7,6},{8,7},{9,8},{10,9... | collective-permute-start | bytes 122888 | tf_op jit(solution)/shard_map/ppermute | solution.py:18
  50.1 1.5 copy-start.7
  50.1 1.5 copy-start.8
  52.8 12.7 %collective-permute-start.3 = (bf16[2,80,128]{2,1,0:T(8,128)(2,1)S(1)}, bf16[2,80,128]{2,1,0:T(8,128)(2,1)S(1)}, u32[]{:S(2)}, u32[]{:S(2)}) collective-permute-start(bf16[2,80,128]{2,1,0:T(8,128)(2,1)S(1)} %bitcast.328), channel_id=1, source_target_pairs={{0,1},{1,2},{2,3},{3,4},{4,5},{5,6},{6,7},{7,8},{8,9},{9,10},{10,1... | collective-permute-start | bytes 122888 | tf_op jit(solution)/shard_map/ppermute | solution.py:18
  54.8 12.0 %all-to-all-start = ((bf16[4,4,80,128]{3,2,1,0:T(8,128)(2,1)}), bf16[4,4,80,128]{3,2,1,0:T(8,128)(2,1)S(1)}, u32[]{:S(2)}, u32[]{:S(2)}) async-start(bf16[4,4,80,128]{3,2,1,0:T(8,128)(2,1)} %pad_maximum_fusion.2), calls=%async_computation | async-start | bytes 655360 | tf_op jit(solution)/shard_map/all_to_all | solution.py:22
  66.8 9.5 %all-to-all-start.1 = ((bf16[4,2,80,128]{3,2,1,0:T(8,128)(2,1)}), bf16[4,2,80,128]{3,2,1,0:T(8,128)(2,1)S(1)}, u32[]{:S(2)}, u32[]{:S(2)}) async-start(bf16[4,2,80,128]{3,2,1,0:T(8,128)(2,1)} %pad_maximum_fusion.9), calls=%async_computation.1 | async-start | bytes 327680 | tf_op jit(solution)/shard_map/all_to_all | solution.py:22
  105.9 7.6 %copy-start.4 = (bf16[1,36,1152]{2,1,0:T(8,128)(2,1)S(1)}, bf16[1,36,1152]{2,1,0:T(8,128)(2,1)}, u32[]{:S(2)}) copy-start(bf16[1,36,1152]{2,1,0:T(8,128)(2,1)} %param.18) | copy-start | bytes 248836
  105.9 7.8 %copy-start.5 = (f32[1,128,128]{2,1,0:T(8,128)S(1)}, f32[1,128,128]{2,1,0:T(8,128)}, u32[]{:S(2)}) copy-start(f32[1,128,128]{2,1,0:T(8,128)} %param.19) | copy-start | bytes 196612
  105.9 8.7 %copy-start.9 = (s32[4]{0:T(128)S(1)}, s32[4]{0:T(128)}, u32[]{:S(2)}) copy-start(s32[4]{0:T(128)} %param.17) | copy-start | bytes 52
  106.8 24.7 %all-to-all-start.3 = ((bf16[16,160,128]{2,1,0:T(8,128)(2,1)}), bf16[16,160,128]{2,1,0:T(8,128)(2,1)S(1)}, u32[]{:S(2)}, u32[]{:S(2)}) async-start(bf16[16,160,128]{2,1,0:T(8,128)(2,1)} %pad_maximum_fusion.1), calls=%async_computation.3 | async-start | bytes 1310720 | tf_op jit(solution)/shard_map/all_to_all | solution.py:22
  113.5 103.2 %all-gather.2.cloned.1.call-start = ((), (), s32[]{:S(2)}) async-start(), calls=%async_computation.10 | async-start | bytes 2019328 | tf_op jit(solution)/shard_map/all_gather | solution.py:161
  115.3 26.2 %collective-permute-start.4 = (bf16[1,80,128]{2,1,0:T(8,128)(2,1)S(1)}, bf16[1,80,128]{2,1,0:T(8,128)(2,1)S(1)}, u32[]{:S(2)}, u32[]{:S(2)}) collective-permute-start(bf16[1,80,128]{2,1,0:T(8,128)(2,1)S(1)} %get-tuple-element.193), channel_id=1, source_target_pairs={{0,1},{1,2},{2,3},{3,4},{4,5},{5,6},{6,7},{7,8},{8,9},{9,10},{10,1... | collective-permute-start | bytes 61448 | tf_op jit(solution)/shard_map/ppermute | solution.py:18
  118.5 22.9 %collective-permute-start.5 = (bf16[1,80,128]{2,1,0:T(8,128)(2,1)S(1)}, bf16[1,80,128]{2,1,0:T(8,128)(2,1)S(1)}, u32[]{:S(2)}, u32[]{:S(2)}) collective-permute-start(bf16[1,80,128]{2,1,0:T(8,128)(2,1)S(1)} %get-tuple-element.194), channel_id=1, source_target_pairs={{1,0},{2,1},{3,2},{4,3},{5,4},{6,5},{7,6},{8,7},{9,8},{10,9},{11,1... | collective-permute-start | bytes 61448 | tf_op jit(solution)/shard_map/ppermute | solution.py:18
  132.3 15.1 %all-to-all-start.4 = ((bf16[4,120,128]{2,1,0:T(8,128)(2,1)}), bf16[4,120,128]{2,1,0:T(8,128)(2,1)S(1)}, u32[]{:S(2)}, u32[]{:S(2)}) async-start(bf16[4,120,128]{2,1,0:T(8,128)(2,1)} %broadcast_in_dim.25), calls=%async_computation.4 | async-start | bytes 245760 | tf_op jit(solution)/shard_map/all_to_all | solution.py:22
  148.1 29.0 %all-to-all-start.5 = ((bf16[4,160,128]{2,1,0:T(8,128)(2,1)}), bf16[4,160,128]{2,1,0:T(8,128)(2,1)S(1)}, u32[]{:S(2)}, u32[]{:S(2)}) async-start(bf16[4,160,128]{2,1,0:T(8,128)(2,1)} %pad_maximum_fusion.10), calls=%async_computation.5 | async-start | bytes 327680 | tf_op jit(solution)/shard_map/all_to_all | solution.py:22
  177.8 20.5 %all-to-all-start.6 = ((bf16[4,160,128]{2,1,0:T(8,128)(2,1)}), bf16[4,160,128]{2,1,0:T(8,128)(2,1)S(1)}, u32[]{:S(2)}, u32[]{:S(2)}) async-start(bf16[4,160,128]{2,1,0:T(8,128)(2,1)} %broadcast_in_dim.27), calls=%async_computation.6 | async-start | bytes 327680 | tf_op jit(solution)/shard_map/all_to_all | solution.py:22
  199.3 18.5 %all-to-all-start.7 = ((bf16[4,4,160,128]{3,2,1,0:T(8,128)(2,1)}), bf16[4,4,160,128]{3,2,1,0:T(8,128)(2,1)S(1)}, u32[]{:S(2)}, u32[]{:S(2)}) async-start(bf16[4,4,160,128]{3,2,1,0:T(8,128)(2,1)} %broadcast_in_dim.28), calls=%async_computation.7 | async-start | bytes 1310720 | tf_op jit(solution)/shard_map/all_to_all | solution.py:22
  222.8 6.0 %copy-start = (s32[81]{0:T(128)S(1)}, s32[81]{0:T(128)}, u32[]{:S(2)}) copy-start(s32[81]{0:T(128)} %constant.87.clone.index_ref) | copy-start | bytes 976
  222.8 5.9 %copy-start.1 = (s32[81]{0:T(128)S(1)}, s32[81]{0:T(128)}, u32[]{:S(2)}) copy-start(s32[81]{0:T(128)} %constant.88.clone.flip_ref) | copy-start | bytes 976
  224.9 8.7 %all-to-all-start.9 = ((bf16[4,36,128]{2,1,0:T(8,128)(2,1)}), bf16[4,36,128]{2,1,0:T(8,128)(2,1)S(1)}, u32[]{:S(2)}, u32[]{:S(2)}) async-start(bf16[4,36,128]{2,1,0:T(8,128)(2,1)} %broadcast_in_dim.30), calls=%async_computation.9 | async-start | bytes 81920 | tf_op jit(solution)/shard_map/all_to_all | solution.py:22
  (1 other events, 0.8 us)
Sparse Core Ops, SparseCore 0:
  117.3 99.3 all-gather.1

commit v6 on v5

--- a/solution.py
+++ b/solution.py
@@ -126,6 +126,39 @@
     )(index, flips, first_row.reshape(1), scale.reshape(1), blocks)
 
 
+def local_sums(gram, cols, dpre):
+    chans = dpre.shape[-1]
+    half = (NG + 1) // 2
+
+    def kernel(gram_ref, cols_ref, dpre_ref, out_ref):
+        def put(kind, index, value):
+            per = half if kind == 0 else 5
+            slot = index // per * (half + 5) + index % per + (half if kind else 0)
+            out_ref[slot * chans : (slot + 1) * chans, :] = value.astype(out_ref.dtype)
+
+        for i, (a, b) in enumerate(PAIRS):
+            put(0, i, gram_ref[a * chans : (a + 1) * chans, b * chans : (b + 1) * chans])
+        across = (((0,), (0,)), ((), ()))
+        mine = dpre_ref[...]
+        put(0, NG, lax.dot_general(mine, mine, across, preferred_element_type=jnp.float32))
+        grad = lax.dot_general(mine, cols_ref[...], across, preferred_element_type=jnp.float32)
+        for t in range(9):
+            put(1, t, grad[:, t * chans : (t + 1) * chans].T)
+        put(1, 9, jnp.zeros((chans, chans), jnp.float32))
+
+    vmem = pl.BlockSpec(memory_space=pltpu.VMEM)
+    return pl.pallas_call(
+        kernel,
+        out_shape=jax.ShapeDtypeStruct(((NG + 11) * chans, chans), jnp.bfloat16),
+        in_specs=[vmem] * 3,
+        out_specs=vmem,
+        compiler_params=pltpu.CompilerParams(vmem_limit_bytes=24 * 2**20),
+        cost_estimate=pl.CostEstimate(
+            flops=2 * cols.size * chans, bytes_accessed=6 * 10**6, transcendentals=0
+        ),
+    )(gram, cols, dpre)
+
+
 def shards(feats, top_grad, weights, table, a_inv, g_inv):
     num_layers, _, rows_dev, width, chans = feats.shape
     owners = lax.axis_size(OWNER)
@@ -151,15 +184,6 @@
         jnp.concatenate([above[2:3], f[2], below[2:3]]),
         wide3[1:5],
     ]
-    local = jnp.concatenate(
-        [
-            a_inv.reshape(-1, chans),
-            g_inv[0].astype(jnp.bfloat16),
-            jnp.zeros((12, chans), jnp.bfloat16),
-        ]
-    )
-    inverses = lax.all_gather(local, OWNER, axis=0, tiled=True).reshape((owners,) + local.shape)
-
     flipped = jnp.transpose(weights.reshape(num_layers, 9, chans, chans), (0, 1, 3, 2)).reshape(
         num_layers, patch, chans
     )
@@ -183,9 +207,20 @@
     after = shifted(dpre2, -1, True)
     dy1 = back(2, cut_windows(jnp.concatenate([dpre2, after]), inner))
     dpre1 = times(dy1, slope(1, cut_windows(strips[1], inner))).reshape(image)
-    stacked, dpre1 = lax.optimization_barrier((jnp.stack(strips), dpre1))
+    strip_rows = (rows_dev + 2) * width
+    local = jnp.concatenate([a_inv.reshape(-1, chans), g_inv[0].astype(jnp.bfloat16)])
+    local = jnp.broadcast_to(local[None], (num_layers,) + local.shape)
+    stacked = jnp.stack(strips).reshape(num_layers, strip_rows, chans)
+    pad = jnp.zeros((num_layers, -local.shape[1] % 16, chans), jnp.bfloat16)
+    stacked, dpre1 = lax.optimization_barrier(
+        (jnp.concatenate([stacked, local, pad], axis=1), dpre1)
+    )
     before = shifted(dpre1, 1, True)
-    layer_strips = exchange(stacked, "y")
+    from_y = exchange(stacked, "y")
+    layer_strips = from_y[:, :strip_rows].reshape(num_layers, rows_dev + 2, width, chans)
+    source = table[y_id]
+    near = lax.dynamic_index_in_dim(from_y, source % Y, 0, keepdims=False)[strip_rows:]
+    inverses = spread(near, "zh")
     edge_top = jnp.where(owner_id > 0, before[:1], jnp.zeros_like(before[:1]))
     edge_end = jnp.where(inner, dpre1[1:], jnp.zeros_like(dpre1[1:]))
     dy0 = back(1, windows(jnp.concatenate([edge_top, before[1:], dpre1[:1], edge_end])))
@@ -205,15 +240,8 @@
         ]
     )
     gram = inner_rows(big_cols, big_cols).astype(jnp.bfloat16)
-    grad = inner_rows(big_cols, big_dpre).astype(jnp.bfloat16)
-    gfac = inner_rows(big_dpre, big_dpre).astype(jnp.bfloat16)
-    blocks = [
-        gram[a * chans : (a + 1) * chans, b * chans : (b + 1) * chans] for a, b in PAIRS
-    ]
     half = (NG + 1) // 2
-    dense = jnp.concatenate([grad, jnp.zeros((chans, chans), jnp.bfloat16)])
-    cut = dense.shape[0] // 2
-    parts = jnp.concatenate(blocks[:half] + [dense[:cut]] + blocks[half:] + [gfac, dense[cut:]])
+    parts = local_sums(gram, big_cols, big_dpre)
 
     mine = scatter_sum(parts, "core")
     rest = ("x", "zl")
@@ -227,6 +255,7 @@
         axis=1,
     )
     piece = scatter_sum(mine.reshape(-1, chans), rest)
+    piece, inverses = lax.optimization_barrier((piece, inverses))
     held = spread(piece[:fac_rows], "y")
     layer_ids = jnp.arange(num_layers, dtype=jnp.int32)
 
@@ -242,7 +271,7 @@
     in_grad_win = jnp.concatenate([shifted(dpre0[1:], 1, False), dpre0, shifted(dpre0[:1], -1, False)])
     in_grad = back(0, windows(in_grad_win)).reshape((1,) + image)
 
-    mine_inv = lax.dynamic_index_in_dim(inverses, table[y_id], 0, keepdims=False)
+    mine_inv = lax.dynamic_index_in_dim(inverses, source // Y, 0, keepdims=False)
     rows_out = patch // samples
     a_mine = mine_inv[: rows_out * 9].reshape(rows_out, patch)
     g_mine = mine_inv[rows_out * 9 : rows_out * 9 + chans]

time: 245 us -> 222 us (0.906)
  the two profiles are of different devices: /device:TPU:34 before, /device:TPU:6 now
where the time goes in v6:
time: 222 us; the launch traced here: 218 us
  starting transfers between devices  79.8 us (36%)
  waiting for transfers between devices  76.4 us (34%)
  local copies, waits for them, and re-layouts  22.5 us (10%)
  between operations  13 us (6%)
  blocking collectives  9.57 us (4%)
  other arithmetic  8.3 us (4%)
  matrix products  7.27 us (3%)
    all_to_all x9, waiting for transfers between devices, exchange(): return lax.all_to_all(x, axis, split_axis=0, concat_axis=0, tiled=True)  65.2 us
    all_to_all x9, starting transfers between devices, exchange(): return lax.all_to_all(x, axis, split_axis=0, concat_axis=0, tiled=True)  46.6 us
    ppermute x6, starting transfers between devices, shifted(): return lax.ppermute(x, OWNER, pairs)  33.2 us
    ppermute x6, waiting for transfers between devices, shifted(): return lax.ppermute(x, OWNER, pairs)  11.2 us
    all_to_all x2, blocking collectives, exchange(): return lax.all_to_all(x, axis, split_axis=0, concat_axis=0, tiled=True)  9.57 us
    unnamed x126, local copies, waits for them, and re-layouts  9.39 us
  transfers between devices with their start and end apart: 15, of which 11 were waited for; matrix products, arithmetic and copies ran while one was open for 10% of the time, Pallas kernels for 0%

profile of v6, /device:TPU:6, one launch (start us, length us, event | category | flops | bytes accessed | tf_op | source)
XLA Modules:
  0.0 218.4 jit_solution(13516319439786471247)
XLA Ops:
  4.5 15.2 %collective-permute-start.1 = (bf16[7,80,128]{2,1,0:T(8,128)(2,1)S(1)}, bf16[7,80,128]{2,1,0:T(8,128)(2,1)S(1)}, u32[]{:S(2)}, u32[]{:S(2)}) collective-permute-start(bf16[7,80,128]{2,1,0:T(8,128)(2,1)S(1)} %constant_dynamic-update-slice_fusion), channel_id=1, source_target_pairs={{0,15},{1,0},{2,1},{3,2},{4,3},{5,4},{6,5},{7,6},{8,7},{9,8},{10,9... | collective-permute-start | bytes 430088 | tf_op jit(solution)/shard_map/ppermute | solution.py:18
  27.5 4.5 %collective-permute-done.1 = bf16[7,80,128]{2,1,0:T(8,128)(2,1)S(1)} collective-permute-done((bf16[7,80,128]{2,1,0:T(8,128)(2,1)S(1)}, bf16[7,80,128]{2,1,0:T(8,128)(2,1)S(1)}, u32[]{:S(2)}, u32[]{:S(2)}) %collective-permute-start.1) | collective-permute-done | bytes 143392 | tf_op jit(solution)/shard_map/ppermute | solution.py:18
  35.7 10.4 %collective-permute-start.2 = (bf16[2,80,128]{2,1,0:T(8,128)(2,1)S(1)}, bf16[2,80,128]{2,1,0:T(8,128)(2,1)S(1)}, u32[]{:S(2)}, u32[]{:S(2)}) collective-permute-start(bf16[2,80,128]{2,1,0:T(8,128)(2,1)S(1)} %bitcast.325), channel_id=1, source_target_pairs={{0,15},{1,0},{2,1},{3,2},{4,3},{5,4},{6,5},{7,6},{8,7},{9,8},{10,9... | collective-permute-start | bytes 122888 | tf_op jit(solution)/shard_map/ppermute | solution.py:18
  51.9 3.5 %all-to-all-start = ((bf16[4,784,128]{2,1,0:T(8,128)(2,1)}), bf16[4,784,128]{2,1,0:T(8,128)(2,1)S(1)}, u32[]{:S(2)}, u32[]{:S(2)}) async-start(bf16[4,784,128]{2,1,0:T(8,128)(2,1)} %maximum_maximum_fusion), calls=%async_computation | async-start | bytes 1605632 | tf_op jit(solution)/shard_map/all_to_all | solution.py:22
  55.4 6.7 %collective-permute-done.3 = bf16[2,80,128]{2,1,0:T(8,128)(2,1)S(1)} collective-permute-done((bf16[2,80,128]{2,1,0:T(8,128)(2,1)S(1)}, bf16[2,80,128]{2,1,0:T(8,128)(2,1)S(1)}, u32[]{:S(2)}, u32[]{:S(2)}) %collective-permute-start.3) | collective-permute-done | bytes 40992 | tf_op jit(solution)/shard_map/ppermute | solution.py:18
  63.4 4.8 %all-to-all-done = bf16[4,784,128]{2,1,0:T(8,128)(2,1)S(1)} async-done(((bf16[4,784,128]{2,1,0:T(8,128)(2,1)}), bf16[4,784,128]{2,1,0:T(8,128)(2,1)S(1)}, u32[]{:S(2)}, u32[]{:S(2)}) %all-to-all-start) | async-done | bytes 802848 | tf_op jit(solution)/shard_map/all_to_all | solution.py:22
  68.1 3.3 %all-to-all-start.1 = ((bf16[4,2,80,128]{3,2,1,0:T(8,128)(2,1)}), bf16[4,2,80,128]{3,2,1,0:T(8,128)(2,1)S(1)}, u32[]{:S(2)}, u32[]{:S(2)}) async-start(bf16[4,2,80,128]{3,2,1,0:T(8,128)(2,1)} %pad_maximum_fusion.6), calls=%async_computation.1 | async-start | bytes 327680 | tf_op jit(solution)/shard_map/all_to_all | solution.py:22
  72.9 3.9 %convolution_convert_fusion.gram_ref = bf16[1152,1152]{1,0:T(8,128)(2,1)} fusion(bf16[160,1152]{1,0:T(8,128)(2,1)S(1)} %constant_dynamic-update-slice_fusion.77, bf16[160,1152]{1,0:T(8,128)(2,1)S(1)} %constant_dynamic-update-slice_fusion.68, bf16[160,1152]{1,0:T(8,128)(2,1)S(1)} %constant_dynamic-update-slice_fusion.59, ...), kind=kOutput, calls=%fused_computation | convolution fusion | flops 1705918464 | bytes 4128768 | tf_op jit(solution)/shard_map/dot_general | solution.py:66
  80.2 4.8 %all_to_all.55 = bf16[2,2560,128]{2,1,0:T(8,128)(2,1)S(1)} all-to-all(bf16[2,2560,128]{2,1,0:T(8,128)(2,1)S(1)} %bitcast.286), channel_id=1, replica_groups=mesh['x'=4,'zl'=4,'core'=2,'zh'=4,'y'=4] {'core'}, dimensions={0} | all-to-all | bytes 2621440 | tf_op jit(solution)/shard_map/all_to_all | solution.py:22
  86.6 4.8 %all-to-all-start.3 = ((bf16[16,160,128]{2,1,0:T(8,128)(2,1)}), bf16[16,160,128]{2,1,0:T(8,128)(2,1)S(1)}, u32[]{:S(2)}, u32[]{:S(2)}) async-start(bf16[16,160,128]{2,1,0:T(8,128)(2,1)} %pad_maximum_fusion.1), calls=%async_computation.3 | async-start | bytes 1310720 | tf_op jit(solution)/shard_map/all_to_all | solution.py:22
  94.0 14.7 %all-to-all-done.3 = bf16[16,160,128]{2,1,0:T(8,128)(2,1)S(1)} async-done(((bf16[16,160,128]{2,1,0:T(8,128)(2,1)}), bf16[16,160,128]{2,1,0:T(8,128)(2,1)S(1)}, u32[]{:S(2)}, u32[]{:S(2)}) %all-to-all-start.3) | async-done | bytes 655392 | tf_op jit(solution)/shard_map/all_to_all | solution.py:22
  109.6 10.6 %all-to-all-start.4 = ((bf16[4,464,128]{2,1,0:T(8,128)(2,1)}), bf16[4,464,128]{2,1,0:T(8,128)(2,1)S(1)}, u32[]{:S(2)}, u32[]{:S(2)}) async-start(bf16[4,464,128]{2,1,0:T(8,128)(2,1)} %broadcast_in_dim.33), calls=%async_computation.4 | async-start | bytes 950272 | tf_op jit(solution)/shard_map/all_to_all | solution.py:22
  120.9 3.2 %collective-permute-start.4 = (bf16[1,80,128]{2,1,0:T(8,128)(2,1)S(1)}, bf16[1,80,128]{2,1,0:T(8,128)(2,1)S(1)}, u32[]{:S(2)}, u32[]{:S(2)}) collective-permute-start(bf16[1,80,128]{2,1,0:T(8,128)(2,1)S(1)} %get-tuple-element.193), channel_id=1, source_target_pairs={{0,1},{1,2},{2,3},{3,4},{4,5},{5,6},{6,7},{7,8},{8,9},{9,10},{10,1... | collective-permute-start | bytes 61448 | tf_op jit(solution)/shard_map/ppermute | solution.py:18
  135.3 11.0 %all-to-all-done.4 = bf16[4,464,128]{2,1,0:T(8,128)(2,1)S(1)} async-done(((bf16[4,464,128]{2,1,0:T(8,128)(2,1)}), bf16[4,464,128]{2,1,0:T(8,128)(2,1)S(1)}, u32[]{:S(2)}, u32[]{:S(2)}) %all-to-all-start.4) | async-done | bytes 475168 | tf_op jit(solution)/shard_map/all_to_all | solution.py:22
  147.0 3.5 %all-to-all-start.5 = ((bf16[4,120,128]{2,1,0:T(8,128)(2,1)}), bf16[4,120,128]{2,1,0:T(8,128)(2,1)S(1)}, u32[]{:S(2)}, u32[]{:S(2)}) async-start(bf16[4,120,128]{2,1,0:T(8,128)(2,1)} %broadcast_in_dim.34), calls=%async_computation.5 | async-start | bytes 245760 | tf_op jit(solution)/shard_map/all_to_all | solution.py:22
  150.6 5.6 %all-to-all-done.5 = bf16[4,120,128]{2,1,0:T(8,128)(2,1)S(1)} async-done(((bf16[4,120,128]{2,1,0:T(8,128)(2,1)}), bf16[4,120,128]{2,1,0:T(8,128)(2,1)S(1)}, u32[]{:S(2)}, u32[]{:S(2)}) %all-to-all-start.5) | async-done | bytes 122912 | tf_op jit(solution)/shard_map/all_to_all | solution.py:22
  157.0 8.4 %all-to-all-start.6 = ((bf16[4,160,128]{2,1,0:T(8,128)(2,1)}), bf16[4,160,128]{2,1,0:T(8,128)(2,1)S(1)}, u32[]{:S(2)}, u32[]{:S(2)}) async-start(bf16[4,160,128]{2,1,0:T(8,128)(2,1)} %pad_maximum_fusion.7), calls=%async_computation.6 | async-start | bytes 327680 | tf_op jit(solution)/shard_map/all_to_all | solution.py:22
  165.5 13.7 %all-to-all-done.6 = bf16[4,160,128]{2,1,0:T(8,128)(2,1)S(1)} async-done(((bf16[4,160,128]{2,1,0:T(8,128)(2,1)}), bf16[4,160,128]{2,1,0:T(8,128)(2,1)S(1)}, u32[]{:S(2)}, u32[]{:S(2)}) %all-to-all-start.6) | async-done | bytes 163872 | tf_op jit(solution)/shard_map/all_to_all | solution.py:22
  179.9 3.3 %all-to-all-start.7 = ((bf16[4,160,128]{2,1,0:T(8,128)(2,1)}), bf16[4,160,128]{2,1,0:T(8,128)(2,1)S(1)}, u32[]{:S(2)}, u32[]{:S(2)}) async-start(bf16[4,160,128]{2,1,0:T(8,128)(2,1)} %broadcast_in_dim.36), calls=%async_computation.7 | async-start | bytes 327680 | tf_op jit(solution)/shard_map/all_to_all | solution.py:22
  183.3 5.9 %all-to-all-done.7 = bf16[4,160,128]{2,1,0:T(8,128)(2,1)S(1)} async-done(((bf16[4,160,128]{2,1,0:T(8,128)(2,1)}), bf16[4,160,128]{2,1,0:T(8,128)(2,1)S(1)}, u32[]{:S(2)}, u32[]{:S(2)}) %all-to-all-start.7) | async-done | bytes 163872 | tf_op jit(solution)/shard_map/all_to_all | solution.py:22
  190.1 5.8 %all-to-all-start.8 = ((bf16[4,4,160,128]{3,2,1,0:T(8,128)(2,1)}), bf16[4,4,160,128]{3,2,1,0:T(8,128)(2,1)S(1)}, u32[]{:S(2)}, u32[]{:S(2)}) async-start(bf16[4,4,160,128]{3,2,1,0:T(8,128)(2,1)} %broadcast_in_dim.37), calls=%async_computation.8 | async-start | bytes 1310720 | tf_op jit(solution)/shard_map/all_to_all | solution.py:22
  197.0 5.7 %all-to-all-done.8 = bf16[4,4,160,128]{3,2,1,0:T(8,128)(2,1)S(1)} async-done(((bf16[4,4,160,128]{3,2,1,0:T(8,128)(2,1)}), bf16[4,4,160,128]{3,2,1,0:T(8,128)(2,1)S(1)}, u32[]{:S(2)}, u32[]{:S(2)}) %all-to-all-start.8) | async-done | bytes 655392 | tf_op jit(solution)/shard_map/all_to_all | solution.py:22
  202.9 4.8 %all_to_all.56 = bf16[2,4,4,160,128]{4,3,2,1,0:T(8,128)(2,1)S(1)} all-to-all(bf16[2,4,4,160,128]{4,3,2,1,0:T(8,128)(2,1)S(1)} %broadcast_in_dim.38), channel_id=1, replica_groups=mesh['x'=4,'zl'=4,'core'=2,'zh'=4,'y'=4] {'core'}, dimensions={0} | all-to-all | bytes 2621440 | tf_op jit(solution)/shard_map/all_to_all | solution.py:22
  209.0 3.3 %all-to-all-start.10 = ((bf16[4,36,128]{2,1,0:T(8,128)(2,1)}), bf16[4,36,128]{2,1,0:T(8,128)(2,1)S(1)}, u32[]{:S(2)}, u32[]{:S(2)}) async-start(bf16[4,36,128]{2,1,0:T(8,128)(2,1)} %broadcast_in_dim.39), calls=%async_computation.10 | async-start | bytes 81920 | tf_op jit(solution)/shard_map/all_to_all | solution.py:22
  (255 shorter events, 44.1 us)
Async XLA Ops:
  0.6 24.6 %copy-start.3 = (bf16[4,1152,128]{2,1,0:T(8,128)(2,1)S(1)}, bf16[4,1152,128]{2,1,0:T(8,128)(2,1)}, u32[]{:S(2)}) copy-start(bf16[4,1152,128]{2,1,0:T(8,128)(2,1)} %param.16) | copy-start | bytes 3538948
  4.5 27.5 %collective-permute-start.1 = (bf16[7,80,128]{2,1,0:T(8,128)(2,1)S(1)}, bf16[7,80,128]{2,1,0:T(8,128)(2,1)S(1)}, u32[]{:S(2)}, u32[]{:S(2)}) collective-permute-start(bf16[7,80,128]{2,1,0:T(8,128)(2,1)S(1)} %constant_dynamic-update-slice_fusion), channel_id=1, source_target_pairs={{0,15},{1,0},{2,1},{3,2},{4,3},{5,4},{6,5},{7,6},{8,7},{9,8},{10,9... | collective-permute-start | bytes 430088 | tf_op jit(solution)/shard_map/ppermute | solution.py:18
  22.1 5.4 %collective-permute-start = (bf16[5,80,128]{2,1,0:T(8,128)(2,1)S(1)}, bf16[5,80,128]{2,1,0:T(8,128)(2,1)S(1)}, u32[]{:S(2)}, u32[]{:S(2)}) collective-permute-start(bf16[5,80,128]{2,1,0:T(8,128)(2,1)S(1)} %pad_maximum_fusion.11), channel_id=1, source_target_pairs={{0,1},{1,2},{2,3},{3,4},{4,5},{5,6},{6,7},{7,8},{8,9},{9,10},{10,1... | collective-permute-start | bytes 307208 | tf_op jit(solution)/shard_map/ppermute | solution.py:18
  34.5 1.0 copy-start.6
  35.1 12.0 %slice-start = ((bf16[6,80,128]{2,1,0:T(8,128)(2,1)}), bf16[4,80,128]{2,1,0:T(8,128)(2,1)S(1)}, s32[]{:S(2)}) async-start(bf16[6,80,128]{2,1,0:T(8,128)(2,1)} %copy-done.4), calls=%async_computation.11 | async-start | bytes 163840 | tf_op jit(solution)/shard_map/slice | solution.py:185
  35.7 12.9 %collective-permute-start.2 = (bf16[2,80,128]{2,1,0:T(8,128)(2,1)S(1)}, bf16[2,80,128]{2,1,0:T(8,128)(2,1)S(1)}, u32[]{:S(2)}, u32[]{:S(2)}) collective-permute-start(bf16[2,80,128]{2,1,0:T(8,128)(2,1)S(1)} %bitcast.325), channel_id=1, source_target_pairs={{0,15},{1,0},{2,1},{3,2},{4,3},{5,4},{6,5},{7,6},{8,7},{9,8},{10,9... | collective-permute-start | bytes 122888 | tf_op jit(solution)/shard_map/ppermute | solution.py:18
  47.0 1.5 copy-start.9
  47.0 1.5 copy-start.10
  50.0 12.1 %collective-permute-start.3 = (bf16[2,80,128]{2,1,0:T(8,128)(2,1)S(1)}, bf16[2,80,128]{2,1,0:T(8,128)(2,1)S(1)}, u32[]{:S(2)}, u32[]{:S(2)}) collective-permute-start(bf16[2,80,128]{2,1,0:T(8,128)(2,1)S(1)} %bitcast.328), channel_id=1, source_target_pairs={{0,1},{1,2},{2,3},{3,4},{4,5},{5,6},{6,7},{7,8},{8,9},{9,10},{10,1... | collective-permute-start | bytes 122888 | tf_op jit(solution)/shard_map/ppermute | solution.py:18
  51.9 16.2 %all-to-all-start = ((bf16[4,784,128]{2,1,0:T(8,128)(2,1)}), bf16[4,784,128]{2,1,0:T(8,128)(2,1)S(1)}, u32[]{:S(2)}, u32[]{:S(2)}) async-start(bf16[4,784,128]{2,1,0:T(8,128)(2,1)} %maximum_maximum_fusion), calls=%async_computation | async-start | bytes 1605632 | tf_op jit(solution)/shard_map/all_to_all | solution.py:22
  68.1 9.5 %all-to-all-start.1 = ((bf16[4,2,80,128]{3,2,1,0:T(8,128)(2,1)}), bf16[4,2,80,128]{3,2,1,0:T(8,128)(2,1)S(1)}, u32[]{:S(2)}, u32[]{:S(2)}) async-start(bf16[4,2,80,128]{3,2,1,0:T(8,128)(2,1)} %pad_maximum_fusion.6), calls=%async_computation.1 | async-start | bytes 327680 | tf_op jit(solution)/shard_map/all_to_all | solution.py:22
  77.6 1.8 copy-start
  85.7 5.7 %copy-start.11 = (s32[4]{0:T(128)S(1)}, s32[4]{0:T(128)}, u32[]{:S(2)}) copy-start(s32[4]{0:T(128)} %param.17) | copy-start | bytes 52
  86.6 22.1 %all-to-all-start.3 = ((bf16[16,160,128]{2,1,0:T(8,128)(2,1)}), bf16[16,160,128]{2,1,0:T(8,128)(2,1)S(1)}, u32[]{:S(2)}, u32[]{:S(2)}) async-start(bf16[16,160,128]{2,1,0:T(8,128)(2,1)} %pad_maximum_fusion.1), calls=%async_computation.3 | async-start | bytes 1310720 | tf_op jit(solution)/shard_map/all_to_all | solution.py:22
  109.6 36.8 %all-to-all-start.4 = ((bf16[4,464,128]{2,1,0:T(8,128)(2,1)}), bf16[4,464,128]{2,1,0:T(8,128)(2,1)S(1)}, u32[]{:S(2)}, u32[]{:S(2)}) async-start(bf16[4,464,128]{2,1,0:T(8,128)(2,1)} %broadcast_in_dim.33), calls=%async_computation.4 | async-start | bytes 950272 | tf_op jit(solution)/shard_map/all_to_all | solution.py:22
  120.9 29.6 %collective-permute-start.4 = (bf16[1,80,128]{2,1,0:T(8,128)(2,1)S(1)}, bf16[1,80,128]{2,1,0:T(8,128)(2,1)S(1)}, u32[]{:S(2)}, u32[]{:S(2)}) collective-permute-start(bf16[1,80,128]{2,1,0:T(8,128)(2,1)S(1)} %get-tuple-element.193), channel_id=1, source_target_pairs={{0,1},{1,2},{2,3},{3,4},{4,5},{5,6},{6,7},{7,8},{8,9},{9,10},{10,1... | collective-permute-start | bytes 61448 | tf_op jit(solution)/shard_map/ppermute | solution.py:18
  124.1 26.4 %collective-permute-start.5 = (bf16[1,80,128]{2,1,0:T(8,128)(2,1)S(1)}, bf16[1,80,128]{2,1,0:T(8,128)(2,1)S(1)}, u32[]{:S(2)}, u32[]{:S(2)}) collective-permute-start(bf16[1,80,128]{2,1,0:T(8,128)(2,1)S(1)} %get-tuple-element.194), channel_id=1, source_target_pairs={{1,0},{2,1},{3,2},{4,3},{5,4},{6,5},{7,6},{8,7},{9,8},{10,9},{11,1... | collective-permute-start | bytes 61448 | tf_op jit(solution)/shard_map/ppermute | solution.py:18
  147.0 9.2 %all-to-all-start.5 = ((bf16[4,120,128]{2,1,0:T(8,128)(2,1)}), bf16[4,120,128]{2,1,0:T(8,128)(2,1)S(1)}, u32[]{:S(2)}, u32[]{:S(2)}) async-start(bf16[4,120,128]{2,1,0:T(8,128)(2,1)} %broadcast_in_dim.34), calls=%async_computation.5 | async-start | bytes 245760 | tf_op jit(solution)/shard_map/all_to_all | solution.py:22
  157.0 22.2 %all-to-all-start.6 = ((bf16[4,160,128]{2,1,0:T(8,128)(2,1)}), bf16[4,160,128]{2,1,0:T(8,128)(2,1)S(1)}, u32[]{:S(2)}, u32[]{:S(2)}) async-start(bf16[4,160,128]{2,1,0:T(8,128)(2,1)} %pad_maximum_fusion.7), calls=%async_computation.6 | async-start | bytes 327680 | tf_op jit(solution)/shard_map/all_to_all | solution.py:22
  179.9 9.3 %all-to-all-start.7 = ((bf16[4,160,128]{2,1,0:T(8,128)(2,1)}), bf16[4,160,128]{2,1,0:T(8,128)(2,1)S(1)}, u32[]{:S(2)}, u32[]{:S(2)}) async-start(bf16[4,160,128]{2,1,0:T(8,128)(2,1)} %broadcast_in_dim.36), calls=%async_computation.7 | async-start | bytes 327680 | tf_op jit(solution)/shard_map/all_to_all | solution.py:22
  190.1 12.6 %all-to-all-start.8 = ((bf16[4,4,160,128]{3,2,1,0:T(8,128)(2,1)}), bf16[4,4,160,128]{3,2,1,0:T(8,128)(2,1)S(1)}, u32[]{:S(2)}, u32[]{:S(2)}) async-start(bf16[4,4,160,128]{3,2,1,0:T(8,128)(2,1)} %broadcast_in_dim.37), calls=%async_computation.8 | async-start | bytes 1310720 | tf_op jit(solution)/shard_map/all_to_all | solution.py:22
  207.7 5.2 %copy-start.1 = (s32[81]{0:T(128)S(1)}, s32[81]{0:T(128)}, u32[]{:S(2)}) copy-start(s32[81]{0:T(128)} %constant.110.clone.flip_ref) | copy-start | bytes 976
  207.7 5.2 %copy-start.2 = (s32[81]{0:T(128)S(1)}, s32[81]{0:T(128)}, u32[]{:S(2)}) copy-start(s32[81]{0:T(128)} %constant.109.clone.index_ref) | copy-start | bytes 976
  209.0 8.7 %all-to-all-start.10 = ((bf16[4,36,128]{2,1,0:T(8,128)(2,1)}), bf16[4,36,128]{2,1,0:T(8,128)(2,1)S(1)}, u32[]{:S(2)}, u32[]{:S(2)}) async-start(bf16[4,36,128]{2,1,0:T(8,128)(2,1)} %broadcast_in_dim.39), calls=%async_computation.10 | async-start | bytes 81920 | tf_op jit(solution)/shard_map/all_to_all | solution.py:22
  (4 other events, 3.1 us)

commit v7 on v4

--- a/solution.py
+++ b/solution.py
@@ -31,6 +31,15 @@
     count = lax.axis_size(axis)
     got = exchange(x.reshape((count, x.shape[0] // count) + x.shape[1:]), axis)
     return jnp.sum(got.astype(jnp.float32), axis=0).astype(jnp.bfloat16)
+
+
+def over_y(x, shift):
+    return lax.ppermute(x, "y", [(y, (y + shift) % Y) for y in range(Y)])
+
+
+def traded(keep, send):
+    got = lax.ppermute(send, "core", [(c, (c + 1) % CORE) for c in range(CORE)])
+    return (keep.astype(jnp.float32) + got.astype(jnp.float32)).astype(jnp.bfloat16)
 
 
 def windows(rows):
@@ -89,12 +98,85 @@
 
 PAIRS, WHERE = block_classes()
 NG = len(PAIRS)
-NBLOCKS = 40
+NB = 32
+ND = 10
+
+
+def put_halves(blocks, core, keep_ref, send_ref):
+    chans = blocks[0].shape[-1]
+    half = len(blocks) // 2
+    for i in range(half):
+        rows = slice(i * chans, (i + 1) * chans)
+        low, high = blocks[i], blocks[half + i]
+        keep_ref[rows, :] = jnp.where(core == 0, low, high)
+        send_ref[rows, :] = jnp.where(core == 0, high, low)
+
+
+def gram_halves(cols, core):
+    chans = cols.shape[1] // 9
+
+    def kernel(core_ref, cols_ref, keep_ref, send_ref, done):
+        for a in range(9):
+            wanted = [b for first, b in PAIRS if first == a]
+            if not wanted:
+                continue
+            low = min(wanted)
+            left = cols_ref[:, a * chans : (a + 1) * chans].T
+            right = cols_ref[:, low * chans : (max(wanted) + 1) * chans]
+            product = jnp.dot(left, right, preferred_element_type=jnp.float32)
+            for i, (first, b) in enumerate(PAIRS):
+                if first == a:
+                    part = product[:, (b - low) * chans : (b - low + 1) * chans]
+                    done[i] = part.astype(done.dtype)
+        for i in range(NG, NB):
+            done[i] = jnp.zeros(done.shape[1:], done.dtype)
+        put_halves([done[i] for i in range(NB)], core_ref[0], keep_ref, send_ref)
+
+    vmem = pl.BlockSpec(memory_space=pltpu.VMEM)
+    half = jax.ShapeDtypeStruct((NB // 2 * chans, chans), jnp.bfloat16)
+    return pl.pallas_call(
+        kernel,
+        out_shape=(half, half),
+        in_specs=[pl.BlockSpec(memory_space=pltpu.SMEM), vmem],
+        out_specs=(vmem, vmem),
+        scratch_shapes=[pltpu.VMEM((NB, chans, chans), jnp.bfloat16)],
+        compiler_params=pltpu.CompilerParams(vmem_limit_bytes=24 * 2**20),
+        cost_estimate=pl.CostEstimate(
+            flops=2 * NB * cols.size * chans // 9, bytes_accessed=4 * 10**6, transcendentals=0
+        ),
+    )(core.reshape(1), cols)
+
+
+def grad_halves(cols, dpre, core):
+    chans = dpre.shape[-1]
+
+    def kernel(core_ref, cols_ref, dpre_ref, keep_ref, send_ref):
+        across = (((0,), (0,)), ((), ()))
+        mine = dpre_ref[...]
+        own = lax.dot_general(mine, mine, across, preferred_element_type=jnp.float32)
+        grad = lax.dot_general(mine, cols_ref[...], across, preferred_element_type=jnp.float32)
+        blocks = [grad[:, t * chans : (t + 1) * chans].T.astype(jnp.bfloat16) for t in range(9)]
+        put_halves(blocks + [own.astype(jnp.bfloat16)], core_ref[0], keep_ref, send_ref)
+
+    vmem = pl.BlockSpec(memory_space=pltpu.VMEM)
+    half = jax.ShapeDtypeStruct((ND // 2 * chans, chans), jnp.bfloat16)
+    return pl.pallas_call(
+        kernel,
+        out_shape=(half, half),
+        in_specs=[pl.BlockSpec(memory_space=pltpu.SMEM), vmem, vmem],
+        out_specs=(vmem, vmem),
+        compiler_params=pltpu.CompilerParams(vmem_limit_bytes=24 * 2**20),
+        cost_estimate=pl.CostEstimate(
+            flops=2 * cols.size * chans, bytes_accessed=3 * 10**6, transcendentals=0
+        ),
+    )(core.reshape(1), cols, dpre)
 
 
 def factor_rows(blocks, first_row, scale, rows):
     chans = blocks.shape[-1]
-    index = jnp.array([WHERE[a, b][0] for a in range(9) for b in range(9)], jnp.int32)
+    count = blocks.shape[0]
+    order = [i % (count // 2) * 2 + i // (count // 2) for i in range(count)]
+    index = jnp.array([order[WHERE[a, b][0]] for a in range(9) for b in range(9)], jnp.int32)
     flips = jnp.array([int(WHERE[a, b][1]) for a in range(9) for b in range(9)], jnp.int32)
 
     def kernel(index_ref, flip_ref, row_ref, scale_ref, blocks_ref, out_ref, band):
@@ -153,6 +235,20 @@
         wide3[1:5],
     ]
     layer_strips = exchange(jnp.stack(strips), "y")
+    last_one = (y_id == 1) & (z_id == ZH - 1)
+    big_cols = jnp.concatenate(
+        [
+            to_columns(
+                windows(layer_strips[j])
+                if j < Y - 1
+                else cut_windows(layer_strips[j], jnp.logical_not(last_one))
+            )
+            for j in range(Y)
+        ]
+    )
+    core_id = lax.axis_index("core")
+    rest = ("x", "zl")
+    fac_core = traded(*gram_halves(big_cols, core_id))
 
     flipped = jnp.transpose(weights.reshape(num_layers, 9, chans, chans), (0, 1, 3, 2)).reshape(
         num_layers, patch, chans
@@ -183,55 +279,50 @@
     dy0 = back(1, windows(jnp.concatenate([edge_top, before[1:], dpre1[:1], edge_end])))
     dpre0 = times(dy0, slope(0, windows(strips[0]))).reshape(image)
 
-    layer_dpre = exchange(jnp.stack([dpre0, dpre1, dpre2, dpre3[1:3]]), "y")
-    big_dpre = layer_dpre.reshape(-1, chans)
-    last_one = (y_id == 1) & (z_id == ZH - 1)
-    big_cols = jnp.concatenate(
-        [
-            to_columns(
-                windows(layer_strips[j])
-                if j < Y - 1
-                else cut_windows(layer_strips[j], jnp.logical_not(last_one))
-            )
-            for j in range(Y)
-        ]
-    )
-    gram = inner_rows(big_cols, big_cols).astype(jnp.bfloat16)
-    grad = inner_rows(big_cols, big_dpre).astype(jnp.bfloat16)
-    gfac = inner_rows(big_dpre, big_dpre).astype(jnp.bfloat16)
-    blocks = [
-        gram[a * chans : (a + 1) * chans, b * chans : (b + 1) * chans] for a, b in PAIRS
-    ]
-    pad = jnp.zeros(((NBLOCKS - NG - 10) * chans, chans), jnp.bfloat16)
-    parts = jnp.concatenate(blocks + [grad, gfac, pad], axis=0)
-
-    piece = scatter_sum(scatter_sum(parts, "core"), ("x", "zl"))
-    held = spread(piece, "y")
+    fac_core, dpre0 = lax.optimization_barrier((fac_core, dpre0))
+    fac_piece = scatter_sum(fac_core, rest)
+
+    all_dpre = jnp.stack([dpre0, dpre1, dpre2, dpre3[1:3]]).reshape(num_layers, -1, chans)
+
+    def dpre_of(lay):
+        return lax.dynamic_index_in_dim(all_dpre, lay % num_layers, 0, keepdims=False)
+
+    got = jnp.stack([dpre_of(y_id)] + [over_y(dpre_of(y_id + s), s) for s in range(1, Y)])
+    got = [lax.dynamic_index_in_dim(got, (y_id - j) % Y, 0, keepdims=False) for j in range(Y)]
+    grad_core = traded(*grad_halves(big_cols, jnp.concatenate(got), core_id))
+    grad_core, fac_piece = lax.optimization_barrier((grad_core, fac_piece))
+    grad_held = spread(scatter_sum(grad_core, rest), "y")
+    fac_held = jnp.stack([fac_piece] + [over_y(fac_piece, s) for s in range(1, Y)])
     layer_ids = jnp.arange(num_layers, dtype=jnp.int32)
 
     def pick(z):
         lay = jnp.sum(jnp.where(table == z * Y + y_id, layer_ids, 0))
-        return lax.dynamic_index_in_dim(held, lay, 0, keepdims=False)
+        fac = lax.dynamic_index_in_dim(fac_held, (y_id - lay) % Y, 0, keepdims=False)
+        return jnp.concatenate([fac, lax.dynamic_index_in_dim(grad_held, lay, 0, keepdims=False)])
 
     total = exchange(jnp.stack([pick(z) for z in range(ZH)]), "zh")
     total = jnp.sum(total.astype(jnp.float32), axis=0).astype(jnp.bfloat16)
-    summed = spread(spread(spread(total, "zl"), "x"), "core")
+    fac_rows = fac_piece.shape[0]
+    stats = lax.all_gather(total[:fac_rows], DP, axis=0, tiled=True).reshape(-1, chans, chans)
+    grads = spread(spread(spread(total[fac_rows:], "zl"), "x"), "core").reshape(-1, chans)
 
     in_grad_win = jnp.concatenate([shifted(dpre0[1:], 1, False), dpre0, shifted(dpre0[:1], -1, False)])
     in_grad = back(0, windows(in_grad_win)).reshape((1,) + image)
 
-    summed = summed.reshape(NBLOCKS, chans, chans)
+    mixed = jnp.dot(
+        grads[:patch].astype(jnp.float32) / jnp.sqrt(jnp.float32(npos)),
+        g_inv[0],
+        precision=lax.Precision.HIGHEST,
+    )
+    panel = jnp.dot(a_inv[0].astype(jnp.float32), mixed, precision=lax.Precision.HIGHEST)
+    panels = spread(panel.astype(jnp.bfloat16), OWNER)
+    step_out = panels[table]
+
     have = jnp.any(table == owner_id).astype(jnp.float32)
     scale = have / npos
     rows_out = patch // samples
-    a_out = factor_rows(summed, dp_id * rows_out, scale, rows_out)[None]
-    g_out = (summed[NG + 9].astype(jnp.float32) * scale)[None]
-    grad_sum = summed[NG : NG + 9].reshape(patch, chans).astype(jnp.float32)
-    grad_scaled = grad_sum / jnp.sqrt(jnp.float32(npos))
-    mixed = jnp.dot(grad_scaled, g_inv[0], precision=lax.Precision.HIGHEST)
-    panel = jnp.dot(a_inv[0].astype(jnp.float32), mixed, precision=lax.Precision.HIGHEST)
-    panels = spread(panel.astype(jnp.bfloat16), OWNER)
-    step_out = panels[table]
+    a_out = factor_rows(stats, dp_id * rows_out, scale, rows_out)[None]
+    g_out = (grads[patch:].astype(jnp.float32) * scale)[None]
     return (step_out, a_out, g_out, in_grad)
 
 

time: 207 us -> 248 us (1.20)
  starting transfers between devices: 81.4 us -> 107 us
  between operations: 10.3 us -> 26.6 us
  blocking collectives: 9.7 us -> 4 us
  waiting for transfers between devices: 68.2 us -> 72.5 us
  matrix products: 7.69 us -> 3.72 us
    ppermute x0 -> x8, starting transfers between devices: none -> 23.2 us  [the longest x6 19.4 us: over_y(): return lax.ppermute(x, 'y', [(y, (y + shift) % Y) for y in range(Y)])]
    all_to_all x8, waiting for transfers between devices: 51.4 us -> 37.9 us  [exchange(): return lax.all_to_all(x, axis, split_axis=0, concat_axis=0, tiled=True)]
    all_gather x0 -> x1, waiting for transfers between devices: none -> 11.6 us  [shards(): lax.all_gather(total[:fac_rows], DP, axis=0, tiled=True)]
    all_to_all x2 -> x1, blocking collectives: 9.7 us -> 4 us  [exchange(): return lax.all_to_all(x, axis, split_axis=0, concat_axis=0, tiled=True)]
    ppermute x0 -> x8, waiting for transfers between devices: none -> 5.66 us  [the longest x2 2.91 us: traded(): got = lax.ppermute(send, 'core', [(c, (c + 1) % CORE) for c in range(CORE)])]
    all_to_all x8, starting transfers between devices: 45.5 us -> 48.9 us  [exchange(): return lax.all_to_all(x, axis, split_axis=0, concat_axis=0, tiled=True)]
    dot_general x4 -> x1, matrix products: 3.95 us -> 0.62 us  [shards(): jnp.dot(grads[:patch].astype(jnp.float32) / jnp.sqrt(jnp.float32(npos)),...]
    unnamed x165 -> x128, local copies, waits for them, and re-layouts: 8.02 us -> 9.78 us
  transfers between devices with their start and end apart: 14 -> 23, of which waited for: 9 -> 14; matrix products, arithmetic and copies ran while one was open for 8% -> 7% of each run, Pallas kernels for 0% -> 0%
where the time goes in v7:
time: 248 us; the launch traced here: 243 us
  starting transfers between devices  107 us (43%)
  waiting for transfers between devices  72.5 us (29%)
  between operations  26.6 us (11%)
  local copies, waits for them, and re-layouts  20.7 us (8%)
  other arithmetic  6.56 us (3%)
  blocking collectives  4 us (2%)
  matrix products  3.72 us (2%)
  Pallas kernels  2.76 us (1%)
    all_to_all x8, starting transfers between devices, exchange(): return lax.all_to_all(x, axis, split_axis=0, concat_axis=0, tiled=True)  48.9 us
    all_to_all x8, waiting for transfers between devices, exchange(): return lax.all_to_all(x, axis, split_axis=0, concat_axis=0, tiled=True)  37.9 us
    ppermute x6, starting transfers between devices, shifted(): return lax.ppermute(x, OWNER, pairs)  34.5 us
    ppermute x6, starting transfers between devices, over_y(): return lax.ppermute(x, 'y', [(y, (y + shift) % Y) for y in range(Y)])  19.4 us
    ppermute x6, waiting for transfers between devices, shifted(): return lax.ppermute(x, OWNER, pairs)  17.4 us
    all_gather x1, waiting for transfers between devices, shards(): lax.all_gather(total[:fac_rows], DP, axis=0, tiled=True)  11.6 us
    unnamed x128, local copies, waits for them, and re-layouts  9.78 us
  transfers between devices with their start and end apart: 23, of which 14 were waited for; matrix products, arithmetic and copies ran while one was open for 7% of the time, Pallas kernels for 0%

profile of v7, /device:TPU:6, one launch (start us, length us, event | category | flops | bytes accessed | tf_op | source)
XLA Modules:
  0.0 243.4 jit_solution(16586109455897791699)
XLA Ops:
  11.0 15.2 %collective-permute-start.1 = (bf16[7,80,128]{2,1,0:T(8,128)(2,1)S(1)}, bf16[7,80,128]{2,1,0:T(8,128)(2,1)S(1)}, u32[]{:S(2)}, u32[]{:S(2)}) collective-permute-start(bf16[7,80,128]{2,1,0:T(8,128)(2,1)S(1)} %constant_dynamic-update-slice_fusion), channel_id=1, source_target_pairs={{0,15},{1,0},{2,1},{3,2},{4,3},{5,4},{6,5},{7,6},{8,7},{9,8},{10,9... | collective-permute-start | bytes 430088 | tf_op jit(solution)/shard_map/ppermute | solution.py:18
  32.1 6.4 %collective-permute-done.1 = bf16[7,80,128]{2,1,0:T(8,128)(2,1)S(1)} collective-permute-done((bf16[7,80,128]{2,1,0:T(8,128)(2,1)S(1)}, bf16[7,80,128]{2,1,0:T(8,128)(2,1)S(1)}, u32[]{:S(2)}, u32[]{:S(2)}) %collective-permute-start.1) | collective-permute-done | bytes 143392 | tf_op jit(solution)/shard_map/ppermute | solution.py:18
  42.5 10.4 %collective-permute-start.3 = (bf16[2,80,128]{2,1,0:T(8,128)(2,1)S(1)}, bf16[2,80,128]{2,1,0:T(8,128)(2,1)S(1)}, u32[]{:S(2)}, u32[]{:S(2)}) collective-permute-start(bf16[2,80,128]{2,1,0:T(8,128)(2,1)S(1)} %bitcast.339), channel_id=1, source_target_pairs={{0,15},{1,0},{2,1},{3,2},{4,3},{5,4},{6,5},{7,6},{8,7},{9,8},{10,9... | collective-permute-start | bytes 122888 | tf_op jit(solution)/shard_map/ppermute | solution.py:18
  55.0 3.5 %all-to-all-start = ((bf16[4,4,80,128]{3,2,1,0:T(8,128)(2,1)}), bf16[4,4,80,128]{3,2,1,0:T(8,128)(2,1)S(1)}, u32[]{:S(2)}, u32[]{:S(2)}) async-start(bf16[4,4,80,128]{3,2,1,0:T(8,128)(2,1)} %pad_maximum_fusion.1), calls=%async_computation | async-start | bytes 655360 | tf_op jit(solution)/shard_map/all_to_all | solution.py:22
  59.7 3.9 %collective-permute-start.4 = (bf16[2,80,128]{2,1,0:T(8,128)(2,1)S(1)}, bf16[2,80,128]{2,1,0:T(8,128)(2,1)S(1)}, u32[]{:S(2)}, u32[]{:S(2)}) collective-permute-start(bf16[2,80,128]{2,1,0:T(8,128)(2,1)S(1)} %bitcast.342), channel_id=1, source_target_pairs={{0,1},{1,2},{2,3},{3,4},{4,5},{5,6},{6,7},{7,8},{8,9},{9,10},{10,1... | collective-permute-start | bytes 122888 | tf_op jit(solution)/shard_map/ppermute | solution.py:18
  63.6 8.0 %collective-permute-done.4 = bf16[2,80,128]{2,1,0:T(8,128)(2,1)S(1)} collective-permute-done((bf16[2,80,128]{2,1,0:T(8,128)(2,1)S(1)}, bf16[2,80,128]{2,1,0:T(8,128)(2,1)S(1)}, u32[]{:S(2)}, u32[]{:S(2)}) %collective-permute-start.4) | collective-permute-done | bytes 40992 | tf_op jit(solution)/shard_map/ppermute | solution.py:18
  80.2 4.8 %all-to-all-start.1 = ((bf16[16,128,128]{2,1,0:T(8,128)(2,1)}), bf16[16,128,128]{2,1,0:T(8,128)(2,1)S(1)}, u32[]{:S(2)}, u32[]{:S(2)}) async-start(bf16[16,128,128]{2,1,0:T(8,128)(2,1)} %bitcast.172), calls=%async_computation.1 | async-start | bytes 1048576 | tf_op jit(solution)/shard_map/all_to_all | solution.py:22
  88.9 5.1 %collective-permute-start.7 = (bf16[160,128]{1,0:T(8,128)(2,1)S(1)}, bf16[160,128]{1,0:T(8,128)(2,1)S(1)}, u32[]{:S(2)}, u32[]{:S(2)}) collective-permute-start(bf16[160,128]{1,0:T(8,128)(2,1)S(1)} %get-tuple-element.63), channel_id=1, source_target_pairs={{0,3},{1,0},{2,1},{3,2},{4,7},{5,4},{6,5},{7,6},{8,11},{9,8},{10,9... | collective-permute-start | bytes 122888 | tf_op jit(solution)/shard_map/ppermute | solution.py:37
  101.6 7.5 %all-to-all-start.2 = ((bf16[16,40,128]{2,1,0:T(8,128)(2,1)}), bf16[16,40,128]{2,1,0:T(8,128)(2,1)S(1)}, u32[]{:S(2)}, u32[]{:S(2)}) async-start(bf16[16,40,128]{2,1,0:T(8,128)(2,1)} %bitcast.178), calls=%async_computation.2 | async-start | bytes 327680 | tf_op jit(solution)/shard_map/all_to_all | solution.py:22
  109.9 3.9 %collective-permute-start.9 = (bf16[128,128]{1,0:T(8,128)(2,1)S(1)}, bf16[128,128]{1,0:T(8,128)(2,1)S(1)}, u32[]{:S(2)}, u32[]{:S(2)}) collective-permute-start(bf16[128,128]{1,0:T(8,128)(2,1)S(1)} %reduce_sum.72), channel_id=1, source_target_pairs={{0,1},{1,2},{2,3},{3,0},{4,5},{5,6},{6,7},{7,4},{8,9},{9,10},{10,1... | collective-permute-start | bytes 98312 | tf_op jit(solution)/shard_map/ppermute | solution.py:37
  113.8 3.7 %collective-permute-start.10 = (bf16[128,128]{1,0:T(8,128)(2,1)S(1)}, bf16[128,128]{1,0:T(8,128)(2,1)S(1)}, u32[]{:S(2)}, u32[]{:S(2)}) collective-permute-start(bf16[128,128]{1,0:T(8,128)(2,1)S(1)} %reduce_sum.72), channel_id=1, source_target_pairs={{0,2},{1,3},{2,0},{3,1},{4,6},{5,7},{6,4},{7,5},{8,10},{9,11},{10,... | collective-permute-start | bytes 98312 | tf_op jit(solution)/shard_map/ppermute | solution.py:37
  131.4 3.3 %all-to-all-start.3 = ((bf16[4,40,128]{2,1,0:T(8,128)(2,1)}), bf16[4,40,128]{2,1,0:T(8,128)(2,1)S(1)}, u32[]{:S(2)}, u32[]{:S(2)}) async-start(bf16[4,40,128]{2,1,0:T(8,128)(2,1)} %broadcast_in_dim.27), calls=%async_computation.3 | async-start | bytes 81920 | tf_op jit(solution)/shard_map/all_to_all | solution.py:22
  134.7 5.4 %all-to-all-done.3 = bf16[4,40,128]{2,1,0:T(8,128)(2,1)S(1)} async-done(((bf16[4,40,128]{2,1,0:T(8,128)(2,1)}), bf16[4,40,128]{2,1,0:T(8,128)(2,1)S(1)}, u32[]{:S(2)}, u32[]{:S(2)}) %all-to-all-start.3) | async-done | bytes 40992 | tf_op jit(solution)/shard_map/all_to_all | solution.py:22
  140.9 7.0 %all-to-all-start.4 = ((bf16[4,168,128]{2,1,0:T(8,128)(2,1)}), bf16[4,168,128]{2,1,0:T(8,128)(2,1)S(1)}, u32[]{:S(2)}, u32[]{:S(2)}) async-start(bf16[4,168,128]{2,1,0:T(8,128)(2,1)} %pad_maximum_fusion.3), calls=%async_computation.4 | async-start | bytes 344064 | tf_op jit(solution)/shard_map/all_to_all | solution.py:22
  153.3 2.8 %collective-permute-done.13 = bf16[1,80,128]{2,1,0:T(8,128)(2,1)S(1)} collective-permute-done((bf16[1,80,128]{2,1,0:T(8,128)(2,1)S(1)}, bf16[1,80,128]{2,1,0:T(8,128)(2,1)S(1)}, u32[]{:S(2)}, u32[]{:S(2)}) %collective-permute-start.13) | collective-permute-done | bytes 20512 | tf_op jit(solution)/shard_map/ppermute | solution.py:18
  156.1 6.9 %all-to-all-done.4 = bf16[4,168,128]{2,1,0:T(8,128)(2,1)S(1)} async-done(((bf16[4,168,128]{2,1,0:T(8,128)(2,1)}), bf16[4,168,128]{2,1,0:T(8,128)(2,1)S(1)}, u32[]{:S(2)}, u32[]{:S(2)}) %all-to-all-start.4) | async-done | bytes 172064 | tf_op jit(solution)/shard_map/all_to_all | solution.py:22
  164.5 4.5 %all-to-all-start.5 = ((bf16[4,40,128]{2,1,0:T(8,128)(2,1)}), bf16[4,40,128]{2,1,0:T(8,128)(2,1)S(1)}, u32[]{:S(2)}, u32[]{:S(2)}) async-start(bf16[4,40,128]{2,1,0:T(8,128)(2,1)} %broadcast_in_dim.28), calls=%async_computation.5 | async-start | bytes 81920 | tf_op jit(solution)/shard_map/all_to_all | solution.py:22
  169.1 5.6 %all-to-all-done.5 = bf16[4,40,128]{2,1,0:T(8,128)(2,1)S(1)} async-done(((bf16[4,40,128]{2,1,0:T(8,128)(2,1)}), bf16[4,40,128]{2,1,0:T(8,128)(2,1)S(1)}, u32[]{:S(2)}, u32[]{:S(2)}) %all-to-all-start.5) | async-done | bytes 40992 | tf_op jit(solution)/shard_map/all_to_all | solution.py:22
  175.4 4.8 %all-to-all-start.6 = ((bf16[4,4,40,128]{3,2,1,0:T(8,128)(2,1)}), bf16[4,4,40,128]{3,2,1,0:T(8,128)(2,1)S(1)}, u32[]{:S(2)}, u32[]{:S(2)}) async-start(bf16[4,4,40,128]{3,2,1,0:T(8,128)(2,1)} %broadcast_in_dim.29), calls=%async_computation.6 | async-start | bytes 327680 | tf_op jit(solution)/shard_map/all_to_all | solution.py:22
  180.2 4.1 %all-to-all-done.6 = bf16[4,4,40,128]{3,2,1,0:T(8,128)(2,1)S(1)} async-done(((bf16[4,4,40,128]{3,2,1,0:T(8,128)(2,1)}), bf16[4,4,40,128]{3,2,1,0:T(8,128)(2,1)S(1)}, u32[]{:S(2)}, u32[]{:S(2)}) %all-to-all-start.6) | async-done | bytes 163872 | tf_op jit(solution)/shard_map/all_to_all | solution.py:22
  184.3 4.0 %all_to_all.45 = bf16[2,4,4,40,128]{4,3,2,1,0:T(8,128)(2,1)S(1)} all-to-all(bf16[2,4,4,40,128]{4,3,2,1,0:T(8,128)(2,1)S(1)} %broadcast_in_dim.30), channel_id=1, replica_groups=mesh['x'=4,'zl'=4,'core'=2,'zh'=4,'y'=4] {'core'}, dimensions={0} | all-to-all | bytes 655360 | tf_op jit(solution)/shard_map/all_to_all | solution.py:22
  190.0 13.6 %all-to-all-start.8 = ((bf16[16,36,128]{2,1,0:T(8,128)(2,1)}), bf16[16,36,128]{2,1,0:T(8,128)(2,1)S(1)}, u32[]{:S(2)}, u32[]{:S(2)}) async-start(bf16[16,36,128]{2,1,0:T(8,128)(2,1)} %broadcast_in_dim.31), calls=%async_computation.8 | async-start | bytes 327680 | tf_op jit(solution)/shard_map/all_to_all | solution.py:22
  205.1 15.8 %all-to-all-done.8 = bf16[16,36,128]{2,1,0:T(8,128)(2,1)S(1)} async-done(((bf16[16,36,128]{2,1,0:T(8,128)(2,1)}), bf16[16,36,128]{2,1,0:T(8,128)(2,1)S(1)}, u32[]{:S(2)}, u32[]{:S(2)}) %all-to-all-start.8) | async-done | bytes 147488 | tf_op jit(solution)/shard_map/all_to_all | solution.py:22
  222.1 11.6 %all-gather.2.cloned.1.call-done = bf16[4096,128]{1,0:T(8,128)(2,1)} async-done(((bf16[128,128]{1,0:T(8,128)(2,1)}), bf16[4096,128]{1,0:T(8,128)(2,1)}) %all-gather.2.cloned.1.call-update) | async-done | bytes 1048592 | tf_op jit(solution)/shard_map/all_gather | solution.py:306
  (267 shorter events, 55.1 us)
Async XLA Ops:
  7.2 181.8 %copy-start = (bf16[1,36,1152]{2,1,0:T(8,128)(2,1)S(1)}, bf16[1,36,1152]{2,1,0:T(8,128)(2,1)}, u32[]{:S(2)}) copy-start(bf16[1,36,1152]{2,1,0:T(8,128)(2,1)} %param.18) | copy-start | bytes 248836
  11.0 27.5 %collective-permute-start.1 = (bf16[7,80,128]{2,1,0:T(8,128)(2,1)S(1)}, bf16[7,80,128]{2,1,0:T(8,128)(2,1)S(1)}, u32[]{:S(2)}, u32[]{:S(2)}) collective-permute-start(bf16[7,80,128]{2,1,0:T(8,128)(2,1)S(1)} %constant_dynamic-update-slice_fusion), channel_id=1, source_target_pairs={{0,15},{1,0},{2,1},{3,2},{4,3},{5,4},{6,5},{7,6},{8,7},{9,8},{10,9... | collective-permute-start | bytes 430088 | tf_op jit(solution)/shard_map/ppermute | solution.py:18
  28.5 3.5 %collective-permute-start = (bf16[5,80,128]{2,1,0:T(8,128)(2,1)S(1)}, bf16[5,80,128]{2,1,0:T(8,128)(2,1)S(1)}, u32[]{:S(2)}, u32[]{:S(2)}) collective-permute-start(bf16[5,80,128]{2,1,0:T(8,128)(2,1)S(1)} %pad_maximum_fusion.13), channel_id=1, source_target_pairs={{0,1},{1,2},{2,3},{3,4},{4,5},{5,6},{6,7},{7,8},{8,9},{9,10},{10,1... | collective-permute-start | bytes 307208 | tf_op jit(solution)/shard_map/ppermute | solution.py:18
  42.5 16.0 %collective-permute-start.3 = (bf16[2,80,128]{2,1,0:T(8,128)(2,1)S(1)}, bf16[2,80,128]{2,1,0:T(8,128)(2,1)S(1)}, u32[]{:S(2)}, u32[]{:S(2)}) collective-permute-start(bf16[2,80,128]{2,1,0:T(8,128)(2,1)S(1)} %bitcast.339), channel_id=1, source_target_pairs={{0,15},{1,0},{2,1},{3,2},{4,3},{5,4},{6,5},{7,6},{8,7},{9,8},{10,9... | collective-permute-start | bytes 122888 | tf_op jit(solution)/shard_map/ppermute | solution.py:18
  55.0 17.6 %all-to-all-start = ((bf16[4,4,80,128]{3,2,1,0:T(8,128)(2,1)}), bf16[4,4,80,128]{3,2,1,0:T(8,128)(2,1)S(1)}, u32[]{:S(2)}, u32[]{:S(2)}) async-start(bf16[4,4,80,128]{3,2,1,0:T(8,128)(2,1)} %pad_maximum_fusion.1), calls=%async_computation | async-start | bytes 655360 | tf_op jit(solution)/shard_map/all_to_all | solution.py:22
  59.7 11.9 %collective-permute-start.4 = (bf16[2,80,128]{2,1,0:T(8,128)(2,1)S(1)}, bf16[2,80,128]{2,1,0:T(8,128)(2,1)S(1)}, u32[]{:S(2)}, u32[]{:S(2)}) collective-permute-start(bf16[2,80,128]{2,1,0:T(8,128)(2,1)S(1)} %bitcast.342), channel_id=1, source_target_pairs={{0,1},{1,2},{2,3},{3,4},{4,5},{5,6},{6,7},{7,8},{8,9},{9,10},{10,1... | collective-permute-start | bytes 122888 | tf_op jit(solution)/shard_map/ppermute | solution.py:18
  75.4 3.8 %collective-permute-start.2 = (bf16[2048,128]{1,0:T(8,128)(2,1)S(1)}, bf16[2048,128]{1,0:T(8,128)(2,1)S(1)}, u32[]{:S(2)}, u32[]{:S(2)}) collective-permute-start(bf16[2048,128]{1,0:T(8,128)(2,1)S(1)} %get-tuple-element.13), channel_id=1, source_target_pairs={{0,16},{16,0},{1,17},{17,1},{2,18},{18,2},{3,19},{19,3},{4,20},{20... | collective-permute-start | bytes 1572872 | tf_op jit(solution)/shard_map/ppermute | solution.py:41
  80.2 21.4 %all-to-all-start.1 = ((bf16[16,128,128]{2,1,0:T(8,128)(2,1)}), bf16[16,128,128]{2,1,0:T(8,128)(2,1)S(1)}, u32[]{:S(2)}, u32[]{:S(2)}) async-start(bf16[16,128,128]{2,1,0:T(8,128)(2,1)} %bitcast.172), calls=%async_computation.1 | async-start | bytes 1048576 | tf_op jit(solution)/shard_map/all_to_all | solution.py:22
  85.1 9.1 %collective-permute-start.5 = (bf16[160,128]{1,0:T(8,128)(2,1)S(1)}, bf16[160,128]{1,0:T(8,128)(2,1)S(1)}, u32[]{:S(2)}, u32[]{:S(2)}) collective-permute-start(bf16[160,128]{1,0:T(8,128)(2,1)S(1)} %get-tuple-element.65), channel_id=1, source_target_pairs={{0,1},{1,2},{2,3},{3,0},{4,5},{5,6},{6,7},{7,4},{8,9},{9,10},{10,1... | collective-permute-start | bytes 122888 | tf_op jit(solution)/shard_map/ppermute | solution.py:37
  87.0 7.4 %collective-permute-start.6 = (bf16[160,128]{1,0:T(8,128)(2,1)S(1)}, bf16[160,128]{1,0:T(8,128)(2,1)S(1)}, u32[]{:S(2)}, u32[]{:S(2)}) collective-permute-start(bf16[160,128]{1,0:T(8,128)(2,1)S(1)} %get-tuple-element.64), channel_id=1, source_target_pairs={{0,2},{1,3},{2,0},{3,1},{4,6},{5,7},{6,4},{7,5},{8,10},{9,11},{10,... | collective-permute-start | bytes 122888 | tf_op jit(solution)/shard_map/ppermute | solution.py:37
  88.9 8.0 %collective-permute-start.7 = (bf16[160,128]{1,0:T(8,128)(2,1)S(1)}, bf16[160,128]{1,0:T(8,128)(2,1)S(1)}, u32[]{:S(2)}, u32[]{:S(2)}) collective-permute-start(bf16[160,128]{1,0:T(8,128)(2,1)S(1)} %get-tuple-element.63), channel_id=1, source_target_pairs={{0,3},{1,0},{2,1},{3,2},{4,7},{5,4},{6,5},{7,6},{8,11},{9,8},{10,9... | collective-permute-start | bytes 122888 | tf_op jit(solution)/shard_map/ppermute | solution.py:37
  97.5 3.3 %collective-permute-start.8 = (bf16[640,128]{1,0:T(8,128)(2,1)S(1)}, bf16[640,128]{1,0:T(8,128)(2,1)S(1)}, u32[]{:S(2)}, u32[]{:S(2)}) collective-permute-start(bf16[640,128]{1,0:T(8,128)(2,1)S(1)} %get-tuple-element.16), channel_id=1, source_target_pairs={{0,16},{16,0},{1,17},{17,1},{2,18},{18,2},{3,19},{19,3},{4,20},{20... | collective-permute-start | bytes 491528 | tf_op jit(solution)/shard_map/ppermute | solution.py:41
  101.6 29.1 %all-to-all-start.2 = ((bf16[16,40,128]{2,1,0:T(8,128)(2,1)}), bf16[16,40,128]{2,1,0:T(8,128)(2,1)S(1)}, u32[]{:S(2)}, u32[]{:S(2)}) async-start(bf16[16,40,128]{2,1,0:T(8,128)(2,1)} %bitcast.178), calls=%async_computation.2 | async-start | bytes 327680 | tf_op jit(solution)/shard_map/all_to_all | solution.py:22
  109.9 20.8 %collective-permute-start.9 = (bf16[128,128]{1,0:T(8,128)(2,1)S(1)}, bf16[128,128]{1,0:T(8,128)(2,1)S(1)}, u32[]{:S(2)}, u32[]{:S(2)}) collective-permute-start(bf16[128,128]{1,0:T(8,128)(2,1)S(1)} %reduce_sum.72), channel_id=1, source_target_pairs={{0,1},{1,2},{2,3},{3,0},{4,5},{5,6},{6,7},{7,4},{8,9},{9,10},{10,1... | collective-permute-start | bytes 98312 | tf_op jit(solution)/shard_map/ppermute | solution.py:37
  113.8 16.8 %collective-permute-start.10 = (bf16[128,128]{1,0:T(8,128)(2,1)S(1)}, bf16[128,128]{1,0:T(8,128)(2,1)S(1)}, u32[]{:S(2)}, u32[]{:S(2)}) collective-permute-start(bf16[128,128]{1,0:T(8,128)(2,1)S(1)} %reduce_sum.72), channel_id=1, source_target_pairs={{0,2},{1,3},{2,0},{3,1},{4,6},{5,7},{6,4},{7,5},{8,10},{9,11},{10,... | collective-permute-start | bytes 98312 | tf_op jit(solution)/shard_map/ppermute | solution.py:37
  117.6 13.1 %collective-permute-start.11 = (bf16[128,128]{1,0:T(8,128)(2,1)S(1)}, bf16[128,128]{1,0:T(8,128)(2,1)S(1)}, u32[]{:S(2)}, u32[]{:S(2)}) collective-permute-start(bf16[128,128]{1,0:T(8,128)(2,1)S(1)} %reduce_sum.72), channel_id=1, source_target_pairs={{0,3},{1,0},{2,1},{3,2},{4,7},{5,4},{6,5},{7,6},{8,11},{9,8},{10,9... | collective-permute-start | bytes 98312 | tf_op jit(solution)/shard_map/ppermute | solution.py:37
  131.4 8.7 %all-to-all-start.3 = ((bf16[4,40,128]{2,1,0:T(8,128)(2,1)}), bf16[4,40,128]{2,1,0:T(8,128)(2,1)S(1)}, u32[]{:S(2)}, u32[]{:S(2)}) async-start(bf16[4,40,128]{2,1,0:T(8,128)(2,1)} %broadcast_in_dim.27), calls=%async_computation.3 | async-start | bytes 81920 | tf_op jit(solution)/shard_map/all_to_all | solution.py:22
  140.9 22.2 %all-to-all-start.4 = ((bf16[4,168,128]{2,1,0:T(8,128)(2,1)}), bf16[4,168,128]{2,1,0:T(8,128)(2,1)S(1)}, u32[]{:S(2)}, u32[]{:S(2)}) async-start(bf16[4,168,128]{2,1,0:T(8,128)(2,1)} %pad_maximum_fusion.3), calls=%async_computation.4 | async-start | bytes 344064 | tf_op jit(solution)/shard_map/all_to_all | solution.py:22
  147.9 85.7 %all-gather.2.cloned.1.call-start = ((), (), s32[]{:S(2)}) async-start(), calls=%async_computation.9 | async-start | bytes 1081344 | tf_op jit(solution)/shard_map/all_gather | solution.py:306
  147.9 5.3 %collective-permute-start.12 = (bf16[1,80,128]{2,1,0:T(8,128)(2,1)S(1)}, bf16[1,80,128]{2,1,0:T(8,128)(2,1)S(1)}, u32[]{:S(2)}, u32[]{:S(2)}) collective-permute-start(bf16[1,80,128]{2,1,0:T(8,128)(2,1)S(1)} %get-tuple-element.209), channel_id=1, source_target_pairs={{0,1},{1,2},{2,3},{3,4},{4,5},{5,6},{6,7},{7,8},{8,9},{9,10},{10,1... | collective-permute-start | bytes 61448 | tf_op jit(solution)/shard_map/ppermute | solution.py:18
  150.4 5.7 %collective-permute-start.13 = (bf16[1,80,128]{2,1,0:T(8,128)(2,1)S(1)}, bf16[1,80,128]{2,1,0:T(8,128)(2,1)S(1)}, u32[]{:S(2)}, u32[]{:S(2)}) collective-permute-start(bf16[1,80,128]{2,1,0:T(8,128)(2,1)S(1)} %get-tuple-element.210), channel_id=1, source_target_pairs={{1,0},{2,1},{3,2},{4,3},{5,4},{6,5},{7,6},{8,7},{9,8},{10,9},{11,1... | collective-permute-start | bytes 61448 | tf_op jit(solution)/shard_map/ppermute | solution.py:18
  164.5 10.2 %all-to-all-start.5 = ((bf16[4,40,128]{2,1,0:T(8,128)(2,1)}), bf16[4,40,128]{2,1,0:T(8,128)(2,1)S(1)}, u32[]{:S(2)}, u32[]{:S(2)}) async-start(bf16[4,40,128]{2,1,0:T(8,128)(2,1)} %broadcast_in_dim.28), calls=%async_computation.5 | async-start | bytes 81920 | tf_op jit(solution)/shard_map/all_to_all | solution.py:22
  175.4 8.9 %all-to-all-start.6 = ((bf16[4,4,40,128]{3,2,1,0:T(8,128)(2,1)}), bf16[4,4,40,128]{3,2,1,0:T(8,128)(2,1)S(1)}, u32[]{:S(2)}, u32[]{:S(2)}) async-start(bf16[4,4,40,128]{3,2,1,0:T(8,128)(2,1)} %broadcast_in_dim.29), calls=%async_computation.6 | async-start | bytes 327680 | tf_op jit(solution)/shard_map/all_to_all | solution.py:22
  190.0 30.9 %all-to-all-start.8 = ((bf16[16,36,128]{2,1,0:T(8,128)(2,1)}), bf16[16,36,128]{2,1,0:T(8,128)(2,1)S(1)}, u32[]{:S(2)}, u32[]{:S(2)}) async-start(bf16[16,36,128]{2,1,0:T(8,128)(2,1)} %broadcast_in_dim.31), calls=%async_computation.8 | async-start | bytes 327680 | tf_op jit(solution)/shard_map/all_to_all | solution.py:22
  (12 other events, 146.4 us)
Sparse Core Ops, SparseCore 0:
  163.9 69.7 all-gather.1

commit v8 on v4

--- a/solution.py
+++ b/solution.py
@@ -89,12 +89,119 @@
 
 PAIRS, WHERE = block_classes()
 NG = len(PAIRS)
-NBLOCKS = 40
+HALF_G = 15
+HALF_D = 5
+HALF = HALF_G + HALF_D
+SMEM = pl.BlockSpec(memory_space=pltpu.SMEM)
+VMEM = pl.BlockSpec(memory_space=pltpu.VMEM)
+
+
+def halo_rows(f, top):
+    def kernel(f_ref, top_ref, up_ref, down_ref):
+        for ref, edge in ((up_ref, 0), (down_ref, 1)):
+            ref[0:2] = f_ref[3]
+            ref[2] = f_ref[2, edge]
+            ref[3] = f_ref[0, edge]
+            ref[4] = top_ref[edge]
+        up_ref[5:7] = f_ref[1]
+
+    row = f.shape[2:]
+    return pl.pallas_call(
+        kernel,
+        out_shape=(
+            jax.ShapeDtypeStruct((7,) + row, f.dtype),
+            jax.ShapeDtypeStruct((5,) + row, f.dtype),
+        ),
+        in_specs=[VMEM, VMEM],
+        out_specs=(VMEM, VMEM),
+        cost_estimate=pl.CostEstimate(flops=0, bytes_accessed=10**6, transcendentals=0),
+    )(f, top)
+
+
+def gram_half(cols, core):
+    chans = cols.shape[1] // 9
+
+    def kernel(core_ref, cols_ref, out_ref):
+        def some(mine):
+            for a in sorted({first for first, _ in mine}):
+                wanted = [b for first, b in mine if first == a]
+                low = min(wanted)
+                left = cols_ref[:, a * chans : (a + 1) * chans].T
+                right = cols_ref[:, low * chans : (max(wanted) + 1) * chans]
+                product = jnp.dot(left, right, preferred_element_type=jnp.float32)
+                for b in wanted:
+                    i = mine.index((a, b))
+                    part = product[:, (b - low) * chans : (b - low + 1) * chans]
+                    out_ref[i * chans : (i + 1) * chans, :] = part.astype(out_ref.dtype)
+            for i in range(len(mine), HALF_G):
+                out_ref[i * chans : (i + 1) * chans, :] = jnp.zeros((chans, chans), out_ref.dtype)
+
+        @pl.when(core_ref[0] == 0)
+        def _():
+            some(PAIRS[:HALF_G])
+
+        @pl.when(core_ref[0] != 0)
+        def _():
+            some(PAIRS[HALF_G:])
+
+    return pl.pallas_call(
+        kernel,
+        out_shape=jax.ShapeDtypeStruct((HALF_G * chans, chans), jnp.bfloat16),
+        in_specs=[SMEM, VMEM],
+        out_specs=VMEM,
+        compiler_params=pltpu.CompilerParams(vmem_limit_bytes=24 * 2**20),
+        cost_estimate=pl.CostEstimate(
+            flops=2 * HALF * cols.shape[0] * chans * chans,
+            bytes_accessed=5 * 10**6,
+            transcendentals=0,
+        ),
+    )(core.reshape(1), cols)
+
+
+def all_half(gram, cols, dpre, core):
+    chans = dpre.shape[-1]
+
+    def kernel(core_ref, gram_ref, cols_ref, dpre_ref, out_ref):
+        out_ref[: HALF_G * chans, :] = gram_ref[...]
+
+        def put(i, value):
+            out_ref[(HALF_G + i) * chans : (HALF_G + i + 1) * chans, :] = value.astype(out_ref.dtype)
+
+        def some(first, last, own):
+            turned = dpre_ref[...].T
+            right = cols_ref[:, first * chans : last * chans]
+            grad = jnp.dot(turned, right, preferred_element_type=jnp.float32)
+            for i in range(last - first):
+                put(i, grad[:, i * chans : (i + 1) * chans].T)
+            if own:
+                put(last - first, jnp.dot(turned, dpre_ref[...], preferred_element_type=jnp.float32))
+
+        @pl.when(core_ref[0] == 0)
+        def _():
+            some(0, HALF_D, False)
+
+        @pl.when(core_ref[0] != 0)
+        def _():
+            some(HALF_D, 9, True)
+
+    return pl.pallas_call(
+        kernel,
+        out_shape=jax.ShapeDtypeStruct((HALF * chans, chans), jnp.bfloat16),
+        in_specs=[SMEM, VMEM, VMEM, VMEM],
+        out_specs=VMEM,
+        compiler_params=pltpu.CompilerParams(vmem_limit_bytes=24 * 2**20),
+        cost_estimate=pl.CostEstimate(
+            flops=2 * HALF_D * cols.shape[0] * chans * chans,
+            bytes_accessed=5 * 10**6,
+            transcendentals=0,
+        ),
+    )(core.reshape(1), gram, cols, dpre)
 
 
 def factor_rows(blocks, first_row, scale, rows):
     chans = blocks.shape[-1]
-    index = jnp.array([WHERE[a, b][0] for a in range(9) for b in range(9)], jnp.int32)
+    slots = [i // HALF_G * HALF + i % HALF_G for i in range(NG)]
+    index = jnp.array([slots[WHERE[a, b][0]] for a in range(9) for b in range(9)], jnp.int32)
     flips = jnp.array([int(WHERE[a, b][1]) for a in range(9) for b in range(9)], jnp.int32)
 
     def kernel(index_ref, flip_ref, row_ref, scale_ref, blocks_ref, out_ref, band):
@@ -114,13 +221,11 @@
         odd = inside != base
         out_ref[...] = jnp.where(odd, got[4:], got[:rows]) * scale_ref[0]
 
-    smem = pl.BlockSpec(memory_space=pltpu.SMEM)
-    vmem = pl.BlockSpec(memory_space=pltpu.VMEM)
     return pl.pallas_call(
         kernel,
         out_shape=jax.ShapeDtypeStruct((rows, 9 * chans), jnp.float32),
-        in_specs=[smem, smem, smem, smem, vmem],
-        out_specs=vmem,
+        in_specs=[SMEM, SMEM, SMEM, SMEM, VMEM],
+        out_specs=VMEM,
         scratch_shapes=[pltpu.VMEM((2 * chans, 9 * chans), jnp.float32)],
         compiler_params=pltpu.CompilerParams(vmem_limit_bytes=16 * 2**20),
         cost_estimate=pl.CostEstimate(flops=10**6, bytes_accessed=2 * 10**6, transcendentals=0),
@@ -141,8 +246,9 @@
     f = feats[:, 0]
     top = top_grad[0]
 
-    above = shifted(jnp.concatenate([f[3], f[2, 1:], f[0, 1:], top[1:]]), 1, False)
-    below = shifted(jnp.concatenate([f[3], f[2, :1], f[0, :1], top[:1], f[1]]), -1, True)
+    to_above, to_below = halo_rows(f, top)
+    below = shifted(to_above, -1, True)
+    above = shifted(to_below, 1, False)
     below1 = below[5:]
     below = jnp.where(inner, below[:5], jnp.zeros_like(below[:5]))
     wide3 = jnp.concatenate([above[:2], f[3], below[:2]])
@@ -152,7 +258,10 @@
         jnp.concatenate([above[2:3], f[2], below[2:3]]),
         wide3[1:5],
     ]
-    layer_strips = exchange(jnp.stack(strips), "y")
+    core_id = lax.axis_index("core")
+
+    def to_layers(x):
+        return exchange(jnp.broadcast_to(x[None], (CORE,) + x.shape).reshape((-1,) + x.shape[1:]), ("core", "y"))
 
     flipped = jnp.transpose(weights.reshape(num_layers, 9, chans, chans), (0, 1, 3, 2)).reshape(
         num_layers, patch, chans
@@ -177,35 +286,30 @@
     after = shifted(dpre2, -1, True)
     dy1 = back(2, cut_windows(jnp.concatenate([dpre2, after]), inner))
     dpre1 = times(dy1, slope(1, cut_windows(strips[1], inner))).reshape(image)
+    stacked, dpre1 = lax.optimization_barrier((jnp.stack(strips), dpre1))
     before = shifted(dpre1, 1, True)
+    layer_strips = to_layers(stacked)
     edge_top = jnp.where(owner_id > 0, before[:1], jnp.zeros_like(before[:1]))
     edge_end = jnp.where(inner, dpre1[1:], jnp.zeros_like(dpre1[1:]))
     dy0 = back(1, windows(jnp.concatenate([edge_top, before[1:], dpre1[:1], edge_end])))
     dpre0 = times(dy0, slope(0, windows(strips[0]))).reshape(image)
 
-    layer_dpre = exchange(jnp.stack([dpre0, dpre1, dpre2, dpre3[1:3]]), "y")
-    big_dpre = layer_dpre.reshape(-1, chans)
     last_one = (y_id == 1) & (z_id == ZH - 1)
-    big_cols = jnp.concatenate(
+    cols = jnp.concatenate(
         [
             to_columns(
                 windows(layer_strips[j])
-                if j < Y - 1
+                if j % Y < Y - 1
                 else cut_windows(layer_strips[j], jnp.logical_not(last_one))
             )
-            for j in range(Y)
+            for j in range(CORE * Y)
         ]
     )
-    gram = inner_rows(big_cols, big_cols).astype(jnp.bfloat16)
-    grad = inner_rows(big_cols, big_dpre).astype(jnp.bfloat16)
-    gfac = inner_rows(big_dpre, big_dpre).astype(jnp.bfloat16)
-    blocks = [
-        gram[a * chans : (a + 1) * chans, b * chans : (b + 1) * chans] for a, b in PAIRS
-    ]
-    pad = jnp.zeros(((NBLOCKS - NG - 10) * chans, chans), jnp.bfloat16)
-    parts = jnp.concatenate(blocks + [grad, gfac, pad], axis=0)
-
-    piece = scatter_sum(scatter_sum(parts, "core"), ("x", "zl"))
+    gram = gram_half(cols, core_id)
+    layer_dpre = to_layers(jnp.stack([dpre0, dpre1, dpre2, dpre3[1:3]]))
+    parts = all_half(gram, cols, layer_dpre.reshape(-1, chans), core_id)
+
+    piece = scatter_sum(parts, ("x", "zl"))
     held = spread(piece, "y")
     layer_ids = jnp.arange(num_layers, dtype=jnp.int32)
 
@@ -220,18 +324,22 @@
     in_grad_win = jnp.concatenate([shifted(dpre0[1:], 1, False), dpre0, shifted(dpre0[:1], -1, False)])
     in_grad = back(0, windows(in_grad_win)).reshape((1,) + image)
 
-    summed = summed.reshape(NBLOCKS, chans, chans)
+    summed = summed.reshape(CORE, HALF * chans, chans)
+    grad_sum = jnp.concatenate(
+        [summed[0, HALF_G * chans :], summed[1, HALF_G * chans : (HALF - 1) * chans]]
+    )
+    grad_scaled = grad_sum.astype(jnp.float32) / jnp.sqrt(jnp.float32(npos))
+    mixed = jnp.dot(grad_scaled, g_inv[0], precision=lax.Precision.HIGHEST)
+    panel = jnp.dot(a_inv[0].astype(jnp.float32), mixed, precision=lax.Precision.HIGHEST)
+    panels = spread(spread(panel.astype(jnp.bfloat16), "zh"), "y")
+    step_out = panels[table % Y, table // Y]
+
+    stats = summed.reshape(-1, chans, chans)
     have = jnp.any(table == owner_id).astype(jnp.float32)
     scale = have / npos
     rows_out = patch // samples
-    a_out = factor_rows(summed, dp_id * rows_out, scale, rows_out)[None]
-    g_out = (summed[NG + 9].astype(jnp.float32) * scale)[None]
-    grad_sum = summed[NG : NG + 9].reshape(patch, chans).astype(jnp.float32)
-    grad_scaled = grad_sum / jnp.sqrt(jnp.float32(npos))
-    mixed = jnp.dot(grad_scaled, g_inv[0], precision=lax.Precision.HIGHEST)
-    panel = jnp.dot(a_inv[0].astype(jnp.float32), mixed, precision=lax.Precision.HIGHEST)
-    panels = spread(panel.astype(jnp.bfloat16), OWNER)
-    step_out = panels[table]
+    a_out = factor_rows(stats, dp_id * rows_out, scale, rows_out)[None]
+    g_out = (stats[-1].astype(jnp.float32) * scale)[None]
     return (step_out, a_out, g_out, in_grad)
 
 

time: 207 us -> 210 us (1.014)
  waiting for transfers between devices: 68.2 us -> 77 us
  blocking collectives: 9.7 us -> 4.79 us
  starting transfers between devices: 81.4 us -> 86.2 us
  Pallas kernels: 0.84 us -> 5.14 us
  matrix products: 7.69 us -> 3.75 us
  local copies, waits for them, and re-layouts: 18.7 us -> 16.1 us
  other arithmetic: 6.57 us -> 4.16 us
    all_to_all x8 -> x9, waiting for transfers between devices: 51.4 us -> 59.3 us  [exchange(): return lax.all_to_all(x, axis, split_axis=0, concat_axis=0, tiled=True)]
    all_to_all x8 -> x9, starting transfers between devices: 45.5 us -> 52.3 us  [exchange(): return lax.all_to_all(x, axis, split_axis=0, concat_axis=0, tiled=True)]
    all_to_all x2 -> x1, blocking collectives: 9.7 us -> 4.79 us  [exchange(): return lax.all_to_all(x, axis, split_axis=0, concat_axis=0, tiled=True)]
    pallas_call x0 -> x3, Pallas kernels: none -> 4.3 us  [the longest x1 1.67 us: halo_rows(): pl.pallas_call(kernel, out_shape=(jax.ShapeDtypeStruct((7,) + row, f.dtyp...]
    dot_general x3 -> x0, matrix products: 3.34 us -> none  [inner_rows(): lax.dot_general(left, right, (((0,), (0,)), ((), ())), preferred_element_...]
    unnamed x165 -> x163, local copies, waits for them, and re-layouts: 8.02 us -> 5.05 us
    ppermute x6, starting transfers between devices: 35.9 us -> 33.8 us  [shifted(): return lax.ppermute(x, OWNER, pairs)]
  transfers between devices with their start and end apart: 14 -> 15, of which waited for: 9 -> 12; matrix products, arithmetic and copies ran while one was open for 8% -> 6% of each run, Pallas kernels for 0% -> 1%
where the time goes in v8:
time: 210 us; the launch traced here: 208 us
  starting transfers between devices  86.2 us (41%)
  waiting for transfers between devices  77 us (37%)
  local copies, waits for them, and re-layouts  16.1 us (8%)
  between operations  10.5 us (5%)
  Pallas kernels  5.14 us (2%)
  blocking collectives  4.79 us (2%)
  other arithmetic  4.16 us (2%)
  matrix products  3.75 us (2%)
    all_to_all x9, waiting for transfers between devices, exchange(): return lax.all_to_all(x, axis, split_axis=0, concat_axis=0, tiled=True)  59.3 us
    all_to_all x9, starting transfers between devices, exchange(): return lax.all_to_all(x, axis, split_axis=0, concat_axis=0, tiled=True)  52.3 us
    ppermute x6, starting transfers between devices, shifted(): return lax.ppermute(x, OWNER, pairs)  33.8 us
    ppermute x6, waiting for transfers between devices, shifted(): return lax.ppermute(x, OWNER, pairs)  17.7 us
    unnamed x163, local copies, waits for them, and re-layouts  5.05 us
    all_to_all x1, blocking collectives, exchange(): return lax.all_to_all(x, axis, split_axis=0, concat_axis=0, tiled=True)  4.79 us
  transfers between devices with their start and end apart: 15, of which 12 were waited for; matrix products, arithmetic and copies ran while one was open for 6% of the time, Pallas kernels for 1%

profile of v8, /device:TPU:6, one launch (start us, length us, event | category | flops | bytes accessed | tf_op | source)
XLA Modules:
  0.0 207.6 jit_solution(5099898123504012825)
XLA Ops:
  2.3 15.2 %collective-permute-start.1 = (bf16[7,80,128]{2,1,0:T(8,128)(2,1)}, bf16[7,80,128]{2,1,0:T(8,128)(2,1)S(1)}, u32[]{:S(2)}, u32[]{:S(2)}) collective-permute-start(bf16[7,80,128]{2,1,0:T(8,128)(2,1)} %get-tuple-element.9), channel_id=1, source_target_pairs={{0,15},{1,0},{2,1},{3,2},{4,3},{5,4},{6,5},{7,6},{8,7},{9,8},{10,9... | collective-permute-start | bytes 430088 | tf_op jit(solution)/shard_map/ppermute | solution.py:18
  22.5 7.6 %collective-permute-done.1 = bf16[7,80,128]{2,1,0:T(8,128)(2,1)S(1)} collective-permute-done((bf16[7,80,128]{2,1,0:T(8,128)(2,1)}, bf16[7,80,128]{2,1,0:T(8,128)(2,1)S(1)}, u32[]{:S(2)}, u32[]{:S(2)}) %collective-permute-start.1) | collective-permute-done | bytes 143392 | tf_op jit(solution)/shard_map/ppermute | solution.py:18
  32.3 10.3 %collective-permute-start.2 = (bf16[2,80,128]{2,1,0:T(8,128)(2,1)S(1)}, bf16[2,80,128]{2,1,0:T(8,128)(2,1)S(1)}, u32[]{:S(2)}, u32[]{:S(2)}) collective-permute-start(bf16[2,80,128]{2,1,0:T(8,128)(2,1)S(1)} %bitcast.330), channel_id=1, source_target_pairs={{0,15},{1,0},{2,1},{3,2},{4,3},{5,4},{6,5},{7,6},{8,7},{9,8},{10,9... | collective-permute-start | bytes 122888 | tf_op jit(solution)/shard_map/ppermute | solution.py:18
  48.4 3.5 %all-to-all-start = ((bf16[8,4,80,128]{3,2,1,0:T(8,128)(2,1)}), bf16[8,4,80,128]{3,2,1,0:T(8,128)(2,1)S(1)}, u32[]{:S(2)}, u32[]{:S(2)}) async-start(bf16[8,4,80,128]{3,2,1,0:T(8,128)(2,1)} %bitcast.80), calls=%async_computation | async-start | bytes 1310720 | tf_op jit(solution)/shard_map/all_to_all | solution.py:22
  51.9 6.3 %collective-permute-done.3 = bf16[2,80,128]{2,1,0:T(8,128)(2,1)S(1)} collective-permute-done((bf16[2,80,128]{2,1,0:T(8,128)(2,1)S(1)}, bf16[2,80,128]{2,1,0:T(8,128)(2,1)S(1)}, u32[]{:S(2)}, u32[]{:S(2)}) %collective-permute-start.3) | collective-permute-done | bytes 40992 | tf_op jit(solution)/shard_map/ppermute | solution.py:18
  59.4 4.0 %all-to-all-done = bf16[8,4,80,128]{3,2,1,0:T(8,128)(2,1)S(1)} async-done(((bf16[8,4,80,128]{3,2,1,0:T(8,128)(2,1)}), bf16[8,4,80,128]{3,2,1,0:T(8,128)(2,1)S(1)}, u32[]{:S(2)}, u32[]{:S(2)}) %all-to-all-start) | async-done | bytes 655392 | tf_op jit(solution)/shard_map/all_to_all | solution.py:22
  64.2 4.1 %all-to-all-start.1 = ((bf16[8,2,80,128]{3,2,1,0:T(8,128)(2,1)}), bf16[8,2,80,128]{3,2,1,0:T(8,128)(2,1)}, u32[]{:S(2)}, u32[]{:S(2)}) async-start(bf16[8,2,80,128]{3,2,1,0:T(8,128)(2,1)} %bitcast.199), calls=%async_computation.1 | async-start | bytes 655360 | tf_op jit(solution)/shard_map/all_to_all | solution.py:22
  71.9 4.0 %all-to-all-done.1 = bf16[8,2,80,128]{3,2,1,0:T(8,128)(2,1)} async-done(((bf16[8,2,80,128]{3,2,1,0:T(8,128)(2,1)}), bf16[8,2,80,128]{3,2,1,0:T(8,128)(2,1)}, u32[]{:S(2)}, u32[]{:S(2)}) %all-to-all-start.1) | async-done | bytes 327712 | tf_op jit(solution)/shard_map/all_to_all | solution.py:22
  78.3 4.9 %all-to-all-start.2 = ((bf16[16,160,128]{2,1,0:T(8,128)(2,1)}), bf16[16,160,128]{2,1,0:T(8,128)(2,1)S(1)}, u32[]{:S(2)}, u32[]{:S(2)}) async-start(bf16[16,160,128]{2,1,0:T(8,128)(2,1)} %bitcast.310), calls=%async_computation.2 | async-start | bytes 1310720 | tf_op jit(solution)/shard_map/all_to_all | solution.py:22
  83.2 17.3 %all-to-all-done.2 = bf16[16,160,128]{2,1,0:T(8,128)(2,1)S(1)} async-done(((bf16[16,160,128]{2,1,0:T(8,128)(2,1)}), bf16[16,160,128]{2,1,0:T(8,128)(2,1)S(1)}, u32[]{:S(2)}, u32[]{:S(2)}) %all-to-all-start.2) | async-done | bytes 655392 | tf_op jit(solution)/shard_map/all_to_all | solution.py:22
  101.3 3.3 %all-to-all-start.3 = ((bf16[4,160,128]{2,1,0:T(8,128)(2,1)}), bf16[4,160,128]{2,1,0:T(8,128)(2,1)S(1)}, u32[]{:S(2)}, u32[]{:S(2)}) async-start(bf16[4,160,128]{2,1,0:T(8,128)(2,1)} %broadcast_in_dim.34), calls=%async_computation.3 | async-start | bytes 327680 | tf_op jit(solution)/shard_map/all_to_all | solution.py:22
  113.7 12.4 %all-to-all-start.4 = ((bf16[4,160,128]{2,1,0:T(8,128)(2,1)}), bf16[4,160,128]{2,1,0:T(8,128)(2,1)S(1)}, u32[]{:S(2)}, u32[]{:S(2)}) async-start(bf16[4,160,128]{2,1,0:T(8,128)(2,1)} %pad_maximum_fusion.7), calls=%async_computation.4 | async-start | bytes 327680 | tf_op jit(solution)/shard_map/all_to_all | solution.py:22
  126.1 3.9 %collective-permute-start.4 = (bf16[1,80,128]{2,1,0:T(8,128)(2,1)S(1)}, bf16[1,80,128]{2,1,0:T(8,128)(2,1)S(1)}, u32[]{:S(2)}, u32[]{:S(2)}) collective-permute-start(bf16[1,80,128]{2,1,0:T(8,128)(2,1)S(1)} %get-tuple-element.248), channel_id=1, source_target_pairs={{0,1},{1,2},{2,3},{3,4},{4,5},{5,6},{6,7},{7,8},{8,9},{9,10},{10,1... | collective-permute-start | bytes 61448 | tf_op jit(solution)/shard_map/ppermute | solution.py:18
  132.8 2.8 %collective-permute-done.5 = bf16[1,80,128]{2,1,0:T(8,128)(2,1)S(1)} collective-permute-done((bf16[1,80,128]{2,1,0:T(8,128)(2,1)S(1)}, bf16[1,80,128]{2,1,0:T(8,128)(2,1)S(1)}, u32[]{:S(2)}, u32[]{:S(2)}) %collective-permute-start.5) | collective-permute-done | bytes 20512 | tf_op jit(solution)/shard_map/ppermute | solution.py:18
  135.7 5.9 %all-to-all-done.4 = bf16[4,160,128]{2,1,0:T(8,128)(2,1)S(1)} async-done(((bf16[4,160,128]{2,1,0:T(8,128)(2,1)}), bf16[4,160,128]{2,1,0:T(8,128)(2,1)S(1)}, u32[]{:S(2)}, u32[]{:S(2)}) %all-to-all-start.4) | async-done | bytes 163872 | tf_op jit(solution)/shard_map/all_to_all | solution.py:22
  142.3 3.3 %all-to-all-start.5 = ((bf16[4,160,128]{2,1,0:T(8,128)(2,1)}), bf16[4,160,128]{2,1,0:T(8,128)(2,1)S(1)}, u32[]{:S(2)}, u32[]{:S(2)}) async-start(bf16[4,160,128]{2,1,0:T(8,128)(2,1)} %broadcast_in_dim.36), calls=%async_computation.5 | async-start | bytes 327680 | tf_op jit(solution)/shard_map/all_to_all | solution.py:22
  145.8 5.8 %all-to-all-done.5 = bf16[4,160,128]{2,1,0:T(8,128)(2,1)S(1)} async-done(((bf16[4,160,128]{2,1,0:T(8,128)(2,1)}), bf16[4,160,128]{2,1,0:T(8,128)(2,1)S(1)}, u32[]{:S(2)}, u32[]{:S(2)}) %all-to-all-start.5) | async-done | bytes 163872 | tf_op jit(solution)/shard_map/all_to_all | solution.py:22
  152.6 5.1 %all-to-all-start.6 = ((bf16[4,4,160,128]{3,2,1,0:T(8,128)(2,1)}), bf16[4,4,160,128]{3,2,1,0:T(8,128)(2,1)S(1)}, u32[]{:S(2)}, u32[]{:S(2)}) async-start(bf16[4,4,160,128]{3,2,1,0:T(8,128)(2,1)} %broadcast_in_dim.37), calls=%async_computation.6 | async-start | bytes 1310720 | tf_op jit(solution)/shard_map/all_to_all | solution.py:22
  157.8 6.6 %all-to-all-done.6 = bf16[4,4,160,128]{3,2,1,0:T(8,128)(2,1)S(1)} async-done(((bf16[4,4,160,128]{3,2,1,0:T(8,128)(2,1)}), bf16[4,4,160,128]{3,2,1,0:T(8,128)(2,1)S(1)}, u32[]{:S(2)}, u32[]{:S(2)}) %all-to-all-start.6) | async-done | bytes 655392 | tf_op jit(solution)/shard_map/all_to_all | solution.py:22
  164.7 4.8 %all_to_all.50 = bf16[2,4,4,160,128]{4,3,2,1,0:T(8,128)(2,1)S(1)} all-to-all(bf16[2,4,4,160,128]{4,3,2,1,0:T(8,128)(2,1)S(1)} %broadcast_in_dim.38), channel_id=1, replica_groups=mesh['x'=4,'zl'=4,'core'=2,'zh'=4,'y'=4] {'core'}, dimensions={0} | all-to-all | bytes 2621440 | tf_op jit(solution)/shard_map/all_to_all | solution.py:22
  171.1 10.9 %all-to-all-start.8 = ((bf16[4,36,128]{2,1,0:T(8,128)(2,1)}), bf16[4,36,128]{2,1,0:T(8,128)(2,1)S(1)}, u32[]{:S(2)}, u32[]{:S(2)}) async-start(bf16[4,36,128]{2,1,0:T(8,128)(2,1)} %broadcast_in_dim.39), calls=%async_computation.8 | async-start | bytes 81920 | tf_op jit(solution)/shard_map/all_to_all | solution.py:22
  182.8 12.0 %all-to-all-done.8 = bf16[4,36,128]{2,1,0:T(8,128)(2,1)S(1)} async-done(((bf16[4,36,128]{2,1,0:T(8,128)(2,1)}), bf16[4,36,128]{2,1,0:T(8,128)(2,1)S(1)}, u32[]{:S(2)}, u32[]{:S(2)}) %all-to-all-start.8) | async-done | bytes 36896 | tf_op jit(solution)/shard_map/all_to_all | solution.py:22
  195.6 4.7 %all-to-all-start.9 = ((bf16[4,4,36,128]{3,1,2,0:T(4,128)(2,1)}), bf16[4,4,36,128]{3,1,2,0:T(4,128)(2,1)S(1)}, u32[]{:S(2)}, u32[]{:S(2)}) async-start(bf16[4,4,36,128]{3,1,2,0:T(4,128)(2,1)} %broadcast_in_dim.40), calls=%async_computation.9 | async-start | bytes 294912 | tf_op jit(solution)/shard_map/all_to_all | solution.py:22
  202.6 3.7 %all-to-all-done.9 = bf16[4,4,36,128]{3,1,2,0:T(4,128)(2,1)S(1)} async-done(((bf16[4,4,36,128]{3,1,2,0:T(4,128)(2,1)}), bf16[4,4,36,128]{3,1,2,0:T(4,128)(2,1)S(1)}, u32[]{:S(2)}, u32[]{:S(2)}) %all-to-all-start.9) | async-done | bytes 147488 | tf_op jit(solution)/shard_map/all_to_all | solution.py:22
  (277 shorter events, 34.6 us)
Async XLA Ops:
  0.6 169.5 %copy-start = (bf16[1,36,1152]{2,1,0:T(8,128)(2,1)S(1)}, bf16[1,36,1152]{2,1,0:T(8,128)(2,1)}, u32[]{:S(2)}) copy-start(bf16[1,36,1152]{2,1,0:T(8,128)(2,1)} %param.20) | copy-start | bytes 248836
  2.3 27.8 %collective-permute-start.1 = (bf16[7,80,128]{2,1,0:T(8,128)(2,1)}, bf16[7,80,128]{2,1,0:T(8,128)(2,1)S(1)}, u32[]{:S(2)}, u32[]{:S(2)}) collective-permute-start(bf16[7,80,128]{2,1,0:T(8,128)(2,1)} %get-tuple-element.9), channel_id=1, source_target_pairs={{0,15},{1,0},{2,1},{3,2},{4,3},{5,4},{6,5},{7,6},{8,7},{9,8},{10,9... | collective-permute-start | bytes 430088 | tf_op jit(solution)/shard_map/ppermute | solution.py:18
  17.5 5.0 %collective-permute-start = (bf16[5,80,128]{2,1,0:T(8,128)(2,1)}, bf16[5,80,128]{2,1,0:T(8,128)(2,1)S(1)}, u32[]{:S(2)}, u32[]{:S(2)}) collective-permute-start(bf16[5,80,128]{2,1,0:T(8,128)(2,1)} %get-tuple-element.8), channel_id=1, source_target_pairs={{0,1},{1,2},{2,3},{3,4},{4,5},{5,6},{6,7},{7,8},{8,9},{9,10},{10,1... | collective-permute-start | bytes 307208 | tf_op jit(solution)/shard_map/ppermute | solution.py:18
  31.7 12.5 %copy-start.10 = (bf16[3]{0:T(256)(128)(2,1)S(1)}, bf16[3]{0:T(256)(128)(2,1)}, u32[]{:S(2)}) copy-start(bf16[3]{0:T(256)(128)(2,1)} %constant.101.clone) | copy-start | bytes 22
  31.8 12.5 %copy-start.11 = (bf16[3]{0:T(256)(128)(2,1)S(1)}, bf16[3]{0:T(256)(128)(2,1)}, u32[]{:S(2)}) copy-start(bf16[3]{0:T(256)(128)(2,1)} %constant.102.clone) | copy-start | bytes 22
  32.3 11.9 %collective-permute-start.2 = (bf16[2,80,128]{2,1,0:T(8,128)(2,1)S(1)}, bf16[2,80,128]{2,1,0:T(8,128)(2,1)S(1)}, u32[]{:S(2)}, u32[]{:S(2)}) collective-permute-start(bf16[2,80,128]{2,1,0:T(8,128)(2,1)S(1)} %bitcast.330), channel_id=1, source_target_pairs={{0,15},{1,0},{2,1},{3,2},{4,3},{5,4},{6,5},{7,6},{8,7},{9,8},{10,9... | collective-permute-start | bytes 122888 | tf_op jit(solution)/shard_map/ppermute | solution.py:18
  45.5 12.7 %collective-permute-start.3 = (bf16[2,80,128]{2,1,0:T(8,128)(2,1)S(1)}, bf16[2,80,128]{2,1,0:T(8,128)(2,1)S(1)}, u32[]{:S(2)}, u32[]{:S(2)}) collective-permute-start(bf16[2,80,128]{2,1,0:T(8,128)(2,1)S(1)} %bitcast.333), channel_id=1, source_target_pairs={{0,1},{1,2},{2,3},{3,4},{4,5},{5,6},{6,7},{7,8},{8,9},{9,10},{10,1... | collective-permute-start | bytes 122888 | tf_op jit(solution)/shard_map/ppermute | solution.py:18
  48.4 15.0 %all-to-all-start = ((bf16[8,4,80,128]{3,2,1,0:T(8,128)(2,1)}), bf16[8,4,80,128]{3,2,1,0:T(8,128)(2,1)S(1)}, u32[]{:S(2)}, u32[]{:S(2)}) async-start(bf16[8,4,80,128]{3,2,1,0:T(8,128)(2,1)} %bitcast.80), calls=%async_computation | async-start | bytes 1310720 | tf_op jit(solution)/shard_map/all_to_all | solution.py:22
  64.2 11.7 %all-to-all-start.1 = ((bf16[8,2,80,128]{3,2,1,0:T(8,128)(2,1)}), bf16[8,2,80,128]{3,2,1,0:T(8,128)(2,1)}, u32[]{:S(2)}, u32[]{:S(2)}) async-start(bf16[8,2,80,128]{3,2,1,0:T(8,128)(2,1)} %bitcast.199), calls=%async_computation.1 | async-start | bytes 655360 | tf_op jit(solution)/shard_map/all_to_all | solution.py:22
  75.9 28.7 %copy-start.12 = (s32[4]{0:T(128)S(1)}, s32[4]{0:T(128)}, u32[]{:S(2)}) copy-start(s32[4]{0:T(128)} %param.19) | copy-start | bytes 52
  78.3 47.8 %copy-start.7 = (bf16[160,128]{1,0:T(8,128)(2,1)S(1)}, bf16[160,128]{1,0:T(8,128)(2,1)}, u32[]{:S(2)}) copy-start(bf16[160,128]{1,0:T(8,128)(2,1)} %copy-done.6) | copy-start | bytes 122884
  78.3 53.6 %copy-start.5 = (bf16[1,9,128,128]{2,3,1,0:T(8,128)(2,1)S(1)}, bf16[1,9,128,128]{2,3,1,0:T(8,128)(2,1)}, u32[]{:S(2)}) copy-start(bf16[1,9,128,128]{2,3,1,0:T(8,128)(2,1)} %get-tuple-element.40) | copy-start | bytes 884740
  78.3 22.2 %all-to-all-start.2 = ((bf16[16,160,128]{2,1,0:T(8,128)(2,1)}), bf16[16,160,128]{2,1,0:T(8,128)(2,1)S(1)}, u32[]{:S(2)}, u32[]{:S(2)}) async-start(bf16[16,160,128]{2,1,0:T(8,128)(2,1)} %bitcast.310), calls=%async_computation.2 | async-start | bytes 1310720 | tf_op jit(solution)/shard_map/all_to_all | solution.py:22
  101.3 11.7 %all-to-all-start.3 = ((bf16[4,160,128]{2,1,0:T(8,128)(2,1)}), bf16[4,160,128]{2,1,0:T(8,128)(2,1)S(1)}, u32[]{:S(2)}, u32[]{:S(2)}) async-start(bf16[4,160,128]{2,1,0:T(8,128)(2,1)} %broadcast_in_dim.34), calls=%async_computation.3 | async-start | bytes 327680 | tf_op jit(solution)/shard_map/all_to_all | solution.py:22
  113.7 27.9 %all-to-all-start.4 = ((bf16[4,160,128]{2,1,0:T(8,128)(2,1)}), bf16[4,160,128]{2,1,0:T(8,128)(2,1)S(1)}, u32[]{:S(2)}, u32[]{:S(2)}) async-start(bf16[4,160,128]{2,1,0:T(8,128)(2,1)} %pad_maximum_fusion.7), calls=%async_computation.4 | async-start | bytes 327680 | tf_op jit(solution)/shard_map/all_to_all | solution.py:22
  126.1 6.7 %collective-permute-start.4 = (bf16[1,80,128]{2,1,0:T(8,128)(2,1)S(1)}, bf16[1,80,128]{2,1,0:T(8,128)(2,1)S(1)}, u32[]{:S(2)}, u32[]{:S(2)}) collective-permute-start(bf16[1,80,128]{2,1,0:T(8,128)(2,1)S(1)} %get-tuple-element.248), channel_id=1, source_target_pairs={{0,1},{1,2},{2,3},{3,4},{4,5},{5,6},{6,7},{7,8},{8,9},{9,10},{10,1... | collective-permute-start | bytes 61448 | tf_op jit(solution)/shard_map/ppermute | solution.py:18
  130.0 5.7 %collective-permute-start.5 = (bf16[1,80,128]{2,1,0:T(8,128)(2,1)S(1)}, bf16[1,80,128]{2,1,0:T(8,128)(2,1)S(1)}, u32[]{:S(2)}, u32[]{:S(2)}) collective-permute-start(bf16[1,80,128]{2,1,0:T(8,128)(2,1)S(1)} %get-tuple-element.249), channel_id=1, source_target_pairs={{1,0},{2,1},{3,2},{4,3},{5,4},{6,5},{7,6},{8,7},{9,8},{10,9},{11,1... | collective-permute-start | bytes 61448 | tf_op jit(solution)/shard_map/ppermute | solution.py:18
  142.3 9.3 %all-to-all-start.5 = ((bf16[4,160,128]{2,1,0:T(8,128)(2,1)}), bf16[4,160,128]{2,1,0:T(8,128)(2,1)S(1)}, u32[]{:S(2)}, u32[]{:S(2)}) async-start(bf16[4,160,128]{2,1,0:T(8,128)(2,1)} %broadcast_in_dim.36), calls=%async_computation.5 | async-start | bytes 327680 | tf_op jit(solution)/shard_map/all_to_all | solution.py:22
  152.6 11.8 %all-to-all-start.6 = ((bf16[4,4,160,128]{3,2,1,0:T(8,128)(2,1)}), bf16[4,4,160,128]{3,2,1,0:T(8,128)(2,1)S(1)}, u32[]{:S(2)}, u32[]{:S(2)}) async-start(bf16[4,4,160,128]{3,2,1,0:T(8,128)(2,1)} %broadcast_in_dim.37), calls=%async_computation.6 | async-start | bytes 1310720 | tf_op jit(solution)/shard_map/all_to_all | solution.py:22
  157.7 11.8 %copy-start.9 = (f32[1,128,128]{2,1,0:T(8,128)S(1)}, f32[1,128,128]{2,1,0:T(8,128)}, u32[]{:S(2)}) copy-start(f32[1,128,128]{2,1,0:T(8,128)} %param.21) | copy-start | bytes 196612
  164.6 36.3 %copy-start.2 = (s32[81]{0:T(128)S(1)}, s32[81]{0:T(128)}, u32[]{:S(2)}) copy-start(s32[81]{0:T(128)} %constant.103.clone.index_ref) | copy-start | bytes 976
  164.6 36.3 %copy-start.3 = (s32[81]{0:T(128)S(1)}, s32[81]{0:T(128)}, u32[]{:S(2)}) copy-start(s32[81]{0:T(128)} %constant.104.clone.flip_ref) | copy-start | bytes 976
  171.1 23.8 %all-to-all-start.8 = ((bf16[4,36,128]{2,1,0:T(8,128)(2,1)}), bf16[4,36,128]{2,1,0:T(8,128)(2,1)S(1)}, u32[]{:S(2)}, u32[]{:S(2)}) async-start(bf16[4,36,128]{2,1,0:T(8,128)(2,1)} %broadcast_in_dim.39), calls=%async_computation.8 | async-start | bytes 81920 | tf_op jit(solution)/shard_map/all_to_all | solution.py:22
  195.6 10.8 %all-to-all-start.9 = ((bf16[4,4,36,128]{3,1,2,0:T(4,128)(2,1)}), bf16[4,4,36,128]{3,1,2,0:T(4,128)(2,1)S(1)}, u32[]{:S(2)}, u32[]{:S(2)}) async-start(bf16[4,4,36,128]{3,1,2,0:T(4,128)(2,1)} %broadcast_in_dim.40), calls=%async_computation.9 | async-start | bytes 294912 | tf_op jit(solution)/shard_map/all_to_all | solution.py:22
  (4 other events, 12.1 us)

commit v9 on v8

--- a/solution.py
+++ b/solution.py
@@ -16,6 +16,10 @@
     if not cyclic:
         pairs = [(a, b) for a, b in pairs if b - a == shift]
     return lax.ppermute(x, OWNER, pairs)
+
+
+def paired(x, axis, step):
+    return lax.ppermute(x, axis, [(i, i ^ 1 if step == 0 else 3 - i) for i in range(4)])
 
 
 def exchange(x, axis):
@@ -89,9 +93,11 @@
 
 PAIRS, WHERE = block_classes()
 NG = len(PAIRS)
-HALF_G = 15
+HALF_G = 16
 HALF_D = 5
-HALF = HALF_G + HALF_D
+FAC_ROWS = 128
+GRAD_ROWS = 40
+PIECE_ROWS = 176
 SMEM = pl.BlockSpec(memory_space=pltpu.SMEM)
 VMEM = pl.BlockSpec(memory_space=pltpu.VMEM)
 
@@ -151,7 +157,7 @@
         out_specs=VMEM,
         compiler_params=pltpu.CompilerParams(vmem_limit_bytes=24 * 2**20),
         cost_estimate=pl.CostEstimate(
-            flops=2 * HALF * cols.shape[0] * chans * chans,
+            flops=2 * (HALF_G + HALF_D) * cols.shape[0] * chans * chans,
             bytes_accessed=5 * 10**6,
             transcendentals=0,
         ),
@@ -161,34 +167,39 @@
 def all_half(gram, cols, dpre, core):
     chans = dpre.shape[-1]
 
-    def kernel(core_ref, gram_ref, cols_ref, dpre_ref, out_ref):
-        out_ref[: HALF_G * chans, :] = gram_ref[...]
-
-        def put(i, value):
-            out_ref[(HALF_G + i) * chans : (HALF_G + i + 1) * chans, :] = value.astype(out_ref.dtype)
-
-        def some(first, last, own):
+    def kernel(core_ref, gram_ref, cols_ref, dpre_ref, out_ref, dense):
+        for k in range(HALF_G):
+            out_ref[k, :FAC_ROWS, :] = gram_ref[k * chans : (k + 1) * chans, :]
+        dense[...] = jnp.zeros(dense.shape, dense.dtype)
+
+        def some(first, last):
             turned = dpre_ref[...].T
             right = cols_ref[:, first * chans : last * chans]
             grad = jnp.dot(turned, right, preferred_element_type=jnp.float32)
             for i in range(last - first):
-                put(i, grad[:, i * chans : (i + 1) * chans].T)
-            if own:
-                put(last - first, jnp.dot(turned, dpre_ref[...], preferred_element_type=jnp.float32))
+                dense[i * chans : (i + 1) * chans, :] = grad[:, i * chans : (i + 1) * chans].T
+            return turned
 
         @pl.when(core_ref[0] == 0)
         def _():
-            some(0, HALF_D, False)
+            some(0, HALF_D)
 
         @pl.when(core_ref[0] != 0)
         def _():
-            some(HALF_D, 9, True)
+            turned = some(HALF_D, 9)
+            own = jnp.dot(turned, dpre_ref[...], preferred_element_type=jnp.float32)
+            out_ref[NG - HALF_G, :FAC_ROWS, :] = own.astype(out_ref.dtype)
+
+        for k in range(HALF_G):
+            rows = dense[k * GRAD_ROWS : k * GRAD_ROWS + PIECE_ROWS - FAC_ROWS, :]
+            out_ref[k, FAC_ROWS:, :] = rows.astype(out_ref.dtype)
 
     return pl.pallas_call(
         kernel,
-        out_shape=jax.ShapeDtypeStruct((HALF * chans, chans), jnp.bfloat16),
+        out_shape=jax.ShapeDtypeStruct((HALF_G, PIECE_ROWS, chans), jnp.bfloat16),
         in_specs=[SMEM, VMEM, VMEM, VMEM],
         out_specs=VMEM,
+        scratch_shapes=[pltpu.VMEM((HALF_D * chans + 16, chans), jnp.float32)],
         compiler_params=pltpu.CompilerParams(vmem_limit_bytes=24 * 2**20),
         cost_estimate=pl.CostEstimate(
             flops=2 * HALF_D * cols.shape[0] * chans * chans,
@@ -200,8 +211,7 @@
 
 def factor_rows(blocks, first_row, scale, rows):
     chans = blocks.shape[-1]
-    slots = [i // HALF_G * HALF + i % HALF_G for i in range(NG)]
-    index = jnp.array([slots[WHERE[a, b][0]] for a in range(9) for b in range(9)], jnp.int32)
+    index = jnp.array([WHERE[a, b][0] for a in range(9) for b in range(9)], jnp.int32)
     flips = jnp.array([int(WHERE[a, b][1]) for a in range(9) for b in range(9)], jnp.int32)
 
     def kernel(index_ref, flip_ref, row_ref, scale_ref, blocks_ref, out_ref, band):
@@ -210,7 +220,7 @@
         for t in range(2):
             a = jnp.minimum(tap + t, 8)
             for b in range(9):
-                block = blocks_ref[index_ref[a * 9 + b]].astype(jnp.float32)
+                block = blocks_ref[index_ref[a * 9 + b], :chans, :].astype(jnp.float32)
                 flip = flip_ref[a * 9 + b] != 0
                 band[t * chans : (t + 1) * chans, b * chans : (b + 1) * chans] = jnp.where(
                     flip, block.T, block
@@ -286,9 +296,11 @@
     after = shifted(dpre2, -1, True)
     dy1 = back(2, cut_windows(jnp.concatenate([dpre2, after]), inner))
     dpre1 = times(dy1, slope(1, cut_windows(strips[1], inner))).reshape(image)
-    stacked, dpre1 = lax.optimization_barrier((jnp.stack(strips), dpre1))
+    local = jnp.concatenate([a_inv.reshape(-1, chans), g_inv[0].astype(jnp.bfloat16)])
+    stacked, dpre1, local = lax.optimization_barrier((jnp.stack(strips), dpre1, local))
     before = shifted(dpre1, 1, True)
     layer_strips = to_layers(stacked)
+    near = paired(local, "y", 0)
     edge_top = jnp.where(owner_id > 0, before[:1], jnp.zeros_like(before[:1]))
     edge_end = jnp.where(inner, dpre1[1:], jnp.zeros_like(dpre1[1:]))
     dy0 = back(1, windows(jnp.concatenate([edge_top, before[1:], dpre1[:1], edge_end])))
@@ -309,13 +321,24 @@
     layer_dpre = to_layers(jnp.stack([dpre0, dpre1, dpre2, dpre3[1:3]]))
     parts = all_half(gram, cols, layer_dpre.reshape(-1, chans), core_id)
 
+    parts, local, near = lax.optimization_barrier((parts, local, near))
+    from_y, from_z = table % Y, table // Y
+    far = paired(jnp.where(from_y[3 - y_id] == y_id, local, near), "y", 1)
+    want = from_y[y_id]
+    found = jnp.where(want == y_id, local, jnp.where(want == (y_id ^ 1), near, far))
+    want = from_z[y_id]
+    found = jnp.where(want == (z_id ^ 1), paired(found, "zh", 0), found)
+
     piece = scatter_sum(parts, ("x", "zl"))
-    held = spread(piece, "y")
+    piece, found = lax.optimization_barrier((piece, found))
+    inverses = jnp.where(want // 2 == z_id // 2, found, paired(found, "zh", 1))
+    held = spread(piece[:, :FAC_ROWS], "y")
     layer_ids = jnp.arange(num_layers, dtype=jnp.int32)
 
     def pick(z):
         lay = jnp.sum(jnp.where(table == z * Y + y_id, layer_ids, 0))
-        return lax.dynamic_index_in_dim(held, lay, 0, keepdims=False)
+        fac = lax.dynamic_index_in_dim(held, lay, 0, keepdims=False)
+        return jnp.concatenate([fac, piece[:, FAC_ROWS:]], axis=1)
 
     total = exchange(jnp.stack([pick(z) for z in range(ZH)]), "zh")
     total = jnp.sum(total.astype(jnp.float32), axis=0).astype(jnp.bfloat16)
@@ -324,22 +347,19 @@
     in_grad_win = jnp.concatenate([shifted(dpre0[1:], 1, False), dpre0, shifted(dpre0[:1], -1, False)])
     in_grad = back(0, windows(in_grad_win)).reshape((1,) + image)
 
-    summed = summed.reshape(CORE, HALF * chans, chans)
-    grad_sum = jnp.concatenate(
-        [summed[0, HALF_G * chans :], summed[1, HALF_G * chans : (HALF - 1) * chans]]
-    )
-    grad_scaled = grad_sum.astype(jnp.float32) / jnp.sqrt(jnp.float32(npos))
-    mixed = jnp.dot(grad_scaled, g_inv[0], precision=lax.Precision.HIGHEST)
-    panel = jnp.dot(a_inv[0].astype(jnp.float32), mixed, precision=lax.Precision.HIGHEST)
-    panels = spread(spread(panel.astype(jnp.bfloat16), "zh"), "y")
-    step_out = panels[table % Y, table // Y]
-
-    stats = summed.reshape(-1, chans, chans)
+    stats = summed.reshape(CORE * HALF_G, PIECE_ROWS, chans)
+    grad_sum = stats[:, FAC_ROWS : FAC_ROWS + GRAD_ROWS].reshape(-1, chans)[:patch]
+    rows_out = patch // samples
+    a_mine = inverses[: rows_out * 9].reshape(rows_out, patch)
+    mixed = jnp.dot(grad_sum, inverses[rows_out * 9 :], preferred_element_type=jnp.float32)
+    mixed = mixed / jnp.sqrt(jnp.float32(npos))
+    panel = jnp.dot(a_mine.astype(jnp.float32), mixed, precision=lax.Precision.HIGHEST)
+    step_out = spread(panel.astype(jnp.bfloat16), "y")
+
     have = jnp.any(table == owner_id).astype(jnp.float32)
     scale = have / npos
-    rows_out = patch // samples
     a_out = factor_rows(stats, dp_id * rows_out, scale, rows_out)[None]
-    g_out = (stats[-1].astype(jnp.float32) * scale)[None]
+    g_out = (stats[NG, :FAC_ROWS].astype(jnp.float32) * scale)[None]
     return (step_out, a_out, g_out, in_grad)
 
 

time: 210 us -> 205 us (0.976)
  waiting for transfers between devices: 77 us -> 59.5 us
  between operations: 10.5 us -> 15.7 us
  starting transfers between devices: 86.2 us -> 91.2 us
    all_to_all x9 -> x8, waiting for transfers between devices: 59.3 us -> 37.3 us  [exchange(): return lax.all_to_all(x, axis, split_axis=0, concat_axis=0, tiled=True)]
    ppermute x0 -> x4, starting transfers between devices: none -> 20.8 us  [paired(): lax.ppermute(x, axis, [(i, i ^ 1 if step == 0 else 3 - i) for i in range(...]
    all_to_all x9 -> x8, starting transfers between devices: 52.3 us -> 39.1 us  [exchange(): return lax.all_to_all(x, axis, split_axis=0, concat_axis=0, tiled=True)]
    ppermute x0 -> x4, waiting for transfers between devices: none -> 11.9 us  [paired(): lax.ppermute(x, axis, [(i, i ^ 1 if step == 0 else 3 - i) for i in range(...]
    ppermute x6, waiting for transfers between devices: 17.7 us -> 10.3 us  [shifted(): return lax.ppermute(x, OWNER, pairs)]
    ppermute x6, starting transfers between devices: 33.8 us -> 31.2 us  [shifted(): return lax.ppermute(x, OWNER, pairs)]
    unnamed x163 -> x157, local copies, waits for them, and re-layouts: 5.05 us -> 4.46 us
  transfers between devices with their start and end apart: 15 -> 18, of which waited for: 12 -> 11; matrix products, arithmetic and copies ran while one was open for 6% -> 9% of each run, Pallas kernels for 1% -> 2%
where the time goes in v9:
time: 205 us; the launch traced here: 202 us
  starting transfers between devices  91.2 us (44%)
  waiting for transfers between devices  59.5 us (29%)
  local copies, waits for them, and re-layouts  16.5 us (8%)
  between operations  15.7 us (8%)
  other arithmetic  5.92 us (3%)
  Pallas kernels  5.16 us (3%)
  blocking collectives  4.89 us (2%)
  matrix products  3.38 us (2%)
    all_to_all x8, starting transfers between devices, exchange(): return lax.all_to_all(x, axis, split_axis=0, concat_axis=0, tiled=True)  39.1 us
    all_to_all x8, waiting for transfers between devices, exchange(): return lax.all_to_all(x, axis, split_axis=0, concat_axis=0, tiled=True)  37.3 us
    ppermute x6, starting transfers between devices, shifted(): return lax.ppermute(x, OWNER, pairs)  31.2 us
    ppermute x4, starting transfers between devices, paired(): lax.ppermute(x, axis, [(i, i ^ 1 if step == 0 else 3 - i) for i in range(...  20.8 us
    ppermute x4, waiting for transfers between devices, paired(): lax.ppermute(x, axis, [(i, i ^ 1 if step == 0 else 3 - i) for i in range(...  11.9 us
    ppermute x6, waiting for transfers between devices, shifted(): return lax.ppermute(x, OWNER, pairs)  10.3 us
    all_to_all x1, blocking collectives, exchange(): return lax.all_to_all(x, axis, split_axis=0, concat_axis=0, tiled=True)  4.89 us
    unnamed x157, local copies, waits for them, and re-layouts  4.46 us
  transfers between devices with their start and end apart: 18, of which 11 were waited for; matrix products, arithmetic and copies ran while one was open for 9% of the time, Pallas kernels for 2%

profile of v9, /device:TPU:6, one launch (start us, length us, event | category | flops | bytes accessed | tf_op | source)
XLA Modules:
  0.0 202.2 jit_solution(2578124628191312340)
XLA Ops:
  2.3 15.2 %collective-permute-start.1 = (bf16[7,80,128]{2,1,0:T(8,128)(2,1)}, bf16[7,80,128]{2,1,0:T(8,128)(2,1)S(1)}, u32[]{:S(2)}, u32[]{:S(2)}) collective-permute-start(bf16[7,80,128]{2,1,0:T(8,128)(2,1)} %get-tuple-element.15), channel_id=1, source_target_pairs={{0,15},{1,0},{2,1},{3,2},{4,3},{5,4},{6,5},{7,6},{8,7},{9,8},{10,9... | collective-permute-start | bytes 430088 | tf_op jit(solution)/shard_map/ppermute | solution.py:18
  23.3 6.8 %collective-permute-done.1 = bf16[7,80,128]{2,1,0:T(8,128)(2,1)S(1)} collective-permute-done((bf16[7,80,128]{2,1,0:T(8,128)(2,1)}, bf16[7,80,128]{2,1,0:T(8,128)(2,1)S(1)}, u32[]{:S(2)}, u32[]{:S(2)}) %collective-permute-start.1) | collective-permute-done | bytes 143392 | tf_op jit(solution)/shard_map/ppermute | solution.py:18
  32.3 10.3 %collective-permute-start.2 = (bf16[2,80,128]{2,1,0:T(8,128)(2,1)S(1)}, bf16[2,80,128]{2,1,0:T(8,128)(2,1)S(1)}, u32[]{:S(2)}, u32[]{:S(2)}) collective-permute-start(bf16[2,80,128]{2,1,0:T(8,128)(2,1)S(1)} %bitcast.351), channel_id=1, source_target_pairs={{0,15},{1,0},{2,1},{3,2},{4,3},{5,4},{6,5},{7,6},{8,7},{9,8},{10,9... | collective-permute-start | bytes 122888 | tf_op jit(solution)/shard_map/ppermute | solution.py:18
  48.4 3.5 %all-to-all-start = ((bf16[8,4,80,128]{3,2,1,0:T(8,128)(2,1)}), bf16[8,4,80,128]{3,2,1,0:T(8,128)(2,1)S(1)}, u32[]{:S(2)}, u32[]{:S(2)}) async-start(bf16[8,4,80,128]{3,2,1,0:T(8,128)(2,1)} %bitcast.82), calls=%async_computation | async-start | bytes 1310720 | tf_op jit(solution)/shard_map/all_to_all | solution.py:26
  51.9 3.8 %collective-permute-start.4 = (bf16[452,128]{1,0:T(8,128)(2,1)}, bf16[452,128]{1,0:T(8,128)(2,1)}, u32[]{:S(2)}, u32[]{:S(2)}) collective-permute-start(bf16[452,128]{1,0:T(8,128)(2,1)} %pad_maximum_fusion.9), channel_id=1, source_target_pairs={{0,1},{1,0},{2,3},{3,2},{4,5},{5,4},{6,7},{7,6},{8,9},{9,8},{10,11... | collective-permute-start | bytes 347144 | tf_op jit(solution)/shard_map/ppermute | solution.py:22
  58.8 4.6 %all-to-all-done = bf16[8,4,80,128]{3,2,1,0:T(8,128)(2,1)S(1)} async-done(((bf16[8,4,80,128]{3,2,1,0:T(8,128)(2,1)}), bf16[8,4,80,128]{3,2,1,0:T(8,128)(2,1)S(1)}, u32[]{:S(2)}, u32[]{:S(2)}) %all-to-all-start) | async-done | bytes 655392 | tf_op jit(solution)/shard_map/all_to_all | solution.py:26
  64.2 4.1 %all-to-all-start.1 = ((bf16[8,2,80,128]{3,2,1,0:T(8,128)(2,1)}), bf16[8,2,80,128]{3,2,1,0:T(8,128)(2,1)}, u32[]{:S(2)}, u32[]{:S(2)}) async-start(bf16[8,2,80,128]{3,2,1,0:T(8,128)(2,1)} %bitcast.201), calls=%async_computation.1 | async-start | bytes 655360 | tf_op jit(solution)/shard_map/all_to_all | solution.py:26
  71.9 4.0 %all-to-all-done.1 = bf16[8,2,80,128]{3,2,1,0:T(8,128)(2,1)} async-done(((bf16[8,2,80,128]{3,2,1,0:T(8,128)(2,1)}), bf16[8,2,80,128]{3,2,1,0:T(8,128)(2,1)}, u32[]{:S(2)}, u32[]{:S(2)}) %all-to-all-start.1) | async-done | bytes 327712 | tf_op jit(solution)/shard_map/all_to_all | solution.py:26
  78.4 4.8 %all-to-all-start.2 = ((bf16[16,1,176,128]{3,2,1,0:T(8,128)(2,1)}), bf16[16,1,176,128]{3,2,1,0:T(8,128)(2,1)S(1)}, u32[]{:S(2)}, u32[]{:S(2)}) async-start(bf16[16,1,176,128]{3,2,1,0:T(8,128)(2,1)} %bitcast.326), calls=%async_computation.2 | async-start | bytes 1441792 | tf_op jit(solution)/shard_map/all_to_all | solution.py:26
  87.3 3.7 %collective-permute-start.5 = (bf16[452,128]{1,0:T(8,128)(2,1)S(1)}, bf16[452,128]{1,0:T(8,128)(2,1)S(1)}, u32[]{:S(2)}, u32[]{:S(2)}) collective-permute-start(bf16[452,128]{1,0:T(8,128)(2,1)S(1)} %broadcast_select_fusion), channel_id=1, source_target_pairs={{0,3},{1,2},{2,1},{3,0},{4,7},{5,6},{6,5},{7,4},{8,11},{9,10},{10,... | collective-permute-start | bytes 347144 | tf_op jit(solution)/shard_map/ppermute | solution.py:22
  105.0 8.7 %collective-permute-start.6 = (bf16[452,128]{1,0:T(8,128)(2,1)S(1)}, bf16[452,128]{1,0:T(8,128)(2,1)S(1)}, u32[]{:S(2)}, u32[]{:S(2)}) collective-permute-start(bf16[452,128]{1,0:T(8,128)(2,1)S(1)} %select_select_fusion), channel_id=1, source_target_pairs={{0,4},{4,0},{8,12},{12,8},{1,5},{5,1},{9,13},{13,9},{2,6},{6,2},{1... | collective-permute-start | bytes 347144 | tf_op jit(solution)/shard_map/ppermute | solution.py:22
  116.3 6.7 %collective-permute-done.6 = bf16[452,128]{1,0:T(8,128)(2,1)S(1)} collective-permute-done((bf16[452,128]{1,0:T(8,128)(2,1)S(1)}, bf16[452,128]{1,0:T(8,128)(2,1)S(1)}, u32[]{:S(2)}, u32[]{:S(2)}) %collective-permute-start.6) | collective-permute-done | bytes 115744 | tf_op jit(solution)/shard_map/ppermute | solution.py:22
  123.9 4.1 %all-to-all-start.3 = ((bf16[4,1,128,128]{3,2,1,0:T(8,128)(2,1)}), bf16[4,1,128,128]{3,2,1,0:T(8,128)(2,1)S(1)}, u32[]{:S(2)}, u32[]{:S(2)}) async-start(bf16[4,1,128,128]{3,2,1,0:T(8,128)(2,1)} %broadcast_in_dim.33), calls=%async_computation.3 | async-start | bytes 262144 | tf_op jit(solution)/shard_map/all_to_all | solution.py:26
  128.0 5.9 %all-to-all-done.3 = bf16[4,1,128,128]{3,2,1,0:T(8,128)(2,1)S(1)} async-done(((bf16[4,1,128,128]{3,2,1,0:T(8,128)(2,1)}), bf16[4,1,128,128]{3,2,1,0:T(8,128)(2,1)S(1)}, u32[]{:S(2)}, u32[]{:S(2)}) %all-to-all-start.3) | async-done | bytes 131104 | tf_op jit(solution)/shard_map/all_to_all | solution.py:26
  134.7 11.2 %all-to-all-start.4 = ((bf16[4,1,176,128]{3,2,1,0:T(8,128)(2,1)}), bf16[4,1,176,128]{3,2,1,0:T(8,128)(2,1)S(1)}, u32[]{:S(2)}, u32[]{:S(2)}) async-start(bf16[4,1,176,128]{3,2,1,0:T(8,128)(2,1)} %pad_maximum_fusion.2), calls=%async_computation.4 | async-start | bytes 360448 | tf_op jit(solution)/shard_map/all_to_all | solution.py:26
  146.0 13.6 %all-to-all-done.4 = bf16[4,1,176,128]{3,2,1,0:T(8,128)(2,1)S(1)} async-done(((bf16[4,1,176,128]{3,2,1,0:T(8,128)(2,1)}), bf16[4,1,176,128]{3,2,1,0:T(8,128)(2,1)S(1)}, u32[]{:S(2)}, u32[]{:S(2)}) %all-to-all-start.4) | async-done | bytes 180256 | tf_op jit(solution)/shard_map/all_to_all | solution.py:26
  160.4 3.4 %all-to-all-start.5 = ((bf16[4,1,176,128]{3,2,1,0:T(8,128)(2,1)}), bf16[4,1,176,128]{3,2,1,0:T(8,128)(2,1)S(1)}, u32[]{:S(2)}, u32[]{:S(2)}) async-start(bf16[4,1,176,128]{3,2,1,0:T(8,128)(2,1)} %broadcast_in_dim.34), calls=%async_computation.5 | async-start | bytes 360448 | tf_op jit(solution)/shard_map/all_to_all | solution.py:26
  163.8 6.0 %all-to-all-done.5 = bf16[4,1,176,128]{3,2,1,0:T(8,128)(2,1)S(1)} async-done(((bf16[4,1,176,128]{3,2,1,0:T(8,128)(2,1)}), bf16[4,1,176,128]{3,2,1,0:T(8,128)(2,1)S(1)}, u32[]{:S(2)}, u32[]{:S(2)}) %all-to-all-start.5) | async-done | bytes 180256 | tf_op jit(solution)/shard_map/all_to_all | solution.py:26
  170.8 4.8 %all-to-all-start.6 = ((bf16[4,4,1,176,128]{4,3,1,2,0:T(8,128)(2,1)}), bf16[4,4,1,176,128]{4,3,1,2,0:T(8,128)(2,1)S(1)}, u32[]{:S(2)}, u32[]{:S(2)}) async-start(bf16[4,4,1,176,128]{4,3,1,2,0:T(8,128)(2,1)} %broadcast_in_dim.36), calls=%async_computation.6 | async-start | bytes 1441792 | tf_op jit(solution)/shard_map/all_to_all | solution.py:26
  175.6 4.6 %collective-permute-start.7 = (bf16[452,128]{1,0:T(8,128)(2,1)S(1)}, bf16[452,128]{1,0:T(8,128)(2,1)S(1)}, u32[]{:S(2)}, u32[]{:S(2)}) collective-permute-start(bf16[452,128]{1,0:T(8,128)(2,1)S(1)} %broadcast_select_fusion.1), channel_id=1, source_target_pairs={{0,12},{4,8},{8,4},{12,0},{1,13},{5,9},{9,5},{13,1},{2,14},{6,10},... | collective-permute-start | bytes 347144 | tf_op jit(solution)/shard_map/ppermute | solution.py:22
  181.1 5.2 %collective-permute-done.7 = bf16[452,128]{1,0:T(8,128)(2,1)S(1)} collective-permute-done((bf16[452,128]{1,0:T(8,128)(2,1)S(1)}, bf16[452,128]{1,0:T(8,128)(2,1)S(1)}, u32[]{:S(2)}, u32[]{:S(2)}) %collective-permute-start.7) | collective-permute-done | bytes 115744 | tf_op jit(solution)/shard_map/ppermute | solution.py:22
  186.7 4.9 %all_to_all.45 = bf16[2,4,4,1,176,128]{5,4,2,1,3,0:T(8,128)(2,1)S(1)} all-to-all(bf16[2,4,4,1,176,128]{5,4,2,1,3,0:T(8,128)(2,1)S(1)} %broadcast_in_dim.38), channel_id=1, replica_groups=mesh['x'=4,'zl'=4,'core'=2,'zh'=4,'y'=4] {'core'}, dimensions={0} | all-to-all | bytes 2883584 | tf_op jit(solution)/shard_map/all_to_all | solution.py:26
  192.9 3.3 %all-to-all-start.8 = ((bf16[4,36,128]{2,1,0:T(8,128)(2,1)}), bf16[4,36,128]{2,1,0:T(8,128)(2,1)S(1)}, u32[]{:S(2)}, u32[]{:S(2)}) async-start(bf16[4,36,128]{2,1,0:T(8,128)(2,1)} %broadcast_in_dim.39), calls=%async_computation.8 | async-start | bytes 81920 | tf_op jit(solution)/shard_map/all_to_all | solution.py:26
  198.5 3.1 %all-to-all-done.8 = bf16[4,36,128]{2,1,0:T(8,128)(2,1)S(1)} async-done(((bf16[4,36,128]{2,1,0:T(8,128)(2,1)}), bf16[4,36,128]{2,1,0:T(8,128)(2,1)S(1)}, u32[]{:S(2)}, u32[]{:S(2)}) %all-to-all-start.8) | async-done | bytes 36896 | tf_op jit(solution)/shard_map/all_to_all | solution.py:26
  (286 shorter events, 40.2 us)
Async XLA Ops:
  0.6 21.5 %copy-start.5 = (bf16[1,36,1152]{2,1,0:T(8,128)(2,1)S(1)}, bf16[1,36,1152]{2,1,0:T(8,128)(2,1)}, u32[]{:S(2)}) copy-start(bf16[1,36,1152]{2,1,0:T(8,128)(2,1)} %param.20) | copy-start | bytes 248836
  0.6 21.7 %copy-start.6 = (f32[1,128,128]{2,1,0:T(8,128)S(1)}, f32[1,128,128]{2,1,0:T(8,128)}, u32[]{:S(2)}) copy-start(f32[1,128,128]{2,1,0:T(8,128)} %param.21) | copy-start | bytes 196612
  2.3 27.8 %collective-permute-start.1 = (bf16[7,80,128]{2,1,0:T(8,128)(2,1)}, bf16[7,80,128]{2,1,0:T(8,128)(2,1)S(1)}, u32[]{:S(2)}, u32[]{:S(2)}) collective-permute-start(bf16[7,80,128]{2,1,0:T(8,128)(2,1)} %get-tuple-element.15), channel_id=1, source_target_pairs={{0,15},{1,0},{2,1},{3,2},{4,3},{5,4},{6,5},{7,6},{8,7},{9,8},{10,9... | collective-permute-start | bytes 430088 | tf_op jit(solution)/shard_map/ppermute | solution.py:18
  17.5 5.7 %collective-permute-start = (bf16[5,80,128]{2,1,0:T(8,128)(2,1)}, bf16[5,80,128]{2,1,0:T(8,128)(2,1)S(1)}, u32[]{:S(2)}, u32[]{:S(2)}) collective-permute-start(bf16[5,80,128]{2,1,0:T(8,128)(2,1)} %get-tuple-element.14), channel_id=1, source_target_pairs={{0,1},{1,2},{2,3},{3,4},{4,5},{5,6},{6,7},{7,8},{8,9},{9,10},{10,1... | collective-permute-start | bytes 307208 | tf_op jit(solution)/shard_map/ppermute | solution.py:18
  31.7 12.5 %copy-start.7 = (bf16[3]{0:T(256)(128)(2,1)S(1)}, bf16[3]{0:T(256)(128)(2,1)}, u32[]{:S(2)}) copy-start(bf16[3]{0:T(256)(128)(2,1)} %constant.118.clone) | copy-start | bytes 22
  31.8 12.5 %copy-start.8 = (bf16[3]{0:T(256)(128)(2,1)S(1)}, bf16[3]{0:T(256)(128)(2,1)}, u32[]{:S(2)}) copy-start(bf16[3]{0:T(256)(128)(2,1)} %constant.119.clone) | copy-start | bytes 22
  32.3 11.9 %collective-permute-start.2 = (bf16[2,80,128]{2,1,0:T(8,128)(2,1)S(1)}, bf16[2,80,128]{2,1,0:T(8,128)(2,1)S(1)}, u32[]{:S(2)}, u32[]{:S(2)}) collective-permute-start(bf16[2,80,128]{2,1,0:T(8,128)(2,1)S(1)} %bitcast.351), channel_id=1, source_target_pairs={{0,15},{1,0},{2,1},{3,2},{4,3},{5,4},{6,5},{7,6},{8,7},{9,8},{10,9... | collective-permute-start | bytes 122888 | tf_op jit(solution)/shard_map/ppermute | solution.py:18
  45.5 12.7 %collective-permute-start.3 = (bf16[2,80,128]{2,1,0:T(8,128)(2,1)S(1)}, bf16[2,80,128]{2,1,0:T(8,128)(2,1)S(1)}, u32[]{:S(2)}, u32[]{:S(2)}) collective-permute-start(bf16[2,80,128]{2,1,0:T(8,128)(2,1)S(1)} %bitcast.354), channel_id=1, source_target_pairs={{0,1},{1,2},{2,3},{3,4},{4,5},{5,6},{6,7},{7,8},{8,9},{9,10},{10,1... | collective-permute-start | bytes 122888 | tf_op jit(solution)/shard_map/ppermute | solution.py:18
  48.4 15.0 %all-to-all-start = ((bf16[8,4,80,128]{3,2,1,0:T(8,128)(2,1)}), bf16[8,4,80,128]{3,2,1,0:T(8,128)(2,1)S(1)}, u32[]{:S(2)}, u32[]{:S(2)}) async-start(bf16[8,4,80,128]{3,2,1,0:T(8,128)(2,1)} %bitcast.82), calls=%async_computation | async-start | bytes 1310720 | tf_op jit(solution)/shard_map/all_to_all | solution.py:26
  51.9 26.5 %collective-permute-start.4 = (bf16[452,128]{1,0:T(8,128)(2,1)}, bf16[452,128]{1,0:T(8,128)(2,1)}, u32[]{:S(2)}, u32[]{:S(2)}) collective-permute-start(bf16[452,128]{1,0:T(8,128)(2,1)} %pad_maximum_fusion.9), channel_id=1, source_target_pairs={{0,1},{1,0},{2,3},{3,2},{4,5},{5,4},{6,7},{7,6},{8,9},{9,8},{10,11... | collective-permute-start | bytes 347144 | tf_op jit(solution)/shard_map/ppermute | solution.py:22
  64.2 11.7 %all-to-all-start.1 = ((bf16[8,2,80,128]{3,2,1,0:T(8,128)(2,1)}), bf16[8,2,80,128]{3,2,1,0:T(8,128)(2,1)}, u32[]{:S(2)}, u32[]{:S(2)}) async-start(bf16[8,2,80,128]{3,2,1,0:T(8,128)(2,1)} %bitcast.201), calls=%async_computation.1 | async-start | bytes 655360 | tf_op jit(solution)/shard_map/all_to_all | solution.py:26
  78.4 44.7 %all-to-all-start.2 = ((bf16[16,1,176,128]{3,2,1,0:T(8,128)(2,1)}), bf16[16,1,176,128]{3,2,1,0:T(8,128)(2,1)S(1)}, u32[]{:S(2)}, u32[]{:S(2)}) async-start(bf16[16,1,176,128]{3,2,1,0:T(8,128)(2,1)} %bitcast.326), calls=%async_computation.2 | async-start | bytes 1441792 | tf_op jit(solution)/shard_map/all_to_all | solution.py:26
  87.3 17.5 %collective-permute-start.5 = (bf16[452,128]{1,0:T(8,128)(2,1)S(1)}, bf16[452,128]{1,0:T(8,128)(2,1)S(1)}, u32[]{:S(2)}, u32[]{:S(2)}) collective-permute-start(bf16[452,128]{1,0:T(8,128)(2,1)S(1)} %broadcast_select_fusion), channel_id=1, source_target_pairs={{0,3},{1,2},{2,1},{3,0},{4,7},{5,6},{6,5},{7,4},{8,11},{9,10},{10,... | collective-permute-start | bytes 347144 | tf_op jit(solution)/shard_map/ppermute | solution.py:22
  105.0 18.1 %collective-permute-start.6 = (bf16[452,128]{1,0:T(8,128)(2,1)S(1)}, bf16[452,128]{1,0:T(8,128)(2,1)S(1)}, u32[]{:S(2)}, u32[]{:S(2)}) collective-permute-start(bf16[452,128]{1,0:T(8,128)(2,1)S(1)} %select_select_fusion), channel_id=1, source_target_pairs={{0,4},{4,0},{8,12},{12,8},{1,5},{5,1},{9,13},{13,9},{2,6},{6,2},{1... | collective-permute-start | bytes 347144 | tf_op jit(solution)/shard_map/ppermute | solution.py:22
  113.7 14.2 %collective-permute-start.8 = (bf16[1,80,128]{2,1,0:T(8,128)(2,1)S(1)}, bf16[1,80,128]{2,1,0:T(8,128)(2,1)S(1)}, u32[]{:S(2)}, u32[]{:S(2)}) collective-permute-start(bf16[1,80,128]{2,1,0:T(8,128)(2,1)S(1)} %get-tuple-element.256), channel_id=1, source_target_pairs={{0,1},{1,2},{2,3},{3,4},{4,5},{5,6},{6,7},{7,8},{8,9},{9,10},{10,1... | collective-permute-start | bytes 61448 | tf_op jit(solution)/shard_map/ppermute | solution.py:18
  115.0 12.9 %collective-permute-start.9 = (bf16[1,80,128]{2,1,0:T(8,128)(2,1)S(1)}, bf16[1,80,128]{2,1,0:T(8,128)(2,1)S(1)}, u32[]{:S(2)}, u32[]{:S(2)}) collective-permute-start(bf16[1,80,128]{2,1,0:T(8,128)(2,1)S(1)} %get-tuple-element.257), channel_id=1, source_target_pairs={{1,0},{2,1},{3,2},{4,3},{5,4},{6,5},{7,6},{8,7},{9,8},{10,9},{11,1... | collective-permute-start | bytes 61448 | tf_op jit(solution)/shard_map/ppermute | solution.py:18
  123.9 10.1 %all-to-all-start.3 = ((bf16[4,1,128,128]{3,2,1,0:T(8,128)(2,1)}), bf16[4,1,128,128]{3,2,1,0:T(8,128)(2,1)S(1)}, u32[]{:S(2)}, u32[]{:S(2)}) async-start(bf16[4,1,128,128]{3,2,1,0:T(8,128)(2,1)} %broadcast_in_dim.33), calls=%async_computation.3 | async-start | bytes 262144 | tf_op jit(solution)/shard_map/all_to_all | solution.py:26
  134.7 25.0 %all-to-all-start.4 = ((bf16[4,1,176,128]{3,2,1,0:T(8,128)(2,1)}), bf16[4,1,176,128]{3,2,1,0:T(8,128)(2,1)S(1)}, u32[]{:S(2)}, u32[]{:S(2)}) async-start(bf16[4,1,176,128]{3,2,1,0:T(8,128)(2,1)} %pad_maximum_fusion.2), calls=%async_computation.4 | async-start | bytes 360448 | tf_op jit(solution)/shard_map/all_to_all | solution.py:26
  160.4 9.4 %all-to-all-start.5 = ((bf16[4,1,176,128]{3,2,1,0:T(8,128)(2,1)}), bf16[4,1,176,128]{3,2,1,0:T(8,128)(2,1)S(1)}, u32[]{:S(2)}, u32[]{:S(2)}) async-start(bf16[4,1,176,128]{3,2,1,0:T(8,128)(2,1)} %broadcast_in_dim.34), calls=%async_computation.5 | async-start | bytes 360448 | tf_op jit(solution)/shard_map/all_to_all | solution.py:26
  170.8 15.7 %all-to-all-start.6 = ((bf16[4,4,1,176,128]{4,3,1,2,0:T(8,128)(2,1)}), bf16[4,4,1,176,128]{4,3,1,2,0:T(8,128)(2,1)S(1)}, u32[]{:S(2)}, u32[]{:S(2)}) async-start(bf16[4,4,1,176,128]{4,3,1,2,0:T(8,128)(2,1)} %broadcast_in_dim.36), calls=%async_computation.6 | async-start | bytes 1441792 | tf_op jit(solution)/shard_map/all_to_all | solution.py:26
  175.6 10.7 %collective-permute-start.7 = (bf16[452,128]{1,0:T(8,128)(2,1)S(1)}, bf16[452,128]{1,0:T(8,128)(2,1)S(1)}, u32[]{:S(2)}, u32[]{:S(2)}) collective-permute-start(bf16[452,128]{1,0:T(8,128)(2,1)S(1)} %broadcast_select_fusion.1), channel_id=1, source_target_pairs={{0,12},{4,8},{8,4},{12,0},{1,13},{5,9},{9,5},{13,1},{2,14},{6,10},... | collective-permute-start | bytes 347144 | tf_op jit(solution)/shard_map/ppermute | solution.py:22
  186.7 10.1 %copy-start.1 = (s32[81]{0:T(128)S(1)}, s32[81]{0:T(128)}, u32[]{:S(2)}) copy-start(s32[81]{0:T(128)} %constant.120.clone.index_ref) | copy-start | bytes 976
  186.7 10.0 %copy-start.2 = (s32[81]{0:T(128)S(1)}, s32[81]{0:T(128)}, u32[]{:S(2)}) copy-start(s32[81]{0:T(128)} %constant.121.clone.flip_ref) | copy-start | bytes 976
  192.9 8.7 %all-to-all-start.8 = ((bf16[4,36,128]{2,1,0:T(8,128)(2,1)}), bf16[4,36,128]{2,1,0:T(8,128)(2,1)S(1)}, u32[]{:S(2)}, u32[]{:S(2)}) async-start(bf16[4,36,128]{2,1,0:T(8,128)(2,1)} %broadcast_in_dim.39), calls=%async_computation.8 | async-start | bytes 81920 | tf_op jit(solution)/shard_map/all_to_all | solution.py:26
  (4 other events, 17.9 us)

commit v10 on v9

--- a/solution.py
+++ b/solution.py
@@ -296,37 +296,39 @@
     after = shifted(dpre2, -1, True)
     dy1 = back(2, cut_windows(jnp.concatenate([dpre2, after]), inner))
     dpre1 = times(dy1, slope(1, cut_windows(strips[1], inner))).reshape(image)
+    trimmed = [
+        jnp.concatenate([jnp.where(y_id == 0, rows[:1], rows[3:]), rows[1:3]]) for rows in strips
+    ]
     local = jnp.concatenate([a_inv.reshape(-1, chans), g_inv[0].astype(jnp.bfloat16)])
-    stacked, dpre1, local = lax.optimization_barrier((jnp.stack(strips), dpre1, local))
+    stacked, dpre1, local = lax.optimization_barrier((jnp.stack(trimmed), dpre1, local))
     before = shifted(dpre1, 1, True)
     layer_strips = to_layers(stacked)
+    from_y, from_z = table % Y, table // Y
     near = paired(local, "y", 0)
+    far = paired(jnp.where(from_y[3 - y_id] == y_id, local, near), "y", 1)
+    want = from_y[y_id]
+    found = jnp.where(want == y_id, local, jnp.where(want == (y_id ^ 1), near, far))
+    want = from_z[y_id]
     edge_top = jnp.where(owner_id > 0, before[:1], jnp.zeros_like(before[:1]))
     edge_end = jnp.where(inner, dpre1[1:], jnp.zeros_like(dpre1[1:]))
     dy0 = back(1, windows(jnp.concatenate([edge_top, before[1:], dpre1[:1], edge_end])))
     dpre0 = times(dy0, slope(0, windows(strips[0]))).reshape(image)
 
+    images = layer_strips.reshape((CORE, Y) + layer_strips.shape[1:])
     last_one = (y_id == 1) & (z_id == ZH - 1)
-    cols = jnp.concatenate(
-        [
-            to_columns(
-                windows(layer_strips[j])
-                if j % Y < Y - 1
-                else cut_windows(layer_strips[j], jnp.logical_not(last_one))
-            )
-            for j in range(CORE * Y)
-        ]
-    )
+    seam = jnp.zeros((Y * rows_dev, 3), bool).at[-2, 2].set(True).at[-1, 0].set(True)
+    cols = []
+    for image_rows in images:
+        middle = image_rows[:, 1:].reshape((-1,) + image_rows.shape[2:])
+        win = windows(jnp.concatenate([image_rows[0, :1], middle, image_rows[-1, :1]]))
+        cut = (seam & last_one)[:, :, None, None]
+        cols.append(to_columns(jnp.where(cut, jnp.zeros_like(win), win)))
+    cols = jnp.concatenate(cols)
     gram = gram_half(cols, core_id)
     layer_dpre = to_layers(jnp.stack([dpre0, dpre1, dpre2, dpre3[1:3]]))
     parts = all_half(gram, cols, layer_dpre.reshape(-1, chans), core_id)
 
-    parts, local, near = lax.optimization_barrier((parts, local, near))
-    from_y, from_z = table % Y, table // Y
-    far = paired(jnp.where(from_y[3 - y_id] == y_id, local, near), "y", 1)
-    want = from_y[y_id]
-    found = jnp.where(want == y_id, local, jnp.where(want == (y_id ^ 1), near, far))
-    want = from_z[y_id]
+    parts, found = lax.optimization_barrier((parts, found))
     found = jnp.where(want == (z_id ^ 1), paired(found, "zh", 0), found)
 
     piece = scatter_sum(parts, ("x", "zl"))

time: 205 us -> 208 us (1.015)
  starting transfers between devices: 91.2 us -> 97.1 us
    ppermute x4, waiting for transfers between devices: 11.9 us -> 18.5 us  [paired(): lax.ppermute(x, axis, [(i, i ^ 1 if step == 0 else 3 - i) for i in range(...]
    ppermute x6, waiting for transfers between devices: 10.3 us -> 5.69 us  [shifted(): return lax.ppermute(x, OWNER, pairs)]
    all_to_all x8, waiting for transfers between devices: 37.3 us -> 33.3 us  [exchange(): return lax.all_to_all(x, axis, split_axis=0, concat_axis=0, tiled=True)]
    all_to_all x8, starting transfers between devices: 39.1 us -> 42.4 us  [exchange(): return lax.all_to_all(x, axis, split_axis=0, concat_axis=0, tiled=True)]
    ppermute x6, starting transfers between devices: 31.2 us -> 34 us  [shifted(): return lax.ppermute(x, OWNER, pairs)]
    unnamed x157 -> x120, local copies, waits for them, and re-layouts: 4.46 us -> 5.27 us
  transfers between devices with their start and end apart: 18 -> 18, of which waited for: 11 -> 11; matrix products, arithmetic and copies ran while one was open for 9% -> 8% of each run, Pallas kernels for 2% -> 1%
where the time goes in v10:
time: 208 us; the launch traced here: 206 us
  starting transfers between devices  97.1 us (47%)
  waiting for transfers between devices  57.5 us (28%)
  local copies, waits for them, and re-layouts  16.7 us (8%)
  between operations  15.1 us (7%)
  other arithmetic  6.67 us (3%)
  Pallas kernels  5.11 us (2%)
  blocking collectives  4.89 us (2%)
  matrix products  3.33 us (2%)
    all_to_all x8, starting transfers between devices, exchange(): return lax.all_to_all(x, axis, split_axis=0, concat_axis=0, tiled=True)  42.4 us
    ppermute x6, starting transfers between devices, shifted(): return lax.ppermute(x, OWNER, pairs)  34 us
    all_to_all x8, waiting for transfers between devices, exchange(): return lax.all_to_all(x, axis, split_axis=0, concat_axis=0, tiled=True)  33.3 us
    ppermute x4, starting transfers between devices, paired(): lax.ppermute(x, axis, [(i, i ^ 1 if step == 0 else 3 - i) for i in range(...  20.6 us
    ppermute x4, waiting for transfers between devices, paired(): lax.ppermute(x, axis, [(i, i ^ 1 if step == 0 else 3 - i) for i in range(...  18.5 us
    ppermute x6, waiting for transfers between devices, shifted(): return lax.ppermute(x, OWNER, pairs)  5.69 us
    unnamed x120, local copies, waits for them, and re-layouts  5.27 us
    all_to_all x1, blocking collectives, exchange(): return lax.all_to_all(x, axis, split_axis=0, concat_axis=0, tiled=True)  4.89 us
  transfers between devices with their start and end apart: 18, of which 11 were waited for; matrix products, arithmetic and copies ran while one was open for 8% of the time, Pallas kernels for 1%

profile of v10, /device:TPU:6, one launch (start us, length us, event | category | flops | bytes accessed | tf_op | source)
XLA Modules:
  0.0 206.3 jit_solution(4164537049793042233)
XLA Ops:
  2.3 3.6 %collective-permute-start = (bf16[5,80,128]{2,1,0:T(8,128)(2,1)}, bf16[5,80,128]{2,1,0:T(8,128)(2,1)S(1)}, u32[]{:S(2)}, u32[]{:S(2)}) collective-permute-start(bf16[5,80,128]{2,1,0:T(8,128)(2,1)} %get-tuple-element.37), channel_id=1, source_target_pairs={{0,1},{1,2},{2,3},{3,4},{4,5},{5,6},{6,7},{7,8},{8,9},{9,10},{10,1... | collective-permute-start | bytes 307208 | tf_op jit(solution)/shard_map/ppermute | solution.py:18
  5.9 13.0 %collective-permute-start.1 = (bf16[7,80,128]{2,1,0:T(8,128)(2,1)}, bf16[7,80,128]{2,1,0:T(8,128)(2,1)S(1)}, u32[]{:S(2)}, u32[]{:S(2)}) collective-permute-start(bf16[7,80,128]{2,1,0:T(8,128)(2,1)} %get-tuple-element.38), channel_id=1, source_target_pairs={{0,15},{1,0},{2,1},{3,2},{4,3},{5,4},{6,5},{7,6},{8,7},{9,8},{10,9... | collective-permute-start | bytes 430088 | tf_op jit(solution)/shard_map/ppermute | solution.py:18
  26.9 3.8 %collective-permute-done.1 = bf16[7,80,128]{2,1,0:T(8,128)(2,1)S(1)} collective-permute-done((bf16[7,80,128]{2,1,0:T(8,128)(2,1)}, bf16[7,80,128]{2,1,0:T(8,128)(2,1)S(1)}, u32[]{:S(2)}, u32[]{:S(2)}) %collective-permute-start.1) | collective-permute-done | bytes 143392 | tf_op jit(solution)/shard_map/ppermute | solution.py:18
  34.5 11.4 %collective-permute-start.2 = (bf16[2,80,128]{2,1,0:T(8,128)(2,1)S(1)}, bf16[2,80,128]{2,1,0:T(8,128)(2,1)S(1)}, u32[]{:S(2)}, u32[]{:S(2)}) collective-permute-start(bf16[2,80,128]{2,1,0:T(8,128)(2,1)S(1)} %bitcast.385), channel_id=1, source_target_pairs={{0,15},{1,0},{2,1},{3,2},{4,3},{5,4},{6,5},{7,6},{8,7},{9,8},{10,9... | collective-permute-start | bytes 122888 | tf_op jit(solution)/shard_map/ppermute | solution.py:18
  53.7 7.1 %all-to-all-start = ((bf16[8,3,80,128]{3,2,1,0:T(8,128)(2,1)}), bf16[8,3,80,128]{3,2,1,0:T(8,128)(2,1)S(1)}, u32[]{:S(2)}, u32[]{:S(2)}) async-start(bf16[8,3,80,128]{3,2,1,0:T(8,128)(2,1)} %bitcast.83), calls=%async_computation | async-start | bytes 983040 | tf_op jit(solution)/shard_map/all_to_all | solution.py:26
  62.4 4.3 %collective-permute-start.5 = (bf16[452,128]{1,0:T(8,128)(2,1)S(1)}, bf16[452,128]{1,0:T(8,128)(2,1)S(1)}, u32[]{:S(2)}, u32[]{:S(2)}) collective-permute-start(bf16[452,128]{1,0:T(8,128)(2,1)S(1)} %broadcast_select_fusion.3), channel_id=1, source_target_pairs={{0,3},{1,2},{2,1},{3,0},{4,7},{5,6},{6,5},{7,4},{8,11},{9,10},{10,... | collective-permute-start | bytes 347144 | tf_op jit(solution)/shard_map/ppermute | solution.py:22
  66.7 6.4 %collective-permute-done.5 = bf16[452,128]{1,0:T(8,128)(2,1)S(1)} collective-permute-done((bf16[452,128]{1,0:T(8,128)(2,1)S(1)}, bf16[452,128]{1,0:T(8,128)(2,1)S(1)}, u32[]{:S(2)}, u32[]{:S(2)}) %collective-permute-start.5) | collective-permute-done | bytes 115744 | tf_op jit(solution)/shard_map/ppermute | solution.py:22
  74.6 4.1 %all-to-all-start.1 = ((bf16[8,2,80,128]{3,2,1,0:T(8,128)(2,1)}), bf16[8,2,80,128]{3,2,1,0:T(8,128)(2,1)}, u32[]{:S(2)}, u32[]{:S(2)}) async-start(bf16[8,2,80,128]{3,2,1,0:T(8,128)(2,1)} %bitcast.166), calls=%async_computation.1 | async-start | bytes 655360 | tf_op jit(solution)/shard_map/all_to_all | solution.py:26
  82.1 4.2 %all-to-all-done.1 = bf16[8,2,80,128]{3,2,1,0:T(8,128)(2,1)} async-done(((bf16[8,2,80,128]{3,2,1,0:T(8,128)(2,1)}), bf16[8,2,80,128]{3,2,1,0:T(8,128)(2,1)}, u32[]{:S(2)}, u32[]{:S(2)}) %all-to-all-start.1) | async-done | bytes 327712 | tf_op jit(solution)/shard_map/all_to_all | solution.py:26
  88.7 8.4 %all-to-all-start.2 = ((bf16[16,1,176,128]{3,2,1,0:T(8,128)(2,1)}), bf16[16,1,176,128]{3,2,1,0:T(8,128)(2,1)S(1)}, u32[]{:S(2)}, u32[]{:S(2)}) async-start(bf16[16,1,176,128]{3,2,1,0:T(8,128)(2,1)} %bitcast.340), calls=%async_computation.2 | async-start | bytes 1441792 | tf_op jit(solution)/shard_map/all_to_all | solution.py:26
  109.7 9.0 %collective-permute-start.6 = (bf16[452,128]{1,0:T(8,128)(2,1)S(1)}, bf16[452,128]{1,0:T(8,128)(2,1)S(1)}, u32[]{:S(2)}, u32[]{:S(2)}) collective-permute-start(bf16[452,128]{1,0:T(8,128)(2,1)S(1)} %copy-done.5), channel_id=1, source_target_pairs={{0,4},{4,0},{8,12},{12,8},{1,5},{5,1},{9,13},{13,9},{2,6},{6,2},{1... | collective-permute-start | bytes 347144 | tf_op jit(solution)/shard_map/ppermute | solution.py:22
  122.9 6.2 %collective-permute-done.6 = bf16[452,128]{1,0:T(8,128)(2,1)S(1)} collective-permute-done((bf16[452,128]{1,0:T(8,128)(2,1)S(1)}, bf16[452,128]{1,0:T(8,128)(2,1)S(1)}, u32[]{:S(2)}, u32[]{:S(2)}) %collective-permute-start.6) | collective-permute-done | bytes 115744 | tf_op jit(solution)/shard_map/ppermute | solution.py:22
  129.9 3.3 %all-to-all-start.3 = ((bf16[4,1,128,128]{3,2,1,0:T(8,128)(2,1)}), bf16[4,1,128,128]{3,2,1,0:T(8,128)(2,1)S(1)}, u32[]{:S(2)}, u32[]{:S(2)}) async-start(bf16[4,1,128,128]{3,2,1,0:T(8,128)(2,1)} %broadcast_in_dim.82), calls=%async_computation.3 | async-start | bytes 262144 | tf_op jit(solution)/shard_map/all_to_all | solution.py:26
  133.3 5.9 %all-to-all-done.3 = bf16[4,1,128,128]{3,2,1,0:T(8,128)(2,1)S(1)} async-done(((bf16[4,1,128,128]{3,2,1,0:T(8,128)(2,1)}), bf16[4,1,128,128]{3,2,1,0:T(8,128)(2,1)S(1)}, u32[]{:S(2)}, u32[]{:S(2)}) %all-to-all-start.3) | async-done | bytes 131104 | tf_op jit(solution)/shard_map/all_to_all | solution.py:26
  139.9 7.5 %all-to-all-start.4 = ((bf16[4,1,176,128]{3,2,1,0:T(8,128)(2,1)}), bf16[4,1,176,128]{3,2,1,0:T(8,128)(2,1)S(1)}, u32[]{:S(2)}, u32[]{:S(2)}) async-start(bf16[4,1,176,128]{3,2,1,0:T(8,128)(2,1)} %pad_maximum_fusion.3), calls=%async_computation.4 | async-start | bytes 360448 | tf_op jit(solution)/shard_map/all_to_all | solution.py:26
  147.6 14.1 %all-to-all-done.4 = bf16[4,1,176,128]{3,2,1,0:T(8,128)(2,1)S(1)} async-done(((bf16[4,1,176,128]{3,2,1,0:T(8,128)(2,1)}), bf16[4,1,176,128]{3,2,1,0:T(8,128)(2,1)S(1)}, u32[]{:S(2)}, u32[]{:S(2)}) %all-to-all-start.4) | async-done | bytes 180256 | tf_op jit(solution)/shard_map/all_to_all | solution.py:26
  162.5 3.9 %all-to-all-start.5 = ((bf16[4,1,176,128]{3,2,1,0:T(8,128)(2,1)}), bf16[4,1,176,128]{3,2,1,0:T(8,128)(2,1)S(1)}, u32[]{:S(2)}, u32[]{:S(2)}) async-start(bf16[4,1,176,128]{3,2,1,0:T(8,128)(2,1)} %broadcast_in_dim.83), calls=%async_computation.5 | async-start | bytes 360448 | tf_op jit(solution)/shard_map/all_to_all | solution.py:26
  166.4 6.0 %all-to-all-done.5 = bf16[4,1,176,128]{3,2,1,0:T(8,128)(2,1)S(1)} async-done(((bf16[4,1,176,128]{3,2,1,0:T(8,128)(2,1)}), bf16[4,1,176,128]{3,2,1,0:T(8,128)(2,1)S(1)}, u32[]{:S(2)}, u32[]{:S(2)}) %all-to-all-start.5) | async-done | bytes 180256 | tf_op jit(solution)/shard_map/all_to_all | solution.py:26
  173.4 4.8 %all-to-all-start.6 = ((bf16[4,4,1,176,128]{4,3,1,2,0:T(8,128)(2,1)}), bf16[4,4,1,176,128]{4,3,1,2,0:T(8,128)(2,1)S(1)}, u32[]{:S(2)}, u32[]{:S(2)}) async-start(bf16[4,4,1,176,128]{4,3,1,2,0:T(8,128)(2,1)} %broadcast_in_dim.85), calls=%async_computation.6 | async-start | bytes 1441792 | tf_op jit(solution)/shard_map/all_to_all | solution.py:26
  178.2 5.4 %collective-permute-start.7 = (bf16[452,128]{1,0:T(8,128)(2,1)S(1)}, bf16[452,128]{1,0:T(8,128)(2,1)S(1)}, u32[]{:S(2)}, u32[]{:S(2)}) collective-permute-start(bf16[452,128]{1,0:T(8,128)(2,1)S(1)} %broadcast_select_fusion.2), channel_id=1, source_target_pairs={{0,12},{4,8},{8,4},{12,0},{1,13},{5,9},{9,5},{13,1},{2,14},{6,10},... | collective-permute-start | bytes 347144 | tf_op jit(solution)/shard_map/ppermute | solution.py:22
  184.5 5.9 %collective-permute-done.7 = bf16[452,128]{1,0:T(8,128)(2,1)S(1)} collective-permute-done((bf16[452,128]{1,0:T(8,128)(2,1)S(1)}, bf16[452,128]{1,0:T(8,128)(2,1)S(1)}, u32[]{:S(2)}, u32[]{:S(2)}) %collective-permute-start.7) | collective-permute-done | bytes 115744 | tf_op jit(solution)/shard_map/ppermute | solution.py:22
  190.8 4.9 %all_to_all.45 = bf16[2,4,4,1,176,128]{5,4,2,1,3,0:T(8,128)(2,1)S(1)} all-to-all(bf16[2,4,4,1,176,128]{5,4,2,1,3,0:T(8,128)(2,1)S(1)} %broadcast_in_dim.87), channel_id=1, replica_groups=mesh['x'=4,'zl'=4,'core'=2,'zh'=4,'y'=4] {'core'}, dimensions={0} | all-to-all | bytes 2883584 | tf_op jit(solution)/shard_map/all_to_all | solution.py:26
  196.9 3.3 %all-to-all-start.8 = ((bf16[4,36,128]{2,1,0:T(8,128)(2,1)}), bf16[4,36,128]{2,1,0:T(8,128)(2,1)S(1)}, u32[]{:S(2)}, u32[]{:S(2)}) async-start(bf16[4,36,128]{2,1,0:T(8,128)(2,1)} %broadcast_in_dim.88), calls=%async_computation.8 | async-start | bytes 81920 | tf_op jit(solution)/shard_map/all_to_all | solution.py:26
  202.5 3.1 %all-to-all-done.8 = bf16[4,36,128]{2,1,0:T(8,128)(2,1)S(1)} async-done(((bf16[4,36,128]{2,1,0:T(8,128)(2,1)}), bf16[4,36,128]{2,1,0:T(8,128)(2,1)S(1)}, u32[]{:S(2)}, u32[]{:S(2)}) %all-to-all-start.8) | async-done | bytes 36896 | tf_op jit(solution)/shard_map/all_to_all | solution.py:26
  (244 shorter events, 41.7 us)
Async XLA Ops:
  0.6 22.0 %copy-start.10 = (s32[4]{0:T(128)S(1)}, s32[4]{0:T(128)}, u32[]{:S(2)}) copy-start(s32[4]{0:T(128)} %param.19) | copy-start | bytes 52
  0.6 22.7 %copy-start.11 = (pred[8,3]{0,1:T(4,128)(4,1)S(1)}, pred[8,3]{0,1:T(4,128)(4,1)}, u32[]{:S(2)}) copy-start(pred[8,3]{0,1:T(4,128)(4,1)} %constant.171.clone.1) | copy-start | bytes 76
  2.3 23.7 %copy-start.7 = (bf16[1,36,1152]{2,1,0:T(8,128)(2,1)S(1)}, bf16[1,36,1152]{2,1,0:T(8,128)(2,1)}, u32[]{:S(2)}) copy-start(bf16[1,36,1152]{2,1,0:T(8,128)(2,1)} %param.20) | copy-start | bytes 248836
  2.3 24.5 %collective-permute-start = (bf16[5,80,128]{2,1,0:T(8,128)(2,1)}, bf16[5,80,128]{2,1,0:T(8,128)(2,1)S(1)}, u32[]{:S(2)}, u32[]{:S(2)}) collective-permute-start(bf16[5,80,128]{2,1,0:T(8,128)(2,1)} %get-tuple-element.37), channel_id=1, source_target_pairs={{0,1},{1,2},{2,3},{3,4},{4,5},{5,6},{6,7},{7,8},{8,9},{9,10},{10,1... | collective-permute-start | bytes 307208 | tf_op jit(solution)/shard_map/ppermute | solution.py:18
  5.9 24.7 %collective-permute-start.1 = (bf16[7,80,128]{2,1,0:T(8,128)(2,1)}, bf16[7,80,128]{2,1,0:T(8,128)(2,1)S(1)}, u32[]{:S(2)}, u32[]{:S(2)}) collective-permute-start(bf16[7,80,128]{2,1,0:T(8,128)(2,1)} %get-tuple-element.38), channel_id=1, source_target_pairs={{0,15},{1,0},{2,1},{3,2},{4,3},{5,4},{6,5},{7,6},{8,7},{9,8},{10,9... | collective-permute-start | bytes 430088 | tf_op jit(solution)/shard_map/ppermute | solution.py:18
  34.0 13.7 %copy-start.8 = (bf16[3]{0:T(256)(128)(2,1)S(1)}, bf16[3]{0:T(256)(128)(2,1)}, u32[]{:S(2)}) copy-start(bf16[3]{0:T(256)(128)(2,1)} %constant.186.clone) | copy-start | bytes 22
  34.5 13.3 %collective-permute-start.2 = (bf16[2,80,128]{2,1,0:T(8,128)(2,1)S(1)}, bf16[2,80,128]{2,1,0:T(8,128)(2,1)S(1)}, u32[]{:S(2)}, u32[]{:S(2)}) collective-permute-start(bf16[2,80,128]{2,1,0:T(8,128)(2,1)S(1)} %bitcast.385), channel_id=1, source_target_pairs={{0,15},{1,0},{2,1},{3,2},{4,3},{5,4},{6,5},{7,6},{8,7},{9,8},{10,9... | collective-permute-start | bytes 122888 | tf_op jit(solution)/shard_map/ppermute | solution.py:18
  49.0 12.8 %collective-permute-start.3 = (bf16[2,80,128]{2,1,0:T(8,128)(2,1)S(1)}, bf16[2,80,128]{2,1,0:T(8,128)(2,1)S(1)}, u32[]{:S(2)}, u32[]{:S(2)}) collective-permute-start(bf16[2,80,128]{2,1,0:T(8,128)(2,1)S(1)} %bitcast.388), channel_id=1, source_target_pairs={{0,1},{1,2},{2,3},{3,4},{4,5},{5,6},{6,7},{7,8},{8,9},{9,10},{10,1... | collective-permute-start | bytes 122888 | tf_op jit(solution)/shard_map/ppermute | solution.py:18
  50.9 11.4 %collective-permute-start.4 = (bf16[452,128]{1,0:T(8,128)(2,1)S(1)}, bf16[452,128]{1,0:T(8,128)(2,1)S(1)}, u32[]{:S(2)}, u32[]{:S(2)}) collective-permute-start(bf16[452,128]{1,0:T(8,128)(2,1)S(1)} %pad_maximum_fusion.7), channel_id=1, source_target_pairs={{0,1},{1,0},{2,3},{3,2},{4,5},{5,4},{6,7},{7,6},{8,9},{9,8},{10,11... | collective-permute-start | bytes 347144 | tf_op jit(solution)/shard_map/ppermute | solution.py:22
  53.7 20.0 %all-to-all-start = ((bf16[8,3,80,128]{3,2,1,0:T(8,128)(2,1)}), bf16[8,3,80,128]{3,2,1,0:T(8,128)(2,1)S(1)}, u32[]{:S(2)}, u32[]{:S(2)}) async-start(bf16[8,3,80,128]{3,2,1,0:T(8,128)(2,1)} %bitcast.83), calls=%async_computation | async-start | bytes 983040 | tf_op jit(solution)/shard_map/all_to_all | solution.py:26
  62.4 10.7 %collective-permute-start.5 = (bf16[452,128]{1,0:T(8,128)(2,1)S(1)}, bf16[452,128]{1,0:T(8,128)(2,1)S(1)}, u32[]{:S(2)}, u32[]{:S(2)}) collective-permute-start(bf16[452,128]{1,0:T(8,128)(2,1)S(1)} %broadcast_select_fusion.3), channel_id=1, source_target_pairs={{0,3},{1,2},{2,1},{3,0},{4,7},{5,6},{6,5},{7,4},{8,11},{9,10},{10,... | collective-permute-start | bytes 347144 | tf_op jit(solution)/shard_map/ppermute | solution.py:22
  74.6 11.7 %all-to-all-start.1 = ((bf16[8,2,80,128]{3,2,1,0:T(8,128)(2,1)}), bf16[8,2,80,128]{3,2,1,0:T(8,128)(2,1)}, u32[]{:S(2)}, u32[]{:S(2)}) async-start(bf16[8,2,80,128]{3,2,1,0:T(8,128)(2,1)} %bitcast.166), calls=%async_computation.1 | async-start | bytes 655360 | tf_op jit(solution)/shard_map/all_to_all | solution.py:26
  88.7 16.9 %copy-start.4 = (bf16[1,9,128,128]{2,3,1,0:T(8,128)(2,1)S(1)}, bf16[1,9,128,128]{2,3,1,0:T(8,128)(2,1)}, u32[]{:S(2)}) copy-start(bf16[1,9,128,128]{2,3,1,0:T(8,128)(2,1)} %get-tuple-element.70) | copy-start | bytes 884740
  88.7 21.0 %copy-start.5 = (bf16[452,128]{1,0:T(8,128)(2,1)S(1)}, bf16[452,128]{1,0:T(8,128)(2,1)}, u32[]{:S(2)}) copy-start(bf16[452,128]{1,0:T(8,128)(2,1)} %select_select_fusion) | copy-start | bytes 347140
  88.7 40.4 %all-to-all-start.2 = ((bf16[16,1,176,128]{3,2,1,0:T(8,128)(2,1)}), bf16[16,1,176,128]{3,2,1,0:T(8,128)(2,1)S(1)}, u32[]{:S(2)}, u32[]{:S(2)}) async-start(bf16[16,1,176,128]{3,2,1,0:T(8,128)(2,1)} %bitcast.340), calls=%async_computation.2 | async-start | bytes 1441792 | tf_op jit(solution)/shard_map/all_to_all | solution.py:26
  109.7 19.4 %collective-permute-start.6 = (bf16[452,128]{1,0:T(8,128)(2,1)S(1)}, bf16[452,128]{1,0:T(8,128)(2,1)S(1)}, u32[]{:S(2)}, u32[]{:S(2)}) collective-permute-start(bf16[452,128]{1,0:T(8,128)(2,1)S(1)} %copy-done.5), channel_id=1, source_target_pairs={{0,4},{4,0},{8,12},{12,8},{1,5},{5,1},{9,13},{13,9},{2,6},{6,2},{1... | collective-permute-start | bytes 347144 | tf_op jit(solution)/shard_map/ppermute | solution.py:22
  118.7 14.5 %collective-permute-start.8 = (bf16[1,80,128]{2,1,0:T(8,128)(2,1)S(1)}, bf16[1,80,128]{2,1,0:T(8,128)(2,1)S(1)}, u32[]{:S(2)}, u32[]{:S(2)}) collective-permute-start(bf16[1,80,128]{2,1,0:T(8,128)(2,1)S(1)} %get-tuple-element.205), channel_id=1, source_target_pairs={{0,1},{1,2},{2,3},{3,4},{4,5},{5,6},{6,7},{7,8},{8,9},{9,10},{10,1... | collective-permute-start | bytes 61448 | tf_op jit(solution)/shard_map/ppermute | solution.py:18
  121.4 11.9 %collective-permute-start.9 = (bf16[1,80,128]{2,1,0:T(8,128)(2,1)S(1)}, bf16[1,80,128]{2,1,0:T(8,128)(2,1)S(1)}, u32[]{:S(2)}, u32[]{:S(2)}) collective-permute-start(bf16[1,80,128]{2,1,0:T(8,128)(2,1)S(1)} %get-tuple-element.206), channel_id=1, source_target_pairs={{1,0},{2,1},{3,2},{4,3},{5,4},{6,5},{7,6},{8,7},{9,8},{10,9},{11,1... | collective-permute-start | bytes 61448 | tf_op jit(solution)/shard_map/ppermute | solution.py:18
  129.9 9.3 %all-to-all-start.3 = ((bf16[4,1,128,128]{3,2,1,0:T(8,128)(2,1)}), bf16[4,1,128,128]{3,2,1,0:T(8,128)(2,1)S(1)}, u32[]{:S(2)}, u32[]{:S(2)}) async-start(bf16[4,1,128,128]{3,2,1,0:T(8,128)(2,1)} %broadcast_in_dim.82), calls=%async_computation.3 | async-start | bytes 262144 | tf_op jit(solution)/shard_map/all_to_all | solution.py:26
  139.9 21.8 %all-to-all-start.4 = ((bf16[4,1,176,128]{3,2,1,0:T(8,128)(2,1)}), bf16[4,1,176,128]{3,2,1,0:T(8,128)(2,1)S(1)}, u32[]{:S(2)}, u32[]{:S(2)}) async-start(bf16[4,1,176,128]{3,2,1,0:T(8,128)(2,1)} %pad_maximum_fusion.3), calls=%async_computation.4 | async-start | bytes 360448 | tf_op jit(solution)/shard_map/all_to_all | solution.py:26
  162.5 10.0 %all-to-all-start.5 = ((bf16[4,1,176,128]{3,2,1,0:T(8,128)(2,1)}), bf16[4,1,176,128]{3,2,1,0:T(8,128)(2,1)S(1)}, u32[]{:S(2)}, u32[]{:S(2)}) async-start(bf16[4,1,176,128]{3,2,1,0:T(8,128)(2,1)} %broadcast_in_dim.83), calls=%async_computation.5 | async-start | bytes 360448 | tf_op jit(solution)/shard_map/all_to_all | solution.py:26
  173.4 17.2 %all-to-all-start.6 = ((bf16[4,4,1,176,128]{4,3,1,2,0:T(8,128)(2,1)}), bf16[4,4,1,176,128]{4,3,1,2,0:T(8,128)(2,1)S(1)}, u32[]{:S(2)}, u32[]{:S(2)}) async-start(bf16[4,4,1,176,128]{4,3,1,2,0:T(8,128)(2,1)} %broadcast_in_dim.85), calls=%async_computation.6 | async-start | bytes 1441792 | tf_op jit(solution)/shard_map/all_to_all | solution.py:26
  178.2 12.2 %collective-permute-start.7 = (bf16[452,128]{1,0:T(8,128)(2,1)S(1)}, bf16[452,128]{1,0:T(8,128)(2,1)S(1)}, u32[]{:S(2)}, u32[]{:S(2)}) collective-permute-start(bf16[452,128]{1,0:T(8,128)(2,1)S(1)} %broadcast_select_fusion.2), channel_id=1, source_target_pairs={{0,12},{4,8},{8,4},{12,0},{1,13},{5,9},{9,5},{13,1},{2,14},{6,10},... | collective-permute-start | bytes 347144 | tf_op jit(solution)/shard_map/ppermute | solution.py:22
  196.9 8.7 %all-to-all-start.8 = ((bf16[4,36,128]{2,1,0:T(8,128)(2,1)}), bf16[4,36,128]{2,1,0:T(8,128)(2,1)S(1)}, u32[]{:S(2)}, u32[]{:S(2)}) async-start(bf16[4,36,128]{2,1,0:T(8,128)(2,1)} %broadcast_in_dim.88), calls=%async_computation.8 | async-start | bytes 81920 | tf_op jit(solution)/shard_map/all_to_all | solution.py:26
  (6 other events, 26.9 us)

commit v11 on v10

--- a/solution.py
+++ b/solution.py
@@ -209,13 +209,57 @@
     )(core.reshape(1), gram, cols, dpre)
 
 
-def factor_rows(blocks, first_row, scale, rows):
+def choose(which, table, place, *arrays):
+    def kernel(table_ref, place_ref, *refs):
+        number = which(table_ref, place_ref[0], place_ref[1])
+        for k, ref in enumerate(refs[:-1]):
+
+            @pl.when(number == k)
+            def _(ref=ref):
+                refs[-1][...] = ref[...]
+
+    return pl.pallas_call(
+        kernel,
+        out_shape=jax.ShapeDtypeStruct(arrays[0].shape, arrays[0].dtype),
+        in_specs=[SMEM, SMEM] + [VMEM] * len(arrays),
+        out_specs=VMEM,
+        cost_estimate=pl.CostEstimate(flops=0, bytes_accessed=500000, transcendentals=0),
+    )(table, place, *arrays)
+
+
+def layer_at(table_ref, owner):
+    lay = jnp.int32(0)
+    for l in range(1, table_ref.shape[0]):
+        lay = jnp.where(table_ref[l] == owner, l, lay)
+    return lay
+
+
+def for_groups(table, place, held, piece):
+    def kernel(table_ref, place_ref, held_ref, piece_ref, out_ref):
+        for z in range(ZH):
+            out_ref[z, :, :FAC_ROWS, :] = held_ref[layer_at(table_ref, z * Y + place_ref[0])]
+            out_ref[z, :, FAC_ROWS:, :] = piece_ref[:, FAC_ROWS:, :]
+
+    return pl.pallas_call(
+        kernel,
+        out_shape=jax.ShapeDtypeStruct((ZH,) + piece.shape, piece.dtype),
+        in_specs=[SMEM, SMEM, VMEM, VMEM],
+        out_specs=VMEM,
+        cost_estimate=pl.CostEstimate(flops=0, bytes_accessed=500000, transcendentals=0),
+    )(table, place, held, piece)
+
+
+def factor_rows(blocks, table, place, rows, count):
     chans = blocks.shape[-1]
     index = jnp.array([WHERE[a, b][0] for a in range(9) for b in range(9)], jnp.int32)
     flips = jnp.array([int(WHERE[a, b][1]) for a in range(9) for b in range(9)], jnp.int32)
 
-    def kernel(index_ref, flip_ref, row_ref, scale_ref, blocks_ref, out_ref, band):
-        start = row_ref[0]
+    def kernel(index_ref, flip_ref, table_ref, place_ref, blocks_ref, out_ref, own_ref, band):
+        owner = place_ref[1] * Y + place_ref[0]
+        scale = jnp.float32(0.0)
+        for l in range(table_ref.shape[0]):
+            scale = jnp.where(table_ref[l] == owner, jnp.float32(1.0 / count), scale)
+        start = place_ref[2] * rows
         tap = lax.div(start, chans)
         for t in range(2):
             a = jnp.minimum(tap + t, 8)
@@ -229,17 +273,21 @@
         base = pl.multiple_of(lax.div(inside, 8) * 8, 8)
         got = band[pl.ds(base, rows + 4), :]
         odd = inside != base
-        out_ref[...] = jnp.where(odd, got[4:], got[:rows]) * scale_ref[0]
-
-    return pl.pallas_call(
-        kernel,
-        out_shape=jax.ShapeDtypeStruct((rows, 9 * chans), jnp.float32),
+        out_ref[...] = jnp.where(odd, got[4:], got[:rows]) * scale
+        own_ref[...] = blocks_ref[NG, :chans, :].astype(jnp.float32) * scale
+
+    return pl.pallas_call(
+        kernel,
+        out_shape=(
+            jax.ShapeDtypeStruct((rows, 9 * chans), jnp.float32),
+            jax.ShapeDtypeStruct((chans, chans), jnp.float32),
+        ),
         in_specs=[SMEM, SMEM, SMEM, SMEM, VMEM],
-        out_specs=VMEM,
+        out_specs=(VMEM, VMEM),
         scratch_shapes=[pltpu.VMEM((2 * chans, 9 * chans), jnp.float32)],
         compiler_params=pltpu.CompilerParams(vmem_limit_bytes=16 * 2**20),
         cost_estimate=pl.CostEstimate(flops=10**6, bytes_accessed=2 * 10**6, transcendentals=0),
-    )(index, flips, first_row.reshape(1), scale.reshape(1), blocks)
+    )(index, flips, table, place, blocks)
 
 
 def shards(feats, top_grad, weights, table, a_inv, g_inv):
@@ -303,12 +351,7 @@
     stacked, dpre1, local = lax.optimization_barrier((jnp.stack(trimmed), dpre1, local))
     before = shifted(dpre1, 1, True)
     layer_strips = to_layers(stacked)
-    from_y, from_z = table % Y, table // Y
     near = paired(local, "y", 0)
-    far = paired(jnp.where(from_y[3 - y_id] == y_id, local, near), "y", 1)
-    want = from_y[y_id]
-    found = jnp.where(want == y_id, local, jnp.where(want == (y_id ^ 1), near, far))
-    want = from_z[y_id]
     edge_top = jnp.where(owner_id > 0, before[:1], jnp.zeros_like(before[:1]))
     edge_end = jnp.where(inner, dpre1[1:], jnp.zeros_like(dpre1[1:]))
     dy0 = back(1, windows(jnp.concatenate([edge_top, before[1:], dpre1[:1], edge_end])))
@@ -325,24 +368,34 @@
         cols.append(to_columns(jnp.where(cut, jnp.zeros_like(win), win)))
     cols = jnp.concatenate(cols)
     gram = gram_half(cols, core_id)
+
+    def for_partner(table_ref, y, z):
+        return jnp.where((table_ref[3 - y] & 3) == y, 0, 1)
+
+    def in_group(table_ref, y, z):
+        want = table_ref[y] & 3
+        return jnp.where(want == y, 0, jnp.where(want == (y ^ 1), 1, 2))
+
+    def beside(table_ref, y, z):
+        return jnp.where((table_ref[y] >> 2) == (z ^ 1), 1, 0)
+
+    def across(table_ref, y, z):
+        return jnp.where((table_ref[y] >> 3) == (z >> 1), 0, 1)
+
+    place = jnp.stack([y_id, z_id, dp_id]).astype(jnp.int32)
+    away = choose(for_partner, table, place, local, near)
+    gram, away = lax.optimization_barrier((gram, away))
+    found = choose(in_group, table, place, local, near, paired(away, "y", 1))
     layer_dpre = to_layers(jnp.stack([dpre0, dpre1, dpre2, dpre3[1:3]]))
     parts = all_half(gram, cols, layer_dpre.reshape(-1, chans), core_id)
 
     parts, found = lax.optimization_barrier((parts, found))
-    found = jnp.where(want == (z_id ^ 1), paired(found, "zh", 0), found)
-
+    found = choose(beside, table, place, found, paired(found, "zh", 0))
     piece = scatter_sum(parts, ("x", "zl"))
     piece, found = lax.optimization_barrier((piece, found))
-    inverses = jnp.where(want // 2 == z_id // 2, found, paired(found, "zh", 1))
+    inverses = choose(across, table, place, found, paired(found, "zh", 1))
     held = spread(piece[:, :FAC_ROWS], "y")
-    layer_ids = jnp.arange(num_layers, dtype=jnp.int32)
-
-    def pick(z):
-        lay = jnp.sum(jnp.where(table == z * Y + y_id, layer_ids, 0))
-        fac = lax.dynamic_index_in_dim(held, lay, 0, keepdims=False)
-        return jnp.concatenate([fac, piece[:, FAC_ROWS:]], axis=1)
-
-    total = exchange(jnp.stack([pick(z) for z in range(ZH)]), "zh")
+    total = exchange(for_groups(table, place, held, piece), "zh")
     total = jnp.sum(total.astype(jnp.float32), axis=0).astype(jnp.bfloat16)
     summed = spread(spread(spread(total, "zl"), "x"), "core")
 
@@ -358,10 +411,8 @@
     panel = jnp.dot(a_mine.astype(jnp.float32), mixed, precision=lax.Precision.HIGHEST)
     step_out = spread(panel.astype(jnp.bfloat16), "y")
 
-    have = jnp.any(table == owner_id).astype(jnp.float32)
-    scale = have / npos
-    a_out = factor_rows(stats, dp_id * rows_out, scale, rows_out)[None]
-    g_out = (stats[NG, :FAC_ROWS].astype(jnp.float32) * scale)[None]
+    a_out, g_out = factor_rows(stats, table, place, rows_out, npos)
+    a_out, g_out = a_out[None], g_out[None]
     return (step_out, a_out, g_out, in_grad)
 
 

time: 208 us -> 210 us (level)
  between operations: 15.1 us -> 2.08 us
  blocking collectives: 4.89 us -> 14.6 us
  Pallas kernels: 5.11 us -> 14 us
  waiting for transfers between devices: 57.5 us -> 51 us
  other arithmetic: 6.67 us -> 2.87 us
  starting transfers between devices: 97.1 us -> 100 us
    all_to_all x8 -> x7, waiting for transfers between devices: 33.3 us -> 21.1 us  [exchange(): return lax.all_to_all(x, axis, split_axis=0, concat_axis=0, tiled=True)]
    all_to_all x1 -> x2, blocking collectives: 4.89 us -> 14.6 us  [exchange(): return lax.all_to_all(x, axis, split_axis=0, concat_axis=0, tiled=True)]
    pallas_call x1 -> x6, Pallas kernels: 0.84 us -> 9.66 us  [the longest x4 6.61 us: choose(): pl.pallas_call(kernel, out_shape=jax.ShapeDtypeStruct(arrays[0].shape, ar...]
    ppermute x6, waiting for transfers between devices: 5.69 us -> 14.1 us  [shifted(): return lax.ppermute(x, OWNER, pairs)]
    ppermute x4, starting transfers between devices: 20.6 us -> 25.5 us  [paired(): lax.ppermute(x, axis, [(i, i ^ 1 if step == 0 else 3 - i) for i in range(...]
    ppermute x4, waiting for transfers between devices: 18.5 us -> 15.8 us  [paired(): lax.ppermute(x, axis, [(i, i ^ 1 if step == 0 else 3 - i) for i in range(...]
    unnamed x120 -> x138, local copies, waits for them, and re-layouts: 5.27 us -> 6.55 us
    all_to_all x8 -> x7, starting transfers between devices: 42.4 us -> 42.3 us  [exchange(): return lax.all_to_all(x, axis, split_axis=0, concat_axis=0, tiled=True)]
  transfers between devices with their start and end apart: 18 -> 17, of which waited for: 11 -> 12; matrix products, arithmetic and copies ran while one was open for 8% -> 6% of each run, Pallas kernels for 1% -> 4%
where the time goes in v11:
time: 210 us; the launch traced here: 206 us
  starting transfers between devices  100 us (48%)
  waiting for transfers between devices  51 us (24%)
  local copies, waits for them, and re-layouts  17.3 us (8%)
  blocking collectives  14.6 us (7%)
  Pallas kernels  14 us (7%)
  matrix products  4.08 us (2%)
  other arithmetic  2.87 us (1%)
    all_to_all x7, starting transfers between devices, exchange(): return lax.all_to_all(x, axis, split_axis=0, concat_axis=0, tiled=True)  42.3 us
    ppermute x6, starting transfers between devices, shifted(): return lax.ppermute(x, OWNER, pairs)  32.7 us
    ppermute x4, starting transfers between devices, paired(): lax.ppermute(x, axis, [(i, i ^ 1 if step == 0 else 3 - i) for i in range(...  25.5 us
    all_to_all x7, waiting for transfers between devices, exchange(): return lax.all_to_all(x, axis, split_axis=0, concat_axis=0, tiled=True)  21.1 us
    ppermute x4, waiting for transfers between devices, paired(): lax.ppermute(x, axis, [(i, i ^ 1 if step == 0 else 3 - i) for i in range(...  15.8 us
    all_to_all x2, blocking collectives, exchange(): return lax.all_to_all(x, axis, split_axis=0, concat_axis=0, tiled=True)  14.6 us
    ppermute x6, waiting for transfers between devices, shifted(): return lax.ppermute(x, OWNER, pairs)  14.1 us
    pallas_call x4, Pallas kernels, choose(): pl.pallas_call(kernel, out_shape=jax.ShapeDtypeStruct(arrays[0].shape, ar...  6.61 us
  transfers between devices with their start and end apart: 17, of which 12 were waited for; matrix products, arithmetic and copies ran while one was open for 6% of the time, Pallas kernels for 4%

profile of v11, /device:TPU:6, one launch (start us, length us, event | category | flops | bytes accessed | tf_op | source)
XLA Modules:
  0.0 206.3 jit_solution(15294233746877115824)
XLA Ops:
  2.3 15.3 %collective-permute-start.1 = (bf16[7,80,128]{2,1,0:T(8,128)(2,1)}, bf16[7,80,128]{2,1,0:T(8,128)(2,1)S(1)}, u32[]{:S(2)}, u32[]{:S(2)}) collective-permute-start(bf16[7,80,128]{2,1,0:T(8,128)(2,1)} %get-tuple-element.42), channel_id=1, source_target_pairs={{0,15},{1,0},{2,1},{3,2},{4,3},{5,4},{6,5},{7,6},{8,7},{9,8},{10,9... | collective-permute-start | bytes 430088 | tf_op jit(solution)/shard_map/ppermute | solution.py:18
  23.4 6.8 %collective-permute-done.1 = bf16[7,80,128]{2,1,0:T(8,128)(2,1)S(1)} collective-permute-done((bf16[7,80,128]{2,1,0:T(8,128)(2,1)}, bf16[7,80,128]{2,1,0:T(8,128)(2,1)S(1)}, u32[]{:S(2)}, u32[]{:S(2)}) %collective-permute-start.1) | collective-permute-done | bytes 143392 | tf_op jit(solution)/shard_map/ppermute | solution.py:18
  33.6 10.3 %collective-permute-start.2 = (bf16[2,80,128]{2,1,0:T(8,128)(2,1)S(1)}, bf16[2,80,128]{2,1,0:T(8,128)(2,1)S(1)}, u32[]{:S(2)}, u32[]{:S(2)}) collective-permute-start(bf16[2,80,128]{2,1,0:T(8,128)(2,1)S(1)} %bitcast.367), channel_id=1, source_target_pairs={{0,15},{1,0},{2,1},{3,2},{4,3},{5,4},{6,5},{7,6},{8,7},{9,8},{10,9... | collective-permute-start | bytes 122888 | tf_op jit(solution)/shard_map/ppermute | solution.py:18
  49.6 3.5 %all-to-all-start = ((bf16[8,3,80,128]{3,2,1,0:T(8,128)(2,1)}), bf16[8,3,80,128]{3,2,1,0:T(8,128)(2,1)S(1)}, u32[]{:S(2)}, u32[]{:S(2)}) async-start(bf16[8,3,80,128]{3,2,1,0:T(8,128)(2,1)} %bitcast.85), calls=%async_computation | async-start | bytes 983040 | tf_op jit(solution)/shard_map/all_to_all | solution.py:26
  53.1 3.8 %collective-permute-start.3 = (bf16[452,128]{1,0:T(8,128)(2,1)S(1)}, bf16[452,128]{1,0:T(8,128)(2,1)S(1)}, u32[]{:S(2)}, u32[]{:S(2)}) collective-permute-start(bf16[452,128]{1,0:T(8,128)(2,1)S(1)} %pad_maximum_fusion.6.refs_0_), channel_id=1, source_target_pairs={{0,1},{1,0},{2,3},{3,2},{4,5},{5,4},{6,7},{7,6},{8,9},{9,8},{10,11... | collective-permute-start | bytes 347144 | tf_op jit(solution)/shard_map/ppermute | solution.py:22
  56.9 2.6 %collective-permute-done.4 = bf16[2,80,128]{2,1,0:T(8,128)(2,1)S(1)} collective-permute-done((bf16[2,80,128]{2,1,0:T(8,128)(2,1)S(1)}, bf16[2,80,128]{2,1,0:T(8,128)(2,1)S(1)}, u32[]{:S(2)}, u32[]{:S(2)}) %collective-permute-start.4) | collective-permute-done | bytes 40992 | tf_op jit(solution)/shard_map/ppermute | solution.py:18
  60.1 3.9 %collective-permute-done.3.refs_1_ = bf16[452,128]{1,0:T(8,128)(2,1)S(1)} collective-permute-done((bf16[452,128]{1,0:T(8,128)(2,1)S(1)}, bf16[452,128]{1,0:T(8,128)(2,1)S(1)}, u32[]{:S(2)}, u32[]{:S(2)}) %collective-permute-start.3) | collective-permute-done | bytes 115744 | tf_op jit(solution)/shard_map/ppermute | solution.py:22
  67.0 4.1 %all-to-all-start.1 = ((bf16[8,2,80,128]{3,2,1,0:T(8,128)(2,1)}), bf16[8,2,80,128]{3,2,1,0:T(8,128)(2,1)}, u32[]{:S(2)}, u32[]{:S(2)}) async-start(bf16[8,2,80,128]{3,2,1,0:T(8,128)(2,1)} %bitcast.168), calls=%async_computation.1 | async-start | bytes 655360 | tf_op jit(solution)/shard_map/all_to_all | solution.py:26
  74.6 5.0 %collective-permute-start.5 = (bf16[452,128]{1,0:T(8,128)(2,1)}, bf16[452,128]{1,0:T(8,128)(2,1)}, u32[]{:S(2)}, u32[]{:S(2)}) collective-permute-start(bf16[452,128]{1,0:T(8,128)(2,1)} %shard_map.149), channel_id=1, source_target_pairs={{0,3},{1,2},{2,1},{3,0},{4,7},{5,6},{6,5},{7,4},{8,11},{9,10},{10,... | collective-permute-start | bytes 347144 | tf_op jit(solution)/shard_map/ppermute | solution.py:22
  85.2 4.8 %all-to-all-start.2 = ((bf16[16,1,176,128]{3,2,1,0:T(8,128)(2,1)}), bf16[16,1,176,128]{3,2,1,0:T(8,128)(2,1)S(1)}, u32[]{:S(2)}, u32[]{:S(2)}) async-start(bf16[16,1,176,128]{3,2,1,0:T(8,128)(2,1)} %bitcast.322), calls=%async_computation.2 | async-start | bytes 1441792 | tf_op jit(solution)/shard_map/all_to_all | solution.py:26
  90.0 9.4 %collective-permute-start.6 = (bf16[452,128]{1,0:T(8,128)(2,1)}, bf16[452,128]{1,0:T(8,128)(2,1)S(1)}, u32[]{:S(2)}, u32[]{:S(2)}) collective-permute-start(bf16[452,128]{1,0:T(8,128)(2,1)} %shard_map.151.refs_0_), channel_id=1, source_target_pairs={{0,4},{4,0},{8,12},{12,8},{1,5},{5,1},{9,13},{13,9},{2,6},{6,2},{1... | collective-permute-start | bytes 347144 | tf_op jit(solution)/shard_map/ppermute | solution.py:22
  99.4 4.5 %collective-permute-done.6.refs_1_ = bf16[452,128]{1,0:T(8,128)(2,1)S(1)} collective-permute-done((bf16[452,128]{1,0:T(8,128)(2,1)}, bf16[452,128]{1,0:T(8,128)(2,1)S(1)}, u32[]{:S(2)}, u32[]{:S(2)}) %collective-permute-start.6) | collective-permute-done | bytes 115744 | tf_op jit(solution)/shard_map/ppermute | solution.py:22
  106.2 7.1 %all-to-all-done.2 = bf16[16,1,176,128]{3,2,1,0:T(8,128)(2,1)S(1)} async-done(((bf16[16,1,176,128]{3,2,1,0:T(8,128)(2,1)}), bf16[16,1,176,128]{3,2,1,0:T(8,128)(2,1)S(1)}, u32[]{:S(2)}, u32[]{:S(2)}) %all-to-all-start.2) | async-done | bytes 720928 | tf_op jit(solution)/shard_map/all_to_all | solution.py:26
  113.4 9.7 %all_to_all.45.held_ref = bf16[4,1,128,128]{3,2,1,0:T(8,128)(2,1)} all-to-all(bf16[4,1,128,128]{3,2,1,0:T(8,128)(2,1)S(1)} %broadcast_in_dim.42), channel_id=1, replica_groups=mesh['x'=4,'zl'=4,'core'=2,'zh'=4,'y'=4] {'y'}, dimensions={0} | all-to-all | bytes 262144 | tf_op jit(solution)/shard_map/all_to_all | solution.py:26
  124.7 12.9 %all-to-all-start.4 = ((bf16[4,1,176,128]{3,2,1,0:T(8,128)(2,1)}), bf16[4,1,176,128]{3,2,1,0:T(8,128)(2,1)S(1)}, u32[]{:S(2)}, u32[]{:S(2)}) async-start(bf16[4,1,176,128]{3,2,1,0:T(8,128)(2,1)} %shard_map.154), calls=%async_computation.4 | async-start | bytes 360448 | tf_op jit(solution)/shard_map/all_to_all | solution.py:26
  141.8 4.0 %collective-permute-done.9 = bf16[1,80,128]{2,1,0:T(8,128)(2,1)S(1)} collective-permute-done((bf16[1,80,128]{2,1,0:T(8,128)(2,1)S(1)}, bf16[1,80,128]{2,1,0:T(8,128)(2,1)S(1)}, u32[]{:S(2)}, u32[]{:S(2)}) %collective-permute-start.9) | collective-permute-done | bytes 20512 | tf_op jit(solution)/shard_map/ppermute | solution.py:18
  145.8 5.7 %all-to-all-done.4 = bf16[4,1,176,128]{3,2,1,0:T(8,128)(2,1)S(1)} async-done(((bf16[4,1,176,128]{3,2,1,0:T(8,128)(2,1)}), bf16[4,1,176,128]{3,2,1,0:T(8,128)(2,1)S(1)}, u32[]{:S(2)}, u32[]{:S(2)}) %all-to-all-start.4) | async-done | bytes 180256 | tf_op jit(solution)/shard_map/all_to_all | solution.py:26
  152.2 5.3 %all-to-all-start.5 = ((bf16[4,1,176,128]{3,2,1,0:T(8,128)(2,1)}), bf16[4,1,176,128]{3,2,1,0:T(8,128)(2,1)S(1)}, u32[]{:S(2)}, u32[]{:S(2)}) async-start(bf16[4,1,176,128]{3,2,1,0:T(8,128)(2,1)} %broadcast_in_dim.80), calls=%async_computation.5 | async-start | bytes 360448 | tf_op jit(solution)/shard_map/all_to_all | solution.py:26
  157.7 6.0 %all-to-all-done.5 = bf16[4,1,176,128]{3,2,1,0:T(8,128)(2,1)S(1)} async-done(((bf16[4,1,176,128]{3,2,1,0:T(8,128)(2,1)}), bf16[4,1,176,128]{3,2,1,0:T(8,128)(2,1)S(1)}, u32[]{:S(2)}, u32[]{:S(2)}) %all-to-all-start.5) | async-done | bytes 180256 | tf_op jit(solution)/shard_map/all_to_all | solution.py:26
  164.6 4.8 %all-to-all-start.6 = ((bf16[4,4,1,176,128]{4,3,1,2,0:T(8,128)(2,1)}), bf16[4,4,1,176,128]{4,3,1,2,0:T(8,128)(2,1)S(1)}, u32[]{:S(2)}, u32[]{:S(2)}) async-start(bf16[4,4,1,176,128]{4,3,1,2,0:T(8,128)(2,1)} %broadcast_in_dim.82), calls=%async_computation.6 | async-start | bytes 1441792 | tf_op jit(solution)/shard_map/all_to_all | solution.py:26
  169.5 7.3 %collective-permute-start.7 = (bf16[452,128]{1,0:T(8,128)(2,1)S(1)}, bf16[452,128]{1,0:T(8,128)(2,1)S(1)}, u32[]{:S(2)}, u32[]{:S(2)}) collective-permute-start(bf16[452,128]{1,0:T(8,128)(2,1)S(1)} %copy-done.10), channel_id=1, source_target_pairs={{0,12},{4,8},{8,4},{12,0},{1,13},{5,9},{9,5},{13,1},{2,14},{6,10},... | collective-permute-start | bytes 347144 | tf_op jit(solution)/shard_map/ppermute | solution.py:22
  176.8 6.1 %collective-permute-done.7.refs_1_ = bf16[452,128]{1,0:T(8,128)(2,1)S(1)} collective-permute-done((bf16[452,128]{1,0:T(8,128)(2,1)S(1)}, bf16[452,128]{1,0:T(8,128)(2,1)S(1)}, u32[]{:S(2)}, u32[]{:S(2)}) %collective-permute-start.7) | collective-permute-done | bytes 115744 | tf_op jit(solution)/shard_map/ppermute | solution.py:22
  186.4 4.9 %all_to_all.46 = bf16[2,4,4,1,176,128]{5,4,2,1,3,0:T(8,128)(2,1)S(1)} all-to-all(bf16[2,4,4,1,176,128]{5,4,2,1,3,0:T(8,128)(2,1)S(1)} %broadcast_in_dim.84), channel_id=1, replica_groups=mesh['x'=4,'zl'=4,'core'=2,'zh'=4,'y'=4] {'core'}, dimensions={0} | all-to-all | bytes 2883584 | tf_op jit(solution)/shard_map/all_to_all | solution.py:26
  193.3 6.9 %all-to-all-start.8 = ((bf16[4,36,128]{2,1,0:T(8,128)(2,1)}), bf16[4,36,128]{2,1,0:T(8,128)(2,1)S(1)}, u32[]{:S(2)}, u32[]{:S(2)}) async-start(bf16[4,36,128]{2,1,0:T(8,128)(2,1)} %broadcast_in_dim.85), calls=%async_computation.8 | async-start | bytes 81920 | tf_op jit(solution)/shard_map/all_to_all | solution.py:26
  (256 shorter events, 49.9 us)
Async XLA Ops:
  0.6 21.3 %copy-start.16 = (bf16[1,36,1152]{2,1,0:T(8,128)(2,1)S(1)}, bf16[1,36,1152]{2,1,0:T(8,128)(2,1)}, u32[]{:S(2)}) copy-start(bf16[1,36,1152]{2,1,0:T(8,128)(2,1)} %param.20) | copy-start | bytes 248836
  2.3 19.7 %copy-start.17 = (f32[1,128,128]{2,1,0:T(8,128)S(1)}, f32[1,128,128]{2,1,0:T(8,128)}, u32[]{:S(2)}) copy-start(f32[1,128,128]{2,1,0:T(8,128)} %param.21) | copy-start | bytes 196612
  2.3 27.9 %collective-permute-start.1 = (bf16[7,80,128]{2,1,0:T(8,128)(2,1)}, bf16[7,80,128]{2,1,0:T(8,128)(2,1)S(1)}, u32[]{:S(2)}, u32[]{:S(2)}) collective-permute-start(bf16[7,80,128]{2,1,0:T(8,128)(2,1)} %get-tuple-element.42), channel_id=1, source_target_pairs={{0,15},{1,0},{2,1},{3,2},{4,3},{5,4},{6,5},{7,6},{8,7},{9,8},{10,9... | collective-permute-start | bytes 430088 | tf_op jit(solution)/shard_map/ppermute | solution.py:18
  17.6 5.8 %collective-permute-start = (bf16[5,80,128]{2,1,0:T(8,128)(2,1)}, bf16[5,80,128]{2,1,0:T(8,128)(2,1)S(1)}, u32[]{:S(2)}, u32[]{:S(2)}) collective-permute-start(bf16[5,80,128]{2,1,0:T(8,128)(2,1)} %get-tuple-element.41), channel_id=1, source_target_pairs={{0,1},{1,2},{2,3},{3,4},{4,5},{5,6},{6,7},{7,8},{8,9},{9,10},{10,1... | collective-permute-start | bytes 307208 | tf_op jit(solution)/shard_map/ppermute | solution.py:18
  22.1 31.0 %copy-start.7 = (bf16[452,128]{1,0:T(8,128)(2,1)}, bf16[452,128]{1,0:T(8,128)(2,1)S(1)}, u32[]{:S(2)}) copy-start(bf16[452,128]{1,0:T(8,128)(2,1)S(1)} %pad_maximum_fusion.6.refs_0_) | copy-start | bytes 347140
  33.2 12.4 %copy-start.18 = (bf16[3]{0:T(256)(128)(2,1)S(1)}, bf16[3]{0:T(256)(128)(2,1)}, u32[]{:S(2)}) copy-start(bf16[3]{0:T(256)(128)(2,1)} %constant.123.clone) | copy-start | bytes 22
  33.2 12.3 %copy-start.19 = (bf16[3]{0:T(256)(128)(2,1)S(1)}, bf16[3]{0:T(256)(128)(2,1)}, u32[]{:S(2)}) copy-start(bf16[3]{0:T(256)(128)(2,1)} %constant.124.clone) | copy-start | bytes 22
  33.6 11.9 %collective-permute-start.2 = (bf16[2,80,128]{2,1,0:T(8,128)(2,1)S(1)}, bf16[2,80,128]{2,1,0:T(8,128)(2,1)S(1)}, u32[]{:S(2)}, u32[]{:S(2)}) collective-permute-start(bf16[2,80,128]{2,1,0:T(8,128)(2,1)S(1)} %bitcast.367), channel_id=1, source_target_pairs={{0,15},{1,0},{2,1},{3,2},{4,3},{5,4},{6,5},{7,6},{8,7},{9,8},{10,9... | collective-permute-start | bytes 122888 | tf_op jit(solution)/shard_map/ppermute | solution.py:18
  46.8 12.7 %collective-permute-start.4 = (bf16[2,80,128]{2,1,0:T(8,128)(2,1)S(1)}, bf16[2,80,128]{2,1,0:T(8,128)(2,1)S(1)}, u32[]{:S(2)}, u32[]{:S(2)}) collective-permute-start(bf16[2,80,128]{2,1,0:T(8,128)(2,1)S(1)} %bitcast.370), channel_id=1, source_target_pairs={{0,1},{1,2},{2,3},{3,4},{4,5},{5,6},{6,7},{7,8},{8,9},{9,10},{10,1... | collective-permute-start | bytes 122888 | tf_op jit(solution)/shard_map/ppermute | solution.py:18
  49.6 16.7 %all-to-all-start = ((bf16[8,3,80,128]{3,2,1,0:T(8,128)(2,1)}), bf16[8,3,80,128]{3,2,1,0:T(8,128)(2,1)S(1)}, u32[]{:S(2)}, u32[]{:S(2)}) async-start(bf16[8,3,80,128]{3,2,1,0:T(8,128)(2,1)} %bitcast.85), calls=%async_computation | async-start | bytes 983040 | tf_op jit(solution)/shard_map/all_to_all | solution.py:26
  53.1 10.9 %collective-permute-start.3 = (bf16[452,128]{1,0:T(8,128)(2,1)S(1)}, bf16[452,128]{1,0:T(8,128)(2,1)S(1)}, u32[]{:S(2)}, u32[]{:S(2)}) collective-permute-start(bf16[452,128]{1,0:T(8,128)(2,1)S(1)} %pad_maximum_fusion.6.refs_0_), channel_id=1, source_target_pairs={{0,1},{1,0},{2,3},{3,2},{4,5},{5,4},{6,7},{7,6},{8,9},{9,8},{10,11... | collective-permute-start | bytes 347144 | tf_op jit(solution)/shard_map/ppermute | solution.py:22
  67.0 12.6 %all-to-all-start.1 = ((bf16[8,2,80,128]{3,2,1,0:T(8,128)(2,1)}), bf16[8,2,80,128]{3,2,1,0:T(8,128)(2,1)}, u32[]{:S(2)}, u32[]{:S(2)}) async-start(bf16[8,2,80,128]{3,2,1,0:T(8,128)(2,1)} %bitcast.168), calls=%async_computation.1 | async-start | bytes 655360 | tf_op jit(solution)/shard_map/all_to_all | solution.py:26
  74.6 8.9 %collective-permute-start.5 = (bf16[452,128]{1,0:T(8,128)(2,1)}, bf16[452,128]{1,0:T(8,128)(2,1)}, u32[]{:S(2)}, u32[]{:S(2)}) collective-permute-start(bf16[452,128]{1,0:T(8,128)(2,1)} %shard_map.149), channel_id=1, source_target_pairs={{0,3},{1,2},{2,1},{3,0},{4,7},{5,6},{6,5},{7,4},{8,11},{9,10},{10,... | collective-permute-start | bytes 347144 | tf_op jit(solution)/shard_map/ppermute | solution.py:22
  85.2 28.0 %all-to-all-start.2 = ((bf16[16,1,176,128]{3,2,1,0:T(8,128)(2,1)}), bf16[16,1,176,128]{3,2,1,0:T(8,128)(2,1)S(1)}, u32[]{:S(2)}, u32[]{:S(2)}) async-start(bf16[16,1,176,128]{3,2,1,0:T(8,128)(2,1)} %bitcast.322), calls=%async_computation.2 | async-start | bytes 1441792 | tf_op jit(solution)/shard_map/all_to_all | solution.py:26
  90.0 51.5 %copy-start.6 = (bf16[1,9,128,128]{2,3,1,0:T(8,128)(2,1)S(1)}, bf16[1,9,128,128]{2,3,1,0:T(8,128)(2,1)}, u32[]{:S(2)}) copy-start(bf16[1,9,128,128]{2,3,1,0:T(8,128)(2,1)} %get-tuple-element.70) | copy-start | bytes 884740
  90.0 13.9 %collective-permute-start.6 = (bf16[452,128]{1,0:T(8,128)(2,1)}, bf16[452,128]{1,0:T(8,128)(2,1)S(1)}, u32[]{:S(2)}, u32[]{:S(2)}) collective-permute-start(bf16[452,128]{1,0:T(8,128)(2,1)} %shard_map.151.refs_0_), channel_id=1, source_target_pairs={{0,4},{4,0},{8,12},{12,8},{1,5},{5,1},{9,13},{13,9},{2,6},{6,2},{1... | collective-permute-start | bytes 347144 | tf_op jit(solution)/shard_map/ppermute | solution.py:22
  124.7 26.8 %all-to-all-start.4 = ((bf16[4,1,176,128]{3,2,1,0:T(8,128)(2,1)}), bf16[4,1,176,128]{3,2,1,0:T(8,128)(2,1)S(1)}, u32[]{:S(2)}, u32[]{:S(2)}) async-start(bf16[4,1,176,128]{3,2,1,0:T(8,128)(2,1)} %shard_map.154), calls=%async_computation.4 | async-start | bytes 360448 | tf_op jit(solution)/shard_map/all_to_all | solution.py:26
  137.6 4.2 %collective-permute-start.8 = (bf16[1,80,128]{2,1,0:T(8,128)(2,1)S(1)}, bf16[1,80,128]{2,1,0:T(8,128)(2,1)S(1)}, u32[]{:S(2)}, u32[]{:S(2)}) collective-permute-start(bf16[1,80,128]{2,1,0:T(8,128)(2,1)S(1)} %get-tuple-element.201), channel_id=1, source_target_pairs={{0,1},{1,2},{2,3},{3,4},{4,5},{5,6},{6,7},{7,8},{8,9},{9,10},{10,1... | collective-permute-start | bytes 61448 | tf_op jit(solution)/shard_map/ppermute | solution.py:18
  140.0 5.7 %collective-permute-start.9 = (bf16[1,80,128]{2,1,0:T(8,128)(2,1)S(1)}, bf16[1,80,128]{2,1,0:T(8,128)(2,1)S(1)}, u32[]{:S(2)}, u32[]{:S(2)}) collective-permute-start(bf16[1,80,128]{2,1,0:T(8,128)(2,1)S(1)} %get-tuple-element.202), channel_id=1, source_target_pairs={{1,0},{2,1},{3,2},{4,3},{5,4},{6,5},{7,6},{8,7},{9,8},{10,9},{11,1... | collective-permute-start | bytes 61448 | tf_op jit(solution)/shard_map/ppermute | solution.py:18
  152.2 11.4 %all-to-all-start.5 = ((bf16[4,1,176,128]{3,2,1,0:T(8,128)(2,1)}), bf16[4,1,176,128]{3,2,1,0:T(8,128)(2,1)S(1)}, u32[]{:S(2)}, u32[]{:S(2)}) async-start(bf16[4,1,176,128]{3,2,1,0:T(8,128)(2,1)} %broadcast_in_dim.80), calls=%async_computation.5 | async-start | bytes 360448 | tf_op jit(solution)/shard_map/all_to_all | solution.py:26
  157.6 11.9 %copy-start.10 = (bf16[452,128]{1,0:T(8,128)(2,1)S(1)}, bf16[452,128]{1,0:T(8,128)(2,1)}, u32[]{:S(2)}) copy-start(bf16[452,128]{1,0:T(8,128)(2,1)} %shard_map.152.refs_0_) | copy-start | bytes 347140
  164.6 21.6 %all-to-all-start.6 = ((bf16[4,4,1,176,128]{4,3,1,2,0:T(8,128)(2,1)}), bf16[4,4,1,176,128]{4,3,1,2,0:T(8,128)(2,1)S(1)}, u32[]{:S(2)}, u32[]{:S(2)}) async-start(bf16[4,4,1,176,128]{4,3,1,2,0:T(8,128)(2,1)} %broadcast_in_dim.82), calls=%async_computation.6 | async-start | bytes 1441792 | tf_op jit(solution)/shard_map/all_to_all | solution.py:26
  169.5 13.4 %collective-permute-start.7 = (bf16[452,128]{1,0:T(8,128)(2,1)S(1)}, bf16[452,128]{1,0:T(8,128)(2,1)S(1)}, u32[]{:S(2)}, u32[]{:S(2)}) collective-permute-start(bf16[452,128]{1,0:T(8,128)(2,1)S(1)} %copy-done.10), channel_id=1, source_target_pairs={{0,12},{4,8},{8,4},{12,0},{1,13},{5,9},{9,5},{13,1},{2,14},{6,10},... | collective-permute-start | bytes 347144 | tf_op jit(solution)/shard_map/ppermute | solution.py:22
  193.3 12.4 %all-to-all-start.8 = ((bf16[4,36,128]{2,1,0:T(8,128)(2,1)}), bf16[4,36,128]{2,1,0:T(8,128)(2,1)S(1)}, u32[]{:S(2)}, u32[]{:S(2)}) async-start(bf16[4,36,128]{2,1,0:T(8,128)(2,1)} %broadcast_in_dim.85), calls=%async_computation.8 | async-start | bytes 81920 | tf_op jit(solution)/shard_map/all_to_all | solution.py:26
  (16 other events, 73.1 us)

commit v12 on v8

--- a/solution.py
+++ b/solution.py
@@ -151,7 +151,7 @@
         out_specs=VMEM,
         compiler_params=pltpu.CompilerParams(vmem_limit_bytes=24 * 2**20),
         cost_estimate=pl.CostEstimate(
-            flops=2 * HALF * cols.shape[0] * chans * chans,
+            flops=2 * (HALF_G + HALF_D) * cols.shape[0] * chans * chans,
             bytes_accessed=5 * 10**6,
             transcendentals=0,
         ),
@@ -198,14 +198,16 @@
     )(core.reshape(1), gram, cols, dpre)
 
 
-def factor_rows(blocks, first_row, scale, rows):
+def owned_rows(blocks, panel, place):
     chans = blocks.shape[-1]
+    rows = panel.shape[0]
+    wide = 9 * chans
     slots = [i // HALF_G * HALF + i % HALF_G for i in range(NG)]
     index = jnp.array([slots[WHERE[a, b][0]] for a in range(9) for b in range(9)], jnp.int32)
     flips = jnp.array([int(WHERE[a, b][1]) for a in range(9) for b in range(9)], jnp.int32)
 
-    def kernel(index_ref, flip_ref, row_ref, scale_ref, blocks_ref, out_ref, band):
-        start = row_ref[0]
+    def kernel(index_ref, flip_ref, place_ref, blocks_ref, panel_ref, out_ref, band):
+        start = place_ref[2] * rows
         tap = lax.div(start, chans)
         for t in range(2):
             a = jnp.minimum(tap + t, 8)
@@ -219,17 +221,57 @@
         base = pl.multiple_of(lax.div(inside, 8) * 8, 8)
         got = band[pl.ds(base, rows + 4), :]
         odd = inside != base
-        out_ref[...] = jnp.where(odd, got[4:], got[:rows]) * scale_ref[0]
+        out_ref[:, :wide] = jnp.where(odd, got[4:], got[:rows]).astype(out_ref.dtype)
+        out_ref[:, wide : wide + chans] = panel_ref[...]
+        out_ref[:, wide + chans :] = jnp.zeros((rows, 4 * chans), out_ref.dtype)
+        part = chans // 4
+        for q in range(4):
+            lanes = slice(wide + (q + 1) * chans, wide + (q + 2) * chans)
+            out_ref[:part, lanes] = blocks_ref[2 * HALF - 1, q * part : (q + 1) * part, :]
 
     return pl.pallas_call(
         kernel,
-        out_shape=jax.ShapeDtypeStruct((rows, 9 * chans), jnp.float32),
-        in_specs=[SMEM, SMEM, SMEM, SMEM, VMEM],
+        out_shape=jax.ShapeDtypeStruct((rows, wide + 5 * chans), jnp.bfloat16),
+        in_specs=[SMEM, SMEM, SMEM, VMEM, VMEM],
         out_specs=VMEM,
-        scratch_shapes=[pltpu.VMEM((2 * chans, 9 * chans), jnp.float32)],
+        scratch_shapes=[pltpu.VMEM((2 * chans, wide), jnp.float32)],
         compiler_params=pltpu.CompilerParams(vmem_limit_bytes=16 * 2**20),
         cost_estimate=pl.CostEstimate(flops=10**6, bytes_accessed=2 * 10**6, transcendentals=0),
-    )(index, flips, first_row.reshape(1), scale.reshape(1), blocks)
+    )(index, flips, place, blocks, panel)
+
+
+def results(got, table, place, chans, count):
+    layers, rows, _ = got.shape
+    wide = 9 * chans
+
+    def kernel(table_ref, place_ref, got_ref, step_ref, fac_ref, own_ref):
+        owner = place_ref[1] * Y + place_ref[0]
+        lay = jnp.int32(0)
+        scale = jnp.float32(0.0)
+        for l in range(layers):
+            mine = table_ref[l] == owner
+            lay = jnp.where(mine, l, lay)
+            scale = jnp.where(mine, jnp.float32(1.0 / count), scale)
+            step_ref[l] = got_ref[l, :, wide : wide + chans]
+        fac_ref[...] = got_ref[lay, :, :wide].astype(jnp.float32) * scale
+        part = chans // 4
+        for q in range(4):
+            lanes = slice(wide + (q + 1) * chans, wide + (q + 2) * chans)
+            own_ref[q * part : (q + 1) * part, :] = (
+                got_ref[lay, :part, lanes].astype(jnp.float32) * scale
+            )
+
+    return pl.pallas_call(
+        kernel,
+        out_shape=(
+            jax.ShapeDtypeStruct((layers, rows, chans), jnp.bfloat16),
+            jax.ShapeDtypeStruct((rows, wide), jnp.float32),
+            jax.ShapeDtypeStruct((chans, chans), jnp.float32),
+        ),
+        in_specs=[SMEM, SMEM, VMEM],
+        out_specs=(VMEM, VMEM, VMEM),
+        cost_estimate=pl.CostEstimate(flops=10**5, bytes_accessed=10**6, transcendentals=0),
+    )(table, place, got)
 
 
 def shards(feats, top_grad, weights, table, a_inv, g_inv):
@@ -286,7 +328,18 @@
     after = shifted(dpre2, -1, True)
     dy1 = back(2, cut_windows(jnp.concatenate([dpre2, after]), inner))
     dpre1 = times(dy1, slope(1, cut_windows(strips[1], inner))).reshape(image)
-    stacked, dpre1 = lax.optimization_barrier((jnp.stack(strips), dpre1))
+    trimmed = [
+        jnp.concatenate([jnp.where(y_id == 0, rows[:1], rows[3:]), rows[1:3]]) for rows in strips
+    ]
+    local = jnp.concatenate(
+        [
+            a_inv.reshape(-1, chans),
+            g_inv[0].astype(jnp.bfloat16),
+            jnp.zeros((12, chans), jnp.bfloat16),
+        ]
+    )
+    inverses = lax.all_gather(local, OWNER, axis=0, tiled=True)
+    stacked, dpre1 = lax.optimization_barrier((jnp.stack(trimmed), dpre1))
     before = shifted(dpre1, 1, True)
     layer_strips = to_layers(stacked)
     edge_top = jnp.where(owner_id > 0, before[:1], jnp.zeros_like(before[:1]))
@@ -294,30 +347,24 @@
     dy0 = back(1, windows(jnp.concatenate([edge_top, before[1:], dpre1[:1], edge_end])))
     dpre0 = times(dy0, slope(0, windows(strips[0]))).reshape(image)
 
+    images = layer_strips.reshape((CORE, Y) + layer_strips.shape[1:])
     last_one = (y_id == 1) & (z_id == ZH - 1)
-    cols = jnp.concatenate(
-        [
-            to_columns(
-                windows(layer_strips[j])
-                if j % Y < Y - 1
-                else cut_windows(layer_strips[j], jnp.logical_not(last_one))
-            )
-            for j in range(CORE * Y)
-        ]
-    )
+    seam = jnp.zeros((Y * rows_dev, 3), bool).at[-2, 2].set(True).at[-1, 0].set(True)
+    cols = []
+    for image_rows in images:
+        middle = image_rows[:, 1:].reshape((-1,) + image_rows.shape[2:])
+        win = windows(jnp.concatenate([image_rows[0, :1], middle, image_rows[-1, :1]]))
+        cut = (seam & last_one)[:, :, None, None]
+        cols.append(to_columns(jnp.where(cut, jnp.zeros_like(win), win)))
+    cols = jnp.concatenate(cols)
     gram = gram_half(cols, core_id)
+
     layer_dpre = to_layers(jnp.stack([dpre0, dpre1, dpre2, dpre3[1:3]]))
     parts = all_half(gram, cols, layer_dpre.reshape(-1, chans), core_id)
 
     piece = scatter_sum(parts, ("x", "zl"))
-    held = spread(piece, "y")
-    layer_ids = jnp.arange(num_layers, dtype=jnp.int32)
-
-    def pick(z):
-        lay = jnp.sum(jnp.where(table == z * Y + y_id, layer_ids, 0))
-        return lax.dynamic_index_in_dim(held, lay, 0, keepdims=False)
-
-    total = exchange(jnp.stack([pick(z) for z in range(ZH)]), "zh")
+    piece, inverses = lax.optimization_barrier((piece, inverses))
+    total = spread(piece, "zh")
     total = jnp.sum(total.astype(jnp.float32), axis=0).astype(jnp.bfloat16)
     summed = spread(spread(spread(total, "zl"), "x"), "core")
 
@@ -328,19 +375,19 @@
     grad_sum = jnp.concatenate(
         [summed[0, HALF_G * chans :], summed[1, HALF_G * chans : (HALF - 1) * chans]]
     )
-    grad_scaled = grad_sum.astype(jnp.float32) / jnp.sqrt(jnp.float32(npos))
-    mixed = jnp.dot(grad_scaled, g_inv[0], precision=lax.Precision.HIGHEST)
-    panel = jnp.dot(a_inv[0].astype(jnp.float32), mixed, precision=lax.Precision.HIGHEST)
-    panels = spread(spread(panel.astype(jnp.bfloat16), "zh"), "y")
-    step_out = panels[table % Y, table // Y]
-
-    stats = summed.reshape(-1, chans, chans)
-    have = jnp.any(table == owner_id).astype(jnp.float32)
-    scale = have / npos
     rows_out = patch // samples
-    a_out = factor_rows(stats, dp_id * rows_out, scale, rows_out)[None]
-    g_out = (stats[-1].astype(jnp.float32) * scale)[None]
-    return (step_out, a_out, g_out, in_grad)
+    inverses = inverses.reshape((owners,) + local.shape)
+    mine_inv = lax.dynamic_index_in_dim(inverses, table[y_id], 0, keepdims=False)
+    a_mine = mine_inv[: rows_out * 9].reshape(rows_out, patch)
+    g_mine = mine_inv[rows_out * 9 : rows_out * 9 + chans]
+    mixed = jnp.dot(grad_sum, g_mine, preferred_element_type=jnp.float32)
+    mixed = mixed / jnp.sqrt(jnp.float32(npos))
+    panel = jnp.dot(a_mine.astype(jnp.float32), mixed, precision=lax.Precision.HIGHEST)
+
+    place = jnp.stack([y_id, z_id, dp_id]).astype(jnp.int32)
+    rows = owned_rows(summed.reshape(-1, chans, chans), panel.astype(jnp.bfloat16), place)
+    step_out, a_out, g_out = results(spread(rows, "y"), table, place, chans, npos)
+    return (step_out, a_out[None], g_out[None], in_grad)
 
 
 def solution(mesh):

time: 210 us -> 219 us (1.043)
  blocking collectives: 4.79 us -> 47.2 us
  waiting for transfers between devices: 77 us -> 52.2 us
  starting transfers between devices: 86.2 us -> 66.5 us
  between operations: 10.5 us -> 17.3 us
    all_to_all x1 -> x2, blocking collectives: 4.79 us -> 47.2 us  [exchange(): return lax.all_to_all(x, axis, split_axis=0, concat_axis=0, tiled=True)]
    all_to_all x9 -> x6, waiting for transfers between devices: 59.3 us -> 33.4 us  [exchange(): return lax.all_to_all(x, axis, split_axis=0, concat_axis=0, tiled=True)]
    all_to_all x9 -> x6, starting transfers between devices: 52.3 us -> 33.1 us  [exchange(): return lax.all_to_all(x, axis, split_axis=0, concat_axis=0, tiled=True)]
    unnamed x163 -> x122, local copies, waits for them, and re-layouts: 5.05 us -> 6.22 us
  transfers between devices with their start and end apart: 15 -> 13, of which waited for: 12 -> 10; matrix products, arithmetic and copies ran while one was open for 6% -> 8% of each run, Pallas kernels for 1% -> 1%
where the time goes in v12:
time: 219 us; the launch traced here: 216 us
  starting transfers between devices  66.5 us (30%)
  waiting for transfers between devices  52.2 us (24%)
  blocking collectives  47.2 us (22%)
  local copies, waits for them, and re-layouts  18.1 us (8%)
  between operations  17.3 us (8%)
  Pallas kernels  6.94 us (3%)
  matrix products  4.14 us (2%)
  other arithmetic  3.95 us (2%)
    all_to_all x2, blocking collectives, exchange(): return lax.all_to_all(x, axis, split_axis=0, concat_axis=0, tiled=True)  47.2 us
    all_to_all x6, waiting for transfers between devices, exchange(): return lax.all_to_all(x, axis, split_axis=0, concat_axis=0, tiled=True)  33.4 us
    ppermute x6, starting transfers between devices, shifted(): return lax.ppermute(x, OWNER, pairs)  33.3 us
    all_to_all x6, starting transfers between devices, exchange(): return lax.all_to_all(x, axis, split_axis=0, concat_axis=0, tiled=True)  33.1 us
    ppermute x6, waiting for transfers between devices, shifted(): return lax.ppermute(x, OWNER, pairs)  18.8 us
    unnamed x122, local copies, waits for them, and re-layouts  6.22 us
  transfers between devices with their start and end apart: 13, of which 10 were waited for; matrix products, arithmetic and copies ran while one was open for 8% of the time, Pallas kernels for 1%

profile of v12, /device:TPU:6, one launch (start us, length us, event | category | flops | bytes accessed | tf_op | source)
XLA Modules:
  0.0 216.2 jit_solution(8577849038497131489)
XLA Ops:
  7.2 1.7 shard_map.147
  8.9 15.2 %collective-permute-start.1 = (bf16[7,80,128]{2,1,0:T(8,128)(2,1)}, bf16[7,80,128]{2,1,0:T(8,128)(2,1)S(1)}, u32[]{:S(2)}, u32[]{:S(2)}) collective-permute-start(bf16[7,80,128]{2,1,0:T(8,128)(2,1)} %get-tuple-element.38), channel_id=1, source_target_pairs={{0,15},{1,0},{2,1},{3,2},{4,3},{5,4},{6,5},{7,6},{8,7},{9,8},{10,9... | collective-permute-start | bytes 430088 | tf_op jit(solution)/shard_map/ppermute | solution.py:18
  30.6 6.2 %collective-permute-done.1 = bf16[7,80,128]{2,1,0:T(8,128)(2,1)S(1)} collective-permute-done((bf16[7,80,128]{2,1,0:T(8,128)(2,1)}, bf16[7,80,128]{2,1,0:T(8,128)(2,1)S(1)}, u32[]{:S(2)}, u32[]{:S(2)}) %collective-permute-start.1) | collective-permute-done | bytes 143392 | tf_op jit(solution)/shard_map/ppermute | solution.py:18
  40.2 10.3 %collective-permute-start.2 = (bf16[2,80,128]{2,1,0:T(8,128)(2,1)S(1)}, bf16[2,80,128]{2,1,0:T(8,128)(2,1)S(1)}, u32[]{:S(2)}, u32[]{:S(2)}) collective-permute-start(bf16[2,80,128]{2,1,0:T(8,128)(2,1)S(1)} %bitcast.365), channel_id=1, source_target_pairs={{0,15},{1,0},{2,1},{3,2},{4,3},{5,4},{6,5},{7,6},{8,7},{9,8},{10,9... | collective-permute-start | bytes 122888 | tf_op jit(solution)/shard_map/ppermute | solution.py:18
  51.3 1.8 collective-permute-done.2
  54.3 1.9 collective-permute-start.3
  57.1 3.5 %all-to-all-start = ((bf16[8,3,80,128]{3,2,1,0:T(8,128)(2,1)}), bf16[8,3,80,128]{3,2,1,0:T(8,128)(2,1)S(1)}, u32[]{:S(2)}, u32[]{:S(2)}) async-start(bf16[8,3,80,128]{3,2,1,0:T(8,128)(2,1)} %bitcast.84), calls=%async_computation | async-start | bytes 983040 | tf_op jit(solution)/shard_map/all_to_all | solution.py:22
  60.6 9.3 %collective-permute-done.3 = bf16[2,80,128]{2,1,0:T(8,128)(2,1)S(1)} collective-permute-done((bf16[2,80,128]{2,1,0:T(8,128)(2,1)S(1)}, bf16[2,80,128]{2,1,0:T(8,128)(2,1)S(1)}, u32[]{:S(2)}, u32[]{:S(2)}) %collective-permute-start.3) | collective-permute-done | bytes 40992 | tf_op jit(solution)/shard_map/ppermute | solution.py:18
  71.8 4.1 %all-to-all-start.1 = ((bf16[8,2,80,128]{3,2,1,0:T(8,128)(2,1)}), bf16[8,2,80,128]{3,2,1,0:T(8,128)(2,1)}, u32[]{:S(2)}, u32[]{:S(2)}) async-start(bf16[8,2,80,128]{3,2,1,0:T(8,128)(2,1)} %bitcast.167), calls=%async_computation.1 | async-start | bytes 655360 | tf_op jit(solution)/shard_map/all_to_all | solution.py:22
  79.4 5.2 %all-to-all-done.1 = bf16[8,2,80,128]{3,2,1,0:T(8,128)(2,1)} async-done(((bf16[8,2,80,128]{3,2,1,0:T(8,128)(2,1)}), bf16[8,2,80,128]{3,2,1,0:T(8,128)(2,1)}, u32[]{:S(2)}, u32[]{:S(2)}) %all-to-all-start.1) | async-done | bytes 327712 | tf_op jit(solution)/shard_map/all_to_all | solution.py:22
  84.5 1.5 shard_map.149
  86.1 42.4 %all_to_all.40 = bf16[16,160,128]{2,1,0:T(8,128)(2,1)S(1)} all-to-all(bf16[16,160,128]{2,1,0:T(8,128)(2,1)S(1)} %bitcast.325), channel_id=1, replica_groups=mesh['x'=4,'zl'=4,'core'=2,'zh'=4,'y'=4] {'x','zl'}, dimensions={0} | all-to-all | bytes 1310720 | tf_op jit(solution)/shard_map/all_to_all | solution.py:22
  129.3 8.8 %all-to-all-start.3 = ((bf16[4,160,128]{2,1,0:T(8,128)(2,1)}), bf16[4,160,128]{2,1,0:T(8,128)(2,1)S(1)}, u32[]{:S(2)}, u32[]{:S(2)}) async-start(bf16[4,160,128]{2,1,0:T(8,128)(2,1)} %broadcast_in_dim.38), calls=%async_computation.3 | async-start | bytes 327680 | tf_op jit(solution)/shard_map/all_to_all | solution.py:22
  138.1 3.4 %collective-permute-start.4 = (bf16[1,80,128]{2,1,0:T(8,128)(2,1)S(1)}, bf16[1,80,128]{2,1,0:T(8,128)(2,1)S(1)}, u32[]{:S(2)}, u32[]{:S(2)}) collective-permute-start(bf16[1,80,128]{2,1,0:T(8,128)(2,1)S(1)} %get-tuple-element.193), channel_id=1, source_target_pairs={{0,1},{1,2},{2,3},{3,4},{4,5},{5,6},{6,7},{7,8},{8,9},{9,10},{10,1... | collective-permute-start | bytes 61448 | tf_op jit(solution)/shard_map/ppermute | solution.py:18
  147.1 6.8 %all-to-all-done.3 = bf16[4,160,128]{2,1,0:T(8,128)(2,1)S(1)} async-done(((bf16[4,160,128]{2,1,0:T(8,128)(2,1)}), bf16[4,160,128]{2,1,0:T(8,128)(2,1)S(1)}, u32[]{:S(2)}, u32[]{:S(2)}) %all-to-all-start.3) | async-done | bytes 163872 | tf_op jit(solution)/shard_map/all_to_all | solution.py:22
  154.7 4.5 %all-to-all-start.4 = ((bf16[4,160,128]{2,1,0:T(8,128)(2,1)}), bf16[4,160,128]{2,1,0:T(8,128)(2,1)S(1)}, u32[]{:S(2)}, u32[]{:S(2)}) async-start(bf16[4,160,128]{2,1,0:T(8,128)(2,1)} %broadcast_in_dim.39), calls=%async_computation.4 | async-start | bytes 327680 | tf_op jit(solution)/shard_map/all_to_all | solution.py:22
  159.3 5.9 %all-to-all-done.4 = bf16[4,160,128]{2,1,0:T(8,128)(2,1)S(1)} async-done(((bf16[4,160,128]{2,1,0:T(8,128)(2,1)}), bf16[4,160,128]{2,1,0:T(8,128)(2,1)S(1)}, u32[]{:S(2)}, u32[]{:S(2)}) %all-to-all-start.4) | async-done | bytes 163872 | tf_op jit(solution)/shard_map/all_to_all | solution.py:22
  166.1 5.4 %all-to-all-start.5 = ((bf16[4,4,160,128]{3,2,1,0:T(8,128)(2,1)}), bf16[4,4,160,128]{3,2,1,0:T(8,128)(2,1)S(1)}, u32[]{:S(2)}, u32[]{:S(2)}) async-start(bf16[4,4,160,128]{3,2,1,0:T(8,128)(2,1)} %broadcast_in_dim.40), calls=%async_computation.5 | async-start | bytes 1310720 | tf_op jit(solution)/shard_map/all_to_all | solution.py:22
  172.6 5.6 %all-to-all-done.5 = bf16[4,4,160,128]{3,2,1,0:T(8,128)(2,1)S(1)} async-done(((bf16[4,4,160,128]{3,2,1,0:T(8,128)(2,1)}), bf16[4,4,160,128]{3,2,1,0:T(8,128)(2,1)S(1)}, u32[]{:S(2)}, u32[]{:S(2)}) %all-to-all-start.5) | async-done | bytes 655392 | tf_op jit(solution)/shard_map/all_to_all | solution.py:22
  178.5 4.8 %all_to_all.41 = bf16[2,4,4,160,128]{4,3,2,1,0:T(8,128)(2,1)S(1)} all-to-all(bf16[2,4,4,160,128]{4,3,2,1,0:T(8,128)(2,1)S(1)} %broadcast_in_dim.41), channel_id=1, replica_groups=mesh['x'=4,'zl'=4,'core'=2,'zh'=4,'y'=4] {'core'}, dimensions={0} | all-to-all | bytes 2621440 | tf_op jit(solution)/shard_map/all_to_all | solution.py:22
  186.4 6.9 %all-to-all-start.7 = ((bf16[4,36,1792]{2,1,0:T(8,128)(2,1)}), bf16[4,36,1792]{2,1,0:T(8,128)(2,1)S(1)}, u32[]{:S(2)}, u32[]{:S(2)}) async-start(bf16[4,36,1792]{2,1,0:T(8,128)(2,1)} %broadcast_in_dim.42), calls=%async_computation.7 | async-start | bytes 1146880 | tf_op jit(solution)/shard_map/all_to_all | solution.py:22
  194.2 9.4 %all-to-all-done.7.got_ref = bf16[4,36,1792]{2,1,0:T(8,128)(2,1)S(1)} async-done(((bf16[4,36,1792]{2,1,0:T(8,128)(2,1)}), bf16[4,36,1792]{2,1,0:T(8,128)(2,1)S(1)}, u32[]{:S(2)}, u32[]{:S(2)}) %all-to-all-start.7) | async-done | bytes 516128 | tf_op jit(solution)/shard_map/all_to_all | solution.py:22
  204.4 1.8 shard_map.151
  206.2 1.8 copy.87
  (232 shorter events, 31.0 us)
Async XLA Ops:
  7.2 21.9 %copy-start.3 = (bf16[4,1152,128]{2,1,0:T(8,128)(2,1)S(1)}, bf16[4,1152,128]{2,1,0:T(8,128)(2,1)}, u32[]{:S(2)}) copy-start(bf16[4,1152,128]{2,1,0:T(8,128)(2,1)} %param.18) | copy-start | bytes 3538948
  7.2 121.4 %all-gather.2.cloned.1.call-start = ((), (), s32[]{:S(2)}) async-start(), calls=%async_computation.8 | async-start | bytes 2019328 | tf_op jit(solution)/shard_map/all_gather | solution.py:341
  8.9 27.8 %collective-permute-start.1 = (bf16[7,80,128]{2,1,0:T(8,128)(2,1)}, bf16[7,80,128]{2,1,0:T(8,128)(2,1)S(1)}, u32[]{:S(2)}, u32[]{:S(2)}) collective-permute-start(bf16[7,80,128]{2,1,0:T(8,128)(2,1)} %get-tuple-element.38), channel_id=1, source_target_pairs={{0,15},{1,0},{2,1},{3,2},{4,3},{5,4},{6,5},{7,6},{8,7},{9,8},{10,9... | collective-permute-start | bytes 430088 | tf_op jit(solution)/shard_map/ppermute | solution.py:18
  24.1 6.4 %collective-permute-start = (bf16[5,80,128]{2,1,0:T(8,128)(2,1)}, bf16[5,80,128]{2,1,0:T(8,128)(2,1)S(1)}, u32[]{:S(2)}, u32[]{:S(2)}) collective-permute-start(bf16[5,80,128]{2,1,0:T(8,128)(2,1)} %get-tuple-element.37), channel_id=1, source_target_pairs={{0,1},{1,2},{2,3},{3,4},{4,5},{5,6},{6,7},{7,8},{8,9},{9,10},{10,1... | collective-permute-start | bytes 307208 | tf_op jit(solution)/shard_map/ppermute | solution.py:18
  27.4 2.5 %copy-start.12 = (pred[8,3]{0,1:T(4,128)(4,1)S(1)}, pred[8,3]{0,1:T(4,128)(4,1)}, u32[]{:S(2)}) copy-start(pred[8,3]{0,1:T(4,128)(4,1)} %constant.119.clone.1) | copy-start | bytes 76
  30.6 6.8 %copy-start.7 = (bf16[5,80,128]{2,1,0:T(8,128)(2,1)}, bf16[5,80,128]{2,1,0:T(8,128)(2,1)S(1)}, u32[]{:S(2)}) copy-start(bf16[5,80,128]{2,1,0:T(8,128)(2,1)S(1)} %collective-permute-done) | copy-start | bytes 307204
  39.7 13.4 %copy-start.10 = (bf16[3]{0:T(256)(128)(2,1)S(1)}, bf16[3]{0:T(256)(128)(2,1)}, u32[]{:S(2)}) copy-start(bf16[3]{0:T(256)(128)(2,1)} %constant.129.clone) | copy-start | bytes 22
  39.7 13.3 %copy-start.11 = (bf16[3]{0:T(256)(128)(2,1)S(1)}, bf16[3]{0:T(256)(128)(2,1)}, u32[]{:S(2)}) copy-start(bf16[3]{0:T(256)(128)(2,1)} %constant.130.clone) | copy-start | bytes 22
  40.2 12.9 %collective-permute-start.2 = (bf16[2,80,128]{2,1,0:T(8,128)(2,1)S(1)}, bf16[2,80,128]{2,1,0:T(8,128)(2,1)S(1)}, u32[]{:S(2)}, u32[]{:S(2)}) collective-permute-start(bf16[2,80,128]{2,1,0:T(8,128)(2,1)S(1)} %bitcast.365), channel_id=1, source_target_pairs={{0,15},{1,0},{2,1},{3,2},{4,3},{5,4},{6,5},{7,6},{8,7},{9,8},{10,9... | collective-permute-start | bytes 122888 | tf_op jit(solution)/shard_map/ppermute | solution.py:18
  54.3 15.6 %collective-permute-start.3 = (bf16[2,80,128]{2,1,0:T(8,128)(2,1)S(1)}, bf16[2,80,128]{2,1,0:T(8,128)(2,1)S(1)}, u32[]{:S(2)}, u32[]{:S(2)}) collective-permute-start(bf16[2,80,128]{2,1,0:T(8,128)(2,1)S(1)} %bitcast.368), channel_id=1, source_target_pairs={{0,1},{1,2},{2,3},{3,4},{4,5},{5,6},{6,7},{7,8},{8,9},{9,10},{10,1... | collective-permute-start | bytes 122888 | tf_op jit(solution)/shard_map/ppermute | solution.py:18
  57.1 14.0 %all-to-all-start = ((bf16[8,3,80,128]{3,2,1,0:T(8,128)(2,1)}), bf16[8,3,80,128]{3,2,1,0:T(8,128)(2,1)S(1)}, u32[]{:S(2)}, u32[]{:S(2)}) async-start(bf16[8,3,80,128]{3,2,1,0:T(8,128)(2,1)} %bitcast.84), calls=%async_computation | async-start | bytes 983040 | tf_op jit(solution)/shard_map/all_to_all | solution.py:22
  71.8 12.7 %all-to-all-start.1 = ((bf16[8,2,80,128]{3,2,1,0:T(8,128)(2,1)}), bf16[8,2,80,128]{3,2,1,0:T(8,128)(2,1)}, u32[]{:S(2)}, u32[]{:S(2)}) async-start(bf16[8,2,80,128]{3,2,1,0:T(8,128)(2,1)} %bitcast.167), calls=%async_computation.1 | async-start | bytes 655360 | tf_op jit(solution)/shard_map/all_to_all | solution.py:22
  86.1 56.7 %copy-start.5 = (bf16[1,9,128,128]{2,3,1,0:T(8,128)(2,1)S(1)}, bf16[1,9,128,128]{2,3,1,0:T(8,128)(2,1)}, u32[]{:S(2)}) copy-start(bf16[1,9,128,128]{2,3,1,0:T(8,128)(2,1)} %get-tuple-element.62) | copy-start | bytes 884740
  86.1 56.9 %copy-start.9 = (s32[4]{0:T(128)S(1)}, s32[4]{0:T(128)}, u32[]{:S(2)}) copy-start(s32[4]{0:T(128)} %table_ref.1) | copy-start | bytes 52
  129.3 24.7 %all-to-all-start.3 = ((bf16[4,160,128]{2,1,0:T(8,128)(2,1)}), bf16[4,160,128]{2,1,0:T(8,128)(2,1)S(1)}, u32[]{:S(2)}, u32[]{:S(2)}) async-start(bf16[4,160,128]{2,1,0:T(8,128)(2,1)} %broadcast_in_dim.38), calls=%async_computation.3 | async-start | bytes 327680 | tf_op jit(solution)/shard_map/all_to_all | solution.py:22
  138.1 7.5 %collective-permute-start.4 = (bf16[1,80,128]{2,1,0:T(8,128)(2,1)S(1)}, bf16[1,80,128]{2,1,0:T(8,128)(2,1)S(1)}, u32[]{:S(2)}, u32[]{:S(2)}) collective-permute-start(bf16[1,80,128]{2,1,0:T(8,128)(2,1)S(1)} %get-tuple-element.193), channel_id=1, source_target_pairs={{0,1},{1,2},{2,3},{3,4},{4,5},{5,6},{6,7},{7,8},{8,9},{9,10},{10,1... | collective-permute-start | bytes 61448 | tf_op jit(solution)/shard_map/ppermute | solution.py:18
  141.4 5.7 %collective-permute-start.5 = (bf16[1,80,128]{2,1,0:T(8,128)(2,1)S(1)}, bf16[1,80,128]{2,1,0:T(8,128)(2,1)S(1)}, u32[]{:S(2)}, u32[]{:S(2)}) collective-permute-start(bf16[1,80,128]{2,1,0:T(8,128)(2,1)S(1)} %get-tuple-element.194), channel_id=1, source_target_pairs={{1,0},{2,1},{3,2},{4,3},{5,4},{6,5},{7,6},{8,7},{9,8},{10,9},{11,1... | collective-permute-start | bytes 61448 | tf_op jit(solution)/shard_map/ppermute | solution.py:18
  142.8 41.8 %copy-start = (s32[3]{0:T(128)}, s32[3]{0:T(128)S(1)}, u32[]{:S(2)}) copy-start(s32[3]{0:T(128)S(1)} %pad_add_fusion.place_ref) | copy-start | bytes 40
  154.7 10.5 %all-to-all-start.4 = ((bf16[4,160,128]{2,1,0:T(8,128)(2,1)}), bf16[4,160,128]{2,1,0:T(8,128)(2,1)S(1)}, u32[]{:S(2)}, u32[]{:S(2)}) async-start(bf16[4,160,128]{2,1,0:T(8,128)(2,1)} %broadcast_in_dim.39), calls=%async_computation.4 | async-start | bytes 327680 | tf_op jit(solution)/shard_map/all_to_all | solution.py:22
  166.1 12.2 %all-to-all-start.5 = ((bf16[4,4,160,128]{3,2,1,0:T(8,128)(2,1)}), bf16[4,4,160,128]{3,2,1,0:T(8,128)(2,1)S(1)}, u32[]{:S(2)}, u32[]{:S(2)}) async-start(bf16[4,4,160,128]{3,2,1,0:T(8,128)(2,1)} %broadcast_in_dim.40), calls=%async_computation.5 | async-start | bytes 1310720 | tf_op jit(solution)/shard_map/all_to_all | solution.py:22
  183.3 1.4 copy-start.1
  183.3 1.4 copy-start.2
  186.4 17.2 %all-to-all-start.7 = ((bf16[4,36,1792]{2,1,0:T(8,128)(2,1)}), bf16[4,36,1792]{2,1,0:T(8,128)(2,1)S(1)}, u32[]{:S(2)}, u32[]{:S(2)}) async-start(bf16[4,36,1792]{2,1,0:T(8,128)(2,1)} %broadcast_in_dim.42), calls=%async_computation.7 | async-start | bytes 1146880 | tf_op jit(solution)/shard_map/all_to_all | solution.py:22
  203.6 0.8 copy-start.4
  (4 other events, 3.0 us)
Sparse Core Ops, SparseCore 0:
  28.3 91.4 all-gather.1

commit v13 on v12

--- a/solution.py
+++ b/solution.py
@@ -158,44 +158,54 @@
     )(core.reshape(1), cols)
 
 
-def all_half(gram, cols, dpre, core):
+def all_half(gram, cols, dpre, parts_g, table, place):
     chans = dpre.shape[-1]
 
-    def kernel(core_ref, gram_ref, cols_ref, dpre_ref, out_ref):
+    def kernel(table_ref, place_ref, gram_ref, cols_ref, dpre_ref, parts_ref, out_ref, spare):
+        core = place_ref[2] % CORE
         out_ref[: HALF_G * chans, :] = gram_ref[...]
 
         def put(i, value):
             out_ref[(HALF_G + i) * chans : (HALF_G + i + 1) * chans, :] = value.astype(out_ref.dtype)
 
-        def some(first, last, own):
+        def some(first, last):
             turned = dpre_ref[...].T
             right = cols_ref[:, first * chans : last * chans]
             grad = jnp.dot(turned, right, preferred_element_type=jnp.float32)
             for i in range(last - first):
                 put(i, grad[:, i * chans : (i + 1) * chans].T)
-            if own:
-                put(last - first, jnp.dot(turned, dpre_ref[...], preferred_element_type=jnp.float32))
-
-        @pl.when(core_ref[0] == 0)
+            return turned
+
+        @pl.when(core == 0)
         def _():
-            some(0, HALF_D, False)
-
-        @pl.when(core_ref[0] != 0)
+            some(0, HALF_D)
+
+        @pl.when(core != 0)
         def _():
-            some(HALF_D, 9, True)
+            turned = some(HALF_D, 9)
+            put(9 - HALF_D, jnp.dot(turned, dpre_ref[...], preferred_element_type=jnp.float32))
+            owner = table_ref[place_ref[0]]
+            mine = lax.div(owner, Y) == place_ref[1]
+            rows = parts_ref[lax.rem(owner, Y)].astype(jnp.float32)
+            size = chans // (X * ZL)
+            first = pl.multiple_of(lax.div(place_ref[2], CORE) * size, size)
+            spare[...] = jnp.zeros(spare.shape, spare.dtype)
+            spare[pl.ds(first, size), :] = jnp.where(mine, rows[:size], 0.0)
+            out_ref[(HALF_G - 1) * chans : HALF_G * chans, :] = spare[...].astype(out_ref.dtype)
 
     return pl.pallas_call(
         kernel,
         out_shape=jax.ShapeDtypeStruct((HALF * chans, chans), jnp.bfloat16),
-        in_specs=[SMEM, VMEM, VMEM, VMEM],
+        in_specs=[SMEM, SMEM, VMEM, VMEM, VMEM, VMEM],
         out_specs=VMEM,
+        scratch_shapes=[pltpu.VMEM((chans, chans), jnp.float32)],
         compiler_params=pltpu.CompilerParams(vmem_limit_bytes=24 * 2**20),
         cost_estimate=pl.CostEstimate(
             flops=2 * HALF_D * cols.shape[0] * chans * chans,
             bytes_accessed=5 * 10**6,
             transcendentals=0,
         ),
-    )(core.reshape(1), gram, cols, dpre)
+    )(table, place, gram, cols, dpre, parts_g)
 
 
 def owned_rows(blocks, panel, place):
@@ -269,7 +279,7 @@
             jax.ShapeDtypeStruct((chans, chans), jnp.float32),
         ),
         in_specs=[SMEM, SMEM, VMEM],
-        out_specs=(VMEM, VMEM, VMEM),
+
         cost_estimate=pl.CostEstimate(flops=10**5, bytes_accessed=10**6, transcendentals=0),
     )(table, place, got)
 
@@ -288,7 +298,11 @@
     f = feats[:, 0]
     top = top_grad[0]
 
-    to_above, to_below = halo_rows(f, top)
+    own_a = a_inv.reshape(-1, chans)
+    own_a = jnp.pad(own_a, ((0, -own_a.shape[0] % 16), (0, 0)))
+    own_a, f_first, top_first = lax.optimization_barrier((own_a, f, top))
+    inverses = lax.all_gather(own_a, OWNER, axis=0, tiled=True)
+    to_above, to_below = halo_rows(f_first, top_first)
     below = shifted(to_above, -1, True)
     above = shifted(to_below, 1, False)
     below1 = below[5:]
@@ -331,17 +345,22 @@
     trimmed = [
         jnp.concatenate([jnp.where(y_id == 0, rows[:1], rows[3:]), rows[1:3]]) for rows in strips
     ]
-    local = jnp.concatenate(
+    place = jnp.stack([y_id, z_id, dp_id]).astype(jnp.int32)
+    size = chans // (X * ZL)
+    own_g = lax.dynamic_slice_in_dim(g_inv[0], dp_id // CORE * size, size, 0).astype(jnp.bfloat16)
+    own_g = jnp.pad(own_g, ((0, -size % 16), (0, 0)))
+    strip_rows = (rows_dev + 1) * width
+    stacked = jnp.concatenate(
         [
-            a_inv.reshape(-1, chans),
-            g_inv[0].astype(jnp.bfloat16),
-            jnp.zeros((12, chans), jnp.bfloat16),
-        ]
-    )
-    inverses = lax.all_gather(local, OWNER, axis=0, tiled=True)
-    stacked, dpre1 = lax.optimization_barrier((jnp.stack(trimmed), dpre1))
+            jnp.stack(trimmed).reshape(num_layers, strip_rows, chans),
+            jnp.broadcast_to(own_g[None], (num_layers,) + own_g.shape),
+        ],
+        axis=1,
+    )
+    stacked, dpre1 = lax.optimization_barrier((stacked, dpre1))
     before = shifted(dpre1, 1, True)
-    layer_strips = to_layers(stacked)
+    from_layers = to_layers(stacked)
+    layer_strips = from_layers[:, :strip_rows].reshape(-1, rows_dev + 1, width, chans)
     edge_top = jnp.where(owner_id > 0, before[:1], jnp.zeros_like(before[:1]))
     edge_end = jnp.where(inner, dpre1[1:], jnp.zeros_like(dpre1[1:]))
     dy0 = back(1, windows(jnp.concatenate([edge_top, before[1:], dpre1[:1], edge_end])))
@@ -360,7 +379,9 @@
     gram = gram_half(cols, core_id)
 
     layer_dpre = to_layers(jnp.stack([dpre0, dpre1, dpre2, dpre3[1:3]]))
-    parts = all_half(gram, cols, layer_dpre.reshape(-1, chans), core_id)
+    parts = all_half(
+        gram, cols, layer_dpre.reshape(-1, chans), from_layers[:Y, strip_rows:], table, place
+    )
 
     piece = scatter_sum(parts, ("x", "zl"))
     piece, inverses = lax.optimization_barrier((piece, inverses))
@@ -376,15 +397,14 @@
         [summed[0, HALF_G * chans :], summed[1, HALF_G * chans : (HALF - 1) * chans]]
     )
     rows_out = patch // samples
-    inverses = inverses.reshape((owners,) + local.shape)
+    inverses = inverses.reshape((owners,) + own_a.shape)
     mine_inv = lax.dynamic_index_in_dim(inverses, table[y_id], 0, keepdims=False)
     a_mine = mine_inv[: rows_out * 9].reshape(rows_out, patch)
-    g_mine = mine_inv[rows_out * 9 : rows_out * 9 + chans]
+    g_mine = summed[1, (HALF_G - 1) * chans : HALF_G * chans]
     mixed = jnp.dot(grad_sum, g_mine, preferred_element_type=jnp.float32)
     mixed = mixed / jnp.sqrt(jnp.float32(npos))
     panel = jnp.dot(a_mine.astype(jnp.float32), mixed, precision=lax.Precision.HIGHEST)
 
-    place = jnp.stack([y_id, z_id, dp_id]).astype(jnp.int32)
     rows = owned_rows(summed.reshape(-1, chans, chans), panel.astype(jnp.bfloat16), place)
     step_out, a_out, g_out = results(spread(rows, "y"), table, place, chans, npos)
     return (step_out, a_out[None], g_out[None], in_grad)

time: 219 us -> 209 us (0.954)
  blocking collectives: 47.2 us -> 35.1 us
  local copies, waits for them, and re-layouts: 18.1 us -> 22.2 us
    all_to_all x2, blocking collectives: 47.2 us -> 35.1 us  [exchange(): return lax.all_to_all(x, axis, split_axis=0, concat_axis=0, tiled=True)]
    unnamed x122 -> x134, local copies, waits for them, and re-layouts: 6.22 us -> 6.88 us
  transfers between devices with their start and end apart: 13 -> 13, of which waited for: 10 -> 10; matrix products, arithmetic and copies ran while one was open for 8% -> 9% of each run, Pallas kernels for 1% -> 1%
where the time goes in v13:
time: 209 us; the launch traced here: 206 us
  starting transfers between devices  66.1 us (32%)
  waiting for transfers between devices  51.7 us (25%)
  blocking collectives  35.1 us (17%)
  local copies, waits for them, and re-layouts  22.2 us (11%)
  between operations  17.3 us (8%)
  Pallas kernels  6.86 us (3%)
  matrix products  3.98 us (2%)
  other arithmetic  2.34 us (1%)
    all_to_all x2, blocking collectives, exchange(): return lax.all_to_all(x, axis, split_axis=0, concat_axis=0, tiled=True)  35.1 us
    all_to_all x6, waiting for transfers between devices, exchange(): return lax.all_to_all(x, axis, split_axis=0, concat_axis=0, tiled=True)  33.8 us
    ppermute x6, starting transfers between devices, shifted(): return lax.ppermute(x, OWNER, pairs)  33.4 us
    all_to_all x6, starting transfers between devices, exchange(): return lax.all_to_all(x, axis, split_axis=0, concat_axis=0, tiled=True)  32.6 us
    ppermute x6, waiting for transfers between devices, shifted(): return lax.ppermute(x, OWNER, pairs)  17.8 us
    unnamed x134, local copies, waits for them, and re-layouts  6.88 us
  transfers between devices with their start and end apart: 13, of which 10 were waited for; matrix products, arithmetic and copies ran while one was open for 9% of the time, Pallas kernels for 1%

profile of v13, /device:TPU:6, one launch (start us, length us, event | category | flops | bytes accessed | tf_op | source)
XLA Modules:
  0.0 205.5 jit_solution(7620980091461530653)
XLA Ops:
  10.5 15.3 %collective-permute-start.1 = (bf16[7,80,128]{2,1,0:T(8,128)(2,1)}, bf16[7,80,128]{2,1,0:T(8,128)(2,1)S(1)}, u32[]{:S(2)}, u32[]{:S(2)}) collective-permute-start(bf16[7,80,128]{2,1,0:T(8,128)(2,1)} %get-tuple-element.43), channel_id=1, source_target_pairs={{0,15},{1,0},{2,1},{3,2},{4,3},{5,4},{6,5},{7,6},{8,7},{9,8},{10,9... | collective-permute-start | bytes 430088 | tf_op jit(solution)/shard_map/ppermute | solution.py:18
  28.0 2.0 fusion.91
  30.9 7.5 %collective-permute-done.1 = bf16[7,80,128]{2,1,0:T(8,128)(2,1)S(1)} collective-permute-done((bf16[7,80,128]{2,1,0:T(8,128)(2,1)}, bf16[7,80,128]{2,1,0:T(8,128)(2,1)S(1)}, u32[]{:S(2)}, u32[]{:S(2)}) %collective-permute-start.1) | collective-permute-done | bytes 143392 | tf_op jit(solution)/shard_map/ppermute | solution.py:18
  43.0 10.3 %collective-permute-start.2 = (bf16[2,80,128]{2,1,0:T(8,128)(2,1)S(1)}, bf16[2,80,128]{2,1,0:T(8,128)(2,1)S(1)}, u32[]{:S(2)}, u32[]{:S(2)}) collective-permute-start(bf16[2,80,128]{2,1,0:T(8,128)(2,1)S(1)} %bitcast.372), channel_id=1, source_target_pairs={{0,15},{1,0},{2,1},{3,2},{4,3},{5,4},{6,5},{7,6},{8,7},{9,8},{10,9... | collective-permute-start | bytes 122888 | tf_op jit(solution)/shard_map/ppermute | solution.py:18
  54.9 1.8 collective-permute-done.2
  58.0 1.9 collective-permute-start.3
  60.8 3.6 %all-to-all-start = ((bf16[8,256,128]{2,1,0:T(8,128)(2,1)}), bf16[8,256,128]{2,1,0:T(8,128)(2,1)S(1)}, u32[]{:S(2)}, u32[]{:S(2)}) async-start(bf16[8,256,128]{2,1,0:T(8,128)(2,1)} %bitcast.85), calls=%async_computation | async-start | bytes 1048576 | tf_op jit(solution)/shard_map/all_to_all | solution.py:22
  64.4 6.9 %collective-permute-done.3 = bf16[2,80,128]{2,1,0:T(8,128)(2,1)S(1)} collective-permute-done((bf16[2,80,128]{2,1,0:T(8,128)(2,1)S(1)}, bf16[2,80,128]{2,1,0:T(8,128)(2,1)S(1)}, u32[]{:S(2)}, u32[]{:S(2)}) %collective-permute-start.3) | collective-permute-done | bytes 40992 | tf_op jit(solution)/shard_map/ppermute | solution.py:18
  72.0 3.0 %all-to-all-done = bf16[8,256,128]{2,1,0:T(8,128)(2,1)S(1)} async-done(((bf16[8,256,128]{2,1,0:T(8,128)(2,1)}), bf16[8,256,128]{2,1,0:T(8,128)(2,1)S(1)}, u32[]{:S(2)}, u32[]{:S(2)}) %all-to-all-start) | async-done | bytes 524320 | tf_op jit(solution)/shard_map/all_to_all | solution.py:22
  75.8 4.1 %all-to-all-start.1 = ((bf16[8,2,80,128]{3,2,1,0:T(8,128)(2,1)}), bf16[8,2,80,128]{3,2,1,0:T(8,128)(2,1)}, u32[]{:S(2)}, u32[]{:S(2)}) async-start(bf16[8,2,80,128]{3,2,1,0:T(8,128)(2,1)} %bitcast.170), calls=%async_computation.1 | async-start | bytes 655360 | tf_op jit(solution)/shard_map/all_to_all | solution.py:22
  84.1 3.4 %all-to-all-done.1 = bf16[8,2,80,128]{3,2,1,0:T(8,128)(2,1)} async-done(((bf16[8,2,80,128]{3,2,1,0:T(8,128)(2,1)}), bf16[8,2,80,128]{3,2,1,0:T(8,128)(2,1)}, u32[]{:S(2)}, u32[]{:S(2)}) %all-to-all-start.1) | async-done | bytes 327712 | tf_op jit(solution)/shard_map/all_to_all | solution.py:22
  89.1 30.3 %all_to_all.40 = bf16[16,160,128]{2,1,0:T(8,128)(2,1)S(1)} all-to-all(bf16[16,160,128]{2,1,0:T(8,128)(2,1)S(1)} %bitcast.324), channel_id=1, replica_groups=mesh['x'=4,'zl'=4,'core'=2,'zh'=4,'y'=4] {'x','zl'}, dimensions={0} | all-to-all | bytes 1310720 | tf_op jit(solution)/shard_map/all_to_all | solution.py:22
  120.1 7.8 %all-to-all-start.3 = ((bf16[4,160,128]{2,1,0:T(8,128)(2,1)}), bf16[4,160,128]{2,1,0:T(8,128)(2,1)S(1)}, u32[]{:S(2)}, u32[]{:S(2)}) async-start(bf16[4,160,128]{2,1,0:T(8,128)(2,1)} %broadcast_in_dim.38), calls=%async_computation.3 | async-start | bytes 327680 | tf_op jit(solution)/shard_map/all_to_all | solution.py:22
  128.0 3.3 %collective-permute-start.4 = (bf16[1,80,128]{2,1,0:T(8,128)(2,1)S(1)}, bf16[1,80,128]{2,1,0:T(8,128)(2,1)S(1)}, u32[]{:S(2)}, u32[]{:S(2)}) collective-permute-start(bf16[1,80,128]{2,1,0:T(8,128)(2,1)S(1)} %get-tuple-element.199), channel_id=1, source_target_pairs={{0,1},{1,2},{2,3},{3,4},{4,5},{5,6},{6,7},{7,8},{8,9},{9,10},{10,1... | collective-permute-start | bytes 61448 | tf_op jit(solution)/shard_map/ppermute | solution.py:18
  137.0 6.6 %all-to-all-done.3 = bf16[4,160,128]{2,1,0:T(8,128)(2,1)S(1)} async-done(((bf16[4,160,128]{2,1,0:T(8,128)(2,1)}), bf16[4,160,128]{2,1,0:T(8,128)(2,1)S(1)}, u32[]{:S(2)}, u32[]{:S(2)}) %all-to-all-start.3) | async-done | bytes 163872 | tf_op jit(solution)/shard_map/all_to_all | solution.py:22
  144.4 4.4 %all-to-all-start.4 = ((bf16[4,160,128]{2,1,0:T(8,128)(2,1)}), bf16[4,160,128]{2,1,0:T(8,128)(2,1)S(1)}, u32[]{:S(2)}, u32[]{:S(2)}) async-start(bf16[4,160,128]{2,1,0:T(8,128)(2,1)} %broadcast_in_dim.39), calls=%async_computation.4 | async-start | bytes 327680 | tf_op jit(solution)/shard_map/all_to_all | solution.py:22
  149.0 5.9 %all-to-all-done.4 = bf16[4,160,128]{2,1,0:T(8,128)(2,1)S(1)} async-done(((bf16[4,160,128]{2,1,0:T(8,128)(2,1)}), bf16[4,160,128]{2,1,0:T(8,128)(2,1)S(1)}, u32[]{:S(2)}, u32[]{:S(2)}) %all-to-all-start.4) | async-done | bytes 163872 | tf_op jit(solution)/shard_map/all_to_all | solution.py:22
  155.7 5.4 %all-to-all-start.5 = ((bf16[4,4,160,128]{3,2,1,0:T(8,128)(2,1)}), bf16[4,4,160,128]{3,2,1,0:T(8,128)(2,1)S(1)}, u32[]{:S(2)}, u32[]{:S(2)}) async-start(bf16[4,4,160,128]{3,2,1,0:T(8,128)(2,1)} %broadcast_in_dim.40), calls=%async_computation.5 | async-start | bytes 1310720 | tf_op jit(solution)/shard_map/all_to_all | solution.py:22
  162.3 5.6 %all-to-all-done.5 = bf16[4,4,160,128]{3,2,1,0:T(8,128)(2,1)S(1)} async-done(((bf16[4,4,160,128]{3,2,1,0:T(8,128)(2,1)}), bf16[4,4,160,128]{3,2,1,0:T(8,128)(2,1)S(1)}, u32[]{:S(2)}, u32[]{:S(2)}) %all-to-all-start.5) | async-done | bytes 655392 | tf_op jit(solution)/shard_map/all_to_all | solution.py:22
  168.1 4.8 %all_to_all.41 = bf16[2,4,4,160,128]{4,3,2,1,0:T(8,128)(2,1)S(1)} all-to-all(bf16[2,4,4,160,128]{4,3,2,1,0:T(8,128)(2,1)S(1)} %broadcast_in_dim.41), channel_id=1, replica_groups=mesh['x'=4,'zl'=4,'core'=2,'zh'=4,'y'=4] {'core'}, dimensions={0} | all-to-all | bytes 2621440 | tf_op jit(solution)/shard_map/all_to_all | solution.py:22
  175.3 7.3 %all-to-all-start.7 = ((bf16[4,36,1792]{2,1,0:T(8,128)(2,1)}), bf16[4,36,1792]{2,1,0:T(8,128)(2,1)S(1)}, u32[]{:S(2)}, u32[]{:S(2)}) async-start(bf16[4,36,1792]{2,1,0:T(8,128)(2,1)} %broadcast_in_dim.42), calls=%async_computation.7 | async-start | bytes 1146880 | tf_op jit(solution)/shard_map/all_to_all | solution.py:22
  183.5 9.4 %all-to-all-done.7.got_ref = bf16[4,36,1792]{2,1,0:T(8,128)(2,1)S(1)} async-done(((bf16[4,36,1792]{2,1,0:T(8,128)(2,1)}), bf16[4,36,1792]{2,1,0:T(8,128)(2,1)S(1)}, u32[]{:S(2)}, u32[]{:S(2)}) %all-to-all-start.7) | async-done | bytes 516128 | tf_op jit(solution)/shard_map/all_to_all | solution.py:22
  193.7 1.8 shard_map.151
  195.5 1.8 copy.87
  (248 shorter events, 34.1 us)
Async XLA Ops:
  7.2 22.9 %copy-start = (f32[1,128,128]{2,1,0:T(8,128)S(1)}, f32[1,128,128]{2,1,0:T(8,128)}, u32[]{:S(2)}) copy-start(f32[1,128,128]{2,1,0:T(8,128)} %param.21) | copy-start | bytes 196612
  7.2 112.3 %all-gather.2.cloned.1.call-start = ((), (), s32[]{:S(2)}) async-start(), calls=%async_computation.8 | async-start | bytes 1462272 | tf_op jit(solution)/shard_map/all_gather | solution.py:304
  10.5 19.5 %copy-start.18 = (pred[8,3]{0,1:T(4,128)(4,1)S(1)}, pred[8,3]{0,1:T(4,128)(4,1)}, u32[]{:S(2)}) copy-start(pred[8,3]{0,1:T(4,128)(4,1)} %constant.130.clone.1) | copy-start | bytes 76
  10.5 27.9 %collective-permute-start.1 = (bf16[7,80,128]{2,1,0:T(8,128)(2,1)}, bf16[7,80,128]{2,1,0:T(8,128)(2,1)S(1)}, u32[]{:S(2)}, u32[]{:S(2)}) collective-permute-start(bf16[7,80,128]{2,1,0:T(8,128)(2,1)} %get-tuple-element.43), channel_id=1, source_target_pairs={{0,15},{1,0},{2,1},{3,2},{4,3},{5,4},{6,5},{7,6},{8,7},{9,8},{10,9... | collective-permute-start | bytes 430088 | tf_op jit(solution)/shard_map/ppermute | solution.py:18
  25.8 5.1 %collective-permute-start = (bf16[5,80,128]{2,1,0:T(8,128)(2,1)}, bf16[5,80,128]{2,1,0:T(8,128)(2,1)S(1)}, u32[]{:S(2)}, u32[]{:S(2)}) collective-permute-start(bf16[5,80,128]{2,1,0:T(8,128)(2,1)} %get-tuple-element.42), channel_id=1, source_target_pairs={{0,1},{1,2},{2,3},{3,4},{4,5},{5,6},{6,7},{7,8},{8,9},{9,10},{10,1... | collective-permute-start | bytes 307208 | tf_op jit(solution)/shard_map/ppermute | solution.py:18
  30.6 8.8 %copy-start.5 = (bf16[4,1152,128]{2,1,0:T(8,128)(2,1)S(1)}, bf16[4,1152,128]{2,1,0:T(8,128)(2,1)}, u32[]{:S(2)}) copy-start(bf16[4,1152,128]{2,1,0:T(8,128)(2,1)} %param.18) | copy-start | bytes 3538948
  30.9 142.6 %copy-start.1 = (s32[3]{0:T(128)}, s32[3]{0:T(128)S(1)}, u32[]{:S(2)}) copy-start(s32[3]{0:T(128)S(1)} %pad_add_fusion.place_ref) | copy-start | bytes 40
  30.9 9.4 %copy-start.13 = (bf16[5,80,128]{2,1,0:T(8,128)(2,1)}, bf16[5,80,128]{2,1,0:T(8,128)(2,1)S(1)}, u32[]{:S(2)}) copy-start(bf16[5,80,128]{2,1,0:T(8,128)(2,1)S(1)} %collective-permute-done) | copy-start | bytes 307204
  42.6 14.2 %copy-start.16 = (bf16[3]{0:T(256)(128)(2,1)S(1)}, bf16[3]{0:T(256)(128)(2,1)}, u32[]{:S(2)}) copy-start(bf16[3]{0:T(256)(128)(2,1)} %constant.142.clone) | copy-start | bytes 22
  42.6 14.1 %copy-start.17 = (bf16[3]{0:T(256)(128)(2,1)S(1)}, bf16[3]{0:T(256)(128)(2,1)}, u32[]{:S(2)}) copy-start(bf16[3]{0:T(256)(128)(2,1)} %constant.143.clone) | copy-start | bytes 22
  43.0 13.7 %collective-permute-start.2 = (bf16[2,80,128]{2,1,0:T(8,128)(2,1)S(1)}, bf16[2,80,128]{2,1,0:T(8,128)(2,1)S(1)}, u32[]{:S(2)}, u32[]{:S(2)}) collective-permute-start(bf16[2,80,128]{2,1,0:T(8,128)(2,1)S(1)} %bitcast.372), channel_id=1, source_target_pairs={{0,15},{1,0},{2,1},{3,2},{4,3},{5,4},{6,5},{7,6},{8,7},{9,8},{10,9... | collective-permute-start | bytes 122888 | tf_op jit(solution)/shard_map/ppermute | solution.py:18
  58.0 13.4 %collective-permute-start.3 = (bf16[2,80,128]{2,1,0:T(8,128)(2,1)S(1)}, bf16[2,80,128]{2,1,0:T(8,128)(2,1)S(1)}, u32[]{:S(2)}, u32[]{:S(2)}) collective-permute-start(bf16[2,80,128]{2,1,0:T(8,128)(2,1)S(1)} %bitcast.375), channel_id=1, source_target_pairs={{0,1},{1,2},{2,3},{3,4},{4,5},{5,6},{6,7},{7,8},{8,9},{9,10},{10,1... | collective-permute-start | bytes 122888 | tf_op jit(solution)/shard_map/ppermute | solution.py:18
  60.8 10.9 %copy-start.15 = (f32[160,128]{1,0:T(8,128)S(1)}, f32[160,128]{1,0:T(8,128)}, u32[]{:S(2)}) copy-start(f32[160,128]{1,0:T(8,128)} %fusion.13) | copy-start | bytes 245764
  60.8 14.2 %all-to-all-start = ((bf16[8,256,128]{2,1,0:T(8,128)(2,1)}), bf16[8,256,128]{2,1,0:T(8,128)(2,1)S(1)}, u32[]{:S(2)}, u32[]{:S(2)}) async-start(bf16[8,256,128]{2,1,0:T(8,128)(2,1)} %bitcast.85), calls=%async_computation | async-start | bytes 1048576 | tf_op jit(solution)/shard_map/all_to_all | solution.py:22
  74.9 5.0 %copy-start.7 = (bf16[8,256,128]{2,1,0:T(8,128)(2,1)}, bf16[8,256,128]{2,1,0:T(8,128)(2,1)S(1)}, u32[]{:S(2)}) copy-start(bf16[8,256,128]{2,1,0:T(8,128)(2,1)S(1)} %all-to-all-done) | copy-start | bytes 1572868
  75.8 11.7 %all-to-all-start.1 = ((bf16[8,2,80,128]{3,2,1,0:T(8,128)(2,1)}), bf16[8,2,80,128]{3,2,1,0:T(8,128)(2,1)}, u32[]{:S(2)}, u32[]{:S(2)}) async-start(bf16[8,2,80,128]{3,2,1,0:T(8,128)(2,1)} %bitcast.170), calls=%async_computation.1 | async-start | bytes 655360 | tf_op jit(solution)/shard_map/all_to_all | solution.py:22
  89.0 38.9 %copy-start.11 = (bf16[160,128]{1,0:T(8,128)(2,1)S(1)}, bf16[160,128]{1,0:T(8,128)(2,1)}, u32[]{:S(2)}) copy-start(bf16[160,128]{1,0:T(8,128)(2,1)} %copy-done.10) | copy-start | bytes 122884
  89.0 43.6 %copy-start.8 = (bf16[1,9,128,128]{2,3,1,0:T(8,128)(2,1)S(1)}, bf16[1,9,128,128]{2,3,1,0:T(8,128)(2,1)}, u32[]{:S(2)}) copy-start(bf16[1,9,128,128]{2,3,1,0:T(8,128)(2,1)} %get-tuple-element.68) | copy-start | bytes 884740
  120.1 23.5 %all-to-all-start.3 = ((bf16[4,160,128]{2,1,0:T(8,128)(2,1)}), bf16[4,160,128]{2,1,0:T(8,128)(2,1)S(1)}, u32[]{:S(2)}, u32[]{:S(2)}) async-start(bf16[4,160,128]{2,1,0:T(8,128)(2,1)} %broadcast_in_dim.38), calls=%async_computation.3 | async-start | bytes 327680 | tf_op jit(solution)/shard_map/all_to_all | solution.py:22
  128.0 7.4 %collective-permute-start.4 = (bf16[1,80,128]{2,1,0:T(8,128)(2,1)S(1)}, bf16[1,80,128]{2,1,0:T(8,128)(2,1)S(1)}, u32[]{:S(2)}, u32[]{:S(2)}) collective-permute-start(bf16[1,80,128]{2,1,0:T(8,128)(2,1)S(1)} %get-tuple-element.199), channel_id=1, source_target_pairs={{0,1},{1,2},{2,3},{3,4},{4,5},{5,6},{6,7},{7,8},{8,9},{9,10},{10,1... | collective-permute-start | bytes 61448 | tf_op jit(solution)/shard_map/ppermute | solution.py:18
  131.3 5.7 %collective-permute-start.5 = (bf16[1,80,128]{2,1,0:T(8,128)(2,1)S(1)}, bf16[1,80,128]{2,1,0:T(8,128)(2,1)S(1)}, u32[]{:S(2)}, u32[]{:S(2)}) collective-permute-start(bf16[1,80,128]{2,1,0:T(8,128)(2,1)S(1)} %get-tuple-element.200), channel_id=1, source_target_pairs={{1,0},{2,1},{3,2},{4,3},{5,4},{6,5},{7,6},{8,7},{9,8},{10,9},{11,1... | collective-permute-start | bytes 61448 | tf_op jit(solution)/shard_map/ppermute | solution.py:18
  144.4 10.4 %all-to-all-start.4 = ((bf16[4,160,128]{2,1,0:T(8,128)(2,1)}), bf16[4,160,128]{2,1,0:T(8,128)(2,1)S(1)}, u32[]{:S(2)}, u32[]{:S(2)}) async-start(bf16[4,160,128]{2,1,0:T(8,128)(2,1)} %broadcast_in_dim.39), calls=%async_computation.4 | async-start | bytes 327680 | tf_op jit(solution)/shard_map/all_to_all | solution.py:22
  155.7 12.1 %all-to-all-start.5 = ((bf16[4,4,160,128]{3,2,1,0:T(8,128)(2,1)}), bf16[4,4,160,128]{3,2,1,0:T(8,128)(2,1)S(1)}, u32[]{:S(2)}, u32[]{:S(2)}) async-start(bf16[4,4,160,128]{3,2,1,0:T(8,128)(2,1)} %broadcast_in_dim.40), calls=%async_computation.5 | async-start | bytes 1310720 | tf_op jit(solution)/shard_map/all_to_all | solution.py:22
  175.3 17.6 %all-to-all-start.7 = ((bf16[4,36,1792]{2,1,0:T(8,128)(2,1)}), bf16[4,36,1792]{2,1,0:T(8,128)(2,1)S(1)}, u32[]{:S(2)}, u32[]{:S(2)}) async-start(bf16[4,36,1792]{2,1,0:T(8,128)(2,1)} %broadcast_in_dim.42), calls=%async_computation.7 | async-start | bytes 1146880 | tf_op jit(solution)/shard_map/all_to_all | solution.py:22
  (10 other events, 15.3 us)
Sparse Core Ops, SparseCore 0:
  27.3 83.7 all-gather.1

commit v14 on v11

--- a/solution.py
+++ b/solution.py
@@ -379,21 +379,18 @@
     def beside(table_ref, y, z):
         return jnp.where((table_ref[y] >> 2) == (z ^ 1), 1, 0)
 
-    def across(table_ref, y, z):
-        return jnp.where((table_ref[y] >> 3) == (z >> 1), 0, 1)
-
-    place = jnp.stack([y_id, z_id, dp_id]).astype(jnp.int32)
-    away = choose(for_partner, table, place, local, near)
-    gram, away = lax.optimization_barrier((gram, away))
-    found = choose(in_group, table, place, local, near, paired(away, "y", 1))
     layer_dpre = to_layers(jnp.stack([dpre0, dpre1, dpre2, dpre3[1:3]]))
     parts = all_half(gram, cols, layer_dpre.reshape(-1, chans), core_id)
 
-    parts, found = lax.optimization_barrier((parts, found))
+    place = jnp.stack([y_id, z_id, dp_id]).astype(jnp.int32)
+    parts, local, near = lax.optimization_barrier((parts, local, near))
+    away = choose(for_partner, table, place, local, near)
+    found = choose(in_group, table, place, local, near, paired(away, "y", 1))
     found = choose(beside, table, place, found, paired(found, "zh", 0))
     piece = scatter_sum(parts, ("x", "zl"))
     piece, found = lax.optimization_barrier((piece, found))
-    inverses = choose(across, table, place, found, paired(found, "zh", 1))
+    source = jnp.sum(jnp.where(jnp.arange(num_layers) == y_id, table, 0))
+    inverses = jnp.where((source >> 3) == (z_id >> 1), found, paired(found, "zh", 1))
     held = spread(piece[:, :FAC_ROWS], "y")
     total = exchange(for_groups(table, place, held, piece), "zh")
     total = jnp.sum(total.astype(jnp.float32), axis=0).astype(jnp.bfloat16)

time: 210 us -> 199 us (0.948)
  waiting for transfers between devices: 51 us -> 61.2 us
  blocking collectives: 14.6 us -> 4.89 us
  starting transfers between devices: 100 us -> 90.6 us
    all_to_all x7 -> x8, waiting for transfers between devices: 21.1 us -> 33.4 us  [exchange(): return lax.all_to_all(x, axis, split_axis=0, concat_axis=0, tiled=True)]
    all_to_all x2 -> x1, blocking collectives: 14.6 us -> 4.89 us  [exchange(): return lax.all_to_all(x, axis, split_axis=0, concat_axis=0, tiled=True)]
    ppermute x4, starting transfers between devices: 25.5 us -> 20.6 us  [paired(): lax.ppermute(x, axis, [(i, i ^ 1 if step == 0 else 3 - i) for i in range(...]
    ppermute x6, waiting for transfers between devices: 14.1 us -> 10.1 us  [shifted(): return lax.ppermute(x, OWNER, pairs)]
    all_to_all x7 -> x8, starting transfers between devices: 42.3 us -> 38.6 us  [exchange(): return lax.all_to_all(x, axis, split_axis=0, concat_axis=0, tiled=True)]
    pallas_call x4 -> x3, Pallas kernels: 6.61 us -> 4.96 us  [choose(): pl.pallas_call(kernel, out_shape=jax.ShapeDtypeStruct(arrays[0].shape, ar...]
  transfers between devices with their start and end apart: 17 -> 18, of which waited for: 12 -> 12; matrix products, arithmetic and copies ran while one was open for 6% -> 7% of each run, Pallas kernels for 4% -> 5%
where the time goes in v14:
time: 199 us; the launch traced here: 196 us
  starting transfers between devices  90.6 us (46%)
  waiting for transfers between devices  61.2 us (31%)
  local copies, waits for them, and re-layouts  17 us (9%)
  Pallas kernels  12.3 us (6%)
  blocking collectives  4.89 us (2%)
  other arithmetic  4.19 us (2%)
  matrix products  3.38 us (2%)
  between operations  2.78 us (1%)
    all_to_all x8, starting transfers between devices, exchange(): return lax.all_to_all(x, axis, split_axis=0, concat_axis=0, tiled=True)  38.6 us
    all_to_all x8, waiting for transfers between devices, exchange(): return lax.all_to_all(x, axis, split_axis=0, concat_axis=0, tiled=True)  33.4 us
    ppermute x6, starting transfers between devices, shifted(): return lax.ppermute(x, OWNER, pairs)  31.4 us
    ppermute x4, starting transfers between devices, paired(): lax.ppermute(x, axis, [(i, i ^ 1 if step == 0 else 3 - i) for i in range(...  20.6 us
    ppermute x4, waiting for transfers between devices, paired(): lax.ppermute(x, axis, [(i, i ^ 1 if step == 0 else 3 - i) for i in range(...  17.7 us
    ppermute x6, waiting for transfers between devices, shifted(): return lax.ppermute(x, OWNER, pairs)  10.1 us
    unnamed x138, local copies, waits for them, and re-layouts  6.56 us
    pallas_call x3, Pallas kernels, choose(): pl.pallas_call(kernel, out_shape=jax.ShapeDtypeStruct(arrays[0].shape, ar...  4.96 us
  transfers between devices with their start and end apart: 18, of which 12 were waited for; matrix products, arithmetic and copies ran while one was open for 7% of the time, Pallas kernels for 5%

profile of v14, /device:TPU:6, one launch (start us, length us, event | category | flops | bytes accessed | tf_op | source)
XLA Modules:
  0.0 196.4 jit_solution(11494829434480682804)
XLA Ops:
  2.3 15.2 %collective-permute-start.1 = (bf16[7,80,128]{2,1,0:T(8,128)(2,1)}, bf16[7,80,128]{2,1,0:T(8,128)(2,1)S(1)}, u32[]{:S(2)}, u32[]{:S(2)}) collective-permute-start(bf16[7,80,128]{2,1,0:T(8,128)(2,1)} %get-tuple-element.41), channel_id=1, source_target_pairs={{0,15},{1,0},{2,1},{3,2},{4,3},{5,4},{6,5},{7,6},{8,7},{9,8},{10,9... | collective-permute-start | bytes 430088 | tf_op jit(solution)/shard_map/ppermute | solution.py:18
  23.3 6.8 %collective-permute-done.1 = bf16[7,80,128]{2,1,0:T(8,128)(2,1)S(1)} collective-permute-done((bf16[7,80,128]{2,1,0:T(8,128)(2,1)}, bf16[7,80,128]{2,1,0:T(8,128)(2,1)S(1)}, u32[]{:S(2)}, u32[]{:S(2)}) %collective-permute-start.1) | collective-permute-done | bytes 143392 | tf_op jit(solution)/shard_map/ppermute | solution.py:18
  33.5 10.3 %collective-permute-start.2 = (bf16[2,80,128]{2,1,0:T(8,128)(2,1)S(1)}, bf16[2,80,128]{2,1,0:T(8,128)(2,1)S(1)}, u32[]{:S(2)}, u32[]{:S(2)}) collective-permute-start(bf16[2,80,128]{2,1,0:T(8,128)(2,1)S(1)} %bitcast.367), channel_id=1, source_target_pairs={{0,15},{1,0},{2,1},{3,2},{4,3},{5,4},{6,5},{7,6},{8,7},{9,8},{10,9... | collective-permute-start | bytes 122888 | tf_op jit(solution)/shard_map/ppermute | solution.py:18
  49.5 3.5 %all-to-all-start = ((bf16[8,3,80,128]{3,2,1,0:T(8,128)(2,1)}), bf16[8,3,80,128]{3,2,1,0:T(8,128)(2,1)S(1)}, u32[]{:S(2)}, u32[]{:S(2)}) async-start(bf16[8,3,80,128]{3,2,1,0:T(8,128)(2,1)} %bitcast.82), calls=%async_computation | async-start | bytes 983040 | tf_op jit(solution)/shard_map/all_to_all | solution.py:26
  53.0 3.8 %collective-permute-start.4 = (bf16[452,128]{1,0:T(8,128)(2,1)}, bf16[452,128]{1,0:T(8,128)(2,1)}, u32[]{:S(2)}, u32[]{:S(2)}) collective-permute-start(bf16[452,128]{1,0:T(8,128)(2,1)} %pad_maximum_fusion.6.refs_0_), channel_id=1, source_target_pairs={{0,1},{1,0},{2,3},{3,2},{4,5},{5,4},{6,7},{7,6},{8,9},{9,8},{10,11... | collective-permute-start | bytes 347144 | tf_op jit(solution)/shard_map/ppermute | solution.py:22
  60.0 2.7 %all-to-all-done = bf16[8,3,80,128]{3,2,1,0:T(8,128)(2,1)S(1)} async-done(((bf16[8,3,80,128]{3,2,1,0:T(8,128)(2,1)}), bf16[8,3,80,128]{3,2,1,0:T(8,128)(2,1)S(1)}, u32[]{:S(2)}, u32[]{:S(2)}) %all-to-all-start) | async-done | bytes 491552 | tf_op jit(solution)/shard_map/all_to_all | solution.py:26
  63.5 4.1 %all-to-all-start.1 = ((bf16[8,2,80,128]{3,2,1,0:T(8,128)(2,1)}), bf16[8,2,80,128]{3,2,1,0:T(8,128)(2,1)}, u32[]{:S(2)}, u32[]{:S(2)}) async-start(bf16[8,2,80,128]{3,2,1,0:T(8,128)(2,1)} %bitcast.165), calls=%async_computation.1 | async-start | bytes 655360 | tf_op jit(solution)/shard_map/all_to_all | solution.py:26
  71.0 4.2 %all-to-all-done.1 = bf16[8,2,80,128]{3,2,1,0:T(8,128)(2,1)} async-done(((bf16[8,2,80,128]{3,2,1,0:T(8,128)(2,1)}), bf16[8,2,80,128]{3,2,1,0:T(8,128)(2,1)}, u32[]{:S(2)}, u32[]{:S(2)}) %all-to-all-start.1) | async-done | bytes 327712 | tf_op jit(solution)/shard_map/all_to_all | solution.py:26
  77.7 4.8 %all-to-all-start.2 = ((bf16[16,1,176,128]{3,2,1,0:T(8,128)(2,1)}), bf16[16,1,176,128]{3,2,1,0:T(8,128)(2,1)S(1)}, u32[]{:S(2)}, u32[]{:S(2)}) async-start(bf16[16,1,176,128]{3,2,1,0:T(8,128)(2,1)} %bitcast.322), calls=%async_computation.2 | async-start | bytes 1441792 | tf_op jit(solution)/shard_map/all_to_all | solution.py:26
  84.7 3.7 %collective-permute-start.5 = (bf16[452,128]{1,0:T(8,128)(2,1)}, bf16[452,128]{1,0:T(8,128)(2,1)S(1)}, u32[]{:S(2)}, u32[]{:S(2)}) collective-permute-start(bf16[452,128]{1,0:T(8,128)(2,1)} %shard_map.150), channel_id=1, source_target_pairs={{0,3},{1,2},{2,1},{3,0},{4,7},{5,6},{6,5},{7,4},{8,11},{9,10},{10,... | collective-permute-start | bytes 347144 | tf_op jit(solution)/shard_map/ppermute | solution.py:22
  88.4 4.4 %collective-permute-done.5.refs_2_ = bf16[452,128]{1,0:T(8,128)(2,1)S(1)} collective-permute-done((bf16[452,128]{1,0:T(8,128)(2,1)}, bf16[452,128]{1,0:T(8,128)(2,1)S(1)}, u32[]{:S(2)}, u32[]{:S(2)}) %collective-permute-start.5) | collective-permute-done | bytes 115744 | tf_op jit(solution)/shard_map/ppermute | solution.py:22
  95.2 8.8 %collective-permute-start.6 = (bf16[452,128]{1,0:T(8,128)(2,1)}, bf16[452,128]{1,0:T(8,128)(2,1)S(1)}, u32[]{:S(2)}, u32[]{:S(2)}) collective-permute-start(bf16[452,128]{1,0:T(8,128)(2,1)} %shard_map.151.refs_0_), channel_id=1, source_target_pairs={{0,4},{4,0},{8,12},{12,8},{1,5},{5,1},{9,13},{13,9},{2,6},{6,2},{1... | collective-permute-start | bytes 347144 | tf_op jit(solution)/shard_map/ppermute | solution.py:22
  106.7 7.0 %collective-permute-done.6.refs_1_ = bf16[452,128]{1,0:T(8,128)(2,1)S(1)} collective-permute-done((bf16[452,128]{1,0:T(8,128)(2,1)}, bf16[452,128]{1,0:T(8,128)(2,1)S(1)}, u32[]{:S(2)}, u32[]{:S(2)}) %collective-permute-start.6) | collective-permute-done | bytes 115744 | tf_op jit(solution)/shard_map/ppermute | solution.py:22
  116.8 3.5 %all-to-all-start.3 = ((bf16[4,1,128,128]{3,2,1,0:T(8,128)(2,1)}), bf16[4,1,128,128]{3,2,1,0:T(8,128)(2,1)S(1)}, u32[]{:S(2)}, u32[]{:S(2)}) async-start(bf16[4,1,128,128]{3,2,1,0:T(8,128)(2,1)} %broadcast_in_dim.84), calls=%async_computation.3 | async-start | bytes 262144 | tf_op jit(solution)/shard_map/all_to_all | solution.py:26
  121.8 4.2 %all-to-all-done.3.held_ref = bf16[4,1,128,128]{3,2,1,0:T(8,128)(2,1)S(1)} async-done(((bf16[4,1,128,128]{3,2,1,0:T(8,128)(2,1)}), bf16[4,1,128,128]{3,2,1,0:T(8,128)(2,1)S(1)}, u32[]{:S(2)}, u32[]{:S(2)}) %all-to-all-start.3) | async-done | bytes 131104 | tf_op jit(solution)/shard_map/all_to_all | solution.py:26
  128.3 11.4 %all-to-all-start.4 = ((bf16[4,1,176,128]{3,2,1,0:T(8,128)(2,1)}), bf16[4,1,176,128]{3,2,1,0:T(8,128)(2,1)S(1)}, u32[]{:S(2)}, u32[]{:S(2)}) async-start(bf16[4,1,176,128]{3,2,1,0:T(8,128)(2,1)} %shard_map.153), calls=%async_computation.4 | async-start | bytes 360448 | tf_op jit(solution)/shard_map/all_to_all | solution.py:26
  139.8 14.0 %all-to-all-done.4 = bf16[4,1,176,128]{3,2,1,0:T(8,128)(2,1)S(1)} async-done(((bf16[4,1,176,128]{3,2,1,0:T(8,128)(2,1)}), bf16[4,1,176,128]{3,2,1,0:T(8,128)(2,1)S(1)}, u32[]{:S(2)}, u32[]{:S(2)}) %all-to-all-start.4) | async-done | bytes 180256 | tf_op jit(solution)/shard_map/all_to_all | solution.py:26
  154.6 3.4 %all-to-all-start.5 = ((bf16[4,1,176,128]{3,2,1,0:T(8,128)(2,1)}), bf16[4,1,176,128]{3,2,1,0:T(8,128)(2,1)S(1)}, u32[]{:S(2)}, u32[]{:S(2)}) async-start(bf16[4,1,176,128]{3,2,1,0:T(8,128)(2,1)} %broadcast_in_dim.85), calls=%async_computation.5 | async-start | bytes 360448 | tf_op jit(solution)/shard_map/all_to_all | solution.py:26
  158.0 6.0 %all-to-all-done.5 = bf16[4,1,176,128]{3,2,1,0:T(8,128)(2,1)S(1)} async-done(((bf16[4,1,176,128]{3,2,1,0:T(8,128)(2,1)}), bf16[4,1,176,128]{3,2,1,0:T(8,128)(2,1)S(1)}, u32[]{:S(2)}, u32[]{:S(2)}) %all-to-all-start.5) | async-done | bytes 180256 | tf_op jit(solution)/shard_map/all_to_all | solution.py:26
  165.0 4.7 %all-to-all-start.6 = ((bf16[4,4,1,176,128]{4,3,1,2,0:T(8,128)(2,1)}), bf16[4,4,1,176,128]{4,3,1,2,0:T(8,128)(2,1)S(1)}, u32[]{:S(2)}, u32[]{:S(2)}) async-start(bf16[4,4,1,176,128]{4,3,1,2,0:T(8,128)(2,1)} %broadcast_in_dim.87), calls=%async_computation.6 | async-start | bytes 1441792 | tf_op jit(solution)/shard_map/all_to_all | solution.py:26
  169.7 4.4 %collective-permute-start.7 = (bf16[452,128]{1,0:T(8,128)(2,1)S(1)}, bf16[452,128]{1,0:T(8,128)(2,1)S(1)}, u32[]{:S(2)}, u32[]{:S(2)}) collective-permute-start(bf16[452,128]{1,0:T(8,128)(2,1)S(1)} %copy-done.10), channel_id=1, source_target_pairs={{0,12},{4,8},{8,4},{12,0},{1,13},{5,9},{9,5},{13,1},{2,14},{6,10},... | collective-permute-start | bytes 347144 | tf_op jit(solution)/shard_map/ppermute | solution.py:22
  174.2 6.3 %collective-permute-done.7 = bf16[452,128]{1,0:T(8,128)(2,1)S(1)} collective-permute-done((bf16[452,128]{1,0:T(8,128)(2,1)S(1)}, bf16[452,128]{1,0:T(8,128)(2,1)S(1)}, u32[]{:S(2)}, u32[]{:S(2)}) %collective-permute-start.7) | collective-permute-done | bytes 115744 | tf_op jit(solution)/shard_map/ppermute | solution.py:22
  180.9 4.9 %all_to_all.45 = bf16[2,4,4,1,176,128]{5,4,2,1,3,0:T(8,128)(2,1)S(1)} all-to-all(bf16[2,4,4,1,176,128]{5,4,2,1,3,0:T(8,128)(2,1)S(1)} %broadcast_in_dim.89), channel_id=1, replica_groups=mesh['x'=4,'zl'=4,'core'=2,'zh'=4,'y'=4] {'core'}, dimensions={0} | all-to-all | bytes 2883584 | tf_op jit(solution)/shard_map/all_to_all | solution.py:26
  187.0 3.3 %all-to-all-start.8 = ((bf16[4,36,128]{2,1,0:T(8,128)(2,1)}), bf16[4,36,128]{2,1,0:T(8,128)(2,1)S(1)}, u32[]{:S(2)}, u32[]{:S(2)}) async-start(bf16[4,36,128]{2,1,0:T(8,128)(2,1)} %broadcast_in_dim.90), calls=%async_computation.8 | async-start | bytes 81920 | tf_op jit(solution)/shard_map/all_to_all | solution.py:26
  (258 shorter events, 48.5 us)
Async XLA Ops:
  0.6 21.1 %copy-start.17 = (f32[1,128,128]{2,1,0:T(8,128)S(1)}, f32[1,128,128]{2,1,0:T(8,128)}, u32[]{:S(2)}) copy-start(f32[1,128,128]{2,1,0:T(8,128)} %param.21) | copy-start | bytes 196612
  0.6 21.1 %copy-start.20 = (pred[8,3]{0,1:T(4,128)(4,1)S(1)}, pred[8,3]{0,1:T(4,128)(4,1)}, u32[]{:S(2)}) copy-start(pred[8,3]{0,1:T(4,128)(4,1)} %constant.113.clone.1) | copy-start | bytes 76
  2.3 27.8 %collective-permute-start.1 = (bf16[7,80,128]{2,1,0:T(8,128)(2,1)}, bf16[7,80,128]{2,1,0:T(8,128)(2,1)S(1)}, u32[]{:S(2)}, u32[]{:S(2)}) collective-permute-start(bf16[7,80,128]{2,1,0:T(8,128)(2,1)} %get-tuple-element.41), channel_id=1, source_target_pairs={{0,15},{1,0},{2,1},{3,2},{4,3},{5,4},{6,5},{7,6},{8,7},{9,8},{10,9... | collective-permute-start | bytes 430088 | tf_op jit(solution)/shard_map/ppermute | solution.py:18
  17.5 5.8 %collective-permute-start = (bf16[5,80,128]{2,1,0:T(8,128)(2,1)}, bf16[5,80,128]{2,1,0:T(8,128)(2,1)S(1)}, u32[]{:S(2)}, u32[]{:S(2)}) collective-permute-start(bf16[5,80,128]{2,1,0:T(8,128)(2,1)} %get-tuple-element.40), channel_id=1, source_target_pairs={{0,1},{1,2},{2,3},{3,4},{4,5},{5,6},{6,7},{7,8},{8,9},{9,10},{10,1... | collective-permute-start | bytes 307208 | tf_op jit(solution)/shard_map/ppermute | solution.py:18
  33.1 12.4 %copy-start.18 = (bf16[3]{0:T(256)(128)(2,1)S(1)}, bf16[3]{0:T(256)(128)(2,1)}, u32[]{:S(2)}) copy-start(bf16[3]{0:T(256)(128)(2,1)} %constant.123.clone) | copy-start | bytes 22
  33.1 12.3 %copy-start.19 = (bf16[3]{0:T(256)(128)(2,1)S(1)}, bf16[3]{0:T(256)(128)(2,1)}, u32[]{:S(2)}) copy-start(bf16[3]{0:T(256)(128)(2,1)} %constant.124.clone) | copy-start | bytes 22
  33.5 11.9 %collective-permute-start.2 = (bf16[2,80,128]{2,1,0:T(8,128)(2,1)S(1)}, bf16[2,80,128]{2,1,0:T(8,128)(2,1)S(1)}, u32[]{:S(2)}, u32[]{:S(2)}) collective-permute-start(bf16[2,80,128]{2,1,0:T(8,128)(2,1)S(1)} %bitcast.367), channel_id=1, source_target_pairs={{0,15},{1,0},{2,1},{3,2},{4,3},{5,4},{6,5},{7,6},{8,7},{9,8},{10,9... | collective-permute-start | bytes 122888 | tf_op jit(solution)/shard_map/ppermute | solution.py:18
  46.7 12.7 %collective-permute-start.3 = (bf16[2,80,128]{2,1,0:T(8,128)(2,1)S(1)}, bf16[2,80,128]{2,1,0:T(8,128)(2,1)S(1)}, u32[]{:S(2)}, u32[]{:S(2)}) collective-permute-start(bf16[2,80,128]{2,1,0:T(8,128)(2,1)S(1)} %bitcast.370), channel_id=1, source_target_pairs={{0,1},{1,2},{2,3},{3,4},{4,5},{5,6},{6,7},{7,8},{8,9},{9,10},{10,1... | collective-permute-start | bytes 122888 | tf_op jit(solution)/shard_map/ppermute | solution.py:18
  49.5 13.2 %all-to-all-start = ((bf16[8,3,80,128]{3,2,1,0:T(8,128)(2,1)}), bf16[8,3,80,128]{3,2,1,0:T(8,128)(2,1)S(1)}, u32[]{:S(2)}, u32[]{:S(2)}) async-start(bf16[8,3,80,128]{3,2,1,0:T(8,128)(2,1)} %bitcast.82), calls=%async_computation | async-start | bytes 983040 | tf_op jit(solution)/shard_map/all_to_all | solution.py:26
  53.0 24.7 %collective-permute-start.4 = (bf16[452,128]{1,0:T(8,128)(2,1)}, bf16[452,128]{1,0:T(8,128)(2,1)}, u32[]{:S(2)}, u32[]{:S(2)}) collective-permute-start(bf16[452,128]{1,0:T(8,128)(2,1)} %pad_maximum_fusion.6.refs_0_), channel_id=1, source_target_pairs={{0,1},{1,0},{2,3},{3,2},{4,5},{5,4},{6,7},{7,6},{8,9},{9,8},{10,11... | collective-permute-start | bytes 347144 | tf_op jit(solution)/shard_map/ppermute | solution.py:22
  63.5 11.7 %all-to-all-start.1 = ((bf16[8,2,80,128]{3,2,1,0:T(8,128)(2,1)}), bf16[8,2,80,128]{3,2,1,0:T(8,128)(2,1)}, u32[]{:S(2)}, u32[]{:S(2)}) async-start(bf16[8,2,80,128]{3,2,1,0:T(8,128)(2,1)} %bitcast.165), calls=%async_computation.1 | async-start | bytes 655360 | tf_op jit(solution)/shard_map/all_to_all | solution.py:26
  77.7 38.3 %all-to-all-start.2 = ((bf16[16,1,176,128]{3,2,1,0:T(8,128)(2,1)}), bf16[16,1,176,128]{3,2,1,0:T(8,128)(2,1)S(1)}, u32[]{:S(2)}, u32[]{:S(2)}) async-start(bf16[16,1,176,128]{3,2,1,0:T(8,128)(2,1)} %bitcast.322), calls=%async_computation.2 | async-start | bytes 1441792 | tf_op jit(solution)/shard_map/all_to_all | solution.py:26
  82.5 37.8 %copy-start.2 = (s32[4]{0:T(128)S(1)}, s32[4]{0:T(128)}, u32[]{:S(2)}) copy-start(s32[4]{0:T(128)} %table_ref.9) | copy-start | bytes 52
  82.5 38.4 %copy-start.7 = (bf16[1,9,128,128]{2,3,1,0:T(8,128)(2,1)S(1)}, bf16[1,9,128,128]{2,3,1,0:T(8,128)(2,1)}, u32[]{:S(2)}) copy-start(bf16[1,9,128,128]{2,3,1,0:T(8,128)(2,1)} %get-tuple-element.68) | copy-start | bytes 884740
  84.7 8.1 %collective-permute-start.5 = (bf16[452,128]{1,0:T(8,128)(2,1)}, bf16[452,128]{1,0:T(8,128)(2,1)S(1)}, u32[]{:S(2)}, u32[]{:S(2)}) collective-permute-start(bf16[452,128]{1,0:T(8,128)(2,1)} %shard_map.150), channel_id=1, source_target_pairs={{0,3},{1,2},{2,1},{3,0},{4,7},{5,6},{6,5},{7,4},{8,11},{9,10},{10,... | collective-permute-start | bytes 347144 | tf_op jit(solution)/shard_map/ppermute | solution.py:22
  95.2 18.5 %collective-permute-start.6 = (bf16[452,128]{1,0:T(8,128)(2,1)}, bf16[452,128]{1,0:T(8,128)(2,1)S(1)}, u32[]{:S(2)}, u32[]{:S(2)}) collective-permute-start(bf16[452,128]{1,0:T(8,128)(2,1)} %shard_map.151.refs_0_), channel_id=1, source_target_pairs={{0,4},{4,0},{8,12},{12,8},{1,5},{5,1},{9,13},{13,9},{2,6},{6,2},{1... | collective-permute-start | bytes 347144 | tf_op jit(solution)/shard_map/ppermute | solution.py:22
  104.0 35.7 %collective-permute-start.8 = (bf16[1,80,128]{2,1,0:T(8,128)(2,1)S(1)}, bf16[1,80,128]{2,1,0:T(8,128)(2,1)S(1)}, u32[]{:S(2)}, u32[]{:S(2)}) collective-permute-start(bf16[1,80,128]{2,1,0:T(8,128)(2,1)S(1)} %get-tuple-element.199), channel_id=1, source_target_pairs={{0,1},{1,2},{2,3},{3,4},{4,5},{5,6},{6,7},{7,8},{8,9},{9,10},{10,1... | collective-permute-start | bytes 61448 | tf_op jit(solution)/shard_map/ppermute | solution.py:18
  105.4 34.3 %collective-permute-start.9 = (bf16[1,80,128]{2,1,0:T(8,128)(2,1)S(1)}, bf16[1,80,128]{2,1,0:T(8,128)(2,1)S(1)}, u32[]{:S(2)}, u32[]{:S(2)}) collective-permute-start(bf16[1,80,128]{2,1,0:T(8,128)(2,1)S(1)} %get-tuple-element.200), channel_id=1, source_target_pairs={{1,0},{2,1},{3,2},{4,3},{5,4},{6,5},{7,6},{8,7},{9,8},{10,9},{11,1... | collective-permute-start | bytes 61448 | tf_op jit(solution)/shard_map/ppermute | solution.py:18
  116.8 9.3 %all-to-all-start.3 = ((bf16[4,1,128,128]{3,2,1,0:T(8,128)(2,1)}), bf16[4,1,128,128]{3,2,1,0:T(8,128)(2,1)S(1)}, u32[]{:S(2)}, u32[]{:S(2)}) async-start(bf16[4,1,128,128]{3,2,1,0:T(8,128)(2,1)} %broadcast_in_dim.84), calls=%async_computation.3 | async-start | bytes 262144 | tf_op jit(solution)/shard_map/all_to_all | solution.py:26
  128.3 25.5 %all-to-all-start.4 = ((bf16[4,1,176,128]{3,2,1,0:T(8,128)(2,1)}), bf16[4,1,176,128]{3,2,1,0:T(8,128)(2,1)S(1)}, u32[]{:S(2)}, u32[]{:S(2)}) async-start(bf16[4,1,176,128]{3,2,1,0:T(8,128)(2,1)} %shard_map.153), calls=%async_computation.4 | async-start | bytes 360448 | tf_op jit(solution)/shard_map/all_to_all | solution.py:26
  154.6 9.4 %all-to-all-start.5 = ((bf16[4,1,176,128]{3,2,1,0:T(8,128)(2,1)}), bf16[4,1,176,128]{3,2,1,0:T(8,128)(2,1)S(1)}, u32[]{:S(2)}, u32[]{:S(2)}) async-start(bf16[4,1,176,128]{3,2,1,0:T(8,128)(2,1)} %broadcast_in_dim.85), calls=%async_computation.5 | async-start | bytes 360448 | tf_op jit(solution)/shard_map/all_to_all | solution.py:26
  165.0 15.7 %all-to-all-start.6 = ((bf16[4,4,1,176,128]{4,3,1,2,0:T(8,128)(2,1)}), bf16[4,4,1,176,128]{4,3,1,2,0:T(8,128)(2,1)S(1)}, u32[]{:S(2)}, u32[]{:S(2)}) async-start(bf16[4,4,1,176,128]{4,3,1,2,0:T(8,128)(2,1)} %broadcast_in_dim.87), calls=%async_computation.6 | async-start | bytes 1441792 | tf_op jit(solution)/shard_map/all_to_all | solution.py:26
  169.7 10.7 %collective-permute-start.7 = (bf16[452,128]{1,0:T(8,128)(2,1)S(1)}, bf16[452,128]{1,0:T(8,128)(2,1)S(1)}, u32[]{:S(2)}, u32[]{:S(2)}) collective-permute-start(bf16[452,128]{1,0:T(8,128)(2,1)S(1)} %copy-done.10), channel_id=1, source_target_pairs={{0,12},{4,8},{8,4},{12,0},{1,13},{5,9},{9,5},{13,1},{2,14},{6,10},... | collective-permute-start | bytes 347144 | tf_op jit(solution)/shard_map/ppermute | solution.py:22
  187.0 8.7 %all-to-all-start.8 = ((bf16[4,36,128]{2,1,0:T(8,128)(2,1)}), bf16[4,36,128]{2,1,0:T(8,128)(2,1)S(1)}, u32[]{:S(2)}, u32[]{:S(2)}) async-start(bf16[4,36,128]{2,1,0:T(8,128)(2,1)} %broadcast_in_dim.90), calls=%async_computation.8 | async-start | bytes 81920 | tf_op jit(solution)/shard_map/all_to_all | solution.py:26
  (17 other events, 67.2 us)

commit v15 on v14

--- a/solution.py
+++ b/solution.py
@@ -386,9 +386,10 @@
     parts, local, near = lax.optimization_barrier((parts, local, near))
     away = choose(for_partner, table, place, local, near)
     found = choose(in_group, table, place, local, near, paired(away, "y", 1))
-    found = choose(beside, table, place, found, paired(found, "zh", 0))
+    other = paired(found, "zh", 0)
     piece = scatter_sum(parts, ("x", "zl"))
-    piece, found = lax.optimization_barrier((piece, found))
+    piece, other = lax.optimization_barrier((piece, other))
+    found = choose(beside, table, place, found, other)
     source = jnp.sum(jnp.where(jnp.arange(num_layers) == y_id, table, 0))
     inverses = jnp.where((source >> 3) == (z_id >> 1), found, paired(found, "zh", 1))
     held = spread(piece[:, :FAC_ROWS], "y")

time: 199 us -> 199 us (level)
    unnamed x138 -> x136, local copies, waits for them, and re-layouts: 6.56 us -> 5.92 us
  transfers between devices with their start and end apart: 18 -> 18, of which waited for: 12 -> 12; matrix products, arithmetic and copies ran while one was open for 7% -> 8% of each run, Pallas kernels for 5% -> 5%
where the time goes in v15:
time: 199 us; the launch traced here: 197 us
  starting transfers between devices  90.7 us (46%)
  waiting for transfers between devices  61.6 us (31%)
  local copies, waits for them, and re-layouts  16.4 us (8%)
  Pallas kernels  12.3 us (6%)
  other arithmetic  5.16 us (3%)
  blocking collectives  4.89 us (2%)
  matrix products  3.37 us (2%)
  between operations  2.76 us (1%)
    all_to_all x8, starting transfers between devices, exchange(): return lax.all_to_all(x, axis, split_axis=0, concat_axis=0, tiled=True)  38.8 us
    all_to_all x8, waiting for transfers between devices, exchange(): return lax.all_to_all(x, axis, split_axis=0, concat_axis=0, tiled=True)  33.6 us
    ppermute x6, starting transfers between devices, shifted(): return lax.ppermute(x, OWNER, pairs)  31.4 us
    ppermute x4, starting transfers between devices, paired(): lax.ppermute(x, axis, [(i, i ^ 1 if step == 0 else 3 - i) for i in range(...  20.5 us
    ppermute x4, waiting for transfers between devices, paired(): lax.ppermute(x, axis, [(i, i ^ 1 if step == 0 else 3 - i) for i in range(...  17.9 us
    ppermute x6, waiting for transfers between devices, shifted(): return lax.ppermute(x, OWNER, pairs)  10.1 us
    unnamed x136, local copies, waits for them, and re-layouts  5.92 us
    pallas_call x3, Pallas kernels, choose(): pl.pallas_call(kernel, out_shape=jax.ShapeDtypeStruct(arrays[0].shape, ar...  4.95 us
  transfers between devices with their start and end apart: 18, of which 12 were waited for; matrix products, arithmetic and copies ran while one was open for 8% of the time, Pallas kernels for 5%

profile of v15, /device:TPU:6, one launch (start us, length us, event | category | flops | bytes accessed | tf_op | source)
XLA Modules:
  0.0 197.2 jit_solution(3568933995718806723)
XLA Ops:
  2.3 15.2 %collective-permute-start.1 = (bf16[7,80,128]{2,1,0:T(8,128)(2,1)}, bf16[7,80,128]{2,1,0:T(8,128)(2,1)S(1)}, u32[]{:S(2)}, u32[]{:S(2)}) collective-permute-start(bf16[7,80,128]{2,1,0:T(8,128)(2,1)} %get-tuple-element.41), channel_id=1, source_target_pairs={{0,15},{1,0},{2,1},{3,2},{4,3},{5,4},{6,5},{7,6},{8,7},{9,8},{10,9... | collective-permute-start | bytes 430088 | tf_op jit(solution)/shard_map/ppermute | solution.py:18
  23.3 6.8 %collective-permute-done.1 = bf16[7,80,128]{2,1,0:T(8,128)(2,1)S(1)} collective-permute-done((bf16[7,80,128]{2,1,0:T(8,128)(2,1)}, bf16[7,80,128]{2,1,0:T(8,128)(2,1)S(1)}, u32[]{:S(2)}, u32[]{:S(2)}) %collective-permute-start.1) | collective-permute-done | bytes 143392 | tf_op jit(solution)/shard_map/ppermute | solution.py:18
  33.5 10.3 %collective-permute-start.2 = (bf16[2,80,128]{2,1,0:T(8,128)(2,1)S(1)}, bf16[2,80,128]{2,1,0:T(8,128)(2,1)S(1)}, u32[]{:S(2)}, u32[]{:S(2)}) collective-permute-start(bf16[2,80,128]{2,1,0:T(8,128)(2,1)S(1)} %bitcast.367), channel_id=1, source_target_pairs={{0,15},{1,0},{2,1},{3,2},{4,3},{5,4},{6,5},{7,6},{8,7},{9,8},{10,9... | collective-permute-start | bytes 122888 | tf_op jit(solution)/shard_map/ppermute | solution.py:18
  49.5 3.5 %all-to-all-start = ((bf16[8,3,80,128]{3,2,1,0:T(8,128)(2,1)}), bf16[8,3,80,128]{3,2,1,0:T(8,128)(2,1)S(1)}, u32[]{:S(2)}, u32[]{:S(2)}) async-start(bf16[8,3,80,128]{3,2,1,0:T(8,128)(2,1)} %bitcast.85), calls=%async_computation | async-start | bytes 983040 | tf_op jit(solution)/shard_map/all_to_all | solution.py:26
  53.0 3.8 %collective-permute-start.4 = (bf16[452,128]{1,0:T(8,128)(2,1)}, bf16[452,128]{1,0:T(8,128)(2,1)}, u32[]{:S(2)}, u32[]{:S(2)}) collective-permute-start(bf16[452,128]{1,0:T(8,128)(2,1)} %pad_maximum_fusion.6.refs_0_), channel_id=1, source_target_pairs={{0,1},{1,0},{2,3},{3,2},{4,5},{5,4},{6,7},{7,6},{8,9},{9,8},{10,11... | collective-permute-start | bytes 347144 | tf_op jit(solution)/shard_map/ppermute | solution.py:22
  60.0 2.7 %all-to-all-done = bf16[8,3,80,128]{3,2,1,0:T(8,128)(2,1)S(1)} async-done(((bf16[8,3,80,128]{3,2,1,0:T(8,128)(2,1)}), bf16[8,3,80,128]{3,2,1,0:T(8,128)(2,1)S(1)}, u32[]{:S(2)}, u32[]{:S(2)}) %all-to-all-start) | async-done | bytes 491552 | tf_op jit(solution)/shard_map/all_to_all | solution.py:26
  63.5 4.1 %all-to-all-start.1 = ((bf16[8,2,80,128]{3,2,1,0:T(8,128)(2,1)}), bf16[8,2,80,128]{3,2,1,0:T(8,128)(2,1)}, u32[]{:S(2)}, u32[]{:S(2)}) async-start(bf16[8,2,80,128]{3,2,1,0:T(8,128)(2,1)} %bitcast.168), calls=%async_computation.1 | async-start | bytes 655360 | tf_op jit(solution)/shard_map/all_to_all | solution.py:26
  71.0 4.2 %all-to-all-done.1 = bf16[8,2,80,128]{3,2,1,0:T(8,128)(2,1)} async-done(((bf16[8,2,80,128]{3,2,1,0:T(8,128)(2,1)}), bf16[8,2,80,128]{3,2,1,0:T(8,128)(2,1)}, u32[]{:S(2)}, u32[]{:S(2)}) %all-to-all-start.1) | async-done | bytes 327712 | tf_op jit(solution)/shard_map/all_to_all | solution.py:26
  77.7 4.9 %all-to-all-start.2 = ((bf16[16,1,176,128]{3,2,1,0:T(8,128)(2,1)}), bf16[16,1,176,128]{3,2,1,0:T(8,128)(2,1)S(1)}, u32[]{:S(2)}, u32[]{:S(2)}) async-start(bf16[16,1,176,128]{3,2,1,0:T(8,128)(2,1)} %bitcast.322), calls=%async_computation.2 | async-start | bytes 1441792 | tf_op jit(solution)/shard_map/all_to_all | solution.py:26
  84.9 3.7 %collective-permute-start.5 = (bf16[452,128]{1,0:T(8,128)(2,1)}, bf16[452,128]{1,0:T(8,128)(2,1)S(1)}, u32[]{:S(2)}, u32[]{:S(2)}) collective-permute-start(bf16[452,128]{1,0:T(8,128)(2,1)} %shard_map.150), channel_id=1, source_target_pairs={{0,3},{1,2},{2,1},{3,0},{4,7},{5,6},{6,5},{7,4},{8,11},{9,10},{10,... | collective-permute-start | bytes 347144 | tf_op jit(solution)/shard_map/ppermute | solution.py:22
  88.6 4.4 %collective-permute-done.5.refs_2_ = bf16[452,128]{1,0:T(8,128)(2,1)S(1)} collective-permute-done((bf16[452,128]{1,0:T(8,128)(2,1)}, bf16[452,128]{1,0:T(8,128)(2,1)S(1)}, u32[]{:S(2)}, u32[]{:S(2)}) %collective-permute-start.5) | collective-permute-done | bytes 115744 | tf_op jit(solution)/shard_map/ppermute | solution.py:22
  95.4 8.8 %collective-permute-start.6 = (bf16[452,128]{1,0:T(8,128)(2,1)}, bf16[452,128]{1,0:T(8,128)(2,1)S(1)}, u32[]{:S(2)}, u32[]{:S(2)}) collective-permute-start(bf16[452,128]{1,0:T(8,128)(2,1)} %shard_map.151.refs_0_), channel_id=1, source_target_pairs={{0,4},{4,0},{8,12},{12,8},{1,5},{5,1},{9,13},{13,9},{2,6},{6,2},{1... | collective-permute-start | bytes 347144 | tf_op jit(solution)/shard_map/ppermute | solution.py:22
  107.0 6.8 %collective-permute-done.6.refs_1_ = bf16[452,128]{1,0:T(8,128)(2,1)S(1)} collective-permute-done((bf16[452,128]{1,0:T(8,128)(2,1)}, bf16[452,128]{1,0:T(8,128)(2,1)S(1)}, u32[]{:S(2)}, u32[]{:S(2)}) %collective-permute-start.6) | collective-permute-done | bytes 115744 | tf_op jit(solution)/shard_map/ppermute | solution.py:22
  114.5 3.3 %all-to-all-start.3 = ((bf16[4,1,128,128]{3,2,1,0:T(8,128)(2,1)}), bf16[4,1,128,128]{3,2,1,0:T(8,128)(2,1)S(1)}, u32[]{:S(2)}, u32[]{:S(2)}) async-start(bf16[4,1,128,128]{3,2,1,0:T(8,128)(2,1)} %broadcast_in_dim.84), calls=%async_computation.3 | async-start | bytes 262144 | tf_op jit(solution)/shard_map/all_to_all | solution.py:26
  119.4 4.4 %all-to-all-done.3.held_ref = bf16[4,1,128,128]{3,2,1,0:T(8,128)(2,1)S(1)} async-done(((bf16[4,1,128,128]{3,2,1,0:T(8,128)(2,1)}), bf16[4,1,128,128]{3,2,1,0:T(8,128)(2,1)S(1)}, u32[]{:S(2)}, u32[]{:S(2)}) %all-to-all-start.3) | async-done | bytes 131104 | tf_op jit(solution)/shard_map/all_to_all | solution.py:26
  126.1 11.5 %all-to-all-start.4 = ((bf16[4,1,176,128]{3,2,1,0:T(8,128)(2,1)}), bf16[4,1,176,128]{3,2,1,0:T(8,128)(2,1)S(1)}, u32[]{:S(2)}, u32[]{:S(2)}) async-start(bf16[4,1,176,128]{3,2,1,0:T(8,128)(2,1)} %shard_map.153), calls=%async_computation.4 | async-start | bytes 360448 | tf_op jit(solution)/shard_map/all_to_all | solution.py:26
  137.8 14.0 %all-to-all-done.4 = bf16[4,1,176,128]{3,2,1,0:T(8,128)(2,1)S(1)} async-done(((bf16[4,1,176,128]{3,2,1,0:T(8,128)(2,1)}), bf16[4,1,176,128]{3,2,1,0:T(8,128)(2,1)S(1)}, u32[]{:S(2)}, u32[]{:S(2)}) %all-to-all-start.4) | async-done | bytes 180256 | tf_op jit(solution)/shard_map/all_to_all | solution.py:26
  152.6 3.4 %all-to-all-start.5 = ((bf16[4,1,176,128]{3,2,1,0:T(8,128)(2,1)}), bf16[4,1,176,128]{3,2,1,0:T(8,128)(2,1)S(1)}, u32[]{:S(2)}, u32[]{:S(2)}) async-start(bf16[4,1,176,128]{3,2,1,0:T(8,128)(2,1)} %broadcast_in_dim.85), calls=%async_computation.5 | async-start | bytes 360448 | tf_op jit(solution)/shard_map/all_to_all | solution.py:26
  156.0 6.0 %all-to-all-done.5 = bf16[4,1,176,128]{3,2,1,0:T(8,128)(2,1)S(1)} async-done(((bf16[4,1,176,128]{3,2,1,0:T(8,128)(2,1)}), bf16[4,1,176,128]{3,2,1,0:T(8,128)(2,1)S(1)}, u32[]{:S(2)}, u32[]{:S(2)}) %all-to-all-start.5) | async-done | bytes 180256 | tf_op jit(solution)/shard_map/all_to_all | solution.py:26
  163.0 4.9 %all-to-all-start.6 = ((bf16[4,4,1,176,128]{4,3,1,2,0:T(8,128)(2,1)}), bf16[4,4,1,176,128]{4,3,1,2,0:T(8,128)(2,1)S(1)}, u32[]{:S(2)}, u32[]{:S(2)}) async-start(bf16[4,4,1,176,128]{4,3,1,2,0:T(8,128)(2,1)} %broadcast_in_dim.87), calls=%async_computation.6 | async-start | bytes 1441792 | tf_op jit(solution)/shard_map/all_to_all | solution.py:26
  169.5 4.3 %collective-permute-start.7 = (bf16[452,128]{1,0:T(8,128)(2,1)}, bf16[452,128]{1,0:T(8,128)(2,1)S(1)}, u32[]{:S(2)}, u32[]{:S(2)}) collective-permute-start(bf16[452,128]{1,0:T(8,128)(2,1)} %shard_map.152), channel_id=1, source_target_pairs={{0,12},{4,8},{8,4},{12,0},{1,13},{5,9},{9,5},{13,1},{2,14},{6,10},... | collective-permute-start | bytes 347144 | tf_op jit(solution)/shard_map/ppermute | solution.py:22
  173.8 6.6 %collective-permute-done.7 = bf16[452,128]{1,0:T(8,128)(2,1)S(1)} collective-permute-done((bf16[452,128]{1,0:T(8,128)(2,1)}, bf16[452,128]{1,0:T(8,128)(2,1)S(1)}, u32[]{:S(2)}, u32[]{:S(2)}) %collective-permute-start.7) | collective-permute-done | bytes 115744 | tf_op jit(solution)/shard_map/ppermute | solution.py:22
  181.7 4.9 %all_to_all.45 = bf16[2,4,4,1,176,128]{5,4,2,1,3,0:T(8,128)(2,1)S(1)} all-to-all(bf16[2,4,4,1,176,128]{5,4,2,1,3,0:T(8,128)(2,1)S(1)} %broadcast_in_dim.89), channel_id=1, replica_groups=mesh['x'=4,'zl'=4,'core'=2,'zh'=4,'y'=4] {'core'}, dimensions={0} | all-to-all | bytes 2883584 | tf_op jit(solution)/shard_map/all_to_all | solution.py:26
  187.8 3.3 %all-to-all-start.8 = ((bf16[4,36,128]{2,1,0:T(8,128)(2,1)}), bf16[4,36,128]{2,1,0:T(8,128)(2,1)S(1)}, u32[]{:S(2)}, u32[]{:S(2)}) async-start(bf16[4,36,128]{2,1,0:T(8,128)(2,1)} %broadcast_in_dim.90), calls=%async_computation.8 | async-start | bytes 81920 | tf_op jit(solution)/shard_map/all_to_all | solution.py:26
  (256 shorter events, 48.8 us)
Async XLA Ops:
  0.6 21.1 %copy-start.16 = (f32[1,128,128]{2,1,0:T(8,128)S(1)}, f32[1,128,128]{2,1,0:T(8,128)}, u32[]{:S(2)}) copy-start(f32[1,128,128]{2,1,0:T(8,128)} %param.21) | copy-start | bytes 196612
  0.6 21.1 %copy-start.19 = (pred[8,3]{0,1:T(4,128)(4,1)S(1)}, pred[8,3]{0,1:T(4,128)(4,1)}, u32[]{:S(2)}) copy-start(pred[8,3]{0,1:T(4,128)(4,1)} %constant.117.clone.1) | copy-start | bytes 76
  2.3 27.8 %collective-permute-start.1 = (bf16[7,80,128]{2,1,0:T(8,128)(2,1)}, bf16[7,80,128]{2,1,0:T(8,128)(2,1)S(1)}, u32[]{:S(2)}, u32[]{:S(2)}) collective-permute-start(bf16[7,80,128]{2,1,0:T(8,128)(2,1)} %get-tuple-element.41), channel_id=1, source_target_pairs={{0,15},{1,0},{2,1},{3,2},{4,3},{5,4},{6,5},{7,6},{8,7},{9,8},{10,9... | collective-permute-start | bytes 430088 | tf_op jit(solution)/shard_map/ppermute | solution.py:18
  17.5 5.8 %collective-permute-start = (bf16[5,80,128]{2,1,0:T(8,128)(2,1)}, bf16[5,80,128]{2,1,0:T(8,128)(2,1)S(1)}, u32[]{:S(2)}, u32[]{:S(2)}) collective-permute-start(bf16[5,80,128]{2,1,0:T(8,128)(2,1)} %get-tuple-element.40), channel_id=1, source_target_pairs={{0,1},{1,2},{2,3},{3,4},{4,5},{5,6},{6,7},{7,8},{8,9},{9,10},{10,1... | collective-permute-start | bytes 307208 | tf_op jit(solution)/shard_map/ppermute | solution.py:18
  33.5 11.9 %collective-permute-start.2 = (bf16[2,80,128]{2,1,0:T(8,128)(2,1)S(1)}, bf16[2,80,128]{2,1,0:T(8,128)(2,1)S(1)}, u32[]{:S(2)}, u32[]{:S(2)}) collective-permute-start(bf16[2,80,128]{2,1,0:T(8,128)(2,1)S(1)} %bitcast.367), channel_id=1, source_target_pairs={{0,15},{1,0},{2,1},{3,2},{4,3},{5,4},{6,5},{7,6},{8,7},{9,8},{10,9... | collective-permute-start | bytes 122888 | tf_op jit(solution)/shard_map/ppermute | solution.py:18
  46.7 12.7 %collective-permute-start.3 = (bf16[2,80,128]{2,1,0:T(8,128)(2,1)S(1)}, bf16[2,80,128]{2,1,0:T(8,128)(2,1)S(1)}, u32[]{:S(2)}, u32[]{:S(2)}) collective-permute-start(bf16[2,80,128]{2,1,0:T(8,128)(2,1)S(1)} %bitcast.370), channel_id=1, source_target_pairs={{0,1},{1,2},{2,3},{3,4},{4,5},{5,6},{6,7},{7,8},{8,9},{9,10},{10,1... | collective-permute-start | bytes 122888 | tf_op jit(solution)/shard_map/ppermute | solution.py:18
  49.5 13.2 %all-to-all-start = ((bf16[8,3,80,128]{3,2,1,0:T(8,128)(2,1)}), bf16[8,3,80,128]{3,2,1,0:T(8,128)(2,1)S(1)}, u32[]{:S(2)}, u32[]{:S(2)}) async-start(bf16[8,3,80,128]{3,2,1,0:T(8,128)(2,1)} %bitcast.85), calls=%async_computation | async-start | bytes 983040 | tf_op jit(solution)/shard_map/all_to_all | solution.py:26
  53.0 24.7 %collective-permute-start.4 = (bf16[452,128]{1,0:T(8,128)(2,1)}, bf16[452,128]{1,0:T(8,128)(2,1)}, u32[]{:S(2)}, u32[]{:S(2)}) collective-permute-start(bf16[452,128]{1,0:T(8,128)(2,1)} %pad_maximum_fusion.6.refs_0_), channel_id=1, source_target_pairs={{0,1},{1,0},{2,3},{3,2},{4,5},{5,4},{6,7},{7,6},{8,9},{9,8},{10,11... | collective-permute-start | bytes 347144 | tf_op jit(solution)/shard_map/ppermute | solution.py:22
  63.5 11.7 %all-to-all-start.1 = ((bf16[8,2,80,128]{3,2,1,0:T(8,128)(2,1)}), bf16[8,2,80,128]{3,2,1,0:T(8,128)(2,1)}, u32[]{:S(2)}, u32[]{:S(2)}) async-start(bf16[8,2,80,128]{3,2,1,0:T(8,128)(2,1)} %bitcast.168), calls=%async_computation.1 | async-start | bytes 655360 | tf_op jit(solution)/shard_map/all_to_all | solution.py:26
  77.7 40.2 %copy-start.2 = (s32[4]{0:T(128)S(1)}, s32[4]{0:T(128)}, u32[]{:S(2)}) copy-start(s32[4]{0:T(128)} %table_ref.9) | copy-start | bytes 52
  77.7 40.8 %copy-start.7 = (bf16[1,9,128,128]{2,3,1,0:T(8,128)(2,1)S(1)}, bf16[1,9,128,128]{2,3,1,0:T(8,128)(2,1)}, u32[]{:S(2)}) copy-start(bf16[1,9,128,128]{2,3,1,0:T(8,128)(2,1)} %get-tuple-element.68) | copy-start | bytes 884740
  77.7 29.2 %all-to-all-start.2 = ((bf16[16,1,176,128]{3,2,1,0:T(8,128)(2,1)}), bf16[16,1,176,128]{3,2,1,0:T(8,128)(2,1)S(1)}, u32[]{:S(2)}, u32[]{:S(2)}) async-start(bf16[16,1,176,128]{3,2,1,0:T(8,128)(2,1)} %bitcast.322), calls=%async_computation.2 | async-start | bytes 1441792 | tf_op jit(solution)/shard_map/all_to_all | solution.py:26
  84.9 8.1 %collective-permute-start.5 = (bf16[452,128]{1,0:T(8,128)(2,1)}, bf16[452,128]{1,0:T(8,128)(2,1)S(1)}, u32[]{:S(2)}, u32[]{:S(2)}) collective-permute-start(bf16[452,128]{1,0:T(8,128)(2,1)} %shard_map.150), channel_id=1, source_target_pairs={{0,3},{1,2},{2,1},{3,0},{4,7},{5,6},{6,5},{7,4},{8,11},{9,10},{10,... | collective-permute-start | bytes 347144 | tf_op jit(solution)/shard_map/ppermute | solution.py:22
  95.4 18.5 %collective-permute-start.6 = (bf16[452,128]{1,0:T(8,128)(2,1)}, bf16[452,128]{1,0:T(8,128)(2,1)S(1)}, u32[]{:S(2)}, u32[]{:S(2)}) collective-permute-start(bf16[452,128]{1,0:T(8,128)(2,1)} %shard_map.151.refs_0_), channel_id=1, source_target_pairs={{0,4},{4,0},{8,12},{12,8},{1,5},{5,1},{9,13},{13,9},{2,6},{6,2},{1... | collective-permute-start | bytes 347144 | tf_op jit(solution)/shard_map/ppermute | solution.py:22
  104.1 33.5 %collective-permute-start.8 = (bf16[1,80,128]{2,1,0:T(8,128)(2,1)S(1)}, bf16[1,80,128]{2,1,0:T(8,128)(2,1)S(1)}, u32[]{:S(2)}, u32[]{:S(2)}) collective-permute-start(bf16[1,80,128]{2,1,0:T(8,128)(2,1)S(1)} %get-tuple-element.199), channel_id=1, source_target_pairs={{0,1},{1,2},{2,3},{3,4},{4,5},{5,6},{6,7},{7,8},{8,9},{9,10},{10,1... | collective-permute-start | bytes 61448 | tf_op jit(solution)/shard_map/ppermute | solution.py:18
  105.6 32.1 %collective-permute-start.9 = (bf16[1,80,128]{2,1,0:T(8,128)(2,1)S(1)}, bf16[1,80,128]{2,1,0:T(8,128)(2,1)S(1)}, u32[]{:S(2)}, u32[]{:S(2)}) collective-permute-start(bf16[1,80,128]{2,1,0:T(8,128)(2,1)S(1)} %get-tuple-element.200), channel_id=1, source_target_pairs={{1,0},{2,1},{3,2},{4,3},{5,4},{6,5},{7,6},{8,7},{9,8},{10,9},{11,1... | collective-permute-start | bytes 61448 | tf_op jit(solution)/shard_map/ppermute | solution.py:18
  107.0 16.8 %copy-start.10 = (bf16[176,128]{1,0:T(8,128)(2,1)}, bf16[176,128]{1,0:T(8,128)(2,1)S(1)}, u32[]{:S(2)}) copy-start(bf16[176,128]{1,0:T(8,128)(2,1)S(1)} %reduce_sum.36) | copy-start | bytes 135172
  113.9 38.0 %copy-start.14 = (bf16[452,128]{1,0:T(8,128)(2,1)}, bf16[452,128]{1,0:T(8,128)(2,1)S(1)}, u32[]{:S(2)}) copy-start(bf16[452,128]{1,0:T(8,128)(2,1)S(1)} %collective-permute-done.6.refs_1_) | copy-start | bytes 347140
  114.5 9.3 %all-to-all-start.3 = ((bf16[4,1,128,128]{3,2,1,0:T(8,128)(2,1)}), bf16[4,1,128,128]{3,2,1,0:T(8,128)(2,1)S(1)}, u32[]{:S(2)}, u32[]{:S(2)}) async-start(bf16[4,1,128,128]{3,2,1,0:T(8,128)(2,1)} %broadcast_in_dim.84), calls=%async_computation.3 | async-start | bytes 262144 | tf_op jit(solution)/shard_map/all_to_all | solution.py:26
  126.1 25.7 %all-to-all-start.4 = ((bf16[4,1,176,128]{3,2,1,0:T(8,128)(2,1)}), bf16[4,1,176,128]{3,2,1,0:T(8,128)(2,1)S(1)}, u32[]{:S(2)}, u32[]{:S(2)}) async-start(bf16[4,1,176,128]{3,2,1,0:T(8,128)(2,1)} %shard_map.153), calls=%async_computation.4 | async-start | bytes 360448 | tf_op jit(solution)/shard_map/all_to_all | solution.py:26
  152.6 9.4 %all-to-all-start.5 = ((bf16[4,1,176,128]{3,2,1,0:T(8,128)(2,1)}), bf16[4,1,176,128]{3,2,1,0:T(8,128)(2,1)S(1)}, u32[]{:S(2)}, u32[]{:S(2)}) async-start(bf16[4,1,176,128]{3,2,1,0:T(8,128)(2,1)} %broadcast_in_dim.85), calls=%async_computation.5 | async-start | bytes 360448 | tf_op jit(solution)/shard_map/all_to_all | solution.py:26
  163.0 18.5 %all-to-all-start.6 = ((bf16[4,4,1,176,128]{4,3,1,2,0:T(8,128)(2,1)}), bf16[4,4,1,176,128]{4,3,1,2,0:T(8,128)(2,1)S(1)}, u32[]{:S(2)}, u32[]{:S(2)}) async-start(bf16[4,4,1,176,128]{4,3,1,2,0:T(8,128)(2,1)} %broadcast_in_dim.87), calls=%async_computation.6 | async-start | bytes 1441792 | tf_op jit(solution)/shard_map/all_to_all | solution.py:26
  169.5 10.9 %collective-permute-start.7 = (bf16[452,128]{1,0:T(8,128)(2,1)}, bf16[452,128]{1,0:T(8,128)(2,1)S(1)}, u32[]{:S(2)}, u32[]{:S(2)}) collective-permute-start(bf16[452,128]{1,0:T(8,128)(2,1)} %shard_map.152), channel_id=1, source_target_pairs={{0,12},{4,8},{8,4},{12,0},{1,13},{5,9},{9,5},{13,1},{2,14},{6,10},... | collective-permute-start | bytes 347144 | tf_op jit(solution)/shard_map/ppermute | solution.py:22
  187.8 8.7 %all-to-all-start.8 = ((bf16[4,36,128]{2,1,0:T(8,128)(2,1)}), bf16[4,36,128]{2,1,0:T(8,128)(2,1)S(1)}, u32[]{:S(2)}, u32[]{:S(2)}) async-start(bf16[4,36,128]{2,1,0:T(8,128)(2,1)} %broadcast_in_dim.90), calls=%async_computation.8 | async-start | bytes 81920 | tf_op jit(solution)/shard_map/all_to_all | solution.py:26
  (16 other events, 69.4 us)
